TPU v7x, 32 devices: a whole 2x2x4 slice. The times are simulated.
32 devices in a mesh: parts: 2 (over y), dp: 4 (over z), tensor: 2 (over x), sub: 2 (over core).
Axes of the slice: x: 2, y: 2, z: 4, core: 2. Of those that a mesh axis runs over, the one named last changes fastest.
Arguments:
- tokens: bfloat16 [8, 8, 128, 8192], P(('parts', 'dp'), None, 'sub', 'tensor'), parts along dimension 0, may hold values from -6 to 6
- cotangent: bfloat16 [8, 8, 128, 1024], P(('parts', 'dp'), None, 'sub', 'tensor'), parts along dimension 0, may hold values from -6 to 6
- frozen_value_weight: bfloat16 [8192, 1024], P('tensor', 'dp'), may hold values from -0.0625 to 0.0625
- adapter_down: bfloat16 [8, 16, 8192], P(('parts', 'dp'), None, 'tensor'), parts along dimension 0, may hold values from -0.25 to 0.25
- adapter_up: bfloat16 [8, 16, 1024], P(('parts', 'dp'), None, 'tensor'), parts along dimension 0, may hold values from -0.375 to 0.375
- tokens_per_job: int32 [8], P('parts'), parts along dimension 0, may hold values from 1 to 1920, as said below
- packed_block_slots: int32 [8, 8], P('parts'), parts along dimension 0, may hold values from 0 to 31, as said below
Outputs:
- layer_output: bfloat16 [8, 8, 128, 1024], P(('parts', 'dp'), None, 'sub', 'tensor'), parts along dimension 0
- token_gradient: bfloat16 [8, 8, 128, 8192], P(('parts', 'dp'), None, 'sub', 'tensor'), parts along dimension 0
- grad_down: float32 [8, 16, 8192], P(('parts', 'dp'), None, 'tensor'), parts along dimension 0
- grad_up: float32 [8, 16, 1024], P(('parts', 'dp'), None, 'tensor'), parts along dimension 0
There are 2 independent parts, one for each index of `parts`. A program takes and returns all parts, laid end to end along the dimension named above; an argument that names none is the same for every part. Nothing has to cross between parts.
Inputs may be any that keep to these rules, and one draw needn't show every extreme that they name: The block counts ceil(tokens_per_job[j] / 128) add up to 32. `packed_block_slots`: A permutation of the packed slots 0 to 31. Every index of dp receives 8 blocks, and no index of dp sends more than 2 of its blocks to one index of dp.
All inputs are finite; a program needn't handle non-finite values.
Results may differ from a plain program's by a relative error of at most 0.015.
Values may be sent and summed in bfloat16 or wider, within the bound.
No kernel may reach another device: no remote copies, remote signals or barrier semaphores. Data moves between devices by JAX's collectives and lax.ppermute only.
A program may use at most 64 MiB of HBM per device.

v0:
```python
import jax
import jax.numpy as jnp
from jax import lax
from jax.sharding import PartitionSpec as P

adapter_scale = 2.0


def block_facts(tokens_per_job, block_ids, block_rows):
    job_total = tokens_per_job.shape[0]
    blocks = (tokens_per_job + (block_rows - 1)) // block_rows
    block_ends = jnp.cumsum(blocks, dtype=jnp.int32)
    starts = block_ends - blocks
    job_index = jnp.sum(
        (block_ends[None, :] <= block_ids[:, None]).astype(jnp.int32), axis=1, dtype=jnp.int32
    )
    chosen = job_index[:, None] == jnp.arange(job_total, dtype=jnp.int32)[None, :]
    job_count = jnp.sum(jnp.where(chosen, tokens_per_job[None, :], 0), axis=1, dtype=jnp.int32)
    first_block = jnp.sum(jnp.where(chosen, starts[None, :], 0), axis=1, dtype=jnp.int32)
    valid_rows = jnp.clip(job_count - block_rows * (block_ids - first_block), 0, block_rows)
    return (job_index, chosen, valid_rows)


def order_rows(values, picks, present):
    taken = jnp.take(values, picks, axis=0)
    return jnp.where(present[:, None, None], taken, jnp.zeros((), values.dtype))


def body(
    tokens,
    cotangent,
    frozen_value_weight,
    adapter_down,
    adapter_up,
    tokens_per_job,
    packed_block_slots,
):
    dp_count = lax.axis_size("dp")
    sub_count = lax.axis_size("sub")
    dp_index = lax.axis_index("dp")
    sub_index = lax.axis_index("sub")
    block_number = tokens.shape[1]
    halved_rows = tokens.shape[2]
    feature_width = tokens.shape[3]
    head_width = cotangent.shape[3]
    job_per_device = adapter_down.shape[0]
    slot_cap = -(-block_number // dp_count)
    row_count = block_number * halved_rows
    dest_group = packed_block_slots // block_number
    same_group = dest_group[:, :, None] == dest_group[:, None, :]
    positions = jnp.arange(block_number, dtype=jnp.int32)
    earlier = positions[None, None, :] < positions[None, :, None]
    send_rank = jnp.sum((same_group & earlier).astype(jnp.int32), axis=2, dtype=jnp.int32)
    own_group = lax.dynamic_index_in_dim(dest_group, dp_index, 0, keepdims=False)
    own_rank = lax.dynamic_index_in_dim(send_rank, dp_index, 0, keepdims=False)
    slot_code = own_group * slot_cap + own_rank
    slot_range = jnp.arange(dp_count * slot_cap, dtype=jnp.int32)
    slot_match = slot_code[None, :] == slot_range[:, None]
    source_pos = jnp.sum(jnp.where(slot_match, positions[None, :], 0), axis=1, dtype=jnp.int32)
    filled = jnp.any(slot_match, axis=1)
    own_blocks = tokens[0]
    flat_slots = packed_block_slots.reshape(-1)
    wanted = dp_index * block_number + positions
    slot_owner = flat_slots[None, :] == wanted[:, None]
    flat_ids = jnp.arange(dp_count * block_number, dtype=jnp.int32)
    block_ids = jnp.sum(jnp.where(slot_owner, flat_ids[None, :], 0), axis=1, dtype=jnp.int32)
    src_rank = jnp.sum(
        jnp.where(slot_owner, send_rank.reshape(-1)[None, :], 0), axis=1, dtype=jnp.int32
    )
    src_flat = block_ids // block_number * slot_cap + src_rank
    job_index, chosen, valid_rows = block_facts(tokens_per_job, block_ids, halved_rows * sub_count)
    row_pos = sub_index * halved_rows + jnp.arange(halved_rows, dtype=jnp.int32)
    row_valid_mask = (row_pos[None, :] < valid_rows[:, None]).astype(jnp.float32)
    masked_grad = jnp.where(
        row_valid_mask[:, :, None] > 0, cotangent[0], jnp.zeros((), jnp.bfloat16)
    )
    weight_full = lax.all_gather(frozen_value_weight, "dp", axis=1, tiled=True)
    down_all, up_all = (
        lax.all_gather(adapter_down, "dp", axis=0, tiled=True),
        lax.all_gather(adapter_up, "dp", axis=0, tiled=True),
    )
    selected_down = jnp.take(down_all, job_index, axis=0)
    selected_up = jnp.take(up_all, job_index, axis=0)
    incoming = lax.all_to_all(
        order_rows(own_blocks, source_pos, filled), "dp", split_axis=0, concat_axis=0, tiled=True
    )
    packed = jnp.take(incoming, src_flat, axis=0)
    partial_base = jnp.dot(
        packed.reshape(row_count, feature_width), weight_full, preferred_element_type=jnp.float32
    )
    frozen_sum = lax.psum_scatter(
        partial_base.astype(jnp.bfloat16), "tensor", scatter_dimension=1, tiled=True
    ).astype(jnp.float32)
    down_part = jnp.einsum(
        "bhf,brf->bhr", packed, selected_down, preferred_element_type=jnp.float32
    )
    back_part = jnp.einsum(
        "bhk,brk->bhr", masked_grad, selected_up, preferred_element_type=jnp.float32
    )
    down_sum = lax.psum(down_part.astype(jnp.bfloat16), "tensor")
    frozen_rows = frozen_sum.reshape(block_number, halved_rows, head_width)
    adapter_output = jnp.einsum(
        "poz,pzv->pov", down_sum, selected_up, preferred_element_type=jnp.float32
    )
    layer_output = (
        (frozen_rows + adapter_scale * adapter_output) * row_valid_mask[:, :, None]
    ).astype(jnp.bfloat16)
    back_sum = lax.psum(back_part.astype(jnp.bfloat16), "tensor")
    grad_full = lax.all_gather(masked_grad, "tensor", axis=2, tiled=True)
    frozen_gradient = lax.dot_general(
        grad_full.reshape(row_count, -1),
        weight_full,
        (((1,), (1,)), ((), ())),
        preferred_element_type=jnp.float32,
    )
    adapter_gradient = jnp.einsum(
        "jpy,jyu->jpu", back_sum, selected_down, preferred_element_type=jnp.float32
    )
    token_gradient = (
        frozen_gradient.reshape(block_number, halved_rows, feature_width)
        + adapter_scale * adapter_gradient
    ).astype(jnp.bfloat16)
    down_blocks = jnp.einsum("bhr,bhf->brf", back_sum, packed, preferred_element_type=jnp.float32)
    down_hot = chosen.astype(jnp.float32)
    up_blocks = jnp.einsum(
        "bhr,bhk->brk", down_sum, masked_grad, preferred_element_type=jnp.float32
    )
    onehot = chosen.astype(jnp.float32)
    table_down = jnp.einsum("bj,brf->jrf", down_hot, down_blocks, precision=lax.Precision.HIGHEST)
    table_up = jnp.einsum("bj,brk->jrk", onehot, up_blocks, precision=lax.Precision.HIGHEST)
    owned_down, owned_up = (
        lax.psum_scatter(
            table_down.astype(jnp.bfloat16), "dp", scatter_dimension=0, tiled=True
        ).astype(jnp.float32),
        lax.psum_scatter(
            table_up.astype(jnp.bfloat16), "dp", scatter_dimension=0, tiled=True
        ).astype(jnp.float32),
    )
    owned_down, owned_up = (
        lax.psum(owned_down.astype(jnp.bfloat16), "sub").astype(jnp.float32),
        lax.psum(owned_up.astype(jnp.bfloat16), "sub").astype(jnp.float32),
    )
    token_counts = lax.dynamic_slice_in_dim(
        tokens_per_job, dp_index * job_per_device, job_per_device
    ).astype(jnp.float32)
    scale_factor = adapter_scale / token_counts
    grad_down = owned_down * scale_factor[:, None, None]
    grad_up = owned_up * scale_factor[:, None, None]
    return (layer_output[None], token_gradient[None], grad_down, grad_up)


def solution(mesh):
    return jax.shard_map(
        body,
        mesh=mesh,
        in_specs=(
            P(("parts", "dp"), None, "sub", "tensor"),
            P(("parts", "dp"), None, "sub", "tensor"),
            P("tensor", "dp"),
            P(("parts", "dp"), None, "tensor"),
            P(("parts", "dp"), None, "tensor"),
            P("parts"),
            P("parts", None),
        ),
        out_specs=(
            P(("parts", "dp"), None, "sub", "tensor"),
            P(("parts", "dp"), None, "sub", "tensor"),
            P(("parts", "dp"), None, "tensor"),
            P(("parts", "dp"), None, "tensor"),
        ),
        check_vma=False,
    )
```

profile of v0, /device:TPU:0, one launch (start us, length us, event | category | flops | bytes accessed | tf_op | source)
XLA Modules:
  0.0 438.3 jit_solution(9346295716574525560)
XLA Ops:
  11.8 5.0 %gather_fusion.2 = bf16[8,64,4096]{2,1,0:T(8,128)(2,1)} fusion(bf16[8,64,4096]{2,1,0:T(8,128)(2,1)} %bitcast.40, s32[1024]{0:T(1024)S(1)} %pad_clamp_fusion.2), kind=kCustom, calls=%fused_computation.clone | custom fusion | bytes 8388640 | tf_op jit(solution)/shard_map/jit(_take)/gather | solution.py:25
  16.8 4.7 %select_select_fusion = bf16[8,64,4096]{2,1,0:T(8,128)(2,1)} fusion(bf16[8,64,4096]{2,1,0:T(8,128)(2,1)} %gather_fusion.2, pred[8]{0:T(512)(128)(4,1)S(1)} %compare_and_fusion.1, pred[8]{0:T(512)(128)(4,1)S(1)} %fusion.11), kind=kLoop, calls=%fused_computation.9 | loop fusion | flops 4194304 | bytes 8388624 | tf_op jit(solution)/shard_map/jit(_where)/select_n | solution.py:26
  21.5 6.4 %all-to-all-start = ((bf16[8,64,4096]{2,1,0:T(8,128)(2,1)}), bf16[8,64,4096]{2,1,0:T(8,128)(2,1)}, u32[]{:S(2)}, u32[]{:S(2)}) async-start(bf16[8,64,4096]{2,1,0:T(8,128)(2,1)} %select_select_fusion), calls=%async_computation | async-start | bytes 8388608 | tf_op jit(solution)/shard_map/all_to_all | solution.py:84
  28.0 103.7 %all_gather.13 = bf16[4,16,4096]{2,1,0:T(8,128)(2,1)S(1)} all-gather(bf16[1,16,4096]{2,1,0:T(8,128)(2,1)S(1)} %copy-done.3), channel_id=1, replica_groups=mesh['parts'=2,'dp'=4,'tensor'=2,'sub'=2] {'dp'}, dimensions={0}, use_global_device_ids=true | all-gather | bytes 655360 | tf_op jit(solution)/shard_map/all_gather | solution.py:79
  132.3 13.2 %all_gather.14 = bf16[4,16,512]{2,1,0:T(8,128)(2,1)S(1)} all-gather(bf16[1,16,512]{2,1,0:T(8,128)(2,1)S(1)} %copy-done.4), channel_id=1, replica_groups=mesh['parts'=2,'dp'=4,'tensor'=2,'sub'=2] {'dp'}, dimensions={0}, use_global_device_ids=true | all-gather | bytes 81920 | tf_op jit(solution)/shard_map/all_gather | solution.py:80
  146.6 5.0 %gather_fusion.3 = bf16[8,64,4096]{2,1,0:T(8,128)(2,1)} fusion(bf16[8,64,4096]{2,1,0:T(8,128)(2,1)} %all-to-all-done, s32[1024]{0:T(1024)S(1)} %pad_clamp_fusion.1), kind=kCustom, calls=%fused_computation.1.clone | custom fusion | bytes 8388640 | tf_op jit(solution)/shard_map/jit(_take)/gather | solution.py:87
  151.7 2.7 broadcast_select_fusion
  154.3 2.0 copy-done
  156.3 1.2 convolution_convert_fusion.4
  157.6 8.9 %all-reduce = (bf16[8,64,16]{1,2,0:T(8,128)(2,1)S(1)}, bf16[8,64,16]{1,2,0:T(8,128)(2,1)S(1)}) all-reduce(bf16[8,64,16]{1,2,0:T(8,128)(2,1)S(1)} %convolution_convert_fusion.4, bf16[8,64,16]{1,2,0:T(8,128)(2,1)S(1)} %convolution_convert_fusion.3), channel_id=1, replica_groups=mesh['parts'=2,'dp'=4,'tensor'=2,'sub'=2] {'tensor'}, use_global_device_ids=true, to_apply=%region_8.10 | all-reduce | flops 16384 | bytes 65536 | tf_op jit(solution)/shard_map/psum | solution.py:100
  166.5 2.9 fusion.24
  169.4 2.2 convolution_convert_fusion
  174.9 19.7 %reduce-scatter.6.cloned.1.call-done = bf16[1,16,4096]{2,1,0:T(8,128)(2,1)} async-done(((bf16[4,16,4096]{2,1,0:T(8,128)(2,1)}), bf16[1,16,4096]{2,1,0:T(8,128)(2,1)}) %reduce-scatter.6.cloned.1.call-update) | async-done | bytes 131088 | tf_op jit(solution)/shard_map/reduce_scatter | solution.py:132
  196.6 18.2 %reduce-scatter.8.cloned.1.call-done = bf16[1,16,512]{2,1,0:T(8,128)(2,1)} async-done(((bf16[4,16,512]{2,1,0:T(8,128)(2,1)}), bf16[1,16,512]{2,1,0:T(8,128)(2,1)}) %reduce-scatter.8.cloned.1.call-update) | async-done | bytes 16400 | tf_op jit(solution)/shard_map/reduce_scatter | solution.py:135
  214.7 4.0 psum.31
  219.4 144.4 %all-gather.3.cloned.1.call-done = bf16[4096,1024]{1,0:T(8,128)(2,1)} async-done(((bf16[4096,256]{1,0:T(8,128)(2,1)}), bf16[4096,1024]{1,0:T(8,128)(2,1)}) %all-gather.3.cloned.1.call-update) | async-done | bytes 8388624 | tf_op jit(solution)/shard_map/all_gather | solution.py:77
  363.7 10.1 %convolution_convert_fusion.1 = bf16[512,1024]{1,0:T(8,128)(2,1)} fusion(bf16[512,4096]{1,0:T(8,128)(2,1)} %bitcast.39, bf16[4096,1024]{1,0:T(8,128)(2,1)} %all-gather.3.cloned.1.call-done), kind=kOutput, calls=%fused_computation.12 | convolution fusion | flops 4295491584 | bytes 13631488 | tf_op jit(solution)/shard_map/dot_general | solution.py:88
  373.9 8.3 %all-reduce.3.cloned.1.call-done = bf16[1,16,4096]{2,1,0:T(8,128)(2,1)} async-done(((bf16[1,16,4096]{2,1,0:T(8,128)(2,1)}), bf16[1,16,4096]{2,1,0:T(8,128)(2,1)}) %all-reduce.3.cloned.1.call-update) | async-done | bytes 131088 | tf_op jit(solution)/shard_map/psum | solution.py:140
  382.1 1.6 convert_multiply_fusion
  383.8 22.9 %all-gather.5.cloned.1.call-done = bf16[8,64,1024]{2,1,0:T(8,128)(2,1)} async-done(((bf16[8,64,512]{2,1,0:T(8,128)(2,1)}), bf16[8,64,1024]{2,1,0:T(8,128)(2,1)}) %all-gather.5.cloned.1.call-update) | async-done | bytes 1048592 | tf_op jit(solution)/shard_map/all_gather | solution.py:109
  406.7 7.3 %fusion = f32[8,64,4096]{2,1,0:T(8,128)S(1)} fusion(bf16[8,64,1024]{2,1,0:T(8,128)(2,1)} %all-gather.5.cloned.1.call-done, bf16[4096,1024]{1,0:T(8,128)(2,1)} %all-gather.3.cloned.1.call-done), kind=kOutput, calls=%fused_computation.4 | convolution fusion | flops 4294967296 | bytes 17825792 | tf_op jit(solution)/shard_map/dot_general | solution.py:110
  414.0 3.3 fusion.2
  417.3 11.9 %reduce-scatter.4.cloned.1.call-done = bf16[512,512]{1,0:T(8,128)(2,1)} async-done(((bf16[512,1024]{1,0:T(8,128)(2,1)}), bf16[512,512]{1,0:T(8,128)(2,1)}) %reduce-scatter.4.cloned.1.call-update) | async-done | bytes 524304 | tf_op jit(solution)/shard_map/reduce_scatter | solution.py:91
  429.2 2.2 fusion.7
  (59 shorter events, 11.4 us)
Async XLA Ops:
  21.5 6.5 %copy-start.3 = (bf16[1,16,4096]{2,1,0:T(8,128)(2,1)S(1)}, bf16[1,16,4096]{2,1,0:T(8,128)(2,1)}, u32[]{:S(2)}) copy-start(bf16[1,16,4096]{2,1,0:T(8,128)(2,1)} %param.12) | copy-start | bytes 393220
  21.5 110.8 %copy-start.4 = (bf16[1,16,512]{2,1,0:T(8,128)(2,1)S(1)}, bf16[1,16,512]{2,1,0:T(8,128)(2,1)}, u32[]{:S(2)}) copy-start(bf16[1,16,512]{2,1,0:T(8,128)(2,1)} %param.13) | copy-start | bytes 49156
  21.5 124.7 %copy-start.2 = (bf16[1,8,64,512]{3,2,1,0:T(8,128)(2,1)S(1)}, bf16[1,8,64,512]{3,2,1,0:T(8,128)(2,1)}, u32[]{:S(2)}) copy-start(bf16[1,8,64,512]{3,2,1,0:T(8,128)(2,1)} %param.10) | copy-start | bytes 1572868
  21.5 125.1 %all-to-all-start = ((bf16[8,64,4096]{2,1,0:T(8,128)(2,1)}), bf16[8,64,4096]{2,1,0:T(8,128)(2,1)}, u32[]{:S(2)}, u32[]{:S(2)}) async-start(bf16[8,64,4096]{2,1,0:T(8,128)(2,1)} %select_select_fusion), calls=%async_computation | async-start | bytes 8388608 | tf_op jit(solution)/shard_map/all_to_all | solution.py:84
  28.0 166.7 %reduce-scatter.6.cloned.1.call-start = ((), (), s32[]{:S(2)}) async-start(), calls=%async_computation.7 | async-start | bytes 655360 | tf_op jit(solution)/shard_map/reduce_scatter | solution.py:132
  146.3 26.5 %copy-start.1 = (bf16[8,64,512]{2,1,0:T(8,128)(2,1)}, bf16[8,64,512]{2,1,0:T(8,128)(2,1)S(1)}, u32[]{:S(2)}) copy-start(bf16[8,64,512]{2,1,0:T(8,128)(2,1)S(1)} %bitcast_select_fusion) | copy-start | bytes 1572868
  154.3 2.0 copy-start
  169.4 25.9 %copy-start.5 = (s32[4]{0:T(128)S(1)}, s32[4]{0:T(128)}, u32[]{:S(2)}) copy-start(s32[4]{0:T(128)} %param.14) | copy-start | bytes 52
  172.8 42.0 %reduce-scatter.8.cloned.1.call-start = ((), (), s32[]{:S(2)}) async-start(), calls=%async_computation.9 | async-start | bytes 81920 | tf_op jit(solution)/shard_map/reduce_scatter | solution.py:135
  174.1 189.6 %all-gather.3.cloned.1.call-start = ((), (), s32[]{:S(2)}) async-start(), calls=%async_computation.4 | async-start | bytes 10485760 | tf_op jit(solution)/shard_map/all_gather | solution.py:77
  174.9 207.3 %all-reduce.3.cloned.1.call-start = ((), (), s32[]{:S(2)}) async-start(), calls=%async_computation.8 | async-start | bytes 262144 | tf_op jit(solution)/shard_map/psum | solution.py:140
  194.6 212.0 %all-gather.5.cloned.1.call-start = ((), (), s32[]{:S(2)}) async-start(), calls=%async_computation.6 | async-start | bytes 1572864 | tf_op jit(solution)/shard_map/all_gather | solution.py:109
  195.2 234.0 %reduce-scatter.4.cloned.1.call-start = ((), (), s32[]{:S(2)}) async-start(), calls=%async_computation.5 | async-start | bytes 1572864 | tf_op jit(solution)/shard_map/reduce_scatter | solution.py:91
Sparse Core Ops, SparseCore 0:
  172.9 21.6 reduce-scatter.5
  197.4 17.2 reduce-scatter.7
  216.4 147.3 all-gather.2
  366.0 16.0 all-reduce.2
  384.2 22.4 all-gather.4
  408.9 20.3 reduce-scatter.3
where the time goes:
time: 439 us; the launch traced here: 438 us
  waiting for transfers between devices  227 us (52%)
  blocking collectives  130 us (30%)
  matrix products  30.1 us (7%)
  local copies, waits for them, and re-layouts  16.5 us (4%)
  between operations  15 us (3%)
  other arithmetic  13.6 us (3%)
  starting transfers between devices  6.65 us (2%)
    all_gather x1, waiting for transfers between devices, body(): weight_full = lax.all_gather(frozen_value_weight, 'dp', axis=1, tiled=True)  144 us
    all_gather x1, blocking collectives, body(): lax.all_gather(adapter_down, 'dp', axis=0, tiled=True)  104 us
    all_gather x1, waiting for transfers between devices, body(): grad_full = lax.all_gather(masked_grad, 'tensor', axis=2, tiled=True)  22.9 us
    reduce_scatter x1, waiting for transfers between devices, body(): lax.psum_scatter(table_down.astype(jnp.bfloat16), 'dp', scatter_dimension...  19.7 us
    reduce_scatter x1, waiting for transfers between devices, body(): lax.psum_scatter(table_up.astype(jnp.bfloat16), 'dp', scatter_dimension=0...  18.2 us
    all_gather x1, blocking collectives, body(): lax.all_gather(adapter_up, 'dp', axis=0, tiled=True)  13.2 us
    reduce_scatter x1, waiting for transfers between devices, body(): lax.psum_scatter(partial_base.astype(jnp.bfloat16), 'tensor', scatter_dim...  11.9 us
    dot_general x1, matrix products, body(): jnp.dot(packed.reshape(row_count, feature_width), weight_full, preferred_...  10.1 us
  transfers between devices with their start and end apart: 7, of which 6 were waited for; matrix products, arithmetic and copies ran while one was open for 6% of the time, Pallas kernels for 0%

commit v1 on v0

v1 whole, which is shorter than its diff:
```python
import jax
import jax.numpy as jnp
from jax import lax
from jax.sharding import PartitionSpec as P

adapter_scale = 2.0


def block_facts(tokens_per_job, block_ids, block_rows):
    job_total = tokens_per_job.shape[0]
    blocks = (tokens_per_job + (block_rows - 1)) // block_rows
    block_ends = jnp.cumsum(blocks, dtype=jnp.int32)
    starts = block_ends - blocks
    job_index = jnp.sum(
        (block_ends[None, :] <= block_ids[:, None]).astype(jnp.int32), axis=1, dtype=jnp.int32
    )
    chosen = job_index[:, None] == jnp.arange(job_total, dtype=jnp.int32)[None, :]
    job_count = jnp.sum(jnp.where(chosen, tokens_per_job[None, :], 0), axis=1, dtype=jnp.int32)
    first_block = jnp.sum(jnp.where(chosen, starts[None, :], 0), axis=1, dtype=jnp.int32)
    valid_rows = jnp.clip(job_count - block_rows * (block_ids - first_block), 0, block_rows)
    return job_index, valid_rows


def shifted(values, axis, count, step):
    if step % count == 0:
        return values
    return lax.ppermute(values, axis, [(i, (i + step) % count) for i in range(count)])


def gather_shifts(values, axis, count):
    return [shifted(values, axis, count, d) for d in range(count)]


def body(
    tokens,
    cotangent,
    frozen_value_weight,
    adapter_down,
    adapter_up,
    tokens_per_job,
    packed_block_slots,
):
    nd, nt, ns, np_ = (lax.axis_size(a) for a in ("dp", "tensor", "sub", "parts"))
    z, t, s, p = (lax.axis_index(a) for a in ("dp", "tensor", "sub", "parts"))
    blocks, halved, width = tokens.shape[1:]
    heads = cotangent.shape[3]
    jobs_dev, rank, _ = adapter_down.shape
    cap = -(-blocks // nd)
    rows = blocks * halved
    f32, bf16, i32 = jnp.float32, jnp.bfloat16, jnp.int32

    quarter = width // (np_ * ns)
    own_quarter = lax.dynamic_slice_in_dim(
        frozen_value_weight, (p * ns + s) * quarter, quarter, axis=0
    )
    weight_all = lax.all_gather(own_quarter, ("dp", "parts", "sub"), axis=0, tiled=True)
    weight_all = weight_all.reshape(nd, width, -1)

    grad_rel = gather_shifts(cotangent[0], "tensor", nt)
    up_rel = jnp.concatenate(gather_shifts(adapter_up, "tensor", nt), axis=2)
    maps = jnp.concatenate([adapter_down, up_rel], axis=2)
    maps = jnp.concatenate(gather_shifts(maps, "dp", nd), axis=0).reshape(nd * jobs_dev * rank, -1)
    down_cat, up_cat = maps[:, :width], maps[:, width:]

    positions = jnp.arange(blocks, dtype=i32)
    dest = packed_block_slots // blocks
    same = dest[:, :, None] == dest[:, None, :]
    earlier = positions[None, None, :] < positions[None, :, None]
    send_rank = jnp.sum((same & earlier).astype(i32), axis=2, dtype=i32)
    flat_slots = packed_block_slots.reshape(-1)
    flat_ids = jnp.arange(nd * blocks, dtype=i32)
    slot_owner = flat_slots[None, :] == (z * blocks + positions)[:, None]
    block_ids = jnp.sum(jnp.where(slot_owner, flat_ids[None, :], 0), axis=1, dtype=i32)
    in_rank = jnp.sum(jnp.where(slot_owner, send_rank.reshape(-1)[None, :], 0), axis=1, dtype=i32)
    in_slot = (z - block_ids // blocks) % nd * cap + in_rank
    own_dest = lax.dynamic_index_in_dim(dest, z, 0, keepdims=False)
    own_rank = lax.dynamic_index_in_dim(send_rank, z, 0, keepdims=False)
    out_slot = (own_dest - z) % nd * cap + own_rank

    slot_range = jnp.arange(nd * cap, dtype=i32)

    def positions_of(slots):
        match = slots[None, :] == slot_range[:, None]
        return jnp.sum(jnp.where(match, positions[None, :], 0), axis=1, dtype=i32), jnp.any(match, axis=1)

    out_pos, out_filled = positions_of(out_slot)
    in_pos, in_filled = positions_of(in_slot)

    def exchange(values, picks, filled, back, direction):
        ordered = jnp.where(filled[:, None, None], jnp.take(values, picks, axis=0), 0).astype(values.dtype)
        ordered = ordered.reshape(nd, cap, *values.shape[1:])
        got = [shifted(ordered[d], "dp", nd, direction * d) for d in range(nd)]
        return jnp.take(jnp.concatenate(got, axis=0), back, axis=0)

    def facts(ids):
        job, valid = block_facts(tokens_per_job, ids, halved * ns)
        row = s * halved + jnp.arange(halved, dtype=i32)
        mask = row[None, :] < valid[:, None]
        rel = (z - job // jobs_dev) % nd * jobs_dev + job % jobs_dev
        hot = rel[:, None] == jnp.arange(nd * jobs_dev, dtype=i32)[None, :]
        return mask, hot

    out_mask, out_hot = facts(z * blocks + positions)
    in_mask, in_hot = facts(block_ids)

    def pick(wide, hot):
        wide = wide.reshape(blocks, halved, nd * jobs_dev, rank)
        return jnp.sum(jnp.where(hot[:, None, :, None], wide, 0.0), axis=2)

    def spread(narrow, hot):
        wide = jnp.where(hot[:, None, :, None], narrow[:, :, None, :], 0).astype(narrow.dtype)
        return wide.reshape(rows, nd * jobs_dev * rank)

    def dot(a, b, dims):
        return lax.dot_general(a, b, (dims, ((), ())), preferred_element_type=f32)

    grad_rel_cat = jnp.concatenate(grad_rel, axis=2)
    grad_rel_cat = jnp.where(in_mask[:, :, None], grad_rel_cat, 0).astype(bf16).reshape(rows, -1)
    own_grad = grad_rel_cat[:, :heads]
    back_sum = pick(dot(grad_rel_cat, up_cat, ((1,), (1,))), in_hot).astype(bf16)
    back_wide = spread(back_sum, in_hot)

    own_tokens = tokens[0].reshape(rows, width)
    down_part = pick(dot(own_tokens, down_cat, ((1,), (1,))), out_hot).astype(bf16)
    down_parts = gather_shifts(down_part, "tensor", nt)
    down_sum = sum(x.astype(f32) for x in down_parts).astype(bf16)
    down_wide = spread(down_sum, out_hot)

    back_at_tokens = exchange(back_sum, in_pos, in_filled, out_slot, -1)
    down_at_grad = exchange(down_sum, out_pos, out_filled, in_slot, 1)
    table_down = dot(spread(back_at_tokens, out_hot), own_tokens, ((0,), (0,)))
    table_up = dot(spread(down_at_grad, in_hot), own_grad, ((0,), (0,)))
    table = jnp.concatenate([table_down, table_up], axis=1).reshape(nd * jobs_dev, ns, rank // ns, -1)

    def half(index):
        return lax.dynamic_index_in_dim(table, index, 1, keepdims=False)

    summed = half(s)
    for d in range(1, ns):
        summed = summed + shifted(half((s + d) % ns), "sub", ns, d)
    summed = summed.reshape(nd, jobs_dev, rank // ns, -1)
    total = summed[0].astype(bf16).astype(f32)
    for d in range(1, nd):
        total = total + shifted(summed[d].astype(bf16), "dp", nd, -d).astype(f32)
    halves = jnp.stack(gather_shifts(total, "sub", ns), axis=1)
    order = (s - jnp.arange(ns, dtype=i32)) % ns
    owned = jnp.take(halves, order, axis=1).reshape(jobs_dev, rank, -1)
    counts = lax.dynamic_slice_in_dim(tokens_per_job, z * jobs_dev, jobs_dev).astype(f32)
    owned = owned * (adapter_scale / counts)[:, None, None]
    grad_down, grad_up = owned[:, :, :width], owned[:, :, width:]

    base = jnp.concatenate([dot(own_tokens, weight_all[i], ((1,), (0,))).astype(bf16) for i in range(nd)], axis=1)
    base = base.reshape(rows, nt, heads)
    frozen = lax.dynamic_index_in_dim(base, t, 1, keepdims=False).astype(f32)
    for d in range(1, nt):
        frozen = frozen + shifted(
            lax.dynamic_index_in_dim(base, (t + d) % nt, 1, keepdims=False), "tensor", nt, d
        ).astype(f32)
    adapter_out = dot(down_wide, up_cat[:, :heads], ((1,), (0,)))
    layer = (frozen + adapter_scale * adapter_out).reshape(blocks, halved, heads)
    layer = jnp.where(out_mask[:, :, None], layer, 0.0).astype(bf16)
    layer_output = exchange(layer, out_pos, out_filled, in_slot, 1)

    grad_abs = jnp.take(
        grad_rel_cat.reshape(rows, nt, heads), (t - jnp.arange(nt, dtype=i32)) % nt, axis=1
    ).reshape(rows, nd, -1)
    gradient = adapter_scale * dot(back_wide, down_cat, ((1,), (0,)))
    for i in range(nd):
        gradient = gradient + dot(grad_abs[:, i], weight_all[i], ((1,), (1,)))
    token_gradient = gradient.astype(bf16).reshape(blocks, halved, width)
    return layer_output[None], token_gradient[None], grad_down, grad_up


def solution(mesh):
    return jax.shard_map(
        body,
        mesh=mesh,
        in_specs=(
            P(("parts", "dp"), None, "sub", "tensor"),
            P(("parts", "dp"), None, "sub", "tensor"),
            P("tensor", "dp"),
            P(("parts", "dp"), None, "tensor"),
            P(("parts", "dp"), None, "tensor"),
            P("parts"),
            P("parts", None),
        ),
        out_specs=(
            P(("parts", "dp"), None, "sub", "tensor"),
            P(("parts", "dp"), None, "sub", "tensor"),
            P(("parts", "dp"), None, "tensor"),
            P(("parts", "dp"), None, "tensor"),
        ),
        check_vma=False,
    )
```

time: 439 us -> 177 us (0.40)
  waiting for transfers between devices: 227 us -> 42.4 us
  blocking collectives: 130 us -> 0 us
  matrix products: 30.1 us -> 58 us
  starting transfers between devices: 6.65 us -> 28.1 us
    all_gather x2 -> x1, waiting for transfers between devices: 167 us -> 0.01 us  [body(): lax.all_gather(own_quarter, ('dp', 'parts', 'sub'), axis=0, tiled=True)]
    all_gather x2 -> x0, blocking collectives: 117 us -> none  [the longest x1 104 us: body(): lax.all_gather(adapter_down, 'dp', axis=0, tiled=True)]
    reduce_scatter x3 -> x0, waiting for transfers between devices: 49.8 us -> none  [the longest x1 19.7 us: body(): lax.psum_scatter(table_down.astype(jnp.bfloat16), 'dp', scatter_dimension...]
    ppermute x0 -> x21, waiting for transfers between devices: none -> 42.4 us  [shifted(): lax.ppermute(values, axis, [(i, (i + step) % count) for i in range(count)])]
    ppermute x0 -> x21, starting transfers between devices: none -> 28.1 us  [shifted(): lax.ppermute(values, axis, [(i, (i + step) % count) for i in range(count)])]
    dot_general x10 -> x14, matrix products: 30.1 us -> 58 us  [dot(): return lax.dot_general(a, b, (dims, ((), ())), preferred_element_type=f32)]
    psum x2 -> x0, blocking collectives: 12.9 us -> none  [the longest x1 8.92 us: body(): down_sum = lax.psum(down_part.astype(jnp.bfloat16), 'tensor')]
    psum x1 -> x0, waiting for transfers between devices: 8.26 us -> none  [body(): lax.psum(owned_down.astype(jnp.bfloat16), 'sub').astype(jnp.float32)]
  transfers between devices with their start and end apart: 7 -> 22, of which waited for: 6 -> 11; matrix products, arithmetic and copies ran while one was open for 6% -> 42% of each run, Pallas kernels for 0% -> 0%
where the time goes in v1:
time: 177 us; the launch traced here: 176 us
  matrix products  58 us (33%)
  waiting for transfers between devices  42.4 us (24%)
  starting transfers between devices  28.1 us (16%)
  local copies, waits for them, and re-layouts  19.7 us (11%)
  between operations  15.4 us (9%)
  other arithmetic  12.8 us (7%)
    dot_general x14, matrix products, dot(): return lax.dot_general(a, b, (dims, ((), ())), preferred_element_type=f32)  58 us
    ppermute x21, waiting for transfers between devices, shifted(): lax.ppermute(values, axis, [(i, (i + step) % count) for i in range(count)])  42.4 us
    ppermute x21, starting transfers between devices, shifted(): lax.ppermute(values, axis, [(i, (i + step) % count) for i in range(count)])  28.1 us
  transfers between devices with their start and end apart: 22, of which 11 were waited for; matrix products, arithmetic and copies ran while one was open for 42% of the time, Pallas kernels for 0%

profile of v1, /device:TPU:0, one launch (start us, length us, event | category | flops | bytes accessed | tf_op | source)
XLA Modules:
  0.0 176.4 jit_solution(14342930700915554639)
XLA Ops:
  7.2 3.0 %collective-permute-start.1 = (bf16[1,16,512]{2,1,0:T(8,128)(2,1)}, bf16[1,16,512]{2,1,0:T(8,128)(2,1)S(1)}, u32[]{:S(2)}, u32[]{:S(2)}) collective-permute-start(bf16[1,16,512]{2,1,0:T(8,128)(2,1)} %param.15), channel_id=1, source_target_pairs={{0,2},{2,0},{1,3},{3,1},{4,6},{6,4},{5,7},{7,5},{8,10},{10,8},{9,1... | collective-permute-start | bytes 49160 | tf_op jit(solution)/shard_map/ppermute | solution.py:27
  19.9 3.7 %collective-permute-start.4 = (bf16[1,16,5120]{2,1,0:T(8,128)(2,1)S(1)}, bf16[1,16,5120]{2,1,0:T(8,128)(2,1)S(1)}, u32[]{:S(2)}, u32[]{:S(2)}) collective-permute-start(bf16[1,16,5120]{2,1,0:T(8,128)(2,1)S(1)} %constant_dynamic-update-slice_fusion), channel_id=1, source_target_pairs={{0,12},{4,0},{8,4},{12,8},{1,13},{5,1},{9,5},{13,9},{2,14},{6,2},{... | collective-permute-start | bytes 491528 | tf_op jit(solution)/shard_map/ppermute | solution.py:27
  24.6 7.0 %collective-permute-done.4 = bf16[1,16,5120]{2,1,0:T(8,128)(2,1)S(1)} collective-permute-done((bf16[1,16,5120]{2,1,0:T(8,128)(2,1)S(1)}, bf16[1,16,5120]{2,1,0:T(8,128)(2,1)S(1)}, u32[]{:S(2)}, u32[]{:S(2)}) %collective-permute-start.4) | collective-permute-done | bytes 163872 | tf_op jit(solution)/shard_map/ppermute | solution.py:27
  31.6 18.4 %collective-permute-done.3 = bf16[1,16,5120]{2,1,0:T(8,128)(2,1)S(1)} collective-permute-done((bf16[1,16,5120]{2,1,0:T(8,128)(2,1)S(1)}, bf16[1,16,5120]{2,1,0:T(8,128)(2,1)S(1)}, u32[]{:S(2)}, u32[]{:S(2)}) %collective-permute-start.3) | collective-permute-done | bytes 163872 | tf_op jit(solution)/shard_map/ppermute | solution.py:27
  50.1 3.6 %convolution_bitcast_fusion = f32[512,64]{0,1:T(8,128)S(1)} fusion(bf16[512,4096]{1,0:T(8,128)(2,1)} %bitcast.115, bf16[64,5120]{1,0:T(8,128)(2,1)S(1)} %bitcast.121), kind=kOutput, calls=%fused_computation.37 | convolution fusion | flops 268435456 | bytes 4849664 | tf_op jit(solution)/shard_map/dot_general | solution.py:115
  54.1 3.8 %collective-permute-done.5 = bf16[8,64,16]{1,2,0:T(8,128)(2,1)S(1)} collective-permute-done((bf16[8,64,16]{1,2,0:T(8,128)(2,1)S(1)}, bf16[8,64,16]{1,2,0:T(8,128)(2,1)S(1)}, u32[]{:S(2)}, u32[]{:S(2)}) %collective-permute-start.5) | collective-permute-done | bytes 16416 | tf_op jit(solution)/shard_map/ppermute | solution.py:27
  58.7 5.5 %collective-permute-start.14 = (bf16[2,64,16]{1,2,0:T(8,128)(2,1)S(1)}, bf16[2,64,16]{1,2,0:T(8,128)(2,1)S(1)}, u32[]{:S(2)}, u32[]{:S(2)}) collective-permute-start(bf16[2,64,16]{1,2,0:T(8,128)(2,1)S(1)} %get-tuple-element.33), channel_id=1, source_target_pairs={{0,8},{4,12},{8,0},{12,4},{1,9},{5,13},{9,1},{13,5},{2,10},{6,14},... | collective-permute-start | bytes 12296 | tf_op jit(solution)/shard_map/ppermute | solution.py:27
  64.2 1.9 %collective-permute-start.13 = (bf16[2,64,16]{1,2,0:T(8,128)(2,1)S(1)}, bf16[2,64,16]{1,2,0:T(8,128)(2,1)S(1)}, u32[]{:S(2)}, u32[]{:S(2)}) collective-permute-start(bf16[2,64,16]{1,2,0:T(8,128)(2,1)S(1)} %get-tuple-element.34), channel_id=1, source_target_pairs={{0,4},{4,8},{8,12},{12,0},{1,5},{5,9},{9,13},{13,1},{2,6},{6,10},{... | collective-permute-start | bytes 12296 | tf_op jit(solution)/shard_map/ppermute | solution.py:27
  66.5 3.4 %collective-permute-done.13 = bf16[2,64,16]{1,2,0:T(8,128)(2,1)S(1)} collective-permute-done((bf16[2,64,16]{1,2,0:T(8,128)(2,1)S(1)}, bf16[2,64,16]{1,2,0:T(8,128)(2,1)S(1)}, u32[]{:S(2)}, u32[]{:S(2)}) %collective-permute-start.13) | collective-permute-done | bytes 4128 | tf_op jit(solution)/shard_map/ppermute | solution.py:27
  72.1 2.3 %collective-permute-start.11 = (bf16[2,64,16]{1,2,0:T(8,128)(2,1)S(1)}, bf16[2,64,16]{1,2,0:T(8,128)(2,1)S(1)}, u32[]{:S(2)}, u32[]{:S(2)}) collective-permute-start(bf16[2,64,16]{1,2,0:T(8,128)(2,1)S(1)} %get-tuple-element.29), channel_id=1, source_target_pairs={{0,8},{4,12},{8,0},{12,4},{1,9},{5,13},{9,1},{13,5},{2,10},{6,14},... | collective-permute-start | bytes 12296 | tf_op jit(solution)/shard_map/ppermute | solution.py:27
  74.3 1.8 %collective-permute-start.10 = (bf16[2,64,16]{1,2,0:T(8,128)(2,1)S(1)}, bf16[2,64,16]{1,2,0:T(8,128)(2,1)S(1)}, u32[]{:S(2)}, u32[]{:S(2)}) collective-permute-start(bf16[2,64,16]{1,2,0:T(8,128)(2,1)S(1)} %get-tuple-element.30), channel_id=1, source_target_pairs={{0,12},{4,0},{8,4},{12,8},{1,13},{5,1},{9,5},{13,9},{2,14},{6,2},{... | collective-permute-start | bytes 12296 | tf_op jit(solution)/shard_map/ppermute | solution.py:27
  80.5 3.0 %fusion.91 = f32[64,4096]{1,0:T(8,128)S(1)} fusion(bf16[512,64]{0,1:T(8,128)(2,1)S(1)} %select_n.341, bf16[512,4096]{1,0:T(8,128)(2,1)} %bitcast.116), kind=kOutput, calls=%fused_computation.212 | convolution fusion | flops 268435456 | bytes 5308416 | tf_op jit(solution)/shard_map/dot_general | solution.py:115
  86.5 2.3 %pad_maximum_fusion.2 = bf16[8,64,1024]{2,1,0:T(8,128)(2,1)} fusion(bf16[8,64,512]{2,1,0:T(8,128)(2,1)} %copy-done.5, bf16[8,64,512]{2,1,0:T(8,128)(2,1)} %bitcast.135), kind=kLoop, calls=%fused_computation.39 | loop fusion | flops 2097152 | bytes 2097152 | tf_op jit(solution)/shard_map/concatenate | solution.py:117
  88.8 2.7 %concatenate.46 = bf16[512,2,512]{2,1,0:T(2,128)(2,1)} reshape(bf16[8,64,1024]{2,1,0:T(8,128)(2,1)} %pad_maximum_fusion.2) | data formatting | bytes 2097152 | tf_op jit(solution)/shard_map/concatenate | solution.py:117
  92.1 2.6 %collective-permute-start.17 = (bf16[1,8,4608]{2,1,0:T(8,128)(2,1)}, bf16[1,8,4608]{2,1,0:T(8,128)(2,1)S(1)}, u32[]{:S(2)}, u32[]{:S(2)}) collective-permute-start(bf16[1,8,4608]{2,1,0:T(8,128)(2,1)} %get-tuple-element.24), channel_id=1, source_target_pairs={{0,12},{4,0},{8,4},{12,8},{1,13},{5,1},{9,5},{13,9},{2,14},{6,2},{... | collective-permute-start | bytes 221192 | tf_op jit(solution)/shard_map/ppermute | solution.py:27
  100.3 2.9 %collective-permute-done.19 = bf16[1,8,4608]{2,1,0:T(8,128)(2,1)S(1)} collective-permute-done((bf16[1,8,4608]{2,1,0:T(8,128)(2,1)S(1)}, bf16[1,8,4608]{2,1,0:T(8,128)(2,1)S(1)}, u32[]{:S(2)}, u32[]{:S(2)}) %collective-permute-start.19) | collective-permute-done | bytes 73760 | tf_op jit(solution)/shard_map/ppermute | solution.py:27
  103.8 2.2 %collective-permute-done.18 = bf16[1,8,4608]{2,1,0:T(8,128)(2,1)} collective-permute-done((bf16[1,8,4608]{2,1,0:T(8,128)(2,1)S(1)}, bf16[1,8,4608]{2,1,0:T(8,128)(2,1)}, u32[]{:S(2)}, u32[]{:S(2)}) %collective-permute-start.18) | collective-permute-done | bytes 73760 | tf_op jit(solution)/shard_map/ppermute | solution.py:27
  110.5 4.3 %fusion.28 = bf16[512,256]{0,1:T(8,128)(2,1)S(1)} fusion(bf16[512,4096]{1,0:T(8,128)(2,1)} %bitcast.117, bf16[16384,256]{1,0:T(8,128)(2,1)} %all-gather.2.cloned.1.call-done), kind=kOutput, calls=%fused_computation.31 | convolution fusion | flops 1073872896 | bytes 6553600 | tf_op jit(solution)/shard_map/dot_general | solution.py:115
  114.8 3.6 %fusion.31 = bf16[512,256]{0,1:T(8,128)(2,1)S(1)} fusion(bf16[512,4096]{1,0:T(8,128)(2,1)S(1)} %bitcast.118, bf16[16384,256]{1,0:T(8,128)(2,1)} %all-gather.2.cloned.1.call-done), kind=kOutput, calls=%fused_computation.32 | convolution fusion | flops 1073872896 | bytes 6553600 | tf_op jit(solution)/shard_map/dot_general | solution.py:115
  124.8 6.1 %fusion = f32[512,4096]{1,0:T(8,128)} fusion(bf16[16384,256]{1,0:T(8,128)(2,1)} %all-gather.2.cloned.1.call-done, bf16[512,4,256]{0,2,1:T(8,128)(2,1)S(1)} %broadcast_select_fusion), kind=kOutput, calls=%fused_computation.9 | convolution fusion | flops 1073741824 | bytes 10747904 | tf_op jit(solution)/shard_map/dot_general | solution.py:115
  130.9 6.1 %fusion.4 = f32[512,4096]{1,0:T(8,128)} fusion(bf16[16384,256]{1,0:T(8,128)(2,1)} %all-gather.2.cloned.1.call-done, bf16[512,4,256]{0,2,1:T(8,128)(2,1)S(1)} %broadcast_select_fusion), kind=kOutput, calls=%fused_computation.13 | convolution fusion | flops 1073741824 | bytes 10747904 | tf_op jit(solution)/shard_map/dot_general | solution.py:115
  137.0 6.1 %fusion.8 = f32[512,4096]{1,0:T(8,128)} fusion(bf16[16384,256]{1,0:T(8,128)(2,1)} %all-gather.2.cloned.1.call-done, bf16[512,4,256]{0,2,1:T(8,128)(2,1)S(1)} %broadcast_select_fusion), kind=kOutput, calls=%fused_computation.17 | convolution fusion | flops 1073741824 | bytes 10747904 | tf_op jit(solution)/shard_map/dot_general | solution.py:115
  143.3 6.1 %fusion.12 = f32[512,4096]{1,0:T(8,128)} fusion(bf16[16384,256]{1,0:T(8,128)(2,1)} %all-gather.2.cloned.1.call-done, bf16[512,4,256]{0,2,1:T(8,128)(2,1)S(1)} %broadcast_select_fusion), kind=kOutput, calls=%fused_computation.21 | convolution fusion | flops 1073741824 | bytes 10747904 | tf_op jit(solution)/shard_map/dot_general | solution.py:115
  153.9 14.0 %add_convert_fusion = bf16[512,4096]{1,0:T(8,128)(2,1)} fusion(f32[512,4096]{1,0:T(8,128)} %fusion, f32[512,4096]{1,0:T(8,128)} %fusion.4, f32[512,4096]{1,0:T(8,128)} %fusion.8, f32[512,4096]{1,0:T(8,128)} %fusion.12, bf16[512,64]{0,1:T(8,128)(2,1)S(1)} %select_n.328, bf16[64,5120]{1,0:T(8,128)(2,1)S(1)} %bitcast.124), kind=kOutput, calls=%fused_computation.8 | convolution fusion | flops 281018368 | bytes 38338560 | tf_op jit(solution)/shard_map/dot_general | solution.py:115
  (176 shorter events, 44.7 us)
Async XLA Ops:
  7.2 103.3 %all-gather.2.cloned.1.call-start = ((), (), s32[]{:S(2)}) async-start(), calls=%async_computation | async-start | bytes 8912896 | tf_op jit(solution)/shard_map/all_gather | solution.py:56
  7.2 12.7 %collective-permute-start.1 = (bf16[1,16,512]{2,1,0:T(8,128)(2,1)}, bf16[1,16,512]{2,1,0:T(8,128)(2,1)S(1)}, u32[]{:S(2)}, u32[]{:S(2)}) collective-permute-start(bf16[1,16,512]{2,1,0:T(8,128)(2,1)} %param.15), channel_id=1, source_target_pairs={{0,2},{2,0},{1,3},{3,1},{4,6},{6,4},{5,7},{7,5},{8,10},{10,8},{9,1... | collective-permute-start | bytes 49160 | tf_op jit(solution)/shard_map/ppermute | solution.py:27
  11.1 59.5 %collective-permute-start.9 = (bf16[8,64,512]{2,1,0:T(8,128)(2,1)}, bf16[8,64,512]{2,1,0:T(8,128)(2,1)S(1)}, u32[]{:S(2)}, u32[]{:S(2)}) collective-permute-start(bf16[8,64,512]{2,1,0:T(8,128)(2,1)} %bitcast.134), channel_id=1, source_target_pairs={{0,2},{2,0},{1,3},{3,1},{4,6},{6,4},{5,7},{7,5},{8,10},{10,8},{9,1... | collective-permute-start | bytes 1572872 | tf_op jit(solution)/shard_map/ppermute | solution.py:27
  14.6 55.9 %copy-start.7 = (pred[8]{0:T(512)(128)(4,1)}, pred[8]{0:T(512)(128)(4,1)S(1)}, u32[]{:S(2)}) copy-start(pred[8]{0:T(512)(128)(4,1)S(1)} %get-tuple-element.16) | copy-start | bytes 28
  15.8 54.8 %copy-start.4 = (bf16[1,8,64,512]{3,2,1,0:T(8,128)(2,1)S(1)}, bf16[1,8,64,512]{3,2,1,0:T(8,128)(2,1)}, u32[]{:S(2)}) copy-start(bf16[1,8,64,512]{3,2,1,0:T(8,128)(2,1)} %param.12) | copy-start | bytes 1572868
  19.9 11.7 %collective-permute-start.4 = (bf16[1,16,5120]{2,1,0:T(8,128)(2,1)S(1)}, bf16[1,16,5120]{2,1,0:T(8,128)(2,1)S(1)}, u32[]{:S(2)}, u32[]{:S(2)}) collective-permute-start(bf16[1,16,5120]{2,1,0:T(8,128)(2,1)S(1)} %constant_dynamic-update-slice_fusion), channel_id=1, source_target_pairs={{0,12},{4,0},{8,4},{12,8},{1,13},{5,1},{9,5},{13,9},{2,14},{6,2},{... | collective-permute-start | bytes 491528 | tf_op jit(solution)/shard_map/ppermute | solution.py:27
  23.6 26.5 %collective-permute-start.3 = (bf16[1,16,5120]{2,1,0:T(8,128)(2,1)S(1)}, bf16[1,16,5120]{2,1,0:T(8,128)(2,1)S(1)}, u32[]{:S(2)}, u32[]{:S(2)}) collective-permute-start(bf16[1,16,5120]{2,1,0:T(8,128)(2,1)S(1)} %constant_dynamic-update-slice_fusion), channel_id=1, source_target_pairs={{0,8},{4,12},{8,0},{12,4},{1,9},{5,13},{9,1},{13,5},{2,10},{6,14},... | collective-permute-start | bytes 491528 | tf_op jit(solution)/shard_map/ppermute | solution.py:27
  23.6 26.5 %collective-permute-start.2 = (bf16[1,16,5120]{2,1,0:T(8,128)(2,1)S(1)}, bf16[1,16,5120]{2,1,0:T(8,128)(2,1)S(1)}, u32[]{:S(2)}, u32[]{:S(2)}) collective-permute-start(bf16[1,16,5120]{2,1,0:T(8,128)(2,1)S(1)} %constant_dynamic-update-slice_fusion), channel_id=1, source_target_pairs={{0,4},{4,8},{8,12},{12,0},{1,5},{5,9},{9,13},{13,1},{2,6},{6,10},{... | collective-permute-start | bytes 491528 | tf_op jit(solution)/shard_map/ppermute | solution.py:27
  53.9 4.0 %collective-permute-start.5 = (bf16[8,64,16]{1,2,0:T(8,128)(2,1)S(1)}, bf16[8,64,16]{1,2,0:T(8,128)(2,1)S(1)}, u32[]{:S(2)}, u32[]{:S(2)}) collective-permute-start(bf16[8,64,16]{1,2,0:T(8,128)(2,1)S(1)} %fusion.56), channel_id=1, source_target_pairs={{0,2},{2,0},{1,3},{3,1},{4,6},{6,4},{5,7},{7,5},{8,10},{10,8},{9,1... | collective-permute-start | bytes 49160 | tf_op jit(solution)/shard_map/ppermute | solution.py:27
  58.6 7.9 %collective-permute-start.15 = (bf16[2,64,16]{1,2,0:T(8,128)(2,1)S(1)}, bf16[2,64,16]{1,2,0:T(8,128)(2,1)S(1)}, u32[]{:S(2)}, u32[]{:S(2)}) collective-permute-start(bf16[2,64,16]{1,2,0:T(8,128)(2,1)S(1)} %get-tuple-element.32), channel_id=1, source_target_pairs={{0,12},{4,0},{8,4},{12,8},{1,13},{5,1},{9,5},{13,9},{2,14},{6,2},{... | collective-permute-start | bytes 12296 | tf_op jit(solution)/shard_map/ppermute | solution.py:27
  58.7 7.9 %collective-permute-start.14 = (bf16[2,64,16]{1,2,0:T(8,128)(2,1)S(1)}, bf16[2,64,16]{1,2,0:T(8,128)(2,1)S(1)}, u32[]{:S(2)}, u32[]{:S(2)}) collective-permute-start(bf16[2,64,16]{1,2,0:T(8,128)(2,1)S(1)} %get-tuple-element.33), channel_id=1, source_target_pairs={{0,8},{4,12},{8,0},{12,4},{1,9},{5,13},{9,1},{13,5},{2,10},{6,14},... | collective-permute-start | bytes 12296 | tf_op jit(solution)/shard_map/ppermute | solution.py:27
  64.2 5.7 %collective-permute-start.13 = (bf16[2,64,16]{1,2,0:T(8,128)(2,1)S(1)}, bf16[2,64,16]{1,2,0:T(8,128)(2,1)S(1)}, u32[]{:S(2)}, u32[]{:S(2)}) collective-permute-start(bf16[2,64,16]{1,2,0:T(8,128)(2,1)S(1)} %get-tuple-element.34), channel_id=1, source_target_pairs={{0,4},{4,8},{8,12},{12,0},{1,5},{5,9},{9,13},{13,1},{2,6},{6,10},{... | collective-permute-start | bytes 12296 | tf_op jit(solution)/shard_map/ppermute | solution.py:27
  72.0 5.7 %collective-permute-start.12 = (bf16[2,64,16]{1,2,0:T(8,128)(2,1)S(1)}, bf16[2,64,16]{1,2,0:T(8,128)(2,1)S(1)}, u32[]{:S(2)}, u32[]{:S(2)}) collective-permute-start(bf16[2,64,16]{1,2,0:T(8,128)(2,1)S(1)} %get-tuple-element.28), channel_id=1, source_target_pairs={{0,4},{4,8},{8,12},{12,0},{1,5},{5,9},{9,13},{13,1},{2,6},{6,10},{... | collective-permute-start | bytes 12296 | tf_op jit(solution)/shard_map/ppermute | solution.py:27
  72.1 5.9 %collective-permute-start.11 = (bf16[2,64,16]{1,2,0:T(8,128)(2,1)S(1)}, bf16[2,64,16]{1,2,0:T(8,128)(2,1)S(1)}, u32[]{:S(2)}, u32[]{:S(2)}) collective-permute-start(bf16[2,64,16]{1,2,0:T(8,128)(2,1)S(1)} %get-tuple-element.29), channel_id=1, source_target_pairs={{0,8},{4,12},{8,0},{12,4},{1,9},{5,13},{9,1},{13,5},{2,10},{6,14},... | collective-permute-start | bytes 12296 | tf_op jit(solution)/shard_map/ppermute | solution.py:27
  74.3 5.1 %collective-permute-start.10 = (bf16[2,64,16]{1,2,0:T(8,128)(2,1)S(1)}, bf16[2,64,16]{1,2,0:T(8,128)(2,1)S(1)}, u32[]{:S(2)}, u32[]{:S(2)}) collective-permute-start(bf16[2,64,16]{1,2,0:T(8,128)(2,1)S(1)} %get-tuple-element.30), channel_id=1, source_target_pairs={{0,12},{4,0},{8,4},{12,8},{1,13},{5,1},{9,5},{13,9},{2,14},{6,2},{... | collective-permute-start | bytes 12296 | tf_op jit(solution)/shard_map/ppermute | solution.py:27
  83.7 7.8 %collective-permute-start.16 = (f32[4,8,4608]{2,1,0:T(8,128)S(1)}, f32[4,8,4608]{2,1,0:T(8,128)S(1)}, u32[]{:S(2)}, u32[]{:S(2)}) collective-permute-start(f32[4,8,4608]{2,1,0:T(8,128)S(1)} %dynamic-slice_bitcast_fusion), channel_id=1, source_target_pairs={{0,1},{1,0},{2,3},{3,2},{4,5},{5,4},{6,7},{7,6},{8,9},{9,8},{10,11... | collective-permute-start | bytes 1769480 | tf_op jit(solution)/shard_map/ppermute | solution.py:27
  92.1 8.2 %collective-permute-start.17 = (bf16[1,8,4608]{2,1,0:T(8,128)(2,1)}, bf16[1,8,4608]{2,1,0:T(8,128)(2,1)S(1)}, u32[]{:S(2)}, u32[]{:S(2)}) collective-permute-start(bf16[1,8,4608]{2,1,0:T(8,128)(2,1)} %get-tuple-element.24), channel_id=1, source_target_pairs={{0,12},{4,0},{8,4},{12,8},{1,13},{5,1},{9,5},{13,9},{2,14},{6,2},{... | collective-permute-start | bytes 221192 | tf_op jit(solution)/shard_map/ppermute | solution.py:27
  94.7 8.5 %collective-permute-start.19 = (bf16[1,8,4608]{2,1,0:T(8,128)(2,1)S(1)}, bf16[1,8,4608]{2,1,0:T(8,128)(2,1)S(1)}, u32[]{:S(2)}, u32[]{:S(2)}) collective-permute-start(bf16[1,8,4608]{2,1,0:T(8,128)(2,1)S(1)} %get-tuple-element.25), channel_id=1, source_target_pairs={{0,4},{4,8},{8,12},{12,0},{1,5},{5,9},{9,13},{13,1},{2,6},{6,10},{... | collective-permute-start | bytes 221192 | tf_op jit(solution)/shard_map/ppermute | solution.py:27
  94.7 11.3 %collective-permute-start.18 = (bf16[1,8,4608]{2,1,0:T(8,128)(2,1)S(1)}, bf16[1,8,4608]{2,1,0:T(8,128)(2,1)}, u32[]{:S(2)}, u32[]{:S(2)}) collective-permute-start(bf16[1,8,4608]{2,1,0:T(8,128)(2,1)S(1)} %get-tuple-element.26), channel_id=1, source_target_pairs={{0,8},{4,12},{8,0},{12,4},{1,9},{5,13},{9,1},{13,5},{2,10},{6,14},... | collective-permute-start | bytes 221192 | tf_op jit(solution)/shard_map/ppermute | solution.py:27
  107.0 1.4 collective-permute-start.20
  123.2 26.2 %collective-permute-start = (bf16[512,512]{1,0:T(8,128)(2,1)S(1)}, bf16[512,512]{1,0:T(8,128)(2,1)}, u32[]{:S(2)}, u32[]{:S(2)}) collective-permute-start(bf16[512,512]{1,0:T(8,128)(2,1)S(1)} %bitcast.133), channel_id=1, source_target_pairs={{0,2},{2,0},{1,3},{3,1},{4,6},{6,4},{5,7},{7,5},{8,10},{10,8},{9,1... | collective-permute-start | bytes 1572872 | tf_op jit(solution)/shard_map/ppermute | solution.py:27
  151.9 16.1 %collective-permute-start.8 = (bf16[2,64,512]{2,1,0:T(8,128)(2,1)S(1)}, bf16[2,64,512]{2,1,0:T(8,128)(2,1)S(1)}, u32[]{:S(2)}, u32[]{:S(2)}) collective-permute-start(bf16[2,64,512]{2,1,0:T(8,128)(2,1)S(1)} %get-tuple-element.21), channel_id=1, source_target_pairs={{0,12},{4,0},{8,4},{12,8},{1,13},{5,1},{9,5},{13,9},{2,14},{6,2},{... | collective-permute-start | bytes 393224 | tf_op jit(solution)/shard_map/ppermute | solution.py:27
  153.2 14.7 %collective-permute-start.7 = (bf16[2,64,512]{2,1,0:T(8,128)(2,1)S(1)}, bf16[2,64,512]{2,1,0:T(8,128)(2,1)S(1)}, u32[]{:S(2)}, u32[]{:S(2)}) collective-permute-start(bf16[2,64,512]{2,1,0:T(8,128)(2,1)S(1)} %get-tuple-element.22), channel_id=1, source_target_pairs={{0,8},{4,12},{8,0},{12,4},{1,9},{5,13},{9,1},{13,5},{2,10},{6,14},... | collective-permute-start | bytes 393224 | tf_op jit(solution)/shard_map/ppermute | solution.py:27
  153.3 14.7 %collective-permute-start.6 = (bf16[2,64,512]{2,1,0:T(8,128)(2,1)S(1)}, bf16[2,64,512]{2,1,0:T(8,128)(2,1)S(1)}, u32[]{:S(2)}, u32[]{:S(2)}) collective-permute-start(bf16[2,64,512]{2,1,0:T(8,128)(2,1)S(1)} %get-tuple-element.23), channel_id=1, source_target_pairs={{0,4},{4,8},{8,12},{12,0},{1,5},{5,9},{9,13},{13,1},{2,6},{6,10},{... | collective-permute-start | bytes 393224 | tf_op jit(solution)/shard_map/ppermute | solution.py:27
  (14 other events, 164.9 us)
Sparse Core Ops, SparseCore 0:
  11.2 93.7 all-gather.1

commit v2 on v1

v2 whole, which is shorter than its diff:
```python
import functools

import jax
import jax.numpy as jnp
from jax import lax
from jax.experimental import pallas as pl
from jax.experimental.pallas import tpu as pltpu
from jax.sharding import PartitionSpec as P

adapter_scale = 2.0


def block_facts(tokens_per_job, block_ids, block_rows):
    job_total = tokens_per_job.shape[0]
    blocks = (tokens_per_job + (block_rows - 1)) // block_rows
    block_ends = jnp.cumsum(blocks, dtype=jnp.int32)
    starts = block_ends - blocks
    job_index = jnp.sum(
        (block_ends[None, :] <= block_ids[:, None]).astype(jnp.int32), axis=1, dtype=jnp.int32
    )
    chosen = job_index[:, None] == jnp.arange(job_total, dtype=jnp.int32)[None, :]
    job_count = jnp.sum(jnp.where(chosen, tokens_per_job[None, :], 0), axis=1, dtype=jnp.int32)
    first_block = jnp.sum(jnp.where(chosen, starts[None, :], 0), axis=1, dtype=jnp.int32)
    valid_rows = jnp.clip(job_count - block_rows * (block_ids - first_block), 0, block_rows)
    return job_index, valid_rows


def shifted(values, axis, count, step):
    if step % count == 0:
        return values
    return lax.ppermute(values, axis, [(i, (i + step) % count) for i in range(count)])


def gather_shifts(values, axis, count):
    return [shifted(values, axis, count, d) for d in range(count)]


def dot(a, b, dims):
    return lax.dot_general(a, b, (dims, ((), ())), preferred_element_type=jnp.float32)


def piece_specs(piece_list, tile, per, whole_rows):
    specs = []
    for d, shard in enumerate(piece_list):
        for r in range(len(shard)):
            columns = shard[r].shape[1]
            if d == 0 and whole_rows:
                index = lambda i, q, r=r: (q[r] * per + jnp.clip(i - r * per, 0, per - 1), 0)
            else:
                index = lambda i, q, r=r: (jnp.clip(i - r * per, 0, per - 1), 0)
            specs.append(pl.BlockSpec((tile, columns), index))
    return specs


def base_kernel(fq, q, tokens, *refs):
    pieces, out = refs[:-1], refs[-1]
    total = None
    for r, piece in enumerate(pieces):
        start = pl.multiple_of(q[r] * fq, fq)
        part = dot(tokens[:, pl.ds(start, fq)], piece[...], ((1,), (0,)))
        total = part if total is None else total + part
    out[...] = total.astype(out.dtype)


def base_product(tokens, pieces, quarters, own, name):
    rows, width = tokens.shape
    fq = width // len(pieces)
    columns = pieces[0].shape[1]
    steps = 4
    if own:
        specs = [pl.BlockSpec((fq, columns), lambda i, q, r=r: (q[r], 0)) for r in range(len(pieces))]
    else:
        specs = [pl.BlockSpec((fq, columns), lambda i, q: (0, 0)) for _ in pieces]
    return pl.pallas_call(
        functools.partial(base_kernel, fq),
        out_shape=jax.ShapeDtypeStruct((rows, columns), jnp.bfloat16),
        grid_spec=pltpu.PrefetchScalarGridSpec(
            num_scalar_prefetch=1,
            grid=(steps,),
            in_specs=[pl.BlockSpec((rows // steps, width), lambda i, q: (i, 0))] + specs,
            out_specs=pl.BlockSpec((rows // steps, columns), lambda i, q: (i, 0)),
        ),
        compiler_params=pltpu.CompilerParams(vmem_limit_bytes=16 << 20),
        cost_estimate=pl.CostEstimate(
            flops=2 * rows * width * columns,
            bytes_accessed=2 * (rows * width + width * columns + rows * columns),
            transcendentals=0,
        ),
        name=name,
    )(quarters, tokens, *pieces)


def gradient_kernel(nq, per, q, grad, back, down, *refs):
    pieces, out = refs[:-1], refs[-1]
    shards = len(pieces) // nq
    step = pl.program_id(0)
    for r in range(nq):

        @pl.when(step // per == r)
        def _():
            total = adapter_scale * dot(back[...], down[...], ((1,), (0,)))
            for d in range(shards):
                total = total + dot(grad[d], pieces[d * nq + r][...], ((1,), (1,)))
            out[...] = total.astype(out.dtype)


def token_gradient_of(grad, back, down, piece_list, quarters, width):
    shards, rows, columns = grad.shape
    nq = len(piece_list[0])
    fq = width // nq
    tile = min(512, fq)
    per = fq // tile
    place = lambda i, q: (0, q[i // per] * per + i % per)
    flat = [x for shard in piece_list for x in shard]
    return pl.pallas_call(
        functools.partial(gradient_kernel, nq, per),
        out_shape=jax.ShapeDtypeStruct((rows, width), jnp.bfloat16),
        grid_spec=pltpu.PrefetchScalarGridSpec(
            num_scalar_prefetch=1,
            grid=(nq * per,),
            in_specs=[
                pl.BlockSpec(grad.shape, lambda i, q: (0, 0, 0)),
                pl.BlockSpec(back.shape, lambda i, q: (0, 0)),
                pl.BlockSpec((down.shape[0], tile), place),
            ]
            + piece_specs(piece_list, tile, per, True),
            out_specs=pl.BlockSpec((rows, tile), place),
        ),
        compiler_params=pltpu.CompilerParams(vmem_limit_bytes=32 << 20),
        cost_estimate=pl.CostEstimate(
            flops=2 * rows * width * (shards * columns + down.shape[0]),
            bytes_accessed=2 * (rows * width + shards * columns * (width + rows)),
            transcendentals=0,
        ),
        name="token_gradient",
    )(quarters, grad, back, down, *flat)


def table_kernel(tiles, back, down, tokens, grad, mine, theirs):
    half = mine.shape[0]
    step = pl.program_id(0)

    def put(wide, values):
        total = dot(wide[...], values[...], ((1,), (0,)))
        mine[...] = total[:half]
        theirs[...] = total[half:]

    @pl.when(step < tiles)
    def _():
        put(back, tokens)

    @pl.when(step == tiles)
    def _():
        put(down, grad)


def tables_of(back, down, tokens, grad):
    total_rank, rows = back.shape
    width, heads = tokens.shape[1], grad.shape[1]
    tiles = width // heads
    half = total_rank // 2
    shape = jax.ShapeDtypeStruct((half, width + heads), jnp.float32)
    out = pl.BlockSpec((half, heads), lambda i: (0, i))
    return pl.pallas_call(
        functools.partial(table_kernel, tiles),
        out_shape=(shape, shape),
        grid=(tiles + 1,),
        in_specs=[
            pl.BlockSpec(back.shape, lambda i: (0, 0)),
            pl.BlockSpec(down.shape, lambda i: (0, 0)),
            pl.BlockSpec((rows, heads), lambda i: (0, jnp.minimum(i, tiles - 1))),
            pl.BlockSpec((rows, heads), lambda i: (0, 0)),
        ],
        out_specs=(out, out),
        compiler_params=pltpu.CompilerParams(vmem_limit_bytes=16 << 20),
        cost_estimate=pl.CostEstimate(
            flops=2 * total_rank * rows * (width + heads),
            bytes_accessed=2 * rows * (width + heads) + 4 * total_rank * (width + heads),
            transcendentals=0,
        ),
        name="job_tables",
    )(back, down, tokens, grad)


def body(
    tokens,
    cotangent,
    frozen_value_weight,
    adapter_down,
    adapter_up,
    tokens_per_job,
    packed_block_slots,
):
    nd, nt, ns, np_ = (lax.axis_size(a) for a in ("dp", "tensor", "sub", "parts"))
    z, t, s, p = (lax.axis_index(a) for a in ("dp", "tensor", "sub", "parts"))
    blocks, halved, width = tokens.shape[1:]
    heads = cotangent.shape[3]
    jobs_dev, rank, _ = adapter_down.shape
    columns = frozen_value_weight.shape[1]
    cap = -(-blocks // nd)
    rows = blocks * halved
    r2 = rank // ns
    f32, bf16, i32 = jnp.float32, jnp.bfloat16, jnp.int32

    maps = jnp.concatenate([adapter_down, adapter_up], axis=2).reshape(jobs_dev, ns, r2, width + heads)
    maps = lax.dynamic_index_in_dim(maps, s, 1, keepdims=False)
    maps = jnp.concatenate(gather_shifts(maps, "dp", nd), axis=0).reshape(nd * jobs_dev * r2, -1)
    maps = jnp.concatenate(gather_shifts(maps, "sub", ns), axis=0)
    down_cat, up_cat = maps[:, :width], maps[:, width:]

    nq = np_ * ns
    quarter = width // nq
    quarters = jnp.stack([(p - a) % np_ * ns + (s - b) % ns for a in range(np_) for b in range(ns)])
    quarters = quarters.astype(i32)
    moving = lax.dynamic_slice_in_dim(frozen_value_weight, quarters[0] * quarter, quarter, axis=0)
    piece_list = [[frozen_value_weight] * nq]
    for d in range(1, nd):
        moving = shifted(moving, "dp", nd, 1)
        piece_list.append(
            [x for y in gather_shifts(moving, "parts", np_) for x in gather_shifts(y, "sub", ns)]
        )

    grad_rel = gather_shifts(cotangent[0], "tensor", nt)

    positions = jnp.arange(blocks, dtype=i32)
    dest = packed_block_slots // blocks
    same = dest[:, :, None] == dest[:, None, :]
    earlier = positions[None, None, :] < positions[None, :, None]
    send_rank = jnp.sum((same & earlier).astype(i32), axis=2, dtype=i32)
    flat_slots = packed_block_slots.reshape(-1)
    flat_ids = jnp.arange(nd * blocks, dtype=i32)
    slot_owner = flat_slots[None, :] == (z * blocks + positions)[:, None]
    block_ids = jnp.sum(jnp.where(slot_owner, flat_ids[None, :], 0), axis=1, dtype=i32)
    in_rank = jnp.sum(jnp.where(slot_owner, send_rank.reshape(-1)[None, :], 0), axis=1, dtype=i32)
    in_slot = (z - block_ids // blocks) % nd * cap + in_rank
    own_dest = lax.dynamic_index_in_dim(dest, z, 0, keepdims=False)
    own_rank = lax.dynamic_index_in_dim(send_rank, z, 0, keepdims=False)
    out_slot = (own_dest - z) % nd * cap + own_rank
    slot_range = jnp.arange(nd * cap, dtype=i32)

    def positions_of(slots):
        match = slots[None, :] == slot_range[:, None]
        return jnp.sum(jnp.where(match, positions[None, :], 0), axis=1, dtype=i32), jnp.any(match, axis=1)

    out_pos, out_filled = positions_of(out_slot)
    in_pos, in_filled = positions_of(in_slot)

    def ordered(values, picks, filled):
        got = jnp.where(filled[:, None, None], jnp.take(values, picks, axis=0), 0).astype(values.dtype)
        return got.reshape(nd, cap, *values.shape[1:])

    def facts(ids):
        job, valid = block_facts(tokens_per_job, ids, halved * ns)
        row = s * halved + jnp.arange(halved, dtype=i32)
        mask = row[None, :] < valid[:, None]
        rel = (z - job // jobs_dev) % nd * jobs_dev + job % jobs_dev
        hot = rel[:, None] == jnp.arange(nd * jobs_dev, dtype=i32)[None, :]
        return mask, hot

    out_mask, out_hot = facts(z * blocks + positions)
    in_mask, in_hot = facts(block_ids)

    def pick(wide, hot):
        wide = wide.reshape(blocks, halved, ns, nd * jobs_dev, r2)
        return jnp.sum(jnp.where(hot[:, None, None, :, None], wide, 0.0), axis=3).reshape(blocks, halved, rank)

    def spread(narrow, hot):
        narrow = narrow.reshape(blocks, halved, ns, 1, r2)
        wide = jnp.where(hot[:, None, None, :, None], narrow, 0).astype(bf16)
        return wide.reshape(rows, ns * nd * jobs_dev * r2)

    own_tokens = tokens[0].reshape(rows, width)
    own_grad = jnp.where(in_mask[:, :, None], cotangent[0], 0).astype(bf16).reshape(rows, heads)
    down_part = pick(dot(own_tokens, down_cat, ((1,), (1,))), out_hot).astype(bf16)
    back_part = pick(dot(own_grad, up_cat, ((1,), (1,))), in_hot).astype(bf16)
    parts = gather_shifts(jnp.concatenate([down_part, back_part], axis=2), "tensor", nt)
    sums = sum(x.astype(f32) for x in parts).astype(bf16)
    down_sum, back_sum = sums[:, :, :rank], sums[:, :, rank:]
    down_wide, back_wide = spread(down_sum, out_hot), spread(back_sum, in_hot)

    down_out = ordered(down_sum, out_pos, out_filled)
    back_out = ordered(back_sum, in_pos, in_filled)
    down_got, back_got = [None] * nd, [None] * nd
    for d in range(nd):
        pair = shifted(jnp.concatenate([down_out[d], back_out[(nd - d) % nd]], axis=2), "dp", nd, d)
        down_got[d], back_got[(nd - d) % nd] = pair[:, :, :rank], pair[:, :, rank:]
    down_at_grad = jnp.take(jnp.concatenate(down_got, axis=0), in_slot, axis=0)
    back_at_tokens = jnp.take(jnp.concatenate(back_got, axis=0), out_slot, axis=0)
    mine, theirs = tables_of(
        spread(back_at_tokens, out_hot).T, spread(down_at_grad, in_hot).T, own_tokens, own_grad
    )

    summed = (mine + shifted(theirs, "sub", ns, 1)).reshape(nd, jobs_dev * r2, -1)
    total = summed[0].astype(bf16).astype(f32)
    for d in range(1, nd):
        total = total + shifted(summed[d].astype(bf16), "dp", nd, -d).astype(f32)
    counts = lax.dynamic_slice_in_dim(tokens_per_job, z * jobs_dev, jobs_dev).astype(f32)
    total = total.reshape(jobs_dev, r2, -1) * (adapter_scale / counts)[:, None, None]
    halves = jnp.stack(gather_shifts(total, "sub", ns), axis=1)
    order = (s - jnp.arange(ns, dtype=i32)) % ns
    owned = jnp.take(halves, order, axis=1).reshape(jobs_dev, rank, -1)
    grad_down, grad_up = owned[:, :, :width], owned[:, :, width:]

    base = [
        base_product(own_tokens, piece_list[d], quarters, d == 0, "base_%d" % d) for d in range(nd)
    ]
    base = jnp.stack(base)
    per_head = nd // nt

    def of_heads(index):
        shard = index * per_head + jnp.arange(per_head, dtype=i32)
        return jnp.take(base, (z - shard) % nd, axis=0)

    frozen = of_heads(t).astype(f32)
    for d in range(1, nt):
        frozen = frozen + shifted(of_heads((t + d) % nt), "tensor", nt, d).astype(f32)
    adapter_out = dot(down_wide, up_cat, ((1,), (0,)))
    layer = frozen.transpose(1, 0, 2).reshape(rows, heads) + adapter_scale * adapter_out
    layer = jnp.where(out_mask[:, :, None], layer.reshape(blocks, halved, heads), 0.0).astype(bf16)
    layer = ordered(layer, out_pos, out_filled)
    layer = jnp.concatenate([shifted(layer[d], "dp", nd, d) for d in range(nd)], axis=0)
    layer_output = jnp.take(layer, in_slot, axis=0)

    grad_abs = jnp.take(jnp.stack(grad_rel), (t - jnp.arange(nt, dtype=i32)) % nt, axis=0)
    grad_abs = jnp.where(in_mask[None, :, :, None], grad_abs, 0).astype(bf16)
    grad_abs = grad_abs.reshape(nt, rows, per_head, columns).transpose(0, 2, 1, 3)
    grad_shift = jnp.take(
        grad_abs.reshape(nd, rows, columns), (z - jnp.arange(nd, dtype=i32)) % nd, axis=0
    )
    token_gradient = token_gradient_of(grad_shift, back_wide, down_cat, piece_list, quarters, width)
    return (
        layer_output[None],
        token_gradient.reshape(1, blocks, halved, width),
        grad_down,
        grad_up,
    )


def solution(mesh):
    return jax.shard_map(
        body,
        mesh=mesh,
        in_specs=(
            P(("parts", "dp"), None, "sub", "tensor"),
            P(("parts", "dp"), None, "sub", "tensor"),
            P("tensor", "dp"),
            P(("parts", "dp"), None, "tensor"),
            P(("parts", "dp"), None, "tensor"),
            P("parts"),
            P("parts", None),
        ),
        out_specs=(
            P(("parts", "dp"), None, "sub", "tensor"),
            P(("parts", "dp"), None, "sub", "tensor"),
            P(("parts", "dp"), None, "tensor"),
            P(("parts", "dp"), None, "tensor"),
        ),
        check_vma=False,
    )
```

time: 177 us -> 215 us (1.21)
  matrix products: 58 us -> 5.58 us
  local copies, waits for them, and re-layouts: 19.7 us -> 50.7 us
  Pallas kernels: 0 us -> 29.4 us
  other arithmetic: 12.8 us -> 38.2 us
  waiting for transfers between devices: 42.4 us -> 59.5 us
  between operations: 15.4 us -> 2 us
    dot_general x14 -> x3, matrix products: 58 us -> 5.58 us  [dot(): lax.dot_general(a, b, (dims, ((), ())), preferred_element_type=jnp.float32)]
    pallas_call x0 -> x6, Pallas kernels: none -> 29.4 us  [the longest x4 13.8 us: base_product(): pl.pallas_call(functools.partial(base_kernel, fq), out_shape=jax.ShapeDty...]
    ppermute x21 -> x30, waiting for transfers between devices: 42.4 us -> 59.5 us  [shifted(): lax.ppermute(values, axis, [(i, (i + step) % count) for i in range(count)])]
    gather x8 -> x11, local copies, waits for them, and re-layouts: 4.75 us -> 18.7 us  [the longest x2 5.49 us: of_heads(): return jnp.take(base, (z - shard) % nd, axis=0)]
    transpose x0 -> x2, other arithmetic: none -> 6.31 us  [the longest x1 3.93 us: body(): grad_abs.reshape(nt, rows, per_head, columns).transpose(0, 2, 1, 3)]
    select_n x8 -> x9, local copies, waits for them, and re-layouts: 0.94 us -> 7.2 us  [spread(): wide = jnp.where(hot[:, None, None, :, None], narrow, 0).astype(bf16)]
    select_n x13 -> x12, other arithmetic: 2.97 us -> 9.03 us  [the longest x2 2.94 us: body(): jnp.take(grad_abs.reshape(nd, rows, columns), (z - jnp.arange(nd, dtype=i...]
    unnamed x35 -> x52, local copies, waits for them, and re-layouts: 2.61 us -> 8.56 us
  transfers between devices with their start and end apart: 22 -> 30, of which waited for: 11 -> 11; matrix products, arithmetic and copies ran while one was open for 42% -> 30% of each run, Pallas kernels for 0% -> 12%
where the time goes in v2:
time: 215 us; the launch traced here: 213 us
  waiting for transfers between devices  59.5 us (28%)
  local copies, waits for them, and re-layouts  50.7 us (24%)
  other arithmetic  38.2 us (18%)
  Pallas kernels  29.4 us (14%)
  starting transfers between devices  28.1 us (13%)
  matrix products  5.58 us (3%)
    ppermute x30, waiting for transfers between devices, shifted(): lax.ppermute(values, axis, [(i, (i + step) % count) for i in range(count)])  59.5 us
    ppermute x30, starting transfers between devices, shifted(): lax.ppermute(values, axis, [(i, (i + step) % count) for i in range(count)])  28.1 us
    pallas_call x4, Pallas kernels, base_product(): pl.pallas_call(functools.partial(base_kernel, fq), out_shape=jax.ShapeDty...  13.8 us
    pallas_call x1, Pallas kernels, token_gradient_of(): pl.pallas_call(functools.partial(gradient_kernel, nq, per), out_shape=jax...  11.2 us
    unnamed x52, local copies, waits for them, and re-layouts  8.56 us
    select_n x9, local copies, waits for them, and re-layouts, spread(): wide = jnp.where(hot[:, None, None, :, None], narrow, 0).astype(bf16)  7.2 us
    dot_general x3, matrix products, dot(): lax.dot_general(a, b, (dims, ((), ())), preferred_element_type=jnp.float32)  5.58 us
    gather x2, local copies, waits for them, and re-layouts, of_heads(): return jnp.take(base, (z - shard) % nd, axis=0)  5.49 us
  transfers between devices with their start and end apart: 30, of which 11 were waited for; matrix products, arithmetic and copies ran while one was open for 30% of the time, Pallas kernels for 12%

profile of v2, /device:TPU:0, one launch (start us, length us, event | category | flops | bytes accessed | tf_op | source)
XLA Modules:
  0.0 213.5 jit_solution(7819998825243050539)
XLA Ops:
  1.6 3.1 %collective-permute-start.13 = (bf16[1,8,4608]{2,1,0:T(8,128)(2,1)S(1)}, bf16[1,8,4608]{2,1,0:T(8,128)(2,1)S(1)}, u32[]{:S(2)}, u32[]{:S(2)}) collective-permute-start(bf16[1,8,4608]{2,1,0:T(8,128)(2,1)S(1)} %dynamic-slice_bitcast_fusion), channel_id=1, source_target_pairs={{0,4},{4,8},{8,12},{12,0},{1,5},{5,9},{9,13},{13,1},{2,6},{6,10},{... | collective-permute-start | bytes 221192 | tf_op jit(solution)/shard_map/ppermute | solution.py:31
  4.7 2.6 %collective-permute-start.14 = (bf16[1,8,4608]{2,1,0:T(8,128)(2,1)S(1)}, bf16[1,8,4608]{2,1,0:T(8,128)(2,1)S(1)}, u32[]{:S(2)}, u32[]{:S(2)}) collective-permute-start(bf16[1,8,4608]{2,1,0:T(8,128)(2,1)S(1)} %dynamic-slice_bitcast_fusion), channel_id=1, source_target_pairs={{0,8},{4,12},{8,0},{12,4},{1,9},{5,13},{9,1},{13,5},{2,10},{6,14},... | collective-permute-start | bytes 221192 | tf_op jit(solution)/shard_map/ppermute | solution.py:31
  23.7 3.6 %convolution_bitcast_fusion = f32[512,64]{0,1:T(8,128)S(1)} fusion(bf16[64,4096]{1,0:T(8,128)(2,1)S(1)} %fusion.3.down, bf16[512,4096]{1,0:T(8,128)(2,1)} %bitcast.114), kind=kOutput, calls=%fused_computation.17 | convolution fusion | flops 268435456 | bytes 4849664 | tf_op jit(solution)/shard_map/dot_general | solution.py:39
  29.2 3.4 %collective-permute-done.17 = bf16[8,64,32]{1,2,0:T(8,128)(2,1)S(1)} collective-permute-done((bf16[8,64,32]{1,2,0:T(8,128)(2,1)S(1)}, bf16[8,64,32]{1,2,0:T(8,128)(2,1)S(1)}, u32[]{:S(2)}, u32[]{:S(2)}) %collective-permute-start.17) | collective-permute-done | bytes 32800 | tf_op jit(solution)/shard_map/ppermute | solution.py:31
  34.0 3.2 %collective-permute-start.22 = (bf16[2,64,32]{1,2,0:T(8,128)(2,1)S(1)}, bf16[2,64,32]{1,2,0:T(8,128)(2,1)S(1)}, u32[]{:S(2)}, u32[]{:S(2)}) collective-permute-start(bf16[2,64,32]{1,2,0:T(8,128)(2,1)S(1)} %pad_maximum_fusion.7), channel_id=1, source_target_pairs={{0,12},{4,0},{8,4},{12,8},{1,13},{5,1},{9,5},{13,9},{2,14},{6,2},{... | collective-permute-start | bytes 24584 | tf_op jit(solution)/shard_map/ppermute | solution.py:31
  38.7 3.2 %collective-permute-done.23 = bf16[2,64,32]{1,2,0:T(8,128)(2,1)S(1)} collective-permute-done((bf16[2,64,32]{1,2,0:T(8,128)(2,1)S(1)}, bf16[2,64,32]{1,2,0:T(8,128)(2,1)S(1)}, u32[]{:S(2)}, u32[]{:S(2)}) %collective-permute-start.23) | collective-permute-done | bytes 8224 | tf_op jit(solution)/shard_map/ppermute | solution.py:31
  48.4 4.4 %job_tables.1 = (f32[32,4608]{1,0:T(8,128)S(1)}, f32[32,4608]{1,0:T(8,128)}) custom-call(bf16[64,512]{1,0:T(8,128)(2,1)S(1)} %bitcast.125, bf16[64,512]{1,0:T(8,128)(2,1)S(1)} %bitcast.124, bf16[512,4096]{1,0:T(8,128)(2,1)S(1)} %bitcast.115, bf16[512,512]{1,0:T(8,128)(2,1)S(1)} %bitcast_select_fusion.grad), custom_call_target="tpu_custom_call" | custom-call | flops 301989888 | bytes 5898240 | tf_op jit(solution)/shard_map/job_tables/pallas_call | solution.py:164
  71.1 2.8 %gather_fusion = bf16[2,8,64,512]{3,2,1,0:T(8,128)(2,1)} fusion(bf16[2,8,64,512]{3,2,1,0:T(8,128)(2,1)} %pad_maximum_fusion.1, s32[1024]{0:T(1024)S(1)} %pad_clamp_fusion.4), kind=kCustom, calls=%fused_computation.8 | custom fusion | bytes 2097160 | tf_op jit(solution)/shard_map/jit(_take)/gather | solution.py:324
  77.4 15.0 %collective-permute-done.4.refs_0_.refs_8_ = bf16[1024,256]{1,0:T(8,128)(2,1)S(1)} collective-permute-done((bf16[1024,256]{1,0:T(8,128)(2,1)}, bf16[1024,256]{1,0:T(8,128)(2,1)S(1)}, u32[]{:S(2)}, u32[]{:S(2)}) %collective-permute-start.4) | collective-permute-done | bytes 524320 | tf_op jit(solution)/shard_map/ppermute | solution.py:31
  93.1 3.8 %collective-permute-start.26 = (bf16[8,4608]{1,0:T(8,128)(2,1)}, bf16[8,4608]{1,0:T(8,128)(2,1)}, u32[]{:S(2)}, u32[]{:S(2)}) collective-permute-start(bf16[8,4608]{1,0:T(8,128)(2,1)} %get-tuple-element.33), channel_id=1, source_target_pairs={{0,12},{4,0},{8,4},{12,8},{1,13},{5,1},{9,5},{13,9},{2,14},{6,2},{... | collective-permute-start | bytes 221192 | tf_op jit(solution)/shard_map/ppermute | solution.py:31
  97.5 3.9 %fusion.2 = bf16[2,2,512,256]{3,1,2,0:T(2,128)(2,1)S(1)} fusion(pred[512]{0:T(512)(128)(4,1)} %get-tuple-element.55, bf16[2,512,2,256]{3,2,1,0:T(2,128)(2,1)} %gather.26, pred[2]{0:T(512)(128)(4,1)} %compare_and_fusion.7), kind=kLoop, calls=%fused_computation.22 | loop fusion | flops 1048576 | bytes 2097666 | tf_op jit(solution)/shard_map/transpose | solution.py:326
  102.5 3.0 %gather_fusion.1 = bf16[4,512,256]{2,1,0:T(8,128)(2,1)} fusion(bf16[4,512,256]{2,1,0:T(8,128)(2,1)} %bitcast.126, s32[1024]{0:T(1024)} %pad_clamp_fusion.3), kind=kCustom, calls=%fused_computation.9 | custom fusion | bytes 2097168 | tf_op jit(solution)/shard_map/jit(_take)/gather | solution.py:327
  109.3 3.6 %collective-permute-done.27 = bf16[8,4608]{1,0:T(8,128)(2,1)} collective-permute-done((bf16[8,4608]{1,0:T(8,128)(2,1)}, bf16[8,4608]{1,0:T(8,128)(2,1)}, u32[]{:S(2)}, u32[]{:S(2)}) %collective-permute-start.27) | collective-permute-done | bytes 73760 | tf_op jit(solution)/shard_map/ppermute | solution.py:31
  122.0 9.9 %collective-permute-done.6.refs_2_.refs_10_ = bf16[1024,256]{1,0:T(8,128)(2,1)} collective-permute-done((bf16[1024,256]{1,0:T(8,128)(2,1)S(1)}, bf16[1024,256]{1,0:T(8,128)(2,1)}, u32[]{:S(2)}, u32[]{:S(2)}) %collective-permute-start.6) | collective-permute-done | bytes 524320 | tf_op jit(solution)/shard_map/ppermute | solution.py:31
  131.9 9.1 %collective-permute-done.10.refs_2_.refs_14_ = bf16[1024,256]{1,0:T(8,128)(2,1)} collective-permute-done((bf16[1024,256]{1,0:T(8,128)(2,1)}, bf16[1024,256]{1,0:T(8,128)(2,1)}, u32[]{:S(2)}, u32[]{:S(2)}) %collective-permute-start.10) | collective-permute-done | bytes 524320 | tf_op jit(solution)/shard_map/ppermute | solution.py:31
  147.3 3.7 %base_1.1 = bf16[512,256]{1,0:T(8,128)(2,1)S(1)} custom-call(s32[4]{0:T(128)S(1)} %pad_add_fusion.q, bf16[512,4096]{1,0:T(8,128)(2,1)S(1)} %bitcast.117, bf16[1024,256]{1,0:T(8,128)(2,1)} %collective-permute-done.refs_0_.refs_4_, bf16[1024,256]{1,0:T(8,128)(2,1)S(1)} %copy-done.5, bf16[1024,256]{1,0:T(8,128)(2,1)} %collective-permute-done.2.refs_2_.refs_6_, ...), custom_call_target="tpu_custom_call" | custom-call | flops 1073741824 | bytes 6553600 | tf_op jit(solution)/shard_map/base_1/pallas_call | solution.py:74
  151.1 3.8 %base_2.1 = bf16[512,256]{1,0:T(8,128)(2,1)S(1)} custom-call(s32[4]{0:T(128)S(1)} %pad_add_fusion.q, bf16[512,4096]{1,0:T(8,128)(2,1)S(1)} %bitcast.118, bf16[1024,256]{1,0:T(8,128)(2,1)S(1)} %collective-permute-done.4.refs_0_.refs_8_, bf16[1024,256]{1,0:T(8,128)(2,1)} %collective-permute-done.5.refs_1_.refs_9_, ...), custom_call_target="tpu_custom_call" | custom-call | flops 1073741824 | bytes 6553600 | tf_op jit(solution)/shard_map/base_2/pallas_call | solution.py:74
  154.9 3.9 %base_3.1 = bf16[512,256]{1,0:T(8,128)(2,1)S(1)} custom-call(s32[4]{0:T(128)S(1)} %pad_add_fusion.q, bf16[512,4096]{1,0:T(8,128)(2,1)S(1)} %bitcast.119, bf16[1024,256]{1,0:T(8,128)(2,1)} %collective-permute-done.8.refs_0_.refs_12_, bf16[1024,256]{1,0:T(8,128)(2,1)} %collective-permute-done.9.refs_1_.refs_13_, ...), custom_call_target="tpu_custom_call" | custom-call | flops 1073741824 | bytes 6553600 | tf_op jit(solution)/shard_map/base_3/pallas_call | solution.py:74
  159.9 2.8 %gather_fusion.4 = bf16[2,512,256]{2,1,0:T(8,128)(2,1)} fusion(bf16[4,512,256]{2,1,0:T(8,128)(2,1)} %pad_maximum_fusion, s32[1024]{0:T(1024)} %pad_clamp_fusion.7), kind=kCustom, calls=%fused_computation.3.clone | custom fusion | bytes 1048584 | tf_op jit(solution)/shard_map/jit(_take)/gather | solution.py:312
  167.6 2.7 %gather_fusion.3 = bf16[2,512,256]{2,1,0:T(8,128)(2,1)} fusion(bf16[4,512,256]{2,1,0:T(8,128)(2,1)} %pad_maximum_fusion, s32[1024]{0:T(1024)} %pad_clamp_fusion.8), kind=kCustom, calls=%fused_computation.clone | custom fusion | bytes 1048584 | tf_op jit(solution)/shard_map/jit(_take)/gather | solution.py:312
  170.4 9.0 %collective-permute-done.12 = bf16[2,512,256]{2,1,0:T(8,128)(2,1)} collective-permute-done((bf16[2,512,256]{2,1,0:T(8,128)(2,1)}, bf16[2,512,256]{2,1,0:T(8,128)(2,1)}, u32[]{:S(2)}, u32[]{:S(2)}) %collective-permute-start.12) | collective-permute-done | bytes 524320 | tf_op jit(solution)/shard_map/ppermute | solution.py:31
  184.3 2.5 %copy.35 = f32[512,512]{1,0:T(8,128)} copy(f32[512,512]{0,1:T(8,128)} %bitcast.127) | data formatting | bytes 2097152 | tf_op jit(solution)/shard_map/reshape | solution.py:318
  193.0 2.7 %collective-permute-start.18 = (bf16[2,64,512]{2,1,0:T(8,128)(2,1)S(1)}, bf16[2,64,512]{2,1,0:T(8,128)(2,1)S(1)}, u32[]{:S(2)}, u32[]{:S(2)}) collective-permute-start(bf16[2,64,512]{2,1,0:T(8,128)(2,1)S(1)} %get-tuple-element.30), channel_id=1, source_target_pairs={{0,4},{4,8},{8,12},{12,0},{1,5},{5,9},{9,13},{13,1},{2,6},{6,10},{... | collective-permute-start | bytes 393224 | tf_op jit(solution)/shard_map/ppermute | solution.py:31
  200.6 11.2 %token_gradient.1 = bf16[512,4096]{1,0:T(8,128)(2,1)} custom-call(s32[4]{0:T(128)S(1)} %pad_add_fusion.q, bf16[4,512,256]{2,1,0:T(8,128)(2,1)S(1)} %copy-done.3, bf16[512,64]{1,0:T(8,128)(2,1)S(1)} %copy.38.back, bf16[64,4096]{1,0:T(8,128)(2,1)S(1)} %fusion.3.down, bf16[4096,256]{1,0:T(8,128)(2,1)S(1)} %copy-done.2, bf16[4096,256]{1,0:T(8,128)(2,1)S(1)} %copy-done.2, ...), custom_call_target="tpu_custom_call" | custom-call | flops 4563402752 | bytes 13631488 | tf_op jit(solution)/shard_map/token_gradient/pallas_call | solution.py:115
  (224 shorter events, 94.5 us)
Async XLA Ops:
  1.6 20.1 %collective-permute-start.13 = (bf16[1,8,4608]{2,1,0:T(8,128)(2,1)S(1)}, bf16[1,8,4608]{2,1,0:T(8,128)(2,1)S(1)}, u32[]{:S(2)}, u32[]{:S(2)}) collective-permute-start(bf16[1,8,4608]{2,1,0:T(8,128)(2,1)S(1)} %dynamic-slice_bitcast_fusion), channel_id=1, source_target_pairs={{0,4},{4,8},{8,12},{12,0},{1,5},{5,9},{9,13},{13,1},{2,6},{6,10},{... | collective-permute-start | bytes 221192 | tf_op jit(solution)/shard_map/ppermute | solution.py:31
  4.7 17.1 %collective-permute-start.14 = (bf16[1,8,4608]{2,1,0:T(8,128)(2,1)S(1)}, bf16[1,8,4608]{2,1,0:T(8,128)(2,1)S(1)}, u32[]{:S(2)}, u32[]{:S(2)}) collective-permute-start(bf16[1,8,4608]{2,1,0:T(8,128)(2,1)S(1)} %dynamic-slice_bitcast_fusion), channel_id=1, source_target_pairs={{0,8},{4,12},{8,0},{12,4},{1,9},{5,13},{9,1},{13,5},{2,10},{6,14},... | collective-permute-start | bytes 221192 | tf_op jit(solution)/shard_map/ppermute | solution.py:31
  7.3 14.5 %collective-permute-start.15 = (bf16[1,8,4608]{2,1,0:T(8,128)(2,1)S(1)}, bf16[1,8,4608]{2,1,0:T(8,128)(2,1)S(1)}, u32[]{:S(2)}, u32[]{:S(2)}) collective-permute-start(bf16[1,8,4608]{2,1,0:T(8,128)(2,1)S(1)} %dynamic-slice_bitcast_fusion), channel_id=1, source_target_pairs={{0,12},{4,0},{8,4},{12,8},{1,13},{5,1},{9,5},{13,9},{2,14},{6,2},{... | collective-permute-start | bytes 221192 | tf_op jit(solution)/shard_map/ppermute | solution.py:31
  10.5 65.6 %collective-permute-start = (bf16[1024,256]{1,0:T(8,128)(2,1)}, bf16[1024,256]{1,0:T(8,128)(2,1)}, u32[]{:S(2)}, u32[]{:S(2)}) collective-permute-start(bf16[1024,256]{1,0:T(8,128)(2,1)} %constant_dynamic-slice_fusion), channel_id=1, source_target_pairs={{0,4},{4,8},{8,12},{12,0},{1,5},{5,9},{9,13},{13,1},{2,6},{6,10},{... | collective-permute-start | bytes 1572872 | tf_op jit(solution)/shard_map/ppermute | solution.py:31
  11.2 57.8 %collective-permute-start.21 = (bf16[8,64,512]{2,1,0:T(8,128)(2,1)}, bf16[8,64,512]{2,1,0:T(8,128)(2,1)}, u32[]{:S(2)}, u32[]{:S(2)}) collective-permute-start(bf16[8,64,512]{2,1,0:T(8,128)(2,1)} %bitcast.130), channel_id=1, source_target_pairs={{0,2},{2,0},{1,3},{3,1},{4,6},{6,4},{5,7},{7,5},{8,10},{10,8},{9,1... | collective-permute-start | bytes 1572872 | tf_op jit(solution)/shard_map/ppermute | solution.py:31
  52.8 23.3 %collective-permute-start.25 = (f32[32,4608]{1,0:T(8,128)}, f32[32,4608]{1,0:T(8,128)}, u32[]{:S(2)}, u32[]{:S(2)}) collective-permute-start(f32[32,4608]{1,0:T(8,128)} %get-tuple-element.10), channel_id=1, source_target_pairs={{0,1},{1,0},{2,3},{3,2},{4,5},{5,4},{6,7},{7,6},{8,9},{9,8},{10,11... | collective-permute-start | bytes 1769480 | tf_op jit(solution)/shard_map/ppermute | solution.py:31
  76.0 16.3 %collective-permute-start.4 = (bf16[1024,256]{1,0:T(8,128)(2,1)}, bf16[1024,256]{1,0:T(8,128)(2,1)S(1)}, u32[]{:S(2)}, u32[]{:S(2)}) collective-permute-start(bf16[1024,256]{1,0:T(8,128)(2,1)} %collective-permute-done.refs_0_.refs_4_), channel_id=1, source_target_pairs={{0,4},{4,8},{8,12},{12,0},{1,5},{5,9},{9,13},{13,1},{2,6},{6,10},{... | collective-permute-start | bytes 1572872 | tf_op jit(solution)/shard_map/ppermute | solution.py:31
  92.4 22.1 %collective-permute-start.8 = (bf16[1024,256]{1,0:T(8,128)(2,1)S(1)}, bf16[1024,256]{1,0:T(8,128)(2,1)}, u32[]{:S(2)}, u32[]{:S(2)}) collective-permute-start(bf16[1024,256]{1,0:T(8,128)(2,1)S(1)} %collective-permute-done.4.refs_0_.refs_8_), channel_id=1, source_target_pairs={{0,4},{4,8},{8,12},{12,0},{1,5},{5,9},{9,13},{13,1},{2,6},{6,10},{... | collective-permute-start | bytes 1572872 | tf_op jit(solution)/shard_map/ppermute | solution.py:31
  93.1 16.3 %collective-permute-start.26 = (bf16[8,4608]{1,0:T(8,128)(2,1)}, bf16[8,4608]{1,0:T(8,128)(2,1)}, u32[]{:S(2)}, u32[]{:S(2)}) collective-permute-start(bf16[8,4608]{1,0:T(8,128)(2,1)} %get-tuple-element.33), channel_id=1, source_target_pairs={{0,12},{4,0},{8,4},{12,8},{1,13},{5,1},{9,5},{13,9},{2,14},{6,2},{... | collective-permute-start | bytes 221192 | tf_op jit(solution)/shard_map/ppermute | solution.py:31
  96.9 16.1 %collective-permute-start.27 = (bf16[8,4608]{1,0:T(8,128)(2,1)}, bf16[8,4608]{1,0:T(8,128)(2,1)}, u32[]{:S(2)}, u32[]{:S(2)}) collective-permute-start(bf16[8,4608]{1,0:T(8,128)(2,1)} %get-tuple-element.35), channel_id=1, source_target_pairs={{0,8},{4,12},{8,0},{12,4},{1,9},{5,13},{9,1},{13,5},{2,10},{6,14},... | collective-permute-start | bytes 221192 | tf_op jit(solution)/shard_map/ppermute | solution.py:31
  96.9 18.1 %collective-permute-start.28 = (bf16[8,4608]{1,0:T(8,128)(2,1)}, bf16[8,4608]{1,0:T(8,128)(2,1)}, u32[]{:S(2)}, u32[]{:S(2)}) collective-permute-start(bf16[8,4608]{1,0:T(8,128)(2,1)} %get-tuple-element.34), channel_id=1, source_target_pairs={{0,4},{4,8},{8,12},{12,0},{1,5},{5,9},{9,13},{13,1},{2,6},{6,10},{... | collective-permute-start | bytes 221192 | tf_op jit(solution)/shard_map/ppermute | solution.py:31
  105.5 15.2 %collective-permute-start.2 = (bf16[1024,256]{1,0:T(8,128)(2,1)}, bf16[1024,256]{1,0:T(8,128)(2,1)}, u32[]{:S(2)}, u32[]{:S(2)}) collective-permute-start(bf16[1024,256]{1,0:T(8,128)(2,1)} %collective-permute-done.refs_0_.refs_4_), channel_id=1, source_target_pairs={{0,16},{16,0},{1,17},{17,1},{2,18},{18,2},{3,19},{19,3},{4,20},{20... | collective-permute-start | bytes 1572872 | tf_op jit(solution)/shard_map/ppermute | solution.py:31
  109.3 11.3 %collective-permute-start.1 = (bf16[1024,256]{1,0:T(8,128)(2,1)}, bf16[1024,256]{1,0:T(8,128)(2,1)S(1)}, u32[]{:S(2)}, u32[]{:S(2)}) collective-permute-start(bf16[1024,256]{1,0:T(8,128)(2,1)} %collective-permute-done.refs_0_.refs_4_), channel_id=1, source_target_pairs={{0,1},{1,0},{2,3},{3,2},{4,5},{5,4},{6,7},{7,6},{8,9},{9,8},{10,11... | collective-permute-start | bytes 1572872 | tf_op jit(solution)/shard_map/ppermute | solution.py:31
  113.0 18.9 %collective-permute-start.6 = (bf16[1024,256]{1,0:T(8,128)(2,1)S(1)}, bf16[1024,256]{1,0:T(8,128)(2,1)}, u32[]{:S(2)}, u32[]{:S(2)}) collective-permute-start(bf16[1024,256]{1,0:T(8,128)(2,1)S(1)} %collective-permute-done.4.refs_0_.refs_8_), channel_id=1, source_target_pairs={{0,16},{16,0},{1,17},{17,1},{2,18},{18,2},{3,19},{19,3},{4,20},{20... | collective-permute-start | bytes 1572872 | tf_op jit(solution)/shard_map/ppermute | solution.py:31
  114.5 26.5 %collective-permute-start.10 = (bf16[1024,256]{1,0:T(8,128)(2,1)}, bf16[1024,256]{1,0:T(8,128)(2,1)}, u32[]{:S(2)}, u32[]{:S(2)}) collective-permute-start(bf16[1024,256]{1,0:T(8,128)(2,1)} %collective-permute-done.8.refs_0_.refs_12_), channel_id=1, source_target_pairs={{0,16},{16,0},{1,17},{17,1},{2,18},{18,2},{3,19},{19,3},{4,20},{20... | collective-permute-start | bytes 1572872 | tf_op jit(solution)/shard_map/ppermute | solution.py:31
  120.7 30.4 %collective-permute-start.5 = (bf16[1024,256]{1,0:T(8,128)(2,1)S(1)}, bf16[1024,256]{1,0:T(8,128)(2,1)}, u32[]{:S(2)}, u32[]{:S(2)}) collective-permute-start(bf16[1024,256]{1,0:T(8,128)(2,1)S(1)} %collective-permute-done.4.refs_0_.refs_8_), channel_id=1, source_target_pairs={{0,1},{1,0},{2,3},{3,2},{4,5},{5,4},{6,7},{7,6},{8,9},{9,8},{10,11... | collective-permute-start | bytes 1572872 | tf_op jit(solution)/shard_map/ppermute | solution.py:31
  121.5 22.6 %collective-permute-start.3 = (bf16[1024,256]{1,0:T(8,128)(2,1)}, bf16[1024,256]{1,0:T(8,128)(2,1)}, u32[]{:S(2)}, u32[]{:S(2)}) collective-permute-start(bf16[1024,256]{1,0:T(8,128)(2,1)} %collective-permute-done.2.refs_2_.refs_6_), channel_id=1, source_target_pairs={{0,1},{1,0},{2,3},{3,2},{4,5},{5,4},{6,7},{7,6},{8,9},{9,8},{10,11... | collective-permute-start | bytes 1572872 | tf_op jit(solution)/shard_map/ppermute | solution.py:31
  122.0 32.9 %collective-permute-start.9 = (bf16[1024,256]{1,0:T(8,128)(2,1)}, bf16[1024,256]{1,0:T(8,128)(2,1)}, u32[]{:S(2)}, u32[]{:S(2)}) collective-permute-start(bf16[1024,256]{1,0:T(8,128)(2,1)} %collective-permute-done.8.refs_0_.refs_12_), channel_id=1, source_target_pairs={{0,1},{1,0},{2,3},{3,2},{4,5},{5,4},{6,7},{7,6},{8,9},{9,8},{10,11... | collective-permute-start | bytes 1572872 | tf_op jit(solution)/shard_map/ppermute | solution.py:31
  131.9 19.2 %collective-permute-start.7 = (bf16[1024,256]{1,0:T(8,128)(2,1)}, bf16[1024,256]{1,0:T(8,128)(2,1)}, u32[]{:S(2)}, u32[]{:S(2)}) collective-permute-start(bf16[1024,256]{1,0:T(8,128)(2,1)} %collective-permute-done.6.refs_2_.refs_10_), channel_id=1, source_target_pairs={{0,1},{1,0},{2,3},{3,2},{4,5},{5,4},{6,7},{7,6},{8,9},{9,8},{10,11... | collective-permute-start | bytes 1572872 | tf_op jit(solution)/shard_map/ppermute | solution.py:31
  141.0 13.9 %collective-permute-start.11 = (bf16[1024,256]{1,0:T(8,128)(2,1)}, bf16[1024,256]{1,0:T(8,128)(2,1)}, u32[]{:S(2)}, u32[]{:S(2)}) collective-permute-start(bf16[1024,256]{1,0:T(8,128)(2,1)} %collective-permute-done.10.refs_2_.refs_14_), channel_id=1, source_target_pairs={{0,1},{1,0},{2,3},{3,2},{4,5},{5,4},{6,7},{7,6},{8,9},{9,8},{10,11... | collective-permute-start | bytes 1572872 | tf_op jit(solution)/shard_map/ppermute | solution.py:31
  164.7 14.6 %collective-permute-start.12 = (bf16[2,512,256]{2,1,0:T(8,128)(2,1)}, bf16[2,512,256]{2,1,0:T(8,128)(2,1)}, u32[]{:S(2)}, u32[]{:S(2)}) collective-permute-start(bf16[2,512,256]{2,1,0:T(8,128)(2,1)} %broadcast_select_fusion.3), channel_id=1, source_target_pairs={{0,2},{2,0},{1,3},{3,1},{4,6},{6,4},{5,7},{7,5},{8,10},{10,8},{9,1... | collective-permute-start | bytes 1572872 | tf_op jit(solution)/shard_map/ppermute | solution.py:31
  193.0 18.8 %collective-permute-start.18 = (bf16[2,64,512]{2,1,0:T(8,128)(2,1)S(1)}, bf16[2,64,512]{2,1,0:T(8,128)(2,1)S(1)}, u32[]{:S(2)}, u32[]{:S(2)}) collective-permute-start(bf16[2,64,512]{2,1,0:T(8,128)(2,1)S(1)} %get-tuple-element.30), channel_id=1, source_target_pairs={{0,4},{4,8},{8,12},{12,0},{1,5},{5,9},{9,13},{13,1},{2,6},{6,10},{... | collective-permute-start | bytes 393224 | tf_op jit(solution)/shard_map/ppermute | solution.py:31
  195.7 16.2 %collective-permute-start.19 = (bf16[2,64,512]{2,1,0:T(8,128)(2,1)S(1)}, bf16[2,64,512]{2,1,0:T(8,128)(2,1)S(1)}, u32[]{:S(2)}, u32[]{:S(2)}) collective-permute-start(bf16[2,64,512]{2,1,0:T(8,128)(2,1)S(1)} %get-tuple-element.29), channel_id=1, source_target_pairs={{0,8},{4,12},{8,0},{12,4},{1,9},{5,13},{9,1},{13,5},{2,10},{6,14},... | collective-permute-start | bytes 393224 | tf_op jit(solution)/shard_map/ppermute | solution.py:31
  196.9 15.0 %collective-permute-start.20 = (bf16[2,64,512]{2,1,0:T(8,128)(2,1)S(1)}, bf16[2,64,512]{2,1,0:T(8,128)(2,1)S(1)}, u32[]{:S(2)}, u32[]{:S(2)}) collective-permute-start(bf16[2,64,512]{2,1,0:T(8,128)(2,1)S(1)} %get-tuple-element.28), channel_id=1, source_target_pairs={{0,12},{4,0},{8,4},{12,8},{1,13},{5,1},{9,5},{13,9},{2,14},{6,2},{... | collective-permute-start | bytes 393224 | tf_op jit(solution)/shard_map/ppermute | solution.py:31
  (32 other events, 341.9 us)

commit v3 on v1

v3 whole, which is shorter than its diff:
```python
import functools

import jax
import jax.numpy as jnp
from jax import lax
from jax.experimental import pallas as pl
from jax.experimental.pallas import tpu as pltpu
from jax.sharding import PartitionSpec as P

adapter_scale = 2.0
f32, bf16, i32 = jnp.float32, jnp.bfloat16, jnp.int32
MIB = 1 << 20


def block_facts(tokens_per_job, block_ids, block_rows):
    job_total = tokens_per_job.shape[0]
    blocks = (tokens_per_job + (block_rows - 1)) // block_rows
    block_ends = jnp.cumsum(blocks, dtype=jnp.int32)
    starts = block_ends - blocks
    job_index = jnp.sum(
        (block_ends[None, :] <= block_ids[:, None]).astype(jnp.int32), axis=1, dtype=jnp.int32
    )
    chosen = job_index[:, None] == jnp.arange(job_total, dtype=jnp.int32)[None, :]
    job_count = jnp.sum(jnp.where(chosen, tokens_per_job[None, :], 0), axis=1, dtype=jnp.int32)
    first_block = jnp.sum(jnp.where(chosen, starts[None, :], 0), axis=1, dtype=jnp.int32)
    valid_rows = jnp.clip(job_count - block_rows * (block_ids - first_block), 0, block_rows)
    return job_index, valid_rows


def shifted(values, axis, count, step):
    if step % count == 0:
        return values
    return lax.ppermute(values, axis, [(i, (i + step) % count) for i in range(count)])


def gather_shifts(values, axis, count):
    return [shifted(values, axis, count, d) for d in range(count)]


def dot(a, b, dims, precision=None):
    return lax.dot_general(a, b, (dims, ((), ())), precision=precision, preferred_element_type=f32)


def tie(*values):
    return lax.optimization_barrier(values)


class Sizes:
    def __init__(self, nd, nt, ns, np_, blocks, halved, width, heads, jobs_dev, rank, columns):
        self.nd, self.nt, self.ns, self.np_ = nd, nt, ns, np_
        self.blocks, self.halved, self.width, self.heads = blocks, halved, width, heads
        self.jobs, self.jobs_dev, self.rank, self.columns = nd * jobs_dev, jobs_dev, rank, columns
        self.wide = self.jobs * rank
        self.rows = blocks * halved
        self.cap = -(-blocks // nd)
        self.slots = nd * self.cap
        self.nq = np_ * ns
        self.fq = width // self.nq
        self.per_head = nd // nt
        at, self.at = 0, {}
        for name, count in (
            ("out_pos", self.slots), ("in_pos", self.slots), ("out_fill", self.slots), ("in_fill", self.slots),
            ("out_rel", blocks), ("in_rel", blocks), ("out_valid", blocks), ("in_valid", blocks),
            ("quarter", self.nq), ("shard", nd), ("head", self.per_head),
        ):
            self.at[name] = at
            at += count

    def get(self, ref, name, index):
        return ref[self.at[name] + index]


def call(kernel, name, grid, scalars, inputs, in_specs, out_shape, out_specs, flops, moved, limit, scratch=(), alias=None):
    return pl.pallas_call(
        kernel,
        out_shape=out_shape,
        grid_spec=pltpu.PrefetchScalarGridSpec(
            num_scalar_prefetch=1, grid=grid, in_specs=in_specs, out_specs=out_specs, scratch_shapes=list(scratch)
        ),
        input_output_aliases=alias or {},
        compiler_params=pltpu.CompilerParams(vmem_limit_bytes=limit),
        cost_estimate=pl.CostEstimate(flops=flops, bytes_accessed=moved, transcendentals=0),
        name=name,
    )(scalars, *inputs)


def whole(x):
    return pl.BlockSpec(x.shape, lambda *_: (0,) * len(x.shape))


def rows_of(index, z):
    return pl.ds(pl.multiple_of(index * z.halved, z.halved), z.halved)


def row_mask(valid, z, lanes):
    return lax.broadcasted_iota(i32, (z.halved, lanes), 0) < valid


def widen(values, rel, unfold, job_of, z):
    wide = dot(values, unfold, ((1,), (0,)))
    return jnp.where(job_of == rel, wide, 0.0).astype(bf16)


def products_kernel(z, n, sc, tokens, grad, maps, fold, job_of, out):
    step = pl.program_id(0)
    down = dot(tokens[...], maps[:, : z.width], ((1,), (1,)))
    back = dot(grad[...], maps[:, z.width :], ((1,), (1,)))
    for k in range(n):
        block = step * n + k
        own = slice(k * z.halved, (k + 1) * z.halved)
        picked = jnp.where(job_of[...] == z.get(sc, "out_rel", block), down[own], 0.0)
        out[own, : z.rank] = dot(picked, fold[...], ((1,), (0,)), lax.Precision.HIGHEST).astype(bf16)
        picked = jnp.where(job_of[...] == z.get(sc, "in_rel", block), back[own], 0.0)
        picked = jnp.where(row_mask(z.get(sc, "in_valid", block), z, z.wide), picked, 0.0)
        out[own, z.rank :] = dot(picked, fold[...], ((1,), (0,)), lax.Precision.HIGHEST).astype(bf16)


def products(z, sc, tokens, grad, maps, fold, job_of):
    n = 2
    return call(
        functools.partial(products_kernel, z, n), "adapter_products", (z.blocks // n,), sc,
        (tokens, grad, maps, fold, job_of),
        [
            pl.BlockSpec((n * z.halved, z.width), lambda i, _: (i, 0)),
            pl.BlockSpec((n * z.halved, z.heads), lambda i, _: (i, 0)),
            whole(maps), whole(fold), whole(job_of),
        ],
        jax.ShapeDtypeStruct((z.rows, 2 * z.rank), bf16),
        pl.BlockSpec((n * z.halved, 2 * z.rank), lambda i, _: (i, 0)),
        2 * z.rows * (z.width + z.heads) * z.wide, 2 * z.rows * (z.width + z.heads), 16 * MIB,
    )


def sums_kernel(z, sc, *refs):
    parts, outs = refs[: z.nt], refs[z.nt :]
    sums, pays = outs[0], outs[1:]
    total = parts[0][...].astype(f32)
    for part in parts[1:]:
        total = total + part[...].astype(f32)
    sums[...] = total.astype(bf16)
    for d in range(z.nd):
        back = (z.nd - d) % z.nd
        for r in range(z.cap):
            own = slice(r * z.halved, (r + 1) * z.halved)
            picked = sums[rows_of(z.get(sc, "out_pos", d * z.cap + r), z), : z.rank]
            pays[d][own, : z.rank] = jnp.where(z.get(sc, "out_fill", d * z.cap + r) > 0, picked, 0)
            picked = sums[rows_of(z.get(sc, "in_pos", back * z.cap + r), z), z.rank :]
            pays[d][own, z.rank :] = jnp.where(z.get(sc, "in_fill", back * z.cap + r) > 0, picked, 0)


def sums_of(z, sc, parts):
    shapes = [jax.ShapeDtypeStruct((z.rows, 2 * z.rank), bf16)]
    shapes += [jax.ShapeDtypeStruct((z.cap * z.halved, 2 * z.rank), bf16)] * z.nd
    return call(
        functools.partial(sums_kernel, z), "adapter_sums", (1,), sc, parts, [whole(x) for x in parts],
        tuple(shapes), tuple(whole(x) for x in shapes), 1000, 8 * z.rows * z.rank, 8 * MIB,
    )


def table_kernel(z, tiles, sc, tokens, grad, unfold, job_of, *refs):
    got, (mine, theirs, back, down) = refs[: z.nd], refs[z.nd :]
    half = mine.shape[0]
    step = pl.program_id(0)

    @pl.when(step == 0)
    def _():
        for d in range(z.nd):
            for r in range(z.cap):
                slot = d * z.cap + r
                own = slice(r * z.halved, (r + 1) * z.halved)

                @pl.when(z.get(sc, "out_fill", slot) > 0)
                def _():
                    at = z.get(sc, "out_pos", slot)
                    values = got[(z.nd - d) % z.nd][own, z.rank :]
                    back[rows_of(at, z), :] = widen(values, z.get(sc, "out_rel", at), unfold[...], job_of[...], z)

                @pl.when(z.get(sc, "in_fill", slot) > 0)
                def _():
                    at = z.get(sc, "in_pos", slot)
                    values = widen(got[d][own, : z.rank], z.get(sc, "in_rel", at), unfold[...], job_of[...], z)
                    mask = row_mask(z.get(sc, "in_valid", at), z, z.wide)
                    down[rows_of(at, z), :] = jnp.where(mask, values, 0).astype(bf16)

    def put(wide, values):
        total = dot(wide[...], values[...], ((0,), (0,)))
        mine[...] = total[:half]
        theirs[...] = total[half:]

    @pl.when(step < tiles)
    def _():
        put(back, tokens)

    @pl.when(step == tiles)
    def _():
        put(down, grad)


def tables_of(z, sc, tokens, grad, unfold, job_of, got):
    tiles = z.width // z.heads
    half = z.wide // z.ns
    shape = jax.ShapeDtypeStruct((half, z.width + z.heads), f32)
    out = pl.BlockSpec((half, z.heads), lambda i, _: (0, i))
    return call(
        functools.partial(table_kernel, z, tiles), "job_tables", (tiles + 1,), sc,
        (tokens, grad, unfold, job_of, *got),
        [
            pl.BlockSpec((z.rows, z.heads), lambda i, _: (0, jnp.minimum(i, tiles - 1))),
            whole(grad), whole(unfold), whole(job_of),
        ]
        + [whole(x) for x in got],
        (shape, shape), (out, out),
        2 * z.wide * z.rows * (z.width + z.heads), 2 * z.rows * z.width + 4 * z.wide * z.width, 16 * MIB,
        scratch=(pltpu.VMEM((z.rows, z.wide), bf16), pltpu.VMEM((z.rows, z.wide), bf16)),
    )


def base_kernel(z, sc, tokens, *refs):
    pieces, (out, total) = refs[: z.nq], refs[z.nq :]
    step = pl.program_id(0)
    for r in range(z.nq):

        @pl.when(step == r)
        def _():
            part = dot(tokens[...], pieces[r][...], ((1,), (0,)))
            if r == 0:
                total[...] = part
            elif r < z.nq - 1:
                total[...] += part
            else:
                out[...] = (total[...] + part).astype(bf16)


def base_product(z, sc, tokens, pieces, d):
    at = z.at["quarter"]
    if d == 0:
        specs = [pl.BlockSpec((z.fq, z.columns), lambda i, q, r=r: (q[at + r], 0)) for r in range(z.nq)]
    else:
        specs = [whole(x) for x in pieces]
    return call(
        functools.partial(base_kernel, z), "base_%d" % d, (z.nq,), sc, (tokens, *pieces),
        [pl.BlockSpec((z.rows, z.fq), lambda i, q: (0, q[at + i]))] + specs,
        jax.ShapeDtypeStruct((z.rows, z.columns), bf16),
        pl.BlockSpec((z.rows, z.columns), lambda i, q: (0, 0)),
        2 * z.rows * z.width * z.columns, 2 * (z.rows * z.width + z.width * z.columns), 16 * MIB,
        scratch=(pltpu.VMEM((z.rows, z.columns), f32),),
    )


def layer_kernel(z, sc, sums, maps, unfold, job_of, *refs):
    m = z.per_head
    given, (outs, frozen) = refs[: m * z.nt], (refs[m * z.nt : -1], refs[-1])
    for j in range(m):
        total = given[j][...].astype(f32)
        for d in range(1, z.nt):
            total = total + given[d * m + j][...].astype(f32)
        for i in range(m):

            @pl.when(z.get(sc, "head", j) == i)
            def _():
                frozen[:, i * z.columns : (i + 1) * z.columns] = total

    for d in range(z.nd):
        for r in range(z.cap):
            slot = d * z.cap + r
            at = z.get(sc, "out_pos", slot)
            valid = jnp.where(z.get(sc, "out_fill", slot) > 0, z.get(sc, "out_valid", at), 0)
            wide = widen(sums[rows_of(at, z), : z.rank], z.get(sc, "out_rel", at), unfold[...], job_of[...], z)
            adapter = dot(wide, maps[...], ((1,), (0,)))
            layer = frozen[rows_of(at, z), :] + adapter_scale * adapter
            layer = jnp.where(row_mask(valid, z, z.heads), layer, 0.0)
            outs[d][r * z.halved : (r + 1) * z.halved, :] = layer.astype(bf16)


def layer_of(z, sc, sums, maps, unfold, job_of, given):
    shapes = [jax.ShapeDtypeStruct((z.cap * z.halved, z.heads), bf16)] * z.nd
    at = z.width // z.heads
    return call(
        functools.partial(layer_kernel, z), "layer", (1,), sc, (sums, maps, unfold, job_of, *given),
        [whole(sums), pl.BlockSpec((z.wide, z.heads), lambda i, _: (0, at)), whole(unfold), whole(job_of)]
        + [whole(x) for x in given],
        tuple(shapes), tuple(whole(x) for x in shapes),
        2 * z.rows * z.wide * z.heads, 6 * z.rows * z.heads, 16 * MIB,
        scratch=(pltpu.VMEM((z.rows, z.heads), f32),),
    )


def place_kernel(z, sc, *refs):
    got, out = refs[: z.nd], refs[z.nd]
    for d in range(z.nd):
        for r in range(z.cap):
            slot = d * z.cap + r

            @pl.when(z.get(sc, "in_fill", slot) > 0)
            def _():
                out[rows_of(z.get(sc, "in_pos", slot), z), :] = got[d][r * z.halved : (r + 1) * z.halved, :]


def place(z, sc, got):
    shape = jax.ShapeDtypeStruct((z.rows, z.heads), bf16)
    return call(
        functools.partial(place_kernel, z), "place", (1,), sc, got, [whole(x) for x in got],
        shape, whole(shape), 1000, 4 * z.rows * z.heads, 8 * MIB,
    )


def gradient_kernel(z, quarters, per, aliased, sc, maps, sums, unfold, job_of, *refs):
    grads, refs = refs[: z.nt], refs[z.nt :]
    count = len(quarters)
    pieces, refs = refs[: z.nd * count], refs[z.nd * count :]
    out, grad, back = refs[1:] if aliased else refs
    step = pl.program_id(0)
    m = z.per_head

    @pl.when(step == 0)
    def _():
        for v in range(z.nt * m):
            grad[v] = grads[v // m][:, v % m * z.columns : (v % m + 1) * z.columns]
        for b in range(z.blocks):
            own = slice(b * z.halved, (b + 1) * z.halved)
            back[own, :] = widen(sums[own, z.rank :], z.get(sc, "in_rel", b), unfold[...], job_of[...], z)

    for k in range(count):

        @pl.when(step // per == k)
        def _():
            total = adapter_scale * dot(back[...], maps[...], ((1,), (0,)))
            for d in range(z.nd):
                total = total + dot(grad[z.get(sc, "shard", d)], pieces[d * count + k][...], ((1,), (1,)))
            for b in range(z.blocks):
                own = slice(b * z.halved, (b + 1) * z.halved)
                mask = row_mask(z.get(sc, "in_valid", b), z, total.shape[1])
                out[own, :] = jnp.where(mask, total[own], 0.0).astype(bf16)


def token_gradient_of(z, sc, grads, maps, sums, unfold, job_of, piece_list, quarters, before):
    tile = min(512, z.fq)
    per = z.fq // tile
    at = z.at["quarter"]
    first = quarters[0]
    block = lambda i, q: (0, q[at + first + i // per] * per + i % per)
    specs, flat = [], []
    for d in range(z.nd):
        for k, r in enumerate(quarters):
            inner = lambda i, k=k: jnp.clip(i - k * per, 0, per - 1)
            if d == 0:
                index = lambda i, q, r=r, inner=inner: (q[at + r] * per + inner(i), 0)
            else:
                index = lambda i, q, inner=inner: (inner(i), 0)
            specs.append(pl.BlockSpec((tile, z.columns), index))
            flat.append(piece_list[d][r])
    inputs = [maps, sums, unfold, job_of, *grads, *flat]
    in_specs = [pl.BlockSpec((z.wide, tile), block), whole(sums), whole(unfold), whole(job_of)]
    in_specs += [whole(x) for x in grads] + specs
    alias = None
    if before is not None:
        alias = {1 + len(inputs): 0}
        inputs.append(before)
        in_specs.append(pl.BlockSpec(memory_space=pl.ANY))
    share = len(quarters) * z.fq
    return call(
        functools.partial(gradient_kernel, z, quarters, per, before is not None),
        "token_gradient_%d" % first, (len(quarters) * per,), sc, inputs, in_specs,
        jax.ShapeDtypeStruct((z.rows, z.width), bf16), pl.BlockSpec((z.rows, tile), block),
        2 * z.rows * share * (z.nd * z.columns + z.wide), 2 * share * (z.rows + z.nd * z.columns), 32 * MIB,
        scratch=(pltpu.VMEM((z.nd, z.rows, z.columns), bf16), pltpu.VMEM((z.rows, z.wide), bf16)),
        alias=alias,
    )


def body(
    tokens,
    cotangent,
    frozen_value_weight,
    adapter_down,
    adapter_up,
    tokens_per_job,
    packed_block_slots,
):
    nd, nt, ns, np_ = (lax.axis_size(a) for a in ("dp", "tensor", "sub", "parts"))
    z, t, s, p = (lax.axis_index(a) for a in ("dp", "tensor", "sub", "parts"))
    blocks, halved, width = tokens.shape[1:]
    heads = cotangent.shape[3]
    jobs_dev, rank, _ = adapter_down.shape
    columns = frozen_value_weight.shape[1]
    zz = Sizes(nd, nt, ns, np_, blocks, halved, width, heads, jobs_dev, rank, columns)
    rows, r2, m, cap = zz.rows, rank // ns, zz.per_head, zz.cap
    own_tokens = tokens.reshape(rows, width)
    own_grad = cotangent.reshape(rows, heads)

    quarters = jnp.stack([(p - a) % np_ * ns + (s - b) % ns for a in range(np_) for b in range(ns)]).astype(i32)
    moving = lax.dynamic_slice_in_dim(frozen_value_weight, (p * ns + s) * zz.fq, zz.fq, axis=0)
    rounds = [None, shifted(moving, "dp", nd, 1)]

    maps = jnp.concatenate([adapter_down, adapter_up], axis=2).reshape(jobs_dev, ns, r2, width + heads)
    maps = lax.dynamic_index_in_dim(maps, s, 1, keepdims=False)
    maps = jnp.concatenate(gather_shifts(maps, "dp", nd), axis=0).reshape(zz.jobs * r2, -1)
    maps = jnp.concatenate(gather_shifts(maps, "sub", ns), axis=0)
    grads = gather_shifts(own_grad, "tensor", nt)

    positions = jnp.arange(blocks, dtype=i32)
    dest = packed_block_slots // blocks
    same = dest[:, :, None] == dest[:, None, :]
    earlier = positions[None, None, :] < positions[None, :, None]
    send_rank = jnp.sum((same & earlier).astype(i32), axis=2, dtype=i32)
    flat_slots = packed_block_slots.reshape(-1)
    flat_ids = jnp.arange(nd * blocks, dtype=i32)
    slot_owner = flat_slots[None, :] == (z * blocks + positions)[:, None]
    block_ids = jnp.sum(jnp.where(slot_owner, flat_ids[None, :], 0), axis=1, dtype=i32)
    in_rank = jnp.sum(jnp.where(slot_owner, send_rank.reshape(-1)[None, :], 0), axis=1, dtype=i32)
    in_slot = (z - block_ids // blocks) % nd * cap + in_rank
    own_dest = lax.dynamic_index_in_dim(dest, z, 0, keepdims=False)
    own_rank = lax.dynamic_index_in_dim(send_rank, z, 0, keepdims=False)
    out_slot = (own_dest - z) % nd * cap + own_rank
    slot_range = jnp.arange(zz.slots, dtype=i32)

    def positions_of(slots):
        match = slots[None, :] == slot_range[:, None]
        return jnp.sum(jnp.where(match, positions[None, :], 0), axis=1, dtype=i32), jnp.any(match, axis=1)

    out_pos, out_fill = positions_of(out_slot)
    in_pos, in_fill = positions_of(in_slot)

    def facts(ids):
        job, valid = block_facts(tokens_per_job, ids, halved * ns)
        return (z - job // jobs_dev) % nd * jobs_dev + job % jobs_dev, valid - s * halved

    out_rel, out_valid = facts(z * blocks + positions)
    in_rel, in_valid = facts(block_ids)

    def arrival(index):
        found = (z - index * m - jnp.arange(m, dtype=i32)) % nd
        place_of = jnp.sum((found[None, :] < found[:, None]).astype(i32), axis=1)
        match = place_of[None, :] == jnp.arange(m, dtype=i32)[:, None]
        return jnp.sum(jnp.where(match, found[None, :], 0), axis=1, dtype=i32)

    shard_of = (z - jnp.arange(nd, dtype=i32)) % nd
    shard_at = (t - shard_of // m) % nt * m + shard_of % m
    head_at = (z - arrival(t)) % nd - t * m
    sc = jnp.concatenate(
        [
            x.astype(i32)
            for x in (out_pos, in_pos, out_fill, in_fill, out_rel, in_rel, out_valid, in_valid, quarters, shard_at, head_at)
        ]
    )
    column = jnp.arange(zz.wide, dtype=i32)
    job_of = (column // r2 % zz.jobs)[None, :]
    rank_of = column // (zz.jobs * r2) * r2 + column % r2
    unfold = (jnp.arange(rank, dtype=i32)[:, None] == rank_of[None, :]).astype(bf16)
    fold = unfold.astype(f32).T

    def spread_round(d, over_parts):
        pieces = []
        for y in over_parts:
            pieces += gather_shifts(y, "sub", ns)
        return pieces

    maps, rounds[1], sc = tie(maps, rounds[1], sc)
    over = [None] * nd
    over[1] = gather_shifts(rounds[1], "parts", np_)
    if nd > 2:
        rounds.append(shifted(rounds[1], "dp", nd, 1))
    part = products(zz, sc, own_tokens, own_grad, maps, fold, job_of)
    parts = gather_shifts(part, "tensor", nt)
    late_tokens, _ = tie(own_tokens, part)
    base = [base_product(zz, sc, late_tokens, [frozen_value_weight] * zz.nq, 0)]
    tied = tie(base[0], *parts)
    base[0], parts = tied[0], tied[1:]
    sums, *pays = sums_of(zz, sc, parts)
    got = [shifted(pays[d], "dp", nd, d) for d in range(nd)]

    if nd > 2:
        tied = tie(rounds[2], *over[1], *got)
        rounds[2], over[1], got = tied[0], list(tied[1 : 1 + np_]), tied[1 + np_ :]
    piece_list = [[frozen_value_weight] * zz.nq, spread_round(1, over[1])]
    for d in range(2, nd):
        over[d] = gather_shifts(rounds[d], "parts", np_)
        if d + 1 < nd:
            rounds.append(shifted(rounds[d], "dp", nd, 1))
        piece_list.append(spread_round(d, over[d]))
    mine, theirs = tables_of(zz, sc, own_tokens, own_grad, unfold, job_of, got)
    theirs = shifted(theirs, "sub", ns, 1)
    late_tokens, mine = tie(own_tokens, mine)
    base.append(base_product(zz, sc, late_tokens, piece_list[1], 1))
    mine, base[1], theirs = tie(mine, base[1], theirs)

    summed = (mine + theirs).reshape(nd, jobs_dev * r2, -1)
    sending = [summed[d].astype(bf16) for d in range(nd)]
    if nd > 3:
        rounds[3], *sending = tie(rounds[3], *sending)
        over[3] = gather_shifts(rounds[3], "parts", np_)
        piece_list[3] = spread_round(3, over[3])
    total = sending[0].astype(f32)
    for d in range(1, nd):
        total = total + shifted(sending[d], "dp", nd, -d).astype(f32)
    counts = lax.dynamic_slice_in_dim(tokens_per_job, z * jobs_dev, jobs_dev).astype(f32)
    total = total.reshape(jobs_dev, r2, -1) * (adapter_scale / counts)[:, None, None]
    halves = gather_shifts(total, "sub", ns)
    owned = jnp.concatenate(
        [sum(jnp.where((s - h) % ns == k, x, 0.0) for k, x in enumerate(halves)) for h in range(ns)], axis=1
    )
    grad_down, grad_up = owned[:, :, :width], owned[:, :, width:]

    for d in range(2, nd):
        base.append(base_product(zz, sc, own_tokens, piece_list[d], d))

    def arriving(index, j):
        d = arrival(index)[j]
        picked = base[j]
        for k in range(j + 1, nd - m + j + 1):
            picked = jnp.where(d == k, base[k], picked)
        return picked

    given = [arriving(t, j) for j in range(m)]
    for d in range(1, nt):
        given += [shifted(arriving((t + d) % nt, j), "tensor", nt, d) for j in range(m)]
    half = zz.nq // 2
    grads = [grads[0]] + list(tie(base[-1], *grads[1:])[1:])
    gradient = token_gradient_of(zz, sc, grads, maps, sums, unfold, job_of, piece_list, list(range(half)), None)
    gradient, *given = tie(gradient, *given)
    layer = layer_of(zz, sc, sums, maps, unfold, job_of, given)
    layer, gradient = tie(layer, gradient)
    landed = [shifted(layer[d], "dp", nd, d) for d in range(nd)]
    gradient = token_gradient_of(
        zz, sc, grads, maps, sums, unfold, job_of, piece_list, list(range(half, zz.nq)), gradient
    )
    gradient, *landed = tie(gradient, *landed)
    layer_output = place(zz, sc, landed)
    return (
        layer_output.reshape(1, blocks, halved, heads),
        gradient.reshape(1, blocks, halved, width),
        grad_down,
        grad_up,
    )


def solution(mesh):
    return jax.shard_map(
        body,
        mesh=mesh,
        in_specs=(
            P(("parts", "dp"), None, "sub", "tensor"),
            P(("parts", "dp"), None, "sub", "tensor"),
            P("tensor", "dp"),
            P(("parts", "dp"), None, "tensor"),
            P(("parts", "dp"), None, "tensor"),
            P("parts"),
            P("parts", None),
        ),
        out_specs=(
            P(("parts", "dp"), None, "sub", "tensor"),
            P(("parts", "dp"), None, "sub", "tensor"),
            P(("parts", "dp"), None, "tensor"),
            P(("parts", "dp"), None, "tensor"),
        ),
        check_vma=False,
    )
```

time: 177 us -> 146 us (0.82)
  matrix products: 58 us -> 0 us
  Pallas kernels: 0 us -> 40.8 us
  local copies, waits for them, and re-layouts: 19.7 us -> 8.95 us
  between operations: 15.4 us -> 6.84 us
  waiting for transfers between devices: 42.4 us -> 50.3 us
  other arithmetic: 12.8 us -> 8.22 us
  starting transfers between devices: 28.1 us -> 30.2 us
    dot_general x14 -> x0, matrix products: 58 us -> none  [dot(): return lax.dot_general(a, b, (dims, ((), ())), preferred_element_type=f32)]
    pallas_call x0 -> x11, Pallas kernels: none -> 40.8 us  [call(): pl.pallas_call(kernel, out_shape=out_shape, grid_spec=pltpu.PrefetchScala...]
    ppermute x21 -> x31, waiting for transfers between devices: 42.4 us -> 50.3 us  [shifted(): lax.ppermute(values, axis, [(i, (i + step) % count) for i in range(count)])]
    gather x9 -> x0, local copies, waits for them, and re-layouts: 5.32 us -> none  [the longest x3 1.71 us: exchange(): return jnp.take(jnp.concatenate(got, axis=0), back, axis=0)]
    select_n x16 -> x4, other arithmetic: 3.01 us -> 0.16 us  [the longest x1 0.12 us: arriving(): picked = jnp.where(d == k, base[k], picked)]
    concatenate x2 -> x1, local copies, waits for them, and re-layouts: 2.68 us -> 0.09 us  [body(): jnp.concatenate([x.astype(i32) for x in (out_pos, in_pos, out_fill, in_fi...]
    unnamed x35 -> x30, local copies, waits for them, and re-layouts: 2.61 us -> 5.1 us
    ppermute x21 -> x31, starting transfers between devices: 28.1 us -> 30.2 us  [shifted(): lax.ppermute(values, axis, [(i, (i + step) % count) for i in range(count)])]
  transfers between devices with their start and end apart: 22 -> 31, of which waited for: 11 -> 13; matrix products, arithmetic and copies ran while one was open for 42% -> 8% of each run, Pallas kernels for 0% -> 26%
where the time goes in v3:
time: 146 us; the launch traced here: 145 us
  waiting for transfers between devices  50.3 us (34%)
  Pallas kernels  40.8 us (28%)
  starting transfers between devices  30.2 us (21%)
  local copies, waits for them, and re-layouts  8.95 us (6%)
  other arithmetic  8.22 us (6%)
  between operations  6.84 us (5%)
    ppermute x31, waiting for transfers between devices, shifted(): lax.ppermute(values, axis, [(i, (i + step) % count) for i in range(count)])  50.3 us
    pallas_call x11, Pallas kernels, call(): pl.pallas_call(kernel, out_shape=out_shape, grid_spec=pltpu.PrefetchScala...  40.8 us
    ppermute x31, starting transfers between devices, shifted(): lax.ppermute(values, axis, [(i, (i + step) % count) for i in range(count)])  30.2 us
    unnamed x30, local copies, waits for them, and re-layouts  5.1 us
  transfers between devices with their start and end apart: 31, of which 13 were waited for; matrix products, arithmetic and copies ran while one was open for 8% of the time, Pallas kernels for 26%

profile of v3, /device:TPU:0, one launch (start us, length us, event | category | flops | bytes accessed | tf_op | source)
XLA Modules:
  0.0 145.3 jit_solution(7326538233691054771)
XLA Ops:
  1.7 5.1 %collective-permute-start.2 = (bf16[1,8,4608]{2,1,0:T(8,128)(2,1)S(1)}, bf16[1,8,4608]{2,1,0:T(8,128)(2,1)S(1)}, u32[]{:S(2)}, u32[]{:S(2)}) collective-permute-start(bf16[1,8,4608]{2,1,0:T(8,128)(2,1)S(1)} %dynamic-slice_bitcast_fusion), channel_id=1, source_target_pairs={{0,12},{4,0},{8,4},{12,8},{1,13},{5,1},{9,5},{13,9},{2,14},{6,2},{... | collective-permute-start | bytes 221192 | tf_op jit(solution)/shard_map/ppermute | solution.py:33
  8.9 2.5 %collective-permute-start.4 = (bf16[1024,256]{1,0:T(8,128)(2,1)S(1)}, bf16[1024,256]{1,0:T(8,128)(2,1)}, u32[]{:S(2)}, u32[]{:S(2)}) collective-permute-start(bf16[1024,256]{1,0:T(8,128)(2,1)S(1)} %constant_dynamic-slice_fusion.2), channel_id=1, source_target_pairs={{0,4},{4,8},{8,12},{12,0},{1,5},{5,9},{9,13},{13,1},{2,6},{6,10},{... | collective-permute-start | bytes 1572872 | tf_op jit(solution)/shard_map/ppermute | solution.py:33
  16.5 8.5 %collective-permute-done.1 = bf16[1,8,4608]{2,1,0:T(8,128)(2,1)S(1)} collective-permute-done((bf16[1,8,4608]{2,1,0:T(8,128)(2,1)S(1)}, bf16[1,8,4608]{2,1,0:T(8,128)(2,1)S(1)}, u32[]{:S(2)}, u32[]{:S(2)}) %collective-permute-start.1) | collective-permute-done | bytes 73760 | tf_op jit(solution)/shard_map/ppermute | solution.py:33
  28.5 2.2 %copy-done = bf16[1,8,64,4096]{3,2,1,0:T(8,128)(2,1)S(1)} copy-done((bf16[1,8,64,4096]{3,2,1,0:T(8,128)(2,1)S(1)}, bf16[1,8,64,4096]{3,2,1,0:T(8,128)(2,1)}, u32[]{:S(2)}) %copy-start) | copy-done | bytes 4194328
  30.6 4.2 %adapter_products.1.refs_0_ = bf16[512,32]{1,0:T(8,128)(2,1)S(1)} custom-call(s32[74]{0:T(128)S(1)} %concatenate.18.sc, bf16[512,4096]{1,0:T(8,128)(2,1)S(1)} %bitcast.34, bf16[512,512]{1,0:T(8,128)(2,1)S(1)} %bitcast.40, bf16[64,4608]{1,0:T(8,128)(2,1)S(1)} %pad_maximum_fusion.maps, f32[64,16]{1,0:T(8,128)S(1)} %fusion.2.fold, ...), custom_call_target="tpu_custom_call" | custom-call | flops 301989888 | bytes 4718592 | tf_op jit(solution)/shard_map/adapter_products/pallas_call | solution.py:74
  36.3 2.7 %base_0.1 = bf16[512,256]{1,0:T(8,128)(2,1)S(1)} custom-call(s32[74]{0:T(128)S(1)} %concatenate.18.sc, bf16[512,4096]{1,0:T(8,128)(2,1)S(1)} %bitcast.35, bf16[4096,256]{1,0:T(8,128)(2,1)S(1)} %copy-done.2, bf16[4096,256]{1,0:T(8,128)(2,1)S(1)} %copy-done.2, bf16[4096,256]{1,0:T(8,128)(2,1)S(1)} %copy-done.2, bf16[4096,256]{1,0:T(8,128)(2,1)S(1)} %copy-done.2), custom_call_target="tpu_custom_call" | custom-call | flops 1073741824 | bytes 6291456 | tf_op jit(solution)/shard_map/base_0/pallas_call | solution.py:74
  41.3 3.6 %collective-permute-start.9 = (bf16[128,32]{1,0:T(8,128)(2,1)S(1)}, bf16[128,32]{1,0:T(8,128)(2,1)S(1)}, u32[]{:S(2)}, u32[]{:S(2)}) collective-permute-start(bf16[128,32]{1,0:T(8,128)(2,1)S(1)} %get-tuple-element.64), channel_id=1, source_target_pairs={{0,8},{4,12},{8,0},{12,4},{1,9},{5,13},{9,1},{13,5},{2,10},{6,14},... | collective-permute-start | bytes 24584 | tf_op jit(solution)/shard_map/ppermute | solution.py:33
  44.9 1.6 %collective-permute-done.8.refs_1_ = bf16[128,32]{1,0:T(8,128)(2,1)S(1)} collective-permute-done((bf16[128,32]{1,0:T(8,128)(2,1)S(1)}, bf16[128,32]{1,0:T(8,128)(2,1)S(1)}, u32[]{:S(2)}, u32[]{:S(2)}) %collective-permute-start.8) | collective-permute-done | bytes 8224 | tf_op jit(solution)/shard_map/ppermute | solution.py:33
  47.2 1.6 %collective-permute-done.10.refs_3_ = bf16[128,32]{1,0:T(8,128)(2,1)S(1)} collective-permute-done((bf16[128,32]{1,0:T(8,128)(2,1)S(1)}, bf16[128,32]{1,0:T(8,128)(2,1)S(1)}, u32[]{:S(2)}, u32[]{:S(2)}) %collective-permute-start.10) | collective-permute-done | bytes 8224 | tf_op jit(solution)/shard_map/ppermute | solution.py:33
  49.4 5.7 %job_tables.1 = (f32[32,4608]{1,0:T(8,128)S(1)}, f32[32,4608]{1,0:T(8,128)S(1)}) custom-call(s32[74]{0:T(128)S(1)} %concatenate.18.sc, bf16[512,4096]{1,0:T(8,128)(2,1)S(1)} %bitcast.36, bf16[512,512]{1,0:T(8,128)(2,1)S(1)} %bitcast.41, bf16[16,64]{1,0:T(8,128)(2,1)S(1)} %fusion.3.unfold, s32[1,64]{1,0:T(1,128)S(1)} %and_select_fusion.1.job_of, ...), custom_call_target="tpu_custom_call" | custom-call | flops 301989888 | bytes 5242880 | tf_op jit(solution)/shard_map/job_tables/pallas_call | solution.py:74
  58.5 3.7 %base_1.1 = bf16[512,256]{1,0:T(8,128)(2,1)S(1)} custom-call(s32[74]{0:T(128)S(1)} %concatenate.18.sc, bf16[512,4096]{1,0:T(8,128)(2,1)S(1)} %bitcast.37, bf16[1024,256]{1,0:T(8,128)(2,1)} %collective-permute-done.4.refs_0_.refs_4_, bf16[1024,256]{1,0:T(8,128)(2,1)S(1)} %collective-permute-done.12.refs_1_.refs_5_, ...), custom_call_target="tpu_custom_call" | custom-call | flops 1073741824 | bytes 6291456 | tf_op jit(solution)/shard_map/base_1/pallas_call | solution.py:74
  63.1 11.3 %collective-permute-done.11.refs_0_.refs_8_ = bf16[1024,256]{1,0:T(8,128)(2,1)} collective-permute-done((bf16[1024,256]{1,0:T(8,128)(2,1)}, bf16[1024,256]{1,0:T(8,128)(2,1)}, u32[]{:S(2)}, u32[]{:S(2)}) %collective-permute-start.11) | collective-permute-done | bytes 524320 | tf_op jit(solution)/shard_map/ppermute | solution.py:33
  74.7 1.7 %collective-permute-start.29 = (bf16[8,4608]{1,0:T(8,128)(2,1)S(1)}, bf16[8,4608]{1,0:T(8,128)(2,1)S(1)}, u32[]{:S(2)}, u32[]{:S(2)}) collective-permute-start(bf16[8,4608]{1,0:T(8,128)(2,1)S(1)} %get-tuple-element.105), channel_id=1, source_target_pairs={{0,4},{4,8},{8,12},{12,0},{1,5},{5,9},{9,13},{13,1},{2,6},{6,10},{... | collective-permute-start | bytes 221192 | tf_op jit(solution)/shard_map/ppermute | solution.py:33
  77.1 1.8 %collective-permute-done.27 = bf16[8,4608]{1,0:T(8,128)(2,1)S(1)} collective-permute-done((bf16[8,4608]{1,0:T(8,128)(2,1)S(1)}, bf16[8,4608]{1,0:T(8,128)(2,1)S(1)}, u32[]{:S(2)}, u32[]{:S(2)}) %collective-permute-start.27) | collective-permute-done | bytes 73760 | tf_op jit(solution)/shard_map/ppermute | solution.py:33
  78.8 3.5 %collective-permute-done.28 = bf16[8,4608]{1,0:T(8,128)(2,1)S(1)} collective-permute-done((bf16[8,4608]{1,0:T(8,128)(2,1)S(1)}, bf16[8,4608]{1,0:T(8,128)(2,1)S(1)}, u32[]{:S(2)}, u32[]{:S(2)}) %collective-permute-start.28) | collective-permute-done | bytes 73760 | tf_op jit(solution)/shard_map/ppermute | solution.py:33
  91.2 12.9 %collective-permute-done.16.refs_2_.refs_8_ = bf16[1024,256]{1,0:T(8,128)(2,1)S(1)} collective-permute-done((bf16[1024,256]{1,0:T(8,128)(2,1)}, bf16[1024,256]{1,0:T(8,128)(2,1)S(1)}, u32[]{:S(2)}, u32[]{:S(2)}) %collective-permute-start.16) | collective-permute-done | bytes 524320 | tf_op jit(solution)/shard_map/ppermute | solution.py:33
  104.8 2.2 %copy-done.1 = bf16[1,8,64,4096]{3,2,1,0:T(8,128)(2,1)S(1)} copy-done((bf16[1,8,64,4096]{3,2,1,0:T(8,128)(2,1)S(1)}, bf16[1,8,64,4096]{3,2,1,0:T(8,128)(2,1)}, u32[]{:S(2)}) %copy-start.1) | copy-done | bytes 4194328
  106.9 3.9 %base_2.1 = bf16[512,256]{1,0:T(8,128)(2,1)S(1)} custom-call(s32[74]{0:T(128)S(1)} %concatenate.18.sc, bf16[512,4096]{1,0:T(8,128)(2,1)S(1)} %bitcast.38, bf16[1024,256]{1,0:T(8,128)(2,1)} %collective-permute-done.6.refs_6_.refs_0_, bf16[1024,256]{1,0:T(8,128)(2,1)S(1)} %collective-permute-done.21.refs_7_.refs_1_, ...), custom_call_target="tpu_custom_call" | custom-call | flops 1073741824 | bytes 6291456 | tf_op jit(solution)/shard_map/base_2/pallas_call | solution.py:74
  110.9 3.7 %base_3.1 = bf16[512,256]{1,0:T(8,128)(2,1)S(1)} custom-call(s32[74]{0:T(128)S(1)} %concatenate.18.sc, bf16[512,4096]{1,0:T(8,128)(2,1)S(1)} %bitcast.39, bf16[1024,256]{1,0:T(8,128)(2,1)} %collective-permute-done.11.refs_0_.refs_8_, bf16[1024,256]{1,0:T(8,128)(2,1)S(1)} %collective-permute-done.15.refs_1_.refs_9_, ...), custom_call_target="tpu_custom_call" | custom-call | flops 1073741824 | bytes 6291456 | tf_op jit(solution)/shard_map/base_3/pallas_call | solution.py:74
  117.5 6.5 %token_gradient_0.1.refs_10_ = bf16[512,4096]{1,0:T(8,128)(2,1)} custom-call(s32[74]{0:T(128)S(1)} %concatenate.18.sc, bf16[64,4608]{1,0:T(8,128)(2,1)S(1)} %pad_maximum_fusion.maps, bf16[512,32]{1,0:T(8,128)(2,1)S(1)} %get-tuple-element.60.sums, bf16[16,64]{1,0:T(8,128)(2,1)S(1)} %fusion.3.unfold, s32[1,64]{1,0:T(1,128)S(1)} %and_select_fusion.1.job_of, ...), custom_call_target="tpu_custom_call" | custom-call | flops 2281701376 | bytes 6291456 | tf_op jit(solution)/shard_map/token_gradient_0/pallas_call | solution.py:74
  124.0 5.2 %collective-permute-done.22.refs_2_ = bf16[512,256]{1,0:T(8,128)(2,1)S(1)} collective-permute-done((bf16[512,256]{1,0:T(8,128)(2,1)S(1)}, bf16[512,256]{1,0:T(8,128)(2,1)S(1)}, u32[]{:S(2)}, u32[]{:S(2)}) %collective-permute-start.22) | collective-permute-done | bytes 262176 | tf_op jit(solution)/shard_map/ppermute | solution.py:33
  129.1 2.1 %layer.1 = (bf16[128,512]{1,0:T(8,128)(2,1)S(1)}, bf16[128,512]{1,0:T(8,128)(2,1)S(1)}, bf16[128,512]{1,0:T(8,128)(2,1)S(1)}, bf16[128,512]{1,0:T(8,128)(2,1)S(1)}) custom-call(s32[74]{0:T(128)S(1)} %concatenate.18.sc, bf16[512,32]{1,0:T(8,128)(2,1)S(1)} %get-tuple-element.60.sums, bf16[64,4608]{1,0:T(8,128)(2,1)S(1)} %pad_maximum_fusion.maps, ...), custom_call_target="tpu_custom_call" | custom-call | flops 33554432 | bytes 1572864 | tf_op jit(solution)/shard_map/layer/pallas_call | solution.py:74
  134.2 2.6 %collective-permute-start.26 = (bf16[128,512]{1,0:T(8,128)(2,1)S(1)}, bf16[128,512]{1,0:T(8,128)(2,1)S(1)}, u32[]{:S(2)}, u32[]{:S(2)}) collective-permute-start(bf16[128,512]{1,0:T(8,128)(2,1)S(1)} %get-tuple-element.96), channel_id=1, source_target_pairs={{0,12},{4,0},{8,4},{12,8},{1,13},{5,1},{9,5},{13,9},{2,14},{6,2},{... | collective-permute-start | bytes 393224 | tf_op jit(solution)/shard_map/ppermute | solution.py:33
  136.8 6.3 %token_gradient_2.1 = bf16[512,4096]{1,0:T(8,128)(2,1)} custom-call(s32[74]{0:T(128)S(1)} %concatenate.18.sc, bf16[64,4608]{1,0:T(8,128)(2,1)S(1)} %pad_maximum_fusion.maps, bf16[512,32]{1,0:T(8,128)(2,1)S(1)} %get-tuple-element.60.sums, bf16[16,64]{1,0:T(8,128)(2,1)S(1)} %fusion.3.unfold, ...), custom_call_target="tpu_custom_call", output_to_operand_aliasing={{}: (15, {})} | custom-call | flops 2281701376 | bytes 6291456 | tf_op jit(solution)/shard_map/token_gradient_2/pallas_call | solution.py:74
  (127 shorter events, 33.6 us)
Async XLA Ops:
  1.7 14.8 %collective-permute-start.2 = (bf16[1,8,4608]{2,1,0:T(8,128)(2,1)S(1)}, bf16[1,8,4608]{2,1,0:T(8,128)(2,1)S(1)}, u32[]{:S(2)}, u32[]{:S(2)}) collective-permute-start(bf16[1,8,4608]{2,1,0:T(8,128)(2,1)S(1)} %dynamic-slice_bitcast_fusion), channel_id=1, source_target_pairs={{0,12},{4,0},{8,4},{12,8},{1,13},{5,1},{9,5},{13,9},{2,14},{6,2},{... | collective-permute-start | bytes 221192 | tf_op jit(solution)/shard_map/ppermute | solution.py:33
  6.8 18.2 %collective-permute-start.1 = (bf16[1,8,4608]{2,1,0:T(8,128)(2,1)S(1)}, bf16[1,8,4608]{2,1,0:T(8,128)(2,1)S(1)}, u32[]{:S(2)}, u32[]{:S(2)}) collective-permute-start(bf16[1,8,4608]{2,1,0:T(8,128)(2,1)S(1)} %dynamic-slice_bitcast_fusion), channel_id=1, source_target_pairs={{0,8},{4,12},{8,0},{12,4},{1,9},{5,13},{9,1},{13,5},{2,10},{6,14},... | collective-permute-start | bytes 221192 | tf_op jit(solution)/shard_map/ppermute | solution.py:33
  6.8 18.2 %collective-permute-start = (bf16[1,8,4608]{2,1,0:T(8,128)(2,1)S(1)}, bf16[1,8,4608]{2,1,0:T(8,128)(2,1)S(1)}, u32[]{:S(2)}, u32[]{:S(2)}) collective-permute-start(bf16[1,8,4608]{2,1,0:T(8,128)(2,1)S(1)} %dynamic-slice_bitcast_fusion), channel_id=1, source_target_pairs={{0,4},{4,8},{8,12},{12,0},{1,5},{5,9},{9,13},{13,1},{2,6},{6,10},{... | collective-permute-start | bytes 221192 | tf_op jit(solution)/shard_map/ppermute | solution.py:33
  8.9 17.9 %collective-permute-start.4 = (bf16[1024,256]{1,0:T(8,128)(2,1)S(1)}, bf16[1024,256]{1,0:T(8,128)(2,1)}, u32[]{:S(2)}, u32[]{:S(2)}) collective-permute-start(bf16[1024,256]{1,0:T(8,128)(2,1)S(1)} %constant_dynamic-slice_fusion.2), channel_id=1, source_target_pairs={{0,4},{4,8},{8,12},{12,0},{1,5},{5,9},{9,13},{13,1},{2,6},{6,10},{... | collective-permute-start | bytes 1572872 | tf_op jit(solution)/shard_map/ppermute | solution.py:33
  26.7 22.1 %collective-permute-start.7 = (bf16[1024,256]{1,0:T(8,128)(2,1)}, bf16[1024,256]{1,0:T(8,128)(2,1)S(1)}, u32[]{:S(2)}, u32[]{:S(2)}) collective-permute-start(bf16[1024,256]{1,0:T(8,128)(2,1)} %collective-permute-done.4.refs_0_.refs_4_), channel_id=1, source_target_pairs={{0,16},{16,0},{1,17},{17,1},{2,18},{18,2},{3,19},{19,3},{4,20},{20... | collective-permute-start | bytes 1572872 | tf_op jit(solution)/shard_map/ppermute | solution.py:33
  28.3 20.5 %collective-permute-start.6 = (bf16[1024,256]{1,0:T(8,128)(2,1)}, bf16[1024,256]{1,0:T(8,128)(2,1)}, u32[]{:S(2)}, u32[]{:S(2)}) collective-permute-start(bf16[1024,256]{1,0:T(8,128)(2,1)} %collective-permute-done.4.refs_0_.refs_4_), channel_id=1, source_target_pairs={{0,4},{4,8},{8,12},{12,0},{1,5},{5,9},{9,13},{13,1},{2,6},{6,10},{... | collective-permute-start | bytes 1572872 | tf_op jit(solution)/shard_map/ppermute | solution.py:33
  48.8 9.7 %collective-permute-start.12 = (bf16[1024,256]{1,0:T(8,128)(2,1)}, bf16[1024,256]{1,0:T(8,128)(2,1)S(1)}, u32[]{:S(2)}, u32[]{:S(2)}) collective-permute-start(bf16[1024,256]{1,0:T(8,128)(2,1)} %collective-permute-done.4.refs_0_.refs_4_), channel_id=1, source_target_pairs={{0,1},{1,0},{2,3},{3,2},{4,5},{5,4},{6,7},{7,6},{8,9},{9,8},{10,11... | collective-permute-start | bytes 1572872 | tf_op jit(solution)/shard_map/ppermute | solution.py:33
  48.9 9.6 %collective-permute-start.13 = (bf16[1024,256]{1,0:T(8,128)(2,1)S(1)}, bf16[1024,256]{1,0:T(8,128)(2,1)S(1)}, u32[]{:S(2)}, u32[]{:S(2)}) collective-permute-start(bf16[1024,256]{1,0:T(8,128)(2,1)S(1)} %collective-permute-done.7.refs_2_.refs_4_), channel_id=1, source_target_pairs={{0,1},{1,0},{2,3},{3,2},{4,5},{5,4},{6,7},{7,6},{8,9},{9,8},{10,11... | collective-permute-start | bytes 1572872 | tf_op jit(solution)/shard_map/ppermute | solution.py:33
  55.1 7.9 %collective-permute-start.14 = (f32[32,4608]{1,0:T(8,128)S(1)}, f32[32,4608]{1,0:T(8,128)S(1)}, u32[]{:S(2)}, u32[]{:S(2)}) collective-permute-start(f32[32,4608]{1,0:T(8,128)S(1)} %get-tuple-element.76), channel_id=1, source_target_pairs={{0,1},{1,0},{2,3},{3,2},{4,5},{5,4},{6,7},{7,6},{8,9},{9,8},{10,11... | collective-permute-start | bytes 1769480 | tf_op jit(solution)/shard_map/ppermute | solution.py:33
  55.2 62.2 %collective-permute-start.18 = (bf16[512,512]{1,0:T(8,128)(2,1)S(1)}, bf16[512,512]{1,0:T(8,128)(2,1)}, u32[]{:S(2)}, u32[]{:S(2)}) collective-permute-start(bf16[512,512]{1,0:T(8,128)(2,1)S(1)} %bitcast.42), channel_id=1, source_target_pairs={{0,2},{2,0},{1,3},{3,1},{4,6},{6,4},{5,7},{7,5},{8,10},{10,8},{9,1... | collective-permute-start | bytes 1572872 | tf_op jit(solution)/shard_map/ppermute | solution.py:33
  58.2 16.2 %collective-permute-start.11 = (bf16[1024,256]{1,0:T(8,128)(2,1)}, bf16[1024,256]{1,0:T(8,128)(2,1)}, u32[]{:S(2)}, u32[]{:S(2)}) collective-permute-start(bf16[1024,256]{1,0:T(8,128)(2,1)} %collective-permute-done.6.refs_6_.refs_0_), channel_id=1, source_target_pairs={{0,4},{4,8},{8,12},{12,0},{1,5},{5,9},{9,13},{13,1},{2,6},{6,10},{... | collective-permute-start | bytes 1572872 | tf_op jit(solution)/shard_map/ppermute | solution.py:33
  74.7 7.6 %collective-permute-start.28 = (bf16[8,4608]{1,0:T(8,128)(2,1)S(1)}, bf16[8,4608]{1,0:T(8,128)(2,1)S(1)}, u32[]{:S(2)}, u32[]{:S(2)}) collective-permute-start(bf16[8,4608]{1,0:T(8,128)(2,1)S(1)} %get-tuple-element.104), channel_id=1, source_target_pairs={{0,8},{4,12},{8,0},{12,4},{1,9},{5,13},{9,1},{13,5},{2,10},{6,14},... | collective-permute-start | bytes 221192 | tf_op jit(solution)/shard_map/ppermute | solution.py:33
  74.7 7.6 %collective-permute-start.29 = (bf16[8,4608]{1,0:T(8,128)(2,1)S(1)}, bf16[8,4608]{1,0:T(8,128)(2,1)S(1)}, u32[]{:S(2)}, u32[]{:S(2)}) collective-permute-start(bf16[8,4608]{1,0:T(8,128)(2,1)S(1)} %get-tuple-element.105), channel_id=1, source_target_pairs={{0,4},{4,8},{8,12},{12,0},{1,5},{5,9},{9,13},{13,1},{2,6},{6,10},{... | collective-permute-start | bytes 221192 | tf_op jit(solution)/shard_map/ppermute | solution.py:33
  76.5 13.0 %collective-permute-start.19 = (bf16[1024,256]{1,0:T(8,128)(2,1)}, bf16[1024,256]{1,0:T(8,128)(2,1)}, u32[]{:S(2)}, u32[]{:S(2)}) collective-permute-start(bf16[1024,256]{1,0:T(8,128)(2,1)} %collective-permute-done.6.refs_6_.refs_0_), channel_id=1, source_target_pairs={{0,16},{16,0},{1,17},{17,1},{2,18},{18,2},{3,19},{19,3},{4,20},{20... | collective-permute-start | bytes 1572872 | tf_op jit(solution)/shard_map/ppermute | solution.py:33
  82.4 7.6 %collective-permute-start.30 = (f32[1,8,4608]{2,1,0:T(8,128)S(1)}, f32[1,8,4608]{2,1,0:T(8,128)}, u32[]{:S(2)}, u32[]{:S(2)}) collective-permute-start(f32[1,8,4608]{2,1,0:T(8,128)S(1)} %bitcast.46), channel_id=1, source_target_pairs={{0,1},{1,0},{2,3},{3,2},{4,5},{5,4},{6,7},{7,6},{8,9},{9,8},{10,11... | collective-permute-start | bytes 442376 | tf_op jit(solution)/shard_map/ppermute | solution.py:33
  88.8 15.9 %collective-permute-start.21 = (bf16[1024,256]{1,0:T(8,128)(2,1)}, bf16[1024,256]{1,0:T(8,128)(2,1)S(1)}, u32[]{:S(2)}, u32[]{:S(2)}) collective-permute-start(bf16[1024,256]{1,0:T(8,128)(2,1)} %collective-permute-done.6.refs_6_.refs_0_), channel_id=1, source_target_pairs={{0,1},{1,0},{2,3},{3,2},{4,5},{5,4},{6,7},{7,6},{8,9},{9,8},{10,11... | collective-permute-start | bytes 1572872 | tf_op jit(solution)/shard_map/ppermute | solution.py:33
  89.5 15.3 %collective-permute-start.20 = (bf16[1024,256]{1,0:T(8,128)(2,1)}, bf16[1024,256]{1,0:T(8,128)(2,1)S(1)}, u32[]{:S(2)}, u32[]{:S(2)}) collective-permute-start(bf16[1024,256]{1,0:T(8,128)(2,1)} %collective-permute-done.19.refs_2_.refs_6_), channel_id=1, source_target_pairs={{0,1},{1,0},{2,3},{3,2},{4,5},{5,4},{6,7},{7,6},{8,9},{9,8},{10,11... | collective-permute-start | bytes 1572872 | tf_op jit(solution)/shard_map/ppermute | solution.py:33
  89.5 14.5 %collective-permute-start.16 = (bf16[1024,256]{1,0:T(8,128)(2,1)}, bf16[1024,256]{1,0:T(8,128)(2,1)S(1)}, u32[]{:S(2)}, u32[]{:S(2)}) collective-permute-start(bf16[1024,256]{1,0:T(8,128)(2,1)} %collective-permute-done.11.refs_0_.refs_8_), channel_id=1, source_target_pairs={{0,16},{16,0},{1,17},{17,1},{2,18},{18,2},{3,19},{19,3},{4,20},{20... | collective-permute-start | bytes 1572872 | tf_op jit(solution)/shard_map/ppermute | solution.py:33
  90.0 20.9 %collective-permute-start.15 = (bf16[1024,256]{1,0:T(8,128)(2,1)}, bf16[1024,256]{1,0:T(8,128)(2,1)S(1)}, u32[]{:S(2)}, u32[]{:S(2)}) collective-permute-start(bf16[1024,256]{1,0:T(8,128)(2,1)} %collective-permute-done.11.refs_0_.refs_8_), channel_id=1, source_target_pairs={{0,1},{1,0},{2,3},{3,2},{4,5},{5,4},{6,7},{7,6},{8,9},{9,8},{10,11... | collective-permute-start | bytes 1572872 | tf_op jit(solution)/shard_map/ppermute | solution.py:33
  114.7 9.2 %collective-permute-start.23 = (bf16[512,256]{1,0:T(8,128)(2,1)S(1)}, bf16[512,256]{1,0:T(8,128)(2,1)S(1)}, u32[]{:S(2)}, u32[]{:S(2)}) collective-permute-start(bf16[512,256]{1,0:T(8,128)(2,1)S(1)} %get-tuple-element.114), channel_id=1, source_target_pairs={{0,2},{2,0},{1,3},{3,1},{4,6},{6,4},{5,7},{7,5},{8,10},{10,8},{9,1... | collective-permute-start | bytes 786440 | tf_op jit(solution)/shard_map/ppermute | solution.py:33
  115.3 13.8 %collective-permute-start.22 = (bf16[512,256]{1,0:T(8,128)(2,1)S(1)}, bf16[512,256]{1,0:T(8,128)(2,1)S(1)}, u32[]{:S(2)}, u32[]{:S(2)}) collective-permute-start(bf16[512,256]{1,0:T(8,128)(2,1)S(1)} %get-tuple-element.119), channel_id=1, source_target_pairs={{0,2},{2,0},{1,3},{3,1},{4,6},{6,4},{5,7},{7,5},{8,10},{10,8},{9,1... | collective-permute-start | bytes 786440 | tf_op jit(solution)/shard_map/ppermute | solution.py:33
  131.2 11.9 %collective-permute-start.24 = (bf16[128,512]{1,0:T(8,128)(2,1)S(1)}, bf16[128,512]{1,0:T(8,128)(2,1)S(1)}, u32[]{:S(2)}, u32[]{:S(2)}) collective-permute-start(bf16[128,512]{1,0:T(8,128)(2,1)S(1)} %get-tuple-element.94), channel_id=1, source_target_pairs={{0,4},{4,8},{8,12},{12,0},{1,5},{5,9},{9,13},{13,1},{2,6},{6,10},{... | collective-permute-start | bytes 393224 | tf_op jit(solution)/shard_map/ppermute | solution.py:33
  132.8 11.1 %collective-permute-start.25 = (bf16[128,512]{1,0:T(8,128)(2,1)S(1)}, bf16[128,512]{1,0:T(8,128)(2,1)S(1)}, u32[]{:S(2)}, u32[]{:S(2)}) collective-permute-start(bf16[128,512]{1,0:T(8,128)(2,1)S(1)} %get-tuple-element.95), channel_id=1, source_target_pairs={{0,8},{4,12},{8,0},{12,4},{1,9},{5,13},{9,1},{13,5},{2,10},{6,14},... | collective-permute-start | bytes 393224 | tf_op jit(solution)/shard_map/ppermute | solution.py:33
  134.2 9.7 %collective-permute-start.26 = (bf16[128,512]{1,0:T(8,128)(2,1)S(1)}, bf16[128,512]{1,0:T(8,128)(2,1)S(1)}, u32[]{:S(2)}, u32[]{:S(2)}) collective-permute-start(bf16[128,512]{1,0:T(8,128)(2,1)S(1)} %get-tuple-element.96), channel_id=1, source_target_pairs={{0,12},{4,0},{8,4},{12,8},{1,13},{5,1},{9,5},{13,9},{2,14},{6,2},{... | collective-permute-start | bytes 393224 | tf_op jit(solution)/shard_map/ppermute | solution.py:33
  (22 other events, 149.2 us)

commit v4 on v3

--- a/solution.py
+++ b/solution.py
@@ -10,6 +10,7 @@
 adapter_scale = 2.0
 f32, bf16, i32 = jnp.float32, jnp.bfloat16, jnp.int32
 MIB = 1 << 20
+TOKEN_LIMIT = 50 * MIB
 
 
 def block_facts(tokens_per_job, block_ids, block_rows):
@@ -79,7 +80,7 @@
         ),
         input_output_aliases=alias or {},
         compiler_params=pltpu.CompilerParams(vmem_limit_bytes=limit),
-        cost_estimate=pl.CostEstimate(flops=flops, bytes_accessed=moved, transcendentals=0),
+        cost_estimate=pl.CostEstimate(flops=1000, bytes_accessed=1000, transcendentals=0),
         name=name,
     )(scalars, *inputs)
 
@@ -127,7 +128,7 @@
         ],
         jax.ShapeDtypeStruct((z.rows, 2 * z.rank), bf16),
         pl.BlockSpec((n * z.halved, 2 * z.rank), lambda i, _: (i, 0)),
-        2 * z.rows * (z.width + z.heads) * z.wide, 2 * z.rows * (z.width + z.heads), 16 * MIB,
+        2 * z.rows * (z.width + z.heads) * z.wide, 2 * z.rows * (z.width + z.heads), TOKEN_LIMIT,
     )
 
 
@@ -210,7 +211,7 @@
         ]
         + [whole(x) for x in got],
         (shape, shape), (out, out),
-        2 * z.wide * z.rows * (z.width + z.heads), 2 * z.rows * z.width + 4 * z.wide * z.width, 16 * MIB,
+        2 * z.wide * z.rows * (z.width + z.heads), 2 * z.rows * z.width + 4 * z.wide * z.width, TOKEN_LIMIT,
         scratch=(pltpu.VMEM((z.rows, z.wide), bf16), pltpu.VMEM((z.rows, z.wide), bf16)),
     )
 
@@ -242,7 +243,7 @@
         [pl.BlockSpec((z.rows, z.fq), lambda i, q: (0, q[at + i]))] + specs,
         jax.ShapeDtypeStruct((z.rows, z.columns), bf16),
         pl.BlockSpec((z.rows, z.columns), lambda i, q: (0, 0)),
-        2 * z.rows * z.width * z.columns, 2 * (z.rows * z.width + z.width * z.columns), 16 * MIB,
+        2 * z.rows * z.width * z.columns, 2 * (z.rows * z.width + z.width * z.columns), TOKEN_LIMIT,
         scratch=(pltpu.VMEM((z.rows, z.columns), f32),),
     )
 
@@ -455,12 +456,12 @@
             pieces += gather_shifts(y, "sub", ns)
         return pieces
 
-    maps, rounds[1], sc = tie(maps, rounds[1], sc)
     over = [None] * nd
+    part = products(zz, sc, own_tokens, own_grad, maps, fold, job_of)
+    part, rounds[1] = tie(part, rounds[1])
     over[1] = gather_shifts(rounds[1], "parts", np_)
     if nd > 2:
         rounds.append(shifted(rounds[1], "dp", nd, 1))
-    part = products(zz, sc, own_tokens, own_grad, maps, fold, job_of)
     parts = gather_shifts(part, "tensor", nt)
     late_tokens, _ = tie(own_tokens, part)
     base = [base_product(zz, sc, late_tokens, [frozen_value_weight] * zz.nq, 0)]
@@ -470,16 +471,15 @@
     got = [shifted(pays[d], "dp", nd, d) for d in range(nd)]
 
     if nd > 2:
-        tied = tie(rounds[2], *over[1], *got)
-        rounds[2], over[1], got = tied[0], list(tied[1 : 1 + np_]), tied[1 + np_ :]
+        rounds[2], over[1], got, grads = tie(rounds[2], over[1], got, grads)
+        for d in range(3, nd):
+            rounds.append(shifted(rounds[d - 1], "dp", nd, 1))
+    mine, theirs = tables_of(zz, sc, own_tokens, own_grad, unfold, job_of, got)
+    if nd > 2:
+        theirs, over[1], late = tie(theirs, over[1], rounds[2])
+        over[2] = gather_shifts(late, "parts", np_)
+    theirs = shifted(theirs, "sub", ns, 1)
     piece_list = [[frozen_value_weight] * zz.nq, spread_round(1, over[1])]
-    for d in range(2, nd):
-        over[d] = gather_shifts(rounds[d], "parts", np_)
-        if d + 1 < nd:
-            rounds.append(shifted(rounds[d], "dp", nd, 1))
-        piece_list.append(spread_round(d, over[d]))
-    mine, theirs = tables_of(zz, sc, own_tokens, own_grad, unfold, job_of, got)
-    theirs = shifted(theirs, "sub", ns, 1)
     late_tokens, mine = tie(own_tokens, mine)
     base.append(base_product(zz, sc, late_tokens, piece_list[1], 1))
     mine, base[1], theirs = tie(mine, base[1], theirs)
@@ -487,21 +487,15 @@
     summed = (mine + theirs).reshape(nd, jobs_dev * r2, -1)
     sending = [summed[d].astype(bf16) for d in range(nd)]
     if nd > 3:
-        rounds[3], *sending = tie(rounds[3], *sending)
+        rounds[3], sending, over[2] = tie(rounds[3], sending, over[2])
         over[3] = gather_shifts(rounds[3], "parts", np_)
-        piece_list[3] = spread_round(3, over[3])
-    total = sending[0].astype(f32)
-    for d in range(1, nd):
-        total = total + shifted(sending[d], "dp", nd, -d).astype(f32)
-    counts = lax.dynamic_slice_in_dim(tokens_per_job, z * jobs_dev, jobs_dev).astype(f32)
-    total = total.reshape(jobs_dev, r2, -1) * (adapter_scale / counts)[:, None, None]
-    halves = gather_shifts(total, "sub", ns)
-    owned = jnp.concatenate(
-        [sum(jnp.where((s - h) % ns == k, x, 0.0) for k, x in enumerate(halves)) for h in range(ns)], axis=1
-    )
-    grad_down, grad_up = owned[:, :, :width], owned[:, :, width:]
-
-    for d in range(2, nd):
+    for d in range(4, nd):
+        over[d] = gather_shifts(rounds[d], "parts", np_)
+    for d in range(2, nd - 1):
+        piece_list.append(spread_round(d, over[d]))
+    tables = [sending[0]] + [shifted(sending[d], "dp", nd, -d) for d in range(1, nd)]
+
+    for d in range(2, nd - 1):
         base.append(base_product(zz, sc, own_tokens, piece_list[d], d))
 
     def arriving(index, j):
@@ -511,15 +505,32 @@
             picked = jnp.where(d == k, base[k], picked)
         return picked
 
-    given = [arriving(t, j) for j in range(m)]
-    for d in range(1, nt):
-        given += [shifted(arriving((t + d) % nt, j), "tensor", nt, d) for j in range(m)]
+    def heads_of(j):
+        own = arriving(t, j)
+        return [own] + [shifted(arriving((t + d) % nt, j), "tensor", nt, d) for d in range(1, nt)]
+
+    early = [heads_of(j) for j in range(m - 1)]
+    tables, over[nd - 1], early = tie(tables, over[nd - 1], early)
+    piece_list.append(spread_round(nd - 1, over[nd - 1]))
+    total = sum(x.astype(f32) for x in tables)
+    counts = lax.dynamic_slice_in_dim(tokens_per_job, z * jobs_dev, jobs_dev).astype(f32)
+    total = total.reshape(jobs_dev, r2, -1) * (adapter_scale / counts)[:, None, None]
+    halves = gather_shifts(total, "sub", ns)
+    base.append(base_product(zz, sc, own_tokens, piece_list[nd - 1], nd - 1))
+    base[-1], halves = tie(base[-1], halves)
+    owned = jnp.concatenate(
+        [sum(jnp.where((s - h) % ns == k, x, 0.0) for k, x in enumerate(halves)) for h in range(ns)], axis=1
+    )
+    grad_down, grad_up = owned[:, :, :width], owned[:, :, width:]
+
+    slots = early + [heads_of(m - 1)]
     half = zz.nq // 2
-    grads = [grads[0]] + list(tie(base[-1], *grads[1:])[1:])
+    _, grads = tie(base[-1], grads)
     gradient = token_gradient_of(zz, sc, grads, maps, sums, unfold, job_of, piece_list, list(range(half)), None)
-    gradient, *given = tie(gradient, *given)
+    given = [slots[j][d] for d in range(nt) for j in range(m)]
+    gradient, grad_down, grad_up, *given = tie(gradient, grad_down, grad_up, *given)
     layer = layer_of(zz, sc, sums, maps, unfold, job_of, given)
-    layer, gradient = tie(layer, gradient)
+    *layer, gradient = tie(*layer, gradient)
     landed = [shifted(layer[d], "dp", nd, d) for d in range(nd)]
     gradient = token_gradient_of(
         zz, sc, grads, maps, sums, unfold, job_of, piece_list, list(range(half, zz.nq)), gradient

time: 146 us -> 136 us (0.932)
  waiting for transfers between devices: 50.3 us -> 31.1 us
  Pallas kernels: 40.8 us -> 50.9 us
  local copies, waits for them, and re-layouts: 8.95 us -> 6.9 us
  other arithmetic: 8.22 us -> 9.74 us
    ppermute x31, waiting for transfers between devices: 50.3 us -> 31.1 us  [shifted(): lax.ppermute(values, axis, [(i, (i + step) % count) for i in range(count)])]
    pallas_call x11, Pallas kernels: 40.8 us -> 50.9 us  [call(): pl.pallas_call(kernel, out_shape=out_shape, grid_spec=pltpu.PrefetchScala...]
    unnamed x30 -> x48, local copies, waits for them, and re-layouts: 5.1 us -> 2.16 us
  transfers between devices with their start and end apart: 31 -> 31, of which waited for: 13 -> 9; matrix products, arithmetic and copies ran while one was open for 8% -> 10% of each run, Pallas kernels for 26% -> 28%
where the time goes in v4:
time: 136 us; the launch traced here: 135 us
  Pallas kernels  50.9 us (37%)
  waiting for transfers between devices  31.1 us (23%)
  starting transfers between devices  30 us (22%)
  other arithmetic  9.74 us (7%)
  between operations  6.98 us (5%)
  local copies, waits for them, and re-layouts  6.9 us (5%)
    pallas_call x11, Pallas kernels, call(): pl.pallas_call(kernel, out_shape=out_shape, grid_spec=pltpu.PrefetchScala...  50.9 us
    ppermute x31, waiting for transfers between devices, shifted(): lax.ppermute(values, axis, [(i, (i + step) % count) for i in range(count)])  31.1 us
    ppermute x31, starting transfers between devices, shifted(): lax.ppermute(values, axis, [(i, (i + step) % count) for i in range(count)])  30 us
  transfers between devices with their start and end apart: 31, of which 9 were waited for; matrix products, arithmetic and copies ran while one was open for 10% of the time, Pallas kernels for 28%

profile of v4, /device:TPU:0, one launch (start us, length us, event | category | flops | bytes accessed | tf_op | source)
XLA Modules:
  0.0 135.5 jit_solution(13202741321338835493)
XLA Ops:
  1.7 5.1 %collective-permute-start.2 = (bf16[1,8,4608]{2,1,0:T(8,128)(2,1)S(1)}, bf16[1,8,4608]{2,1,0:T(8,128)(2,1)S(1)}, u32[]{:S(2)}, u32[]{:S(2)}) collective-permute-start(bf16[1,8,4608]{2,1,0:T(8,128)(2,1)S(1)} %dynamic-slice_bitcast_fusion), channel_id=1, source_target_pairs={{0,12},{4,0},{8,4},{12,8},{1,13},{5,1},{9,5},{13,9},{2,14},{6,2},{... | collective-permute-start | bytes 221192 | tf_op jit(solution)/shard_map/ppermute | solution.py:34
  7.8 1.9 %constant_dynamic-slice_fusion = bf16[1024,256]{1,0:T(8,128)(2,1)} fusion(bf16[4096,256]{1,0:T(8,128)(2,1)} %refs_3_.5, s32[]{:T(128)S(6)} %select_n.381), kind=kLoop, calls=%fused_computation.106 | loop fusion | bytes 1048580 | tf_op jit(solution)/shard_map/dynamic_slice | solution.py:393
  9.6 2.5 %collective-permute-start.4 = (bf16[1024,256]{1,0:T(8,128)(2,1)}, bf16[1024,256]{1,0:T(8,128)(2,1)}, u32[]{:S(2)}, u32[]{:S(2)}) collective-permute-start(bf16[1024,256]{1,0:T(8,128)(2,1)} %constant_dynamic-slice_fusion), channel_id=1, source_target_pairs={{0,4},{4,8},{8,12},{12,0},{1,5},{5,9},{9,13},{13,1},{2,6},{6,10},{... | collective-permute-start | bytes 1572872 | tf_op jit(solution)/shard_map/ppermute | solution.py:34
  12.1 1.5 %collective-permute-start.11 = (bf16[512,512]{1,0:T(8,128)(2,1)}, bf16[512,512]{1,0:T(8,128)(2,1)}, u32[]{:S(2)}, u32[]{:S(2)}) collective-permute-start(bf16[512,512]{1,0:T(8,128)(2,1)} %bitcast.31), channel_id=1, source_target_pairs={{0,2},{2,0},{1,3},{3,1},{4,6},{6,4},{5,7},{7,5},{8,10},{10,8},{9,1... | collective-permute-start | bytes 1572872 | tf_op jit(solution)/shard_map/ppermute | solution.py:34
  19.0 6.0 %collective-permute-done.1 = bf16[1,8,4608]{2,1,0:T(8,128)(2,1)S(1)} collective-permute-done((bf16[1,8,4608]{2,1,0:T(8,128)(2,1)S(1)}, bf16[1,8,4608]{2,1,0:T(8,128)(2,1)S(1)}, u32[]{:S(2)}, u32[]{:S(2)}) %collective-permute-start.1) | collective-permute-done | bytes 73760 | tf_op jit(solution)/shard_map/ppermute | solution.py:34
  26.8 5.8 %adapter_products.1.refs_0_ = bf16[512,32]{1,0:T(8,128)(2,1)S(1)} custom-call(s32[74]{0:T(128)S(1)} %concatenate.15.sc, bf16[512,4096]{1,0:T(8,128)(2,1)} %bitcast.36, bf16[512,512]{1,0:T(8,128)(2,1)S(1)} %bitcast.32, bf16[64,4608]{1,0:T(8,128)(2,1)S(1)} %pad_maximum_fusion.maps, f32[64,16]{1,0:T(8,128)S(1)} %fusion.2.fold, s32[1,64]{1,0:T(1,128)S(1)} %and_select_fusion.1.job_of), custom_call_target="tpu_custom_call" | custom-call | flops 1000 | bytes 1000 | tf_op jit(solution)/shard_map/adapter_products/pallas_call | solution.py:75
  32.6 1.6 %collective-permute-start.7 = (bf16[1024,256]{1,0:T(8,128)(2,1)}, bf16[1024,256]{1,0:T(8,128)(2,1)S(1)}, u32[]{:S(2)}, u32[]{:S(2)}) collective-permute-start(bf16[1024,256]{1,0:T(8,128)(2,1)} %collective-permute-done.4.refs_0_.refs_4_), channel_id=1, source_target_pairs={{0,16},{16,0},{1,17},{17,1},{2,18},{18,2},{3,19},{19,3},{4,20},{20... | collective-permute-start | bytes 1572872 | tf_op jit(solution)/shard_map/ppermute | solution.py:34
  34.2 1.5 %collective-permute-start.5 = (bf16[512,32]{1,0:T(8,128)(2,1)S(1)}, bf16[512,32]{1,0:T(8,128)(2,1)S(1)}, u32[]{:S(2)}, u32[]{:S(2)}) collective-permute-start(bf16[512,32]{1,0:T(8,128)(2,1)S(1)} %adapter_products.1.refs_0_), channel_id=1, source_target_pairs={{0,2},{2,0},{1,3},{3,1},{4,6},{6,4},{5,7},{7,5},{8,10},{10,8},{9,1... | collective-permute-start | bytes 98312 | tf_op jit(solution)/shard_map/ppermute | solution.py:34
  35.7 4.5 %base_0.1 = bf16[512,256]{1,0:T(8,128)(2,1)S(1)} custom-call(s32[74]{0:T(128)S(1)} %concatenate.15.sc, bf16[512,4096]{1,0:T(8,128)(2,1)} %bitcast.37, bf16[4096,256]{1,0:T(8,128)(2,1)S(1)} %copy-done, bf16[4096,256]{1,0:T(8,128)(2,1)S(1)} %copy-done, bf16[4096,256]{1,0:T(8,128)(2,1)S(1)} %copy-done, bf16[4096,256]{1,0:T(8,128)(2,1)S(1)} %copy-done), custom_call_target="tpu_custom_call" | custom-call | flops 1000 | bytes 1000 | tf_op jit(solution)/shard_map/base_0/pallas_call | solution.py:75
  41.7 4.2 %collective-permute-start.9 = (bf16[128,32]{1,0:T(8,128)(2,1)S(1)}, bf16[128,32]{1,0:T(8,128)(2,1)S(1)}, u32[]{:S(2)}, u32[]{:S(2)}) collective-permute-start(bf16[128,32]{1,0:T(8,128)(2,1)S(1)} %get-tuple-element.84), channel_id=1, source_target_pairs={{0,8},{4,12},{8,0},{12,4},{1,9},{5,13},{9,1},{13,5},{2,10},{6,14},... | collective-permute-start | bytes 24584 | tf_op jit(solution)/shard_map/ppermute | solution.py:34
  45.9 5.5 %collective-permute-done.8.refs_1_ = bf16[128,32]{1,0:T(8,128)(2,1)S(1)} collective-permute-done((bf16[128,32]{1,0:T(8,128)(2,1)S(1)}, bf16[128,32]{1,0:T(8,128)(2,1)S(1)}, u32[]{:S(2)}, u32[]{:S(2)}) %collective-permute-start.8) | collective-permute-done | bytes 8224 | tf_op jit(solution)/shard_map/ppermute | solution.py:34
  52.2 8.9 %job_tables.1 = (f32[32,4608]{1,0:T(8,128)S(1)}, f32[32,4608]{1,0:T(8,128)S(1)}) custom-call(s32[74]{0:T(128)S(1)} %concatenate.15.sc, bf16[512,4096]{1,0:T(8,128)(2,1)} %bitcast.38, bf16[512,512]{1,0:T(8,128)(2,1)S(1)} %bitcast.33, bf16[16,64]{1,0:T(8,128)(2,1)S(1)} %fusion.3.unfold, s32[1,64]{1,0:T(1,128)S(1)} %and_select_fusion.1.job_of, ...), custom_call_target="tpu_custom_call" | custom-call | flops 1000 | bytes 1000 | tf_op jit(solution)/shard_map/job_tables/pallas_call | solution.py:75
  64.8 4.6 %base_1.1 = bf16[512,256]{1,0:T(8,128)(2,1)S(1)} custom-call(s32[74]{0:T(128)S(1)} %concatenate.15.sc, bf16[512,4096]{1,0:T(8,128)(2,1)} %bitcast.39, bf16[1024,256]{1,0:T(8,128)(2,1)} %collective-permute-done.4.refs_0_.refs_4_, bf16[1024,256]{1,0:T(8,128)(2,1)S(1)} %collective-permute-done.13.refs_1_.refs_5_, ...), custom_call_target="tpu_custom_call" | custom-call | flops 1000 | bytes 1000 | tf_op jit(solution)/shard_map/base_1/pallas_call | solution.py:75
  69.6 8.3 %collective-permute-done.12.refs_0_.refs_8_ = bf16[1024,256]{1,0:T(8,128)(2,1)} collective-permute-done((bf16[1024,256]{1,0:T(8,128)(2,1)S(1)}, bf16[1024,256]{1,0:T(8,128)(2,1)}, u32[]{:S(2)}, u32[]{:S(2)}) %collective-permute-start.12) | collective-permute-done | bytes 524320 | tf_op jit(solution)/shard_map/ppermute | solution.py:34
  83.1 4.5 %base_2.1 = bf16[512,256]{1,0:T(8,128)(2,1)S(1)} custom-call(s32[74]{0:T(128)S(1)} %concatenate.15.sc, bf16[512,4096]{1,0:T(8,128)(2,1)} %bitcast.40, bf16[1024,256]{1,0:T(8,128)(2,1)S(1)} %collective-permute-done.6.refs_0_.refs_6_, bf16[1024,256]{1,0:T(8,128)(2,1)S(1)} %collective-permute-done.21.refs_1_.refs_7_, ...), custom_call_target="tpu_custom_call" | custom-call | flops 1000 | bytes 1000 | tf_op jit(solution)/shard_map/base_2/pallas_call | solution.py:75
  90.6 1.6 %collective-permute-start.17 = (bf16[8,4608]{1,0:T(8,128)(2,1)S(1)}, bf16[8,4608]{1,0:T(8,128)(2,1)S(1)}, u32[]{:S(2)}, u32[]{:S(2)}) collective-permute-start(bf16[8,4608]{1,0:T(8,128)(2,1)S(1)} %get-tuple-element.104), channel_id=1, source_target_pairs={{0,12},{4,0},{8,4},{12,8},{1,13},{5,1},{9,5},{13,9},{2,14},{6,2},{... | collective-permute-start | bytes 221192 | tf_op jit(solution)/shard_map/ppermute | solution.py:34
  95.0 4.6 %collective-permute-done.18 = bf16[8,4608]{1,0:T(8,128)(2,1)S(1)} collective-permute-done((bf16[8,4608]{1,0:T(8,128)(2,1)S(1)}, bf16[8,4608]{1,0:T(8,128)(2,1)S(1)}, u32[]{:S(2)}, u32[]{:S(2)}) %collective-permute-start.18) | collective-permute-done | bytes 73760 | tf_op jit(solution)/shard_map/ppermute | solution.py:34
  104.0 5.1 %base_3.1 = bf16[512,256]{1,0:T(8,128)(2,1)S(1)} custom-call(s32[74]{0:T(128)S(1)} %concatenate.15.sc, bf16[512,4096]{1,0:T(8,128)(2,1)} %bitcast.41, bf16[1024,256]{1,0:T(8,128)(2,1)} %collective-permute-done.12.refs_0_.refs_8_, bf16[1024,256]{1,0:T(8,128)(2,1)} %collective-permute-done.24.refs_1_.refs_9_, ...), custom_call_target="tpu_custom_call" | custom-call | flops 1000 | bytes 1000 | tf_op jit(solution)/shard_map/base_3/pallas_call | solution.py:75
  111.7 6.7 %token_gradient_0.1.refs_10_ = bf16[512,4096]{1,0:T(8,128)(2,1)} custom-call(s32[74]{0:T(128)S(1)} %concatenate.15.sc, bf16[64,4608]{1,0:T(8,128)(2,1)S(1)} %pad_maximum_fusion.maps, bf16[512,32]{1,0:T(8,128)(2,1)S(1)} %copy-done.19, bf16[16,64]{1,0:T(8,128)(2,1)S(1)} %fusion.3.unfold, s32[1,64]{1,0:T(1,128)S(1)} %and_select_fusion.1.job_of, ...), custom_call_target="tpu_custom_call" | custom-call | flops 1000 | bytes 1000 | tf_op jit(solution)/shard_map/token_gradient_0/pallas_call | solution.py:75
  119.0 2.1 %layer.1 = (bf16[128,512]{1,0:T(8,128)(2,1)S(1)}, bf16[128,512]{1,0:T(8,128)(2,1)S(1)}, bf16[128,512]{1,0:T(8,128)(2,1)S(1)}, bf16[128,512]{1,0:T(8,128)(2,1)S(1)}) custom-call(s32[74]{0:T(128)S(1)} %concatenate.15.sc, bf16[512,32]{1,0:T(8,128)(2,1)S(1)} %copy-done.19, bf16[64,4608]{1,0:T(8,128)(2,1)S(1)} %pad_maximum_fusion.maps, ...), custom_call_target="tpu_custom_call" | custom-call | flops 1000 | bytes 1000 | tf_op jit(solution)/shard_map/layer/pallas_call | solution.py:75
  121.1 1.8 %collective-permute-start.29 = (bf16[128,512]{1,0:T(8,128)(2,1)S(1)}, bf16[128,512]{1,0:T(8,128)(2,1)S(1)}, u32[]{:S(2)}, u32[]{:S(2)}) collective-permute-start(bf16[128,512]{1,0:T(8,128)(2,1)S(1)} %get-tuple-element.139), channel_id=1, source_target_pairs={{0,8},{4,12},{8,0},{12,4},{1,9},{5,13},{9,1},{13,5},{2,10},{6,14},... | collective-permute-start | bytes 393224 | tf_op jit(solution)/shard_map/ppermute | solution.py:34
  122.9 2.3 %collective-permute-start.30 = (bf16[128,512]{1,0:T(8,128)(2,1)S(1)}, bf16[128,512]{1,0:T(8,128)(2,1)S(1)}, u32[]{:S(2)}, u32[]{:S(2)}) collective-permute-start(bf16[128,512]{1,0:T(8,128)(2,1)S(1)} %get-tuple-element.140), channel_id=1, source_target_pairs={{0,12},{4,0},{8,4},{12,8},{1,13},{5,1},{9,5},{13,9},{2,14},{6,2},{... | collective-permute-start | bytes 393224 | tf_op jit(solution)/shard_map/ppermute | solution.py:34
  125.2 6.6 %token_gradient_2.1 = bf16[512,4096]{1,0:T(8,128)(2,1)} custom-call(s32[74]{0:T(128)S(1)} %concatenate.15.sc, bf16[64,4608]{1,0:T(8,128)(2,1)S(1)} %pad_maximum_fusion.maps, bf16[512,32]{1,0:T(8,128)(2,1)S(1)} %copy-done.19, bf16[16,64]{1,0:T(8,128)(2,1)S(1)} %fusion.3.unfold, s32[1,64]{1,0:T(1,128)S(1)} %and_select_fusion.1.job_of, ...), custom_call_target="tpu_custom_call", output_to_operand_aliasing={{}: (15, {})} | custom-call | flops 1000 | bytes 1000 | tf_op jit(solution)/shard_map/token_gradient_2/pallas_call | solution.py:75
  131.8 2.3 %collective-permute-done.29.refs_2_ = bf16[128,512]{1,0:T(8,128)(2,1)S(1)} collective-permute-done((bf16[128,512]{1,0:T(8,128)(2,1)S(1)}, bf16[128,512]{1,0:T(8,128)(2,1)S(1)}, u32[]{:S(2)}, u32[]{:S(2)}) %collective-permute-start.29) | collective-permute-done | bytes 131104 | tf_op jit(solution)/shard_map/ppermute | solution.py:34
  (147 shorter events, 29.1 us)
Async XLA Ops:
  1.7 17.3 %collective-permute-start.2 = (bf16[1,8,4608]{2,1,0:T(8,128)(2,1)S(1)}, bf16[1,8,4608]{2,1,0:T(8,128)(2,1)S(1)}, u32[]{:S(2)}, u32[]{:S(2)}) collective-permute-start(bf16[1,8,4608]{2,1,0:T(8,128)(2,1)S(1)} %dynamic-slice_bitcast_fusion), channel_id=1, source_target_pairs={{0,12},{4,0},{8,4},{12,8},{1,13},{5,1},{9,5},{13,9},{2,14},{6,2},{... | collective-permute-start | bytes 221192 | tf_op jit(solution)/shard_map/ppermute | solution.py:34
  6.8 18.2 %collective-permute-start.1 = (bf16[1,8,4608]{2,1,0:T(8,128)(2,1)S(1)}, bf16[1,8,4608]{2,1,0:T(8,128)(2,1)S(1)}, u32[]{:S(2)}, u32[]{:S(2)}) collective-permute-start(bf16[1,8,4608]{2,1,0:T(8,128)(2,1)S(1)} %dynamic-slice_bitcast_fusion), channel_id=1, source_target_pairs={{0,8},{4,12},{8,0},{12,4},{1,9},{5,13},{9,1},{13,5},{2,10},{6,14},... | collective-permute-start | bytes 221192 | tf_op jit(solution)/shard_map/ppermute | solution.py:34
  6.8 18.2 %collective-permute-start = (bf16[1,8,4608]{2,1,0:T(8,128)(2,1)S(1)}, bf16[1,8,4608]{2,1,0:T(8,128)(2,1)S(1)}, u32[]{:S(2)}, u32[]{:S(2)}) collective-permute-start(bf16[1,8,4608]{2,1,0:T(8,128)(2,1)S(1)} %dynamic-slice_bitcast_fusion), channel_id=1, source_target_pairs={{0,4},{4,8},{8,12},{12,0},{1,5},{5,9},{9,13},{13,1},{2,6},{6,10},{... | collective-permute-start | bytes 221192 | tf_op jit(solution)/shard_map/ppermute | solution.py:34
  9.6 23.0 %collective-permute-start.4 = (bf16[1024,256]{1,0:T(8,128)(2,1)}, bf16[1024,256]{1,0:T(8,128)(2,1)}, u32[]{:S(2)}, u32[]{:S(2)}) collective-permute-start(bf16[1024,256]{1,0:T(8,128)(2,1)} %constant_dynamic-slice_fusion), channel_id=1, source_target_pairs={{0,4},{4,8},{8,12},{12,0},{1,5},{5,9},{9,13},{13,1},{2,6},{6,10},{... | collective-permute-start | bytes 1572872 | tf_op jit(solution)/shard_map/ppermute | solution.py:34
  12.1 33.8 %collective-permute-start.11 = (bf16[512,512]{1,0:T(8,128)(2,1)}, bf16[512,512]{1,0:T(8,128)(2,1)}, u32[]{:S(2)}, u32[]{:S(2)}) collective-permute-start(bf16[512,512]{1,0:T(8,128)(2,1)} %bitcast.31), channel_id=1, source_target_pairs={{0,2},{2,0},{1,3},{3,1},{4,6},{6,4},{5,7},{7,5},{8,10},{10,8},{9,1... | collective-permute-start | bytes 1572872 | tf_op jit(solution)/shard_map/ppermute | solution.py:34
  32.6 19.5 %collective-permute-start.7 = (bf16[1024,256]{1,0:T(8,128)(2,1)}, bf16[1024,256]{1,0:T(8,128)(2,1)S(1)}, u32[]{:S(2)}, u32[]{:S(2)}) collective-permute-start(bf16[1024,256]{1,0:T(8,128)(2,1)} %collective-permute-done.4.refs_0_.refs_4_), channel_id=1, source_target_pairs={{0,16},{16,0},{1,17},{17,1},{2,18},{18,2},{3,19},{19,3},{4,20},{20... | collective-permute-start | bytes 1572872 | tf_op jit(solution)/shard_map/ppermute | solution.py:34
  34.2 17.9 %collective-permute-start.6 = (bf16[1024,256]{1,0:T(8,128)(2,1)}, bf16[1024,256]{1,0:T(8,128)(2,1)S(1)}, u32[]{:S(2)}, u32[]{:S(2)}) collective-permute-start(bf16[1024,256]{1,0:T(8,128)(2,1)} %collective-permute-done.4.refs_0_.refs_4_), channel_id=1, source_target_pairs={{0,4},{4,8},{8,12},{12,0},{1,5},{5,9},{9,13},{13,1},{2,6},{6,10},{... | collective-permute-start | bytes 1572872 | tf_op jit(solution)/shard_map/ppermute | solution.py:34
  34.2 6.0 %collective-permute-start.5 = (bf16[512,32]{1,0:T(8,128)(2,1)S(1)}, bf16[512,32]{1,0:T(8,128)(2,1)S(1)}, u32[]{:S(2)}, u32[]{:S(2)}) collective-permute-start(bf16[512,32]{1,0:T(8,128)(2,1)S(1)} %adapter_products.1.refs_0_), channel_id=1, source_target_pairs={{0,2},{2,0},{1,3},{3,1},{4,6},{6,4},{5,7},{7,5},{8,10},{10,8},{9,1... | collective-permute-start | bytes 98312 | tf_op jit(solution)/shard_map/ppermute | solution.py:34
  41.5 9.9 %collective-permute-start.8 = (bf16[128,32]{1,0:T(8,128)(2,1)S(1)}, bf16[128,32]{1,0:T(8,128)(2,1)S(1)}, u32[]{:S(2)}, u32[]{:S(2)}) collective-permute-start(bf16[128,32]{1,0:T(8,128)(2,1)S(1)} %get-tuple-element.83), channel_id=1, source_target_pairs={{0,4},{4,8},{8,12},{12,0},{1,5},{5,9},{9,13},{13,1},{2,6},{6,10},{... | collective-permute-start | bytes 24584 | tf_op jit(solution)/shard_map/ppermute | solution.py:34
  41.7 10.5 %collective-permute-start.9 = (bf16[128,32]{1,0:T(8,128)(2,1)S(1)}, bf16[128,32]{1,0:T(8,128)(2,1)S(1)}, u32[]{:S(2)}, u32[]{:S(2)}) collective-permute-start(bf16[128,32]{1,0:T(8,128)(2,1)S(1)} %get-tuple-element.84), channel_id=1, source_target_pairs={{0,8},{4,12},{8,0},{12,4},{1,9},{5,13},{9,1},{13,5},{2,10},{6,14},... | collective-permute-start | bytes 24584 | tf_op jit(solution)/shard_map/ppermute | solution.py:34
  45.9 6.2 %collective-permute-start.10 = (bf16[128,32]{1,0:T(8,128)(2,1)S(1)}, bf16[128,32]{1,0:T(8,128)(2,1)S(1)}, u32[]{:S(2)}, u32[]{:S(2)}) collective-permute-start(bf16[128,32]{1,0:T(8,128)(2,1)S(1)} %get-tuple-element.85), channel_id=1, source_target_pairs={{0,12},{4,0},{8,4},{12,8},{1,13},{5,1},{9,5},{13,9},{2,14},{6,2},{... | collective-permute-start | bytes 24584 | tf_op jit(solution)/shard_map/ppermute | solution.py:34
  61.1 8.4 %collective-permute-start.15 = (f32[32,4608]{1,0:T(8,128)S(1)}, f32[32,4608]{1,0:T(8,128)S(1)}, u32[]{:S(2)}, u32[]{:S(2)}) collective-permute-start(f32[32,4608]{1,0:T(8,128)S(1)} %get-tuple-element.99), channel_id=1, source_target_pairs={{0,1},{1,0},{2,3},{3,2},{4,5},{5,4},{6,7},{7,6},{8,9},{9,8},{10,11... | collective-permute-start | bytes 1769480 | tf_op jit(solution)/shard_map/ppermute | solution.py:34
  61.7 16.2 %collective-permute-start.12 = (bf16[1024,256]{1,0:T(8,128)(2,1)S(1)}, bf16[1024,256]{1,0:T(8,128)(2,1)}, u32[]{:S(2)}, u32[]{:S(2)}) collective-permute-start(bf16[1024,256]{1,0:T(8,128)(2,1)S(1)} %collective-permute-done.6.refs_0_.refs_6_), channel_id=1, source_target_pairs={{0,4},{4,8},{8,12},{12,0},{1,5},{5,9},{9,13},{13,1},{2,6},{6,10},{... | collective-permute-start | bytes 1572872 | tf_op jit(solution)/shard_map/ppermute | solution.py:34
  62.9 15.0 %collective-permute-start.16 = (bf16[1024,256]{1,0:T(8,128)(2,1)S(1)}, bf16[1024,256]{1,0:T(8,128)(2,1)S(1)}, u32[]{:S(2)}, u32[]{:S(2)}) collective-permute-start(bf16[1024,256]{1,0:T(8,128)(2,1)S(1)} %collective-permute-done.6.refs_0_.refs_6_), channel_id=1, source_target_pairs={{0,16},{16,0},{1,17},{17,1},{2,18},{18,2},{3,19},{19,3},{4,20},{20... | collective-permute-start | bytes 1572872 | tf_op jit(solution)/shard_map/ppermute | solution.py:34
  77.9 5.2 %collective-permute-start.22 = (bf16[1024,256]{1,0:T(8,128)(2,1)S(1)}, bf16[1024,256]{1,0:T(8,128)(2,1)S(1)}, u32[]{:S(2)}, u32[]{:S(2)}) collective-permute-start(bf16[1024,256]{1,0:T(8,128)(2,1)S(1)} %collective-permute-done.16.refs_2_.refs_6_), channel_id=1, source_target_pairs={{0,1},{1,0},{2,3},{3,2},{4,5},{5,4},{6,7},{7,6},{8,9},{9,8},{10,11... | collective-permute-start | bytes 1572872 | tf_op jit(solution)/shard_map/ppermute | solution.py:34
  79.4 20.2 %collective-permute-start.20 = (bf16[1024,256]{1,0:T(8,128)(2,1)}, bf16[1024,256]{1,0:T(8,128)(2,1)}, u32[]{:S(2)}, u32[]{:S(2)}) collective-permute-start(bf16[1024,256]{1,0:T(8,128)(2,1)} %collective-permute-done.12.refs_0_.refs_8_), channel_id=1, source_target_pairs={{0,16},{16,0},{1,17},{17,1},{2,18},{18,2},{3,19},{19,3},{4,20},{20... | collective-permute-start | bytes 1572872 | tf_op jit(solution)/shard_map/ppermute | solution.py:34
  89.1 10.4 %collective-permute-start.23 = (bf16[512,256]{1,0:T(8,128)(2,1)S(1)}, bf16[512,256]{1,0:T(8,128)(2,1)S(1)}, u32[]{:S(2)}, u32[]{:S(2)}) collective-permute-start(bf16[512,256]{1,0:T(8,128)(2,1)S(1)} %get-tuple-element.158), channel_id=1, source_target_pairs={{0,2},{2,0},{1,3},{3,1},{4,6},{6,4},{5,7},{7,5},{8,10},{10,8},{9,1... | collective-permute-start | bytes 786440 | tf_op jit(solution)/shard_map/ppermute | solution.py:34
  92.2 7.3 %collective-permute-start.18 = (bf16[8,4608]{1,0:T(8,128)(2,1)S(1)}, bf16[8,4608]{1,0:T(8,128)(2,1)S(1)}, u32[]{:S(2)}, u32[]{:S(2)}) collective-permute-start(bf16[8,4608]{1,0:T(8,128)(2,1)S(1)} %get-tuple-element.105), channel_id=1, source_target_pairs={{0,8},{4,12},{8,0},{12,4},{1,9},{5,13},{9,1},{13,5},{2,10},{6,14},... | collective-permute-start | bytes 221192 | tf_op jit(solution)/shard_map/ppermute | solution.py:34
  92.2 7.3 %collective-permute-start.19 = (bf16[8,4608]{1,0:T(8,128)(2,1)S(1)}, bf16[8,4608]{1,0:T(8,128)(2,1)S(1)}, u32[]{:S(2)}, u32[]{:S(2)}) collective-permute-start(bf16[8,4608]{1,0:T(8,128)(2,1)S(1)} %get-tuple-element.106), channel_id=1, source_target_pairs={{0,4},{4,8},{8,12},{12,0},{1,5},{5,9},{9,13},{13,1},{2,6},{6,10},{... | collective-permute-start | bytes 221192 | tf_op jit(solution)/shard_map/ppermute | solution.py:34
  101.5 7.7 %collective-permute-start.26 = (f32[1,8,4608]{2,1,0:T(8,128)}, f32[1,8,4608]{2,1,0:T(8,128)}, u32[]{:S(2)}, u32[]{:S(2)}) collective-permute-start(f32[1,8,4608]{2,1,0:T(8,128)} %multiply_bitcast_fusion), channel_id=1, source_target_pairs={{0,1},{1,0},{2,3},{3,2},{4,5},{5,4},{6,7},{7,6},{8,9},{9,8},{10,11... | collective-permute-start | bytes 442376 | tf_op jit(solution)/shard_map/ppermute | solution.py:34
  109.3 9.7 %collective-permute-start.27 = (bf16[512,256]{1,0:T(8,128)(2,1)S(1)}, bf16[512,256]{1,0:T(8,128)(2,1)S(1)}, u32[]{:S(2)}, u32[]{:S(2)}) collective-permute-start(bf16[512,256]{1,0:T(8,128)(2,1)S(1)} %get-tuple-element.156), channel_id=1, source_target_pairs={{0,2},{2,0},{1,3},{3,1},{4,6},{6,4},{5,7},{7,5},{8,10},{10,8},{9,1... | collective-permute-start | bytes 786440 | tf_op jit(solution)/shard_map/ppermute | solution.py:34
  121.0 10.8 %collective-permute-start.28 = (bf16[128,512]{1,0:T(8,128)(2,1)S(1)}, bf16[128,512]{1,0:T(8,128)(2,1)S(1)}, u32[]{:S(2)}, u32[]{:S(2)}) collective-permute-start(bf16[128,512]{1,0:T(8,128)(2,1)S(1)} %get-tuple-element.138), channel_id=1, source_target_pairs={{0,4},{4,8},{8,12},{12,0},{1,5},{5,9},{9,13},{13,1},{2,6},{6,10},{... | collective-permute-start | bytes 393224 | tf_op jit(solution)/shard_map/ppermute | solution.py:34
  121.1 12.9 %collective-permute-start.29 = (bf16[128,512]{1,0:T(8,128)(2,1)S(1)}, bf16[128,512]{1,0:T(8,128)(2,1)S(1)}, u32[]{:S(2)}, u32[]{:S(2)}) collective-permute-start(bf16[128,512]{1,0:T(8,128)(2,1)S(1)} %get-tuple-element.139), channel_id=1, source_target_pairs={{0,8},{4,12},{8,0},{12,4},{1,9},{5,13},{9,1},{13,5},{2,10},{6,14},... | collective-permute-start | bytes 393224 | tf_op jit(solution)/shard_map/ppermute | solution.py:34
  122.9 11.2 %collective-permute-start.30 = (bf16[128,512]{1,0:T(8,128)(2,1)S(1)}, bf16[128,512]{1,0:T(8,128)(2,1)S(1)}, u32[]{:S(2)}, u32[]{:S(2)}) collective-permute-start(bf16[128,512]{1,0:T(8,128)(2,1)S(1)} %get-tuple-element.140), channel_id=1, source_target_pairs={{0,12},{4,0},{8,4},{12,8},{1,13},{5,1},{9,5},{13,9},{2,14},{6,2},{... | collective-permute-start | bytes 393224 | tf_op jit(solution)/shard_map/ppermute | solution.py:34
  (31 other events, 201.2 us)

commit v5 on v4

--- a/solution.py
+++ b/solution.py
@@ -58,11 +58,14 @@
         self.nq = np_ * ns
         self.fq = width // self.nq
         self.per_head = nd // nt
+        self.chunks = 2
+        self.fe = self.fq // self.chunks
         at, self.at = 0, {}
         for name, count in (
             ("out_pos", self.slots), ("in_pos", self.slots), ("out_fill", self.slots), ("in_fill", self.slots),
             ("out_rel", blocks), ("in_rel", blocks), ("out_valid", blocks), ("in_valid", blocks),
             ("quarter", self.nq), ("shard", nd), ("head", self.per_head),
+            ("step", self.nq * self.chunks), ("pick", self.per_head * nt),
         ):
             self.at[name] = at
             at += count
@@ -159,7 +162,7 @@
 
 
 def table_kernel(z, tiles, sc, tokens, grad, unfold, job_of, *refs):
-    got, (mine, theirs, back, down) = refs[: z.nd], refs[z.nd :]
+    got, (mine, theirs, back, down, back_t, down_t) = refs[: z.nd], refs[z.nd :]
     half = mine.shape[0]
     step = pl.program_id(0)
 
@@ -183,18 +186,23 @@
                     mask = row_mask(z.get(sc, "in_valid", at), z, z.wide)
                     down[rows_of(at, z), :] = jnp.where(mask, values, 0).astype(bf16)
 
+        same = lax.broadcasted_iota(i32, (z.rows, z.rows), 0) == lax.broadcasted_iota(i32, (z.rows, z.rows), 1)
+        unit = jnp.where(same, 1.0, 0.0).astype(bf16)
+        back_t[...] = dot(back[...], unit, ((0,), (0,))).astype(bf16)
+        down_t[...] = dot(down[...], unit, ((0,), (0,))).astype(bf16)
+
     def put(wide, values):
-        total = dot(wide[...], values[...], ((0,), (0,)))
+        total = dot(wide[...], values[...], ((1,), (0,)))
         mine[...] = total[:half]
         theirs[...] = total[half:]
 
     @pl.when(step < tiles)
     def _():
-        put(back, tokens)
+        put(back_t, tokens)
 
     @pl.when(step == tiles)
     def _():
-        put(down, grad)
+        put(down_t, grad)
 
 
 def tables_of(z, sc, tokens, grad, unfold, job_of, got):
@@ -212,38 +220,67 @@
         + [whole(x) for x in got],
         (shape, shape), (out, out),
         2 * z.wide * z.rows * (z.width + z.heads), 2 * z.rows * z.width + 4 * z.wide * z.width, TOKEN_LIMIT,
-        scratch=(pltpu.VMEM((z.rows, z.wide), bf16), pltpu.VMEM((z.rows, z.wide), bf16)),
-    )
-
-
-def base_kernel(z, sc, tokens, *refs):
-    pieces, (out, total) = refs[: z.nq], refs[z.nq :]
+        scratch=(pltpu.VMEM((z.rows, z.wide), bf16),) * 2 + (pltpu.VMEM((z.wide, z.rows), bf16),) * 2,
+    )
+
+
+def base_kernel(z, d, count, started, partial, slot, others, sc, tokens, *refs):
+    pieces, refs = refs[:count], refs[count:]
+    if started:
+        begun, refs = refs[0], refs[1:]
+    earlier, refs = refs[: len(others)], refs[len(others) :]
+    outs, total = refs[:-1], refs[-1]
     step = pl.program_id(0)
-    for r in range(z.nq):
-
-        @pl.when(step == r)
+    for k in range(count):
+
+        @pl.when(step == k)
         def _():
-            part = dot(tokens[...], pieces[r][...], ((1,), (0,)))
-            if r == 0:
+            part = dot(tokens[...], pieces[k][...], ((1,), (0,)))
+            if k > 0:
+                part = part + total[...]
+            elif started:
+                part = part + begun[...]
+            if k < count - 1:
                 total[...] = part
-            elif r < z.nq - 1:
-                total[...] += part
+            elif partial:
+                outs[0][...] = part
             else:
-                out[...] = (total[...] + part).astype(bf16)
-
-
-def base_product(z, sc, tokens, pieces, d):
-    at = z.at["quarter"]
+                done = part.astype(bf16)
+                outs[0][...] = done
+                for g in range(len(outs) - 1):
+                    outs[1 + g][...] = done
+                    for at, values in zip(others, earlier):
+
+                        @pl.when(z.get(sc, "pick", g * z.per_head + slot) == at)
+                        def _():
+                            outs[1 + g][...] = values[...]
+
+
+def base_product(z, sc, tokens, pieces, d, base, first=0, begun=None, partial=False):
+    count, features = len(pieces), pieces[0].shape[0] if d else z.fq
+    at = z.at["quarter"] if features == z.fq else z.at["step"]
     if d == 0:
         specs = [pl.BlockSpec((z.fq, z.columns), lambda i, q, r=r: (q[at + r], 0)) for r in range(z.nq)]
     else:
         specs = [whole(x) for x in pieces]
+    inputs = [tokens, *pieces]
+    if begun is not None:
+        inputs.append(begun)
+        specs.append(whole(begun))
+    slot = d - (z.nd - z.per_head)
+    others = []
+    shapes = [jax.ShapeDtypeStruct((z.rows, z.columns), f32 if partial else bf16)]
+    if slot >= 0 and not partial:
+        others = list(range(slot, d))
+        inputs += [base[k] for k in others]
+        specs += [whole(base[k]) for k in others]
+        shapes += [jax.ShapeDtypeStruct((z.rows, z.columns), bf16)] * z.nt
     return call(
-        functools.partial(base_kernel, z), "base_%d" % d, (z.nq,), sc, (tokens, *pieces),
-        [pl.BlockSpec((z.rows, z.fq), lambda i, q: (0, q[at + i]))] + specs,
-        jax.ShapeDtypeStruct((z.rows, z.columns), bf16),
-        pl.BlockSpec((z.rows, z.columns), lambda i, q: (0, 0)),
-        2 * z.rows * z.width * z.columns, 2 * (z.rows * z.width + z.width * z.columns), TOKEN_LIMIT,
+        functools.partial(base_kernel, z, d, count, begun is not None, partial, slot, others),
+        "base_%d_%d" % (d, first), (count,), sc, inputs,
+        [pl.BlockSpec((z.rows, features), lambda i, q: (0, q[at + first + i]))] + specs,
+        tuple(shapes), tuple(whole(x) for x in shapes),
+        1000, 1000, TOKEN_LIMIT,
         scratch=(pltpu.VMEM((z.rows, z.columns), f32),),
     )
 
@@ -305,10 +342,10 @@
     )
 
 
-def gradient_kernel(z, quarters, per, aliased, sc, maps, sums, unfold, job_of, *refs):
+def gradient_kernel(z, count, per, aliased, sc, maps, sums, unfold, job_of, *refs):
     grads, refs = refs[: z.nt], refs[z.nt :]
-    count = len(quarters)
-    pieces, refs = refs[: z.nd * count], refs[z.nd * count :]
+    whole_pieces, refs = refs[: (z.nd - 1) * count], refs[(z.nd - 1) * count :]
+    last_pieces, refs = refs[: count * per], refs[count * per :]
     out, grad, back = refs[1:] if aliased else refs
     step = pl.program_id(0)
     m = z.per_head
@@ -321,13 +358,14 @@
             own = slice(b * z.halved, (b + 1) * z.halved)
             back[own, :] = widen(sums[own, z.rank :], z.get(sc, "in_rel", b), unfold[...], job_of[...], z)
 
-    for k in range(count):
-
-        @pl.when(step // per == k)
+    for i in range(count * per):
+
+        @pl.when(step == i)
         def _():
             total = adapter_scale * dot(back[...], maps[...], ((1,), (0,)))
             for d in range(z.nd):
-                total = total + dot(grad[z.get(sc, "shard", d)], pieces[d * count + k][...], ((1,), (1,)))
+                piece = last_pieces[i] if d == z.nd - 1 else whole_pieces[d * count + i // per]
+                total = total + dot(grad[z.get(sc, "shard", d)], piece[...], ((1,), (1,)))
             for b in range(z.blocks):
                 own = slice(b * z.halved, (b + 1) * z.halved)
                 mask = row_mask(z.get(sc, "in_valid", b), z, total.shape[1])
@@ -335,13 +373,12 @@
 
 
 def token_gradient_of(z, sc, grads, maps, sums, unfold, job_of, piece_list, quarters, before):
-    tile = min(512, z.fq)
-    per = z.fq // tile
+    tile, per = z.fe, z.chunks
     at = z.at["quarter"]
-    first = quarters[0]
+    first, count = quarters[0], len(quarters)
     block = lambda i, q: (0, q[at + first + i // per] * per + i % per)
     specs, flat = [], []
-    for d in range(z.nd):
+    for d in range(z.nd - 1):
         for k, r in enumerate(quarters):
             inner = lambda i, k=k: jnp.clip(i - k * per, 0, per - 1)
             if d == 0:
@@ -350,6 +387,10 @@
                 index = lambda i, q, inner=inner: (inner(i), 0)
             specs.append(pl.BlockSpec((tile, z.columns), index))
             flat.append(piece_list[d][r])
+    for r in quarters:
+        for c in range(per):
+            flat.append(piece_list[z.nd - 1][c * z.nq + r])
+            specs.append(whole(flat[-1]))
     inputs = [maps, sums, unfold, job_of, *grads, *flat]
     in_specs = [pl.BlockSpec((z.wide, tile), block), whole(sums), whole(unfold), whole(job_of)]
     in_specs += [whole(x) for x in grads] + specs
@@ -358,12 +399,11 @@
         alias = {1 + len(inputs): 0}
         inputs.append(before)
         in_specs.append(pl.BlockSpec(memory_space=pl.ANY))
-    share = len(quarters) * z.fq
     return call(
-        functools.partial(gradient_kernel, z, quarters, per, before is not None),
-        "token_gradient_%d" % first, (len(quarters) * per,), sc, inputs, in_specs,
+        functools.partial(gradient_kernel, z, count, per, before is not None),
+        "token_gradient_%d" % first, (count * per,), sc, inputs, in_specs,
         jax.ShapeDtypeStruct((z.rows, z.width), bf16), pl.BlockSpec((z.rows, tile), block),
-        2 * z.rows * share * (z.nd * z.columns + z.wide), 2 * share * (z.rows + z.nd * z.columns), 32 * MIB,
+        1000, 1000, 32 * MIB,
         scratch=(pltpu.VMEM((z.nd, z.rows, z.columns), bf16), pltpu.VMEM((z.rows, z.wide), bf16)),
         alias=alias,
     )
@@ -395,7 +435,8 @@
 
     maps = jnp.concatenate([adapter_down, adapter_up], axis=2).reshape(jobs_dev, ns, r2, width + heads)
     maps = lax.dynamic_index_in_dim(maps, s, 1, keepdims=False)
-    maps = jnp.concatenate(gather_shifts(maps, "dp", nd), axis=0).reshape(zz.jobs * r2, -1)
+    maps, rounds[1] = tie(gather_shifts(maps, "dp", nd), rounds[1])
+    maps = jnp.concatenate(maps, axis=0).reshape(zz.jobs * r2, -1)
     maps = jnp.concatenate(gather_shifts(maps, "sub", ns), axis=0)
     grads = gather_shifts(own_grad, "tensor", nt)
 
@@ -437,11 +478,13 @@
 
     shard_of = (z - jnp.arange(nd, dtype=i32)) % nd
     shard_at = (t - shard_of // m) % nt * m + shard_of % m
-    head_at = (z - arrival(t)) % nd - t * m
+    arrivals = [arrival((t + g) % nt) for g in range(nt)]
+    head_at = (z - arrivals[0]) % nd - t * m
+    steps = (quarters[None, :] * zz.chunks + jnp.arange(zz.chunks, dtype=i32)[:, None]).reshape(-1)
     sc = jnp.concatenate(
         [
             x.astype(i32)
-            for x in (out_pos, in_pos, out_fill, in_fill, out_rel, in_rel, out_valid, in_valid, quarters, shard_at, head_at)
+            for x in (out_pos, in_pos, out_fill, in_fill, out_rel, in_rel, out_valid, in_valid, quarters, shard_at, head_at, steps, *arrivals)
         ]
     )
     column = jnp.arange(zz.wide, dtype=i32)
@@ -450,82 +493,72 @@
     unfold = (jnp.arange(rank, dtype=i32)[:, None] == rank_of[None, :]).astype(bf16)
     fold = unfold.astype(f32).T
 
-    def spread_round(d, over_parts):
-        pieces = []
-        for y in over_parts:
-            pieces += gather_shifts(y, "sub", ns)
-        return pieces
-
+    def spread_round(over_parts):
+        return [x for y in over_parts for x in gather_shifts(y, "sub", ns)]
+
+    last = nd - 1
     over = [None] * nd
+    over[1] = gather_shifts(rounds[1], "parts", np_)
+    for d in range(2, last):
+        rounds.append(shifted(rounds[-1], "dp", nd, 1))
     part = products(zz, sc, own_tokens, own_grad, maps, fold, job_of)
-    part, rounds[1] = tie(part, rounds[1])
-    over[1] = gather_shifts(rounds[1], "parts", np_)
-    if nd > 2:
-        rounds.append(shifted(rounds[1], "dp", nd, 1))
     parts = gather_shifts(part, "tensor", nt)
     late_tokens, _ = tie(own_tokens, part)
-    base = [base_product(zz, sc, late_tokens, [frozen_value_weight] * zz.nq, 0)]
-    tied = tie(base[0], *parts)
-    base[0], parts = tied[0], tied[1:]
+    base = [base_product(zz, sc, late_tokens, [frozen_value_weight] * zz.nq, 0, None)[0]]
+    base[0], parts = tie(base[0], parts)
     sums, *pays = sums_of(zz, sc, parts)
+
+    rounds[last - 1], over[1], pays, grads = tie(rounds[last - 1], over[1], pays, grads)
+    ends = [
+        shifted(rounds[last - 1][c * zz.fe : (c + 1) * zz.fe], "dp", nd, 1) for c in range(zz.chunks)
+    ]
     got = [shifted(pays[d], "dp", nd, d) for d in range(nd)]
-
-    if nd > 2:
-        rounds[2], over[1], got, grads = tie(rounds[2], over[1], got, grads)
-        for d in range(3, nd):
-            rounds.append(shifted(rounds[d - 1], "dp", nd, 1))
     mine, theirs = tables_of(zz, sc, own_tokens, own_grad, unfold, job_of, got)
-    if nd > 2:
-        theirs, over[1], late = tie(theirs, over[1], rounds[2])
-        over[2] = gather_shifts(late, "parts", np_)
+    for d in range(2, last):
+        over[d] = gather_shifts(rounds[d], "parts", np_)
+    mine, theirs, ends[0] = tie(mine, theirs, ends[0])
+    end_over = [gather_shifts(ends[0], "parts", np_)]
     theirs = shifted(theirs, "sub", ns, 1)
-    piece_list = [[frozen_value_weight] * zz.nq, spread_round(1, over[1])]
+    piece_list = [[frozen_value_weight] * zz.nq, spread_round(over[1])]
     late_tokens, mine = tie(own_tokens, mine)
-    base.append(base_product(zz, sc, late_tokens, piece_list[1], 1))
-    mine, base[1], theirs = tie(mine, base[1], theirs)
+    base.append(base_product(zz, sc, late_tokens, piece_list[1], 1, base)[0])
+    base[1], ends[1:], over[2:last] = tie(base[1], ends[1:], over[2:last])
+    end_over += [gather_shifts(x, "parts", np_) for x in ends[1:]]
+    piece_list += [spread_round(over[d]) for d in range(2, last)]
+    end_over[0], *piece_list[2:] = tie(end_over[0], *piece_list[2:])
+
+    slots = []
+
+    def finish(d, made):
+        base.append(made[0])
+        if len(made) > 1:
+            slots.append([made[1]] + [shifted(made[1 + g], "tensor", nt, g) for g in range(1, nt)])
+
+    for d in range(2, last):
+        finish(d, base_product(zz, sc, own_tokens, piece_list[d], d, base))
+    base[-1], mine, theirs = tie(base[-1], mine, theirs)
 
     summed = (mine + theirs).reshape(nd, jobs_dev * r2, -1)
     sending = [summed[d].astype(bf16) for d in range(nd)]
-    if nd > 3:
-        rounds[3], sending, over[2] = tie(rounds[3], sending, over[2])
-        over[3] = gather_shifts(rounds[3], "parts", np_)
-    for d in range(4, nd):
-        over[d] = gather_shifts(rounds[d], "parts", np_)
-    for d in range(2, nd - 1):
-        piece_list.append(spread_round(d, over[d]))
     tables = [sending[0]] + [shifted(sending[d], "dp", nd, -d) for d in range(1, nd)]
-
-    for d in range(2, nd - 1):
-        base.append(base_product(zz, sc, own_tokens, piece_list[d], d))
-
-    def arriving(index, j):
-        d = arrival(index)[j]
-        picked = base[j]
-        for k in range(j + 1, nd - m + j + 1):
-            picked = jnp.where(d == k, base[k], picked)
-        return picked
-
-    def heads_of(j):
-        own = arriving(t, j)
-        return [own] + [shifted(arriving((t + d) % nt, j), "tensor", nt, d) for d in range(1, nt)]
-
-    early = [heads_of(j) for j in range(m - 1)]
-    tables, over[nd - 1], early = tie(tables, over[nd - 1], early)
-    piece_list.append(spread_round(nd - 1, over[nd - 1]))
+    ahead, behind = [x for y in end_over[:-1] for x in spread_round(y)], end_over[-1]
+    ahead += gather_shifts(behind[0], "sub", ns)
+    begun = base_product(zz, sc, own_tokens, ahead, last, base, 0, None, True)[0]
+    begun, tables, behind, slots = tie(begun, tables, behind, slots)
+    tail = spread_round(behind[1:])
+    piece_list.append(ahead + tail)
     total = sum(x.astype(f32) for x in tables)
     counts = lax.dynamic_slice_in_dim(tokens_per_job, z * jobs_dev, jobs_dev).astype(f32)
     total = total.reshape(jobs_dev, r2, -1) * (adapter_scale / counts)[:, None, None]
     halves = gather_shifts(total, "sub", ns)
-    base.append(base_product(zz, sc, own_tokens, piece_list[nd - 1], nd - 1))
-    base[-1], halves = tie(base[-1], halves)
+    finish(last, base_product(zz, sc, own_tokens, tail, last, base, len(ahead), begun))
+    base[-1], halves, grads = tie(base[-1], halves, grads)
     owned = jnp.concatenate(
         [sum(jnp.where((s - h) % ns == k, x, 0.0) for k, x in enumerate(halves)) for h in range(ns)], axis=1
     )
     grad_down, grad_up = owned[:, :, :width], owned[:, :, width:]
 
-    slots = early + [heads_of(m - 1)]
     half = zz.nq // 2
-    _, grads = tie(base[-1], grads)
     gradient = token_gradient_of(zz, sc, grads, maps, sums, unfold, job_of, piece_list, list(range(half)), None)
     given = [slots[j][d] for d in range(nt) for j in range(m)]
     gradient, grad_down, grad_up, *given = tie(gradient, grad_down, grad_up, *given)

time: 136 us -> 142 us (1.044)
  waiting for transfers between devices: 31.1 us -> 38.5 us
  between operations: 6.98 us -> 2.07 us
  Pallas kernels: 50.9 us -> 53.5 us
    ppermute x31 -> x35, waiting for transfers between devices: 31.1 us -> 38.5 us  [shifted(): lax.ppermute(values, axis, [(i, (i + step) % count) for i in range(count)])]
    pallas_call x11 -> x12, Pallas kernels: 50.9 us -> 53.5 us  [call(): pl.pallas_call(kernel, out_shape=out_shape, grid_spec=pltpu.PrefetchScala...]
    unnamed x48 -> x78, local copies, waits for them, and re-layouts: 2.16 us -> 4.32 us
    ppermute x31 -> x35, starting transfers between devices: 30 us -> 30.8 us  [shifted(): lax.ppermute(values, axis, [(i, (i + step) % count) for i in range(count)])]
  transfers between devices with their start and end apart: 31 -> 35, of which waited for: 9 -> 8; matrix products, arithmetic and copies ran while one was open for 10% -> 7% of each run, Pallas kernels for 28% -> 33%
where the time goes in v5:
time: 142 us; the launch traced here: 141 us
  Pallas kernels  53.5 us (38%)
  waiting for transfers between devices  38.5 us (27%)
  starting transfers between devices  30.8 us (22%)
  other arithmetic  8.99 us (6%)
  local copies, waits for them, and re-layouts  7.08 us (5%)
  between operations  2.07 us (1%)
    pallas_call x12, Pallas kernels, call(): pl.pallas_call(kernel, out_shape=out_shape, grid_spec=pltpu.PrefetchScala...  53.5 us
    ppermute x35, waiting for transfers between devices, shifted(): lax.ppermute(values, axis, [(i, (i + step) % count) for i in range(count)])  38.5 us
    ppermute x35, starting transfers between devices, shifted(): lax.ppermute(values, axis, [(i, (i + step) % count) for i in range(count)])  30.8 us
    unnamed x78, local copies, waits for them, and re-layouts  4.32 us
  transfers between devices with their start and end apart: 35, of which 8 were waited for; matrix products, arithmetic and copies ran while one was open for 7% of the time, Pallas kernels for 33%

profile of v5, /device:TPU:0, one launch (start us, length us, event | category | flops | bytes accessed | tf_op | source)
XLA Modules:
  0.0 141.0 jit_solution(9615222713255448693)
XLA Ops:
  1.7 5.1 %collective-permute-start.2 = (bf16[1,8,4608]{2,1,0:T(8,128)(2,1)S(1)}, bf16[1,8,4608]{2,1,0:T(8,128)(2,1)S(1)}, u32[]{:S(2)}, u32[]{:S(2)}) collective-permute-start(bf16[1,8,4608]{2,1,0:T(8,128)(2,1)S(1)} %dynamic-slice_bitcast_fusion), channel_id=1, source_target_pairs={{0,12},{4,0},{8,4},{12,8},{1,13},{5,1},{9,5},{13,9},{2,14},{6,2},{... | collective-permute-start | bytes 221192 | tf_op jit(solution)/shard_map/ppermute | solution.py:34
  8.9 2.5 %collective-permute-start.3 = (bf16[1024,256]{1,0:T(8,128)(2,1)S(1)}, bf16[1024,256]{1,0:T(8,128)(2,1)}, u32[]{:S(2)}, u32[]{:S(2)}) collective-permute-start(bf16[1024,256]{1,0:T(8,128)(2,1)S(1)} %constant_dynamic-slice_fusion), channel_id=1, source_target_pairs={{0,4},{4,8},{8,12},{12,0},{1,5},{5,9},{9,13},{13,1},{2,6},{6,10},{... | collective-permute-start | bytes 1572872 | tf_op jit(solution)/shard_map/ppermute | solution.py:34
  18.7 6.3 %collective-permute-done.1 = bf16[1,8,4608]{2,1,0:T(8,128)(2,1)S(1)} collective-permute-done((bf16[1,8,4608]{2,1,0:T(8,128)(2,1)S(1)}, bf16[1,8,4608]{2,1,0:T(8,128)(2,1)S(1)}, u32[]{:S(2)}, u32[]{:S(2)}) %collective-permute-start.1) | collective-permute-done | bytes 73760 | tf_op jit(solution)/shard_map/ppermute | solution.py:34
  25.2 1.6 %collective-permute-start.7 = (bf16[1024,256]{1,0:T(8,128)(2,1)}, bf16[1024,256]{1,0:T(8,128)(2,1)S(1)}, u32[]{:S(2)}, u32[]{:S(2)}) collective-permute-start(bf16[1024,256]{1,0:T(8,128)(2,1)} %collective-permute-done.3.refs_0_.refs_4_), channel_id=1, source_target_pairs={{0,16},{16,0},{1,17},{17,1},{2,18},{18,2},{3,19},{19,3},{4,20},{20... | collective-permute-start | bytes 1572872 | tf_op jit(solution)/shard_map/ppermute | solution.py:34
  27.2 5.8 %adapter_products.1.refs_0_ = bf16[512,32]{1,0:T(8,128)(2,1)S(1)} custom-call(s32[86]{0:T(128)S(1)} %concatenate.20.sc, bf16[512,4096]{1,0:T(8,128)(2,1)} %bitcast.28, bf16[512,512]{1,0:T(8,128)(2,1)S(1)} %bitcast.24, bf16[64,4608]{1,0:T(8,128)(2,1)S(1)} %pad_maximum_fusion.maps, f32[64,16]{1,0:T(8,128)S(1)} %fusion.2.fold, s32[1,64]{1,0:T(1,128)S(1)} %and_select_fusion.job_of), custom_call_target="tpu_custom_call" | custom-call | flops 1000 | bytes 1000 | tf_op jit(solution)/shard_map/adapter_products/pallas_call | solution.py:78
  33.0 1.5 %collective-permute-start.5 = (bf16[512,32]{1,0:T(8,128)(2,1)S(1)}, bf16[512,32]{1,0:T(8,128)(2,1)S(1)}, u32[]{:S(2)}, u32[]{:S(2)}) collective-permute-start(bf16[512,32]{1,0:T(8,128)(2,1)S(1)} %adapter_products.1.refs_0_), channel_id=1, source_target_pairs={{0,2},{2,0},{1,3},{3,1},{4,6},{6,4},{5,7},{7,5},{8,10},{10,8},{9,1... | collective-permute-start | bytes 98312 | tf_op jit(solution)/shard_map/ppermute | solution.py:34
  34.5 4.5 %base_0_0.1.refs_4_ = bf16[512,256]{1,0:T(8,128)(2,1)S(1)} custom-call(s32[86]{0:T(128)S(1)} %concatenate.20.sc, bf16[512,4096]{1,0:T(8,128)(2,1)} %bitcast.29, bf16[4096,256]{1,0:T(8,128)(2,1)S(1)} %copy-done, bf16[4096,256]{1,0:T(8,128)(2,1)S(1)} %copy-done, bf16[4096,256]{1,0:T(8,128)(2,1)S(1)} %copy-done, bf16[4096,256]{1,0:T(8,128)(2,1)S(1)} %copy-done), custom_call_target="tpu_custom_call" | custom-call | flops 1000 | bytes 1000 | tf_op jit(solution)/shard_map/base_0_0/pallas_call | solution.py:78
  40.4 2.5 %collective-permute-done.6.refs_0_.refs_6_ = bf16[1024,256]{1,0:T(8,128)(2,1)S(1)} collective-permute-done((bf16[1024,256]{1,0:T(8,128)(2,1)}, bf16[1024,256]{1,0:T(8,128)(2,1)S(1)}, u32[]{:S(2)}, u32[]{:S(2)}) %collective-permute-start.6) | collective-permute-done | bytes 524320 | tf_op jit(solution)/shard_map/ppermute | solution.py:34
  44.8 9.9 %collective-permute-done.9.refs_1_ = bf16[128,32]{1,0:T(8,128)(2,1)S(1)} collective-permute-done((bf16[128,32]{1,0:T(8,128)(2,1)S(1)}, bf16[128,32]{1,0:T(8,128)(2,1)S(1)}, u32[]{:S(2)}, u32[]{:S(2)}) %collective-permute-start.9) | collective-permute-done | bytes 8224 | tf_op jit(solution)/shard_map/ppermute | solution.py:34
  54.6 4.8 %collective-permute-done.10.refs_2_ = bf16[128,32]{1,0:T(8,128)(2,1)S(1)} collective-permute-done((bf16[128,32]{1,0:T(8,128)(2,1)S(1)}, bf16[128,32]{1,0:T(8,128)(2,1)S(1)}, u32[]{:S(2)}, u32[]{:S(2)}) %collective-permute-start.10) | collective-permute-done | bytes 8224 | tf_op jit(solution)/shard_map/ppermute | solution.py:34
  59.5 3.9 %collective-permute-done.11.refs_3_ = bf16[128,32]{1,0:T(8,128)(2,1)S(1)} collective-permute-done((bf16[128,32]{1,0:T(8,128)(2,1)S(1)}, bf16[128,32]{1,0:T(8,128)(2,1)S(1)}, u32[]{:S(2)}, u32[]{:S(2)}) %collective-permute-start.11) | collective-permute-done | bytes 8224 | tf_op jit(solution)/shard_map/ppermute | solution.py:34
  63.4 9.1 %job_tables.1 = (f32[32,4608]{1,0:T(8,128)S(1)}, f32[32,4608]{1,0:T(8,128)S(1)}) custom-call(s32[86]{0:T(128)S(1)} %concatenate.20.sc, bf16[512,4096]{1,0:T(8,128)(2,1)} %bitcast.30, bf16[512,512]{1,0:T(8,128)(2,1)S(1)} %bitcast.25, bf16[16,64]{1,0:T(8,128)(2,1)S(1)} %fusion.3.unfold, s32[1,64]{1,0:T(1,128)S(1)} %and_select_fusion.job_of, ...), custom_call_target="tpu_custom_call" | custom-call | flops 1000 | bytes 1000 | tf_op jit(solution)/shard_map/job_tables/pallas_call | solution.py:78
  72.6 4.6 %base_1_0.1.refs_5_.refs_3_ = bf16[512,256]{1,0:T(8,128)(2,1)S(1)} custom-call(s32[86]{0:T(128)S(1)} %concatenate.20.sc, bf16[512,4096]{1,0:T(8,128)(2,1)} %bitcast.31, bf16[1024,256]{1,0:T(8,128)(2,1)} %collective-permute-done.3.refs_0_.refs_4_, bf16[1024,256]{1,0:T(8,128)(2,1)S(1)} %collective-permute-done.14.refs_1_.refs_5_, ...), custom_call_target="tpu_custom_call" | custom-call | flops 1000 | bytes 1000 | tf_op jit(solution)/shard_map/base_1_0/pallas_call | solution.py:78
  80.0 7.1 %collective-permute-done.13.refs_2_.refs_8_ = bf16[512,256]{1,0:T(8,128)(2,1)S(1)} collective-permute-done((bf16[512,256]{1,0:T(8,128)(2,1)S(1)}, bf16[512,256]{1,0:T(8,128)(2,1)S(1)}, u32[]{:S(2)}, u32[]{:S(2)}) %collective-permute-start.13) | collective-permute-done | bytes 262176 | tf_op jit(solution)/shard_map/ppermute | solution.py:34
  87.7 4.6 %base_2_0.1 = (bf16[512,256]{1,0:T(8,128)(2,1)S(1)}, bf16[512,256]{1,0:T(8,128)(2,1)S(1)}, bf16[512,256]{1,0:T(8,128)(2,1)S(1)}) custom-call(s32[86]{0:T(128)S(1)} %concatenate.20.sc, bf16[512,4096]{1,0:T(8,128)(2,1)} %bitcast.32, bf16[1024,256]{1,0:T(8,128)(2,1)S(1)} %collective-permute-done.6.refs_0_.refs_6_, ...), custom_call_target="tpu_custom_call" | custom-call | flops 1000 | bytes 1000 | tf_op jit(solution)/shard_map/base_2_0/pallas_call | solution.py:78
  92.3 1.6 %collective-permute-start.28 = (bf16[512,256]{1,0:T(8,128)(2,1)S(1)}, bf16[512,256]{1,0:T(8,128)(2,1)S(1)}, u32[]{:S(2)}, u32[]{:S(2)}) collective-permute-start(bf16[512,256]{1,0:T(8,128)(2,1)S(1)} %get-tuple-element.127), channel_id=1, source_target_pairs={{0,2},{2,0},{1,3},{3,1},{4,6},{6,4},{5,7},{7,5},{8,10},{10,8},{9,1... | collective-permute-start | bytes 786440 | tf_op jit(solution)/shard_map/ppermute | solution.py:34
  94.6 3.8 %collective-permute-start.25 = (bf16[8,4608]{1,0:T(8,128)(2,1)S(1)}, bf16[8,4608]{1,0:T(8,128)(2,1)S(1)}, u32[]{:S(2)}, u32[]{:S(2)}) collective-permute-start(bf16[8,4608]{1,0:T(8,128)(2,1)S(1)} %get-tuple-element.179), channel_id=1, source_target_pairs={{0,8},{4,12},{8,0},{12,4},{1,9},{5,13},{9,1},{13,5},{2,10},{6,14},... | collective-permute-start | bytes 221192 | tf_op jit(solution)/shard_map/ppermute | solution.py:34
  100.8 5.1 %base_3_0.1.refs_2_ = f32[512,256]{1,0:T(8,128)S(1)} custom-call(s32[86]{0:T(128)S(1)} %concatenate.20.sc, bf16[512,4096]{1,0:T(8,128)(2,1)} %bitcast.33, bf16[512,256]{1,0:T(8,128)(2,1)S(1)} %collective-permute-done.12.refs_0_.refs_8_, bf16[512,256]{1,0:T(8,128)(2,1)S(1)} %collective-permute-done.20.refs_1_.refs_10_, ...), custom_call_target="tpu_custom_call" | custom-call | flops 1000 | bytes 1000 | tf_op jit(solution)/shard_map/base_3_0/pallas_call | solution.py:78
  113.2 3.1 %base_3_6.1 = (bf16[512,256]{1,0:T(8,128)(2,1)}, bf16[512,256]{1,0:T(8,128)(2,1)S(1)}, bf16[512,256]{1,0:T(8,128)(2,1)S(1)}) custom-call(s32[86]{0:T(128)S(1)} %concatenate.20.sc, bf16[512,4096]{1,0:T(8,128)(2,1)} %bitcast.34, bf16[512,256]{1,0:T(8,128)(2,1)} %collective-permute-done.27.refs_0_.refs_9_, ...), custom_call_target="tpu_custom_call" | custom-call | flops 1000 | bytes 1000 | tf_op jit(solution)/shard_map/base_3_6/pallas_call | solution.py:78
  117.7 6.3 %token_gradient_0.1.refs_12_ = bf16[512,4096]{1,0:T(8,128)(2,1)} custom-call(s32[86]{0:T(128)S(1)} %concatenate.20.sc, bf16[64,4608]{1,0:T(8,128)(2,1)S(1)} %pad_maximum_fusion.maps, bf16[512,32]{1,0:T(8,128)(2,1)S(1)} %copy-done.19, bf16[16,64]{1,0:T(8,128)(2,1)S(1)} %fusion.3.unfold, s32[1,64]{1,0:T(1,128)S(1)} %and_select_fusion.job_of, ...), custom_call_target="tpu_custom_call" | custom-call | flops 1000 | bytes 1000 | tf_op jit(solution)/shard_map/token_gradient_0/pallas_call | solution.py:78
  124.7 2.1 %layer.1 = (bf16[128,512]{1,0:T(8,128)(2,1)S(1)}, bf16[128,512]{1,0:T(8,128)(2,1)S(1)}, bf16[128,512]{1,0:T(8,128)(2,1)S(1)}, bf16[128,512]{1,0:T(8,128)(2,1)S(1)}) custom-call(s32[86]{0:T(128)S(1)} %concatenate.20.sc, bf16[512,32]{1,0:T(8,128)(2,1)S(1)} %copy-done.19, bf16[64,4608]{1,0:T(8,128)(2,1)S(1)} %pad_maximum_fusion.maps, ...), custom_call_target="tpu_custom_call" | custom-call | flops 1000 | bytes 1000 | tf_op jit(solution)/shard_map/layer/pallas_call | solution.py:78
  128.0 2.6 %collective-permute-start.34 = (bf16[128,512]{1,0:T(8,128)(2,1)S(1)}, bf16[128,512]{1,0:T(8,128)(2,1)S(1)}, u32[]{:S(2)}, u32[]{:S(2)}) collective-permute-start(bf16[128,512]{1,0:T(8,128)(2,1)S(1)} %get-tuple-element.158), channel_id=1, source_target_pairs={{0,12},{4,0},{8,4},{12,8},{1,13},{5,1},{9,5},{13,9},{2,14},{6,2},{... | collective-permute-start | bytes 393224 | tf_op jit(solution)/shard_map/ppermute | solution.py:34
  130.7 6.3 %token_gradient_2.1 = bf16[512,4096]{1,0:T(8,128)(2,1)} custom-call(s32[86]{0:T(128)S(1)} %concatenate.20.sc, bf16[64,4608]{1,0:T(8,128)(2,1)S(1)} %pad_maximum_fusion.maps, bf16[512,32]{1,0:T(8,128)(2,1)S(1)} %copy-done.19, bf16[16,64]{1,0:T(8,128)(2,1)S(1)} %fusion.3.unfold, s32[1,64]{1,0:T(1,128)S(1)} %and_select_fusion.job_of, ...), custom_call_target="tpu_custom_call", output_to_operand_aliasing={{}: (17, {})} | custom-call | flops 1000 | bytes 1000 | tf_op jit(solution)/shard_map/token_gradient_2/pallas_call | solution.py:78
  137.0 2.6 %collective-permute-done.33.refs_2_ = bf16[128,512]{1,0:T(8,128)(2,1)S(1)} collective-permute-done((bf16[128,512]{1,0:T(8,128)(2,1)S(1)}, bf16[128,512]{1,0:T(8,128)(2,1)S(1)}, u32[]{:S(2)}, u32[]{:S(2)}) %collective-permute-start.33) | collective-permute-done | bytes 131104 | tf_op jit(solution)/shard_map/ppermute | solution.py:34
  (186 shorter events, 31.8 us)
Async XLA Ops:
  1.7 17.0 %collective-permute-start.2 = (bf16[1,8,4608]{2,1,0:T(8,128)(2,1)S(1)}, bf16[1,8,4608]{2,1,0:T(8,128)(2,1)S(1)}, u32[]{:S(2)}, u32[]{:S(2)}) collective-permute-start(bf16[1,8,4608]{2,1,0:T(8,128)(2,1)S(1)} %dynamic-slice_bitcast_fusion), channel_id=1, source_target_pairs={{0,12},{4,0},{8,4},{12,8},{1,13},{5,1},{9,5},{13,9},{2,14},{6,2},{... | collective-permute-start | bytes 221192 | tf_op jit(solution)/shard_map/ppermute | solution.py:34
  6.8 18.2 %collective-permute-start.1 = (bf16[1,8,4608]{2,1,0:T(8,128)(2,1)S(1)}, bf16[1,8,4608]{2,1,0:T(8,128)(2,1)S(1)}, u32[]{:S(2)}, u32[]{:S(2)}) collective-permute-start(bf16[1,8,4608]{2,1,0:T(8,128)(2,1)S(1)} %dynamic-slice_bitcast_fusion), channel_id=1, source_target_pairs={{0,8},{4,12},{8,0},{12,4},{1,9},{5,13},{9,1},{13,5},{2,10},{6,14},... | collective-permute-start | bytes 221192 | tf_op jit(solution)/shard_map/ppermute | solution.py:34
  6.8 18.2 %collective-permute-start = (bf16[1,8,4608]{2,1,0:T(8,128)(2,1)S(1)}, bf16[1,8,4608]{2,1,0:T(8,128)(2,1)S(1)}, u32[]{:S(2)}, u32[]{:S(2)}) collective-permute-start(bf16[1,8,4608]{2,1,0:T(8,128)(2,1)S(1)} %dynamic-slice_bitcast_fusion), channel_id=1, source_target_pairs={{0,4},{4,8},{8,12},{12,0},{1,5},{5,9},{9,13},{13,1},{2,6},{6,10},{... | collective-permute-start | bytes 221192 | tf_op jit(solution)/shard_map/ppermute | solution.py:34
  8.9 16.1 %collective-permute-start.3 = (bf16[1024,256]{1,0:T(8,128)(2,1)S(1)}, bf16[1024,256]{1,0:T(8,128)(2,1)}, u32[]{:S(2)}, u32[]{:S(2)}) collective-permute-start(bf16[1024,256]{1,0:T(8,128)(2,1)S(1)} %constant_dynamic-slice_fusion), channel_id=1, source_target_pairs={{0,4},{4,8},{8,12},{12,0},{1,5},{5,9},{9,13},{13,1},{2,6},{6,10},{... | collective-permute-start | bytes 1572872 | tf_op jit(solution)/shard_map/ppermute | solution.py:34
  11.4 29.0 %collective-permute-start.8 = (bf16[512,512]{1,0:T(8,128)(2,1)}, bf16[512,512]{1,0:T(8,128)(2,1)}, u32[]{:S(2)}, u32[]{:S(2)}) collective-permute-start(bf16[512,512]{1,0:T(8,128)(2,1)} %bitcast.23), channel_id=1, source_target_pairs={{0,2},{2,0},{1,3},{3,1},{4,6},{6,4},{5,7},{7,5},{8,10},{10,8},{9,1... | collective-permute-start | bytes 1572872 | tf_op jit(solution)/shard_map/ppermute | solution.py:34
  25.2 15.1 %collective-permute-start.7 = (bf16[1024,256]{1,0:T(8,128)(2,1)}, bf16[1024,256]{1,0:T(8,128)(2,1)S(1)}, u32[]{:S(2)}, u32[]{:S(2)}) collective-permute-start(bf16[1024,256]{1,0:T(8,128)(2,1)} %collective-permute-done.3.refs_0_.refs_4_), channel_id=1, source_target_pairs={{0,16},{16,0},{1,17},{17,1},{2,18},{18,2},{3,19},{19,3},{4,20},{20... | collective-permute-start | bytes 1572872 | tf_op jit(solution)/shard_map/ppermute | solution.py:34
  26.8 16.0 %collective-permute-start.6 = (bf16[1024,256]{1,0:T(8,128)(2,1)}, bf16[1024,256]{1,0:T(8,128)(2,1)S(1)}, u32[]{:S(2)}, u32[]{:S(2)}) collective-permute-start(bf16[1024,256]{1,0:T(8,128)(2,1)} %collective-permute-done.3.refs_0_.refs_4_), channel_id=1, source_target_pairs={{0,4},{4,8},{8,12},{12,0},{1,5},{5,9},{9,13},{13,1},{2,6},{6,10},{... | collective-permute-start | bytes 1572872 | tf_op jit(solution)/shard_map/ppermute | solution.py:34
  42.8 34.5 %collective-permute-start.17 = (bf16[1024,256]{1,0:T(8,128)(2,1)S(1)}, bf16[1024,256]{1,0:T(8,128)(2,1)S(1)}, u32[]{:S(2)}, u32[]{:S(2)}) collective-permute-start(bf16[1024,256]{1,0:T(8,128)(2,1)S(1)} %collective-permute-done.6.refs_0_.refs_6_), channel_id=1, source_target_pairs={{0,16},{16,0},{1,17},{17,1},{2,18},{18,2},{3,19},{19,3},{4,20},{20... | collective-permute-start | bytes 1572872 | tf_op jit(solution)/shard_map/ppermute | solution.py:34
  43.3 29.2 %collective-permute-start.14 = (bf16[1024,256]{1,0:T(8,128)(2,1)}, bf16[1024,256]{1,0:T(8,128)(2,1)S(1)}, u32[]{:S(2)}, u32[]{:S(2)}) collective-permute-start(bf16[1024,256]{1,0:T(8,128)(2,1)} %collective-permute-done.3.refs_0_.refs_4_), channel_id=1, source_target_pairs={{0,1},{1,0},{2,3},{3,2},{4,5},{5,4},{6,7},{7,6},{8,9},{9,8},{10,11... | collective-permute-start | bytes 1572872 | tf_op jit(solution)/shard_map/ppermute | solution.py:34
  43.3 29.2 %collective-permute-start.15 = (bf16[1024,256]{1,0:T(8,128)(2,1)S(1)}, bf16[1024,256]{1,0:T(8,128)(2,1)S(1)}, u32[]{:S(2)}, u32[]{:S(2)}) collective-permute-start(bf16[1024,256]{1,0:T(8,128)(2,1)S(1)} %collective-permute-done.7.refs_2_.refs_4_), channel_id=1, source_target_pairs={{0,1},{1,0},{2,3},{3,2},{4,5},{5,4},{6,7},{7,6},{8,9},{9,8},{10,11... | collective-permute-start | bytes 1572872 | tf_op jit(solution)/shard_map/ppermute | solution.py:34
  43.9 28.6 %collective-permute-start.12 = (bf16[512,256]{1,0:T(8,128)(2,1)S(1)}, bf16[512,256]{1,0:T(8,128)(2,1)S(1)}, u32[]{:S(2)}, u32[]{:S(2)}) collective-permute-start(bf16[512,256]{1,0:T(8,128)(2,1)S(1)} %get-tuple-element.175), channel_id=1, source_target_pairs={{0,4},{4,8},{8,12},{12,0},{1,5},{5,9},{9,13},{13,1},{2,6},{6,10},{... | collective-permute-start | bytes 786440 | tf_op jit(solution)/shard_map/ppermute | solution.py:34
  43.9 10.7 %collective-permute-start.9 = (bf16[128,32]{1,0:T(8,128)(2,1)S(1)}, bf16[128,32]{1,0:T(8,128)(2,1)S(1)}, u32[]{:S(2)}, u32[]{:S(2)}) collective-permute-start(bf16[128,32]{1,0:T(8,128)(2,1)S(1)} %get-tuple-element.99), channel_id=1, source_target_pairs={{0,4},{4,8},{8,12},{12,0},{1,5},{5,9},{9,13},{13,1},{2,6},{6,10},{... | collective-permute-start | bytes 24584 | tf_op jit(solution)/shard_map/ppermute | solution.py:34
  63.4 13.9 %collective-permute-start.16 = (bf16[512,256]{1,0:T(8,128)(2,1)S(1)}, bf16[512,256]{1,0:T(8,128)(2,1)S(1)}, u32[]{:S(2)}, u32[]{:S(2)}) collective-permute-start(bf16[512,256]{1,0:T(8,128)(2,1)S(1)} %get-tuple-element.174), channel_id=1, source_target_pairs={{0,4},{4,8},{8,12},{12,0},{1,5},{5,9},{9,13},{13,1},{2,6},{6,10},{... | collective-permute-start | bytes 786440 | tf_op jit(solution)/shard_map/ppermute | solution.py:34
  72.5 19.9 %collective-permute-start.23 = (f32[32,4608]{1,0:T(8,128)S(1)}, f32[32,4608]{1,0:T(8,128)S(1)}, u32[]{:S(2)}, u32[]{:S(2)}) collective-permute-start(f32[32,4608]{1,0:T(8,128)S(1)} %get-tuple-element.123), channel_id=1, source_target_pairs={{0,1},{1,0},{2,3},{3,2},{4,5},{5,4},{6,7},{7,6},{8,9},{9,8},{10,11... | collective-permute-start | bytes 1769480 | tf_op jit(solution)/shard_map/ppermute | solution.py:34
  77.3 9.7 %collective-permute-start.18 = (bf16[1024,256]{1,0:T(8,128)(2,1)S(1)}, bf16[1024,256]{1,0:T(8,128)(2,1)S(1)}, u32[]{:S(2)}, u32[]{:S(2)}) collective-permute-start(bf16[1024,256]{1,0:T(8,128)(2,1)S(1)} %collective-permute-done.6.refs_0_.refs_6_), channel_id=1, source_target_pairs={{0,1},{1,0},{2,3},{3,2},{4,5},{5,4},{6,7},{7,6},{8,9},{9,8},{10,11... | collective-permute-start | bytes 1572872 | tf_op jit(solution)/shard_map/ppermute | solution.py:34
  77.9 9.2 %collective-permute-start.19 = (bf16[1024,256]{1,0:T(8,128)(2,1)S(1)}, bf16[1024,256]{1,0:T(8,128)(2,1)S(1)}, u32[]{:S(2)}, u32[]{:S(2)}) collective-permute-start(bf16[1024,256]{1,0:T(8,128)(2,1)S(1)} %collective-permute-done.17.refs_2_.refs_6_), channel_id=1, source_target_pairs={{0,1},{1,0},{2,3},{3,2},{4,5},{5,4},{6,7},{7,6},{8,9},{9,8},{10,11... | collective-permute-start | bytes 1572872 | tf_op jit(solution)/shard_map/ppermute | solution.py:34
  79.5 27.3 %collective-permute-start.27 = (bf16[512,256]{1,0:T(8,128)(2,1)S(1)}, bf16[512,256]{1,0:T(8,128)(2,1)}, u32[]{:S(2)}, u32[]{:S(2)}) collective-permute-start(bf16[512,256]{1,0:T(8,128)(2,1)S(1)} %collective-permute-done.16.refs_4_.refs_9_), channel_id=1, source_target_pairs={{0,16},{16,0},{1,17},{17,1},{2,18},{18,2},{3,19},{19,3},{4,20},{20... | collective-permute-start | bytes 786440 | tf_op jit(solution)/shard_map/ppermute | solution.py:34
  87.6 10.8 %collective-permute-start.21 = (bf16[512,256]{1,0:T(8,128)(2,1)S(1)}, bf16[512,256]{1,0:T(8,128)(2,1)S(1)}, u32[]{:S(2)}, u32[]{:S(2)}) collective-permute-start(bf16[512,256]{1,0:T(8,128)(2,1)S(1)} %collective-permute-done.13.refs_2_.refs_8_), channel_id=1, source_target_pairs={{0,1},{1,0},{2,3},{3,2},{4,5},{5,4},{6,7},{7,6},{8,9},{9,8},{10,11... | collective-permute-start | bytes 786440 | tf_op jit(solution)/shard_map/ppermute | solution.py:34
  92.3 14.4 %collective-permute-start.28 = (bf16[512,256]{1,0:T(8,128)(2,1)S(1)}, bf16[512,256]{1,0:T(8,128)(2,1)S(1)}, u32[]{:S(2)}, u32[]{:S(2)}) collective-permute-start(bf16[512,256]{1,0:T(8,128)(2,1)S(1)} %get-tuple-element.127), channel_id=1, source_target_pairs={{0,2},{2,0},{1,3},{3,1},{4,6},{6,4},{5,7},{7,5},{8,10},{10,8},{9,1... | collective-permute-start | bytes 786440 | tf_op jit(solution)/shard_map/ppermute | solution.py:34
  94.0 12.7 %collective-permute-start.26 = (bf16[8,4608]{1,0:T(8,128)(2,1)S(1)}, bf16[8,4608]{1,0:T(8,128)(2,1)S(1)}, u32[]{:S(2)}, u32[]{:S(2)}) collective-permute-start(bf16[8,4608]{1,0:T(8,128)(2,1)S(1)} %get-tuple-element.178), channel_id=1, source_target_pairs={{0,4},{4,8},{8,12},{12,0},{1,5},{5,9},{9,13},{13,1},{2,6},{6,10},{... | collective-permute-start | bytes 221192 | tf_op jit(solution)/shard_map/ppermute | solution.py:34
  94.6 12.1 %collective-permute-start.25 = (bf16[8,4608]{1,0:T(8,128)(2,1)S(1)}, bf16[8,4608]{1,0:T(8,128)(2,1)S(1)}, u32[]{:S(2)}, u32[]{:S(2)}) collective-permute-start(bf16[8,4608]{1,0:T(8,128)(2,1)S(1)} %get-tuple-element.179), channel_id=1, source_target_pairs={{0,8},{4,12},{8,0},{12,4},{1,9},{5,13},{9,1},{13,5},{2,10},{6,14},... | collective-permute-start | bytes 221192 | tf_op jit(solution)/shard_map/ppermute | solution.py:34
  126.8 10.2 %collective-permute-start.32 = (bf16[128,512]{1,0:T(8,128)(2,1)S(1)}, bf16[128,512]{1,0:T(8,128)(2,1)S(1)}, u32[]{:S(2)}, u32[]{:S(2)}) collective-permute-start(bf16[128,512]{1,0:T(8,128)(2,1)S(1)} %get-tuple-element.156), channel_id=1, source_target_pairs={{0,4},{4,8},{8,12},{12,0},{1,5},{5,9},{9,13},{13,1},{2,6},{6,10},{... | collective-permute-start | bytes 393224 | tf_op jit(solution)/shard_map/ppermute | solution.py:34
  127.7 11.8 %collective-permute-start.33 = (bf16[128,512]{1,0:T(8,128)(2,1)S(1)}, bf16[128,512]{1,0:T(8,128)(2,1)S(1)}, u32[]{:S(2)}, u32[]{:S(2)}) collective-permute-start(bf16[128,512]{1,0:T(8,128)(2,1)S(1)} %get-tuple-element.157), channel_id=1, source_target_pairs={{0,8},{4,12},{8,0},{12,4},{1,9},{5,13},{9,1},{13,5},{2,10},{6,14},... | collective-permute-start | bytes 393224 | tf_op jit(solution)/shard_map/ppermute | solution.py:34
  128.0 11.6 %collective-permute-start.34 = (bf16[128,512]{1,0:T(8,128)(2,1)S(1)}, bf16[128,512]{1,0:T(8,128)(2,1)S(1)}, u32[]{:S(2)}, u32[]{:S(2)}) collective-permute-start(bf16[128,512]{1,0:T(8,128)(2,1)S(1)} %get-tuple-element.158), channel_id=1, source_target_pairs={{0,12},{4,0},{8,4},{12,8},{1,13},{5,1},{9,5},{13,9},{2,14},{6,2},{... | collective-permute-start | bytes 393224 | tf_op jit(solution)/shard_map/ppermute | solution.py:34
  (50 other events, 461.8 us)

commit v6 on v5

--- a/solution.py
+++ b/solution.py
@@ -88,6 +88,9 @@
     )(scalars, *inputs)
 
 
+ANY = pl.BlockSpec(memory_space=pl.ANY)
+
+
 def whole(x):
     return pl.BlockSpec(x.shape, lambda *_: (0,) * len(x.shape))
 
@@ -105,33 +108,43 @@
     return jnp.where(job_of == rel, wide, 0.0).astype(bf16)
 
 
-def products_kernel(z, n, sc, tokens, grad, maps, fold, job_of, out):
-    step = pl.program_id(0)
-    down = dot(tokens[...], maps[:, : z.width], ((1,), (1,)))
+def products_kernel(z, n, sc, tokens, grad, maps, fold, job_of, out, held, sems):
+    many = z.blocks // n
+    copies = [
+        pltpu.make_async_copy(tokens.at[pl.ds(k * n * z.halved, n * z.halved), :], held.at[k], sems.at[k])
+        for k in range(many)
+    ]
+    for copy in copies:
+        copy.start()
     back = dot(grad[...], maps[:, z.width :], ((1,), (1,)))
-    for k in range(n):
-        block = step * n + k
-        own = slice(k * z.halved, (k + 1) * z.halved)
-        picked = jnp.where(job_of[...] == z.get(sc, "out_rel", block), down[own], 0.0)
-        out[own, : z.rank] = dot(picked, fold[...], ((1,), (0,)), lax.Precision.HIGHEST).astype(bf16)
+    for block in range(z.blocks):
+        own = slice(block * z.halved, (block + 1) * z.halved)
         picked = jnp.where(job_of[...] == z.get(sc, "in_rel", block), back[own], 0.0)
         picked = jnp.where(row_mask(z.get(sc, "in_valid", block), z, z.wide), picked, 0.0)
         out[own, z.rank :] = dot(picked, fold[...], ((1,), (0,)), lax.Precision.HIGHEST).astype(bf16)
+    for k in range(many):
+        copies[k].wait()
+        down = dot(held[k], maps[:, : z.width], ((1,), (1,)))
+        for r in range(n):
+            block = k * n + r
+            own = slice(block * z.halved, (block + 1) * z.halved)
+            mine = slice(r * z.halved, (r + 1) * z.halved)
+            picked = jnp.where(job_of[...] == z.get(sc, "out_rel", block), down[mine], 0.0)
+            out[own, : z.rank] = dot(picked, fold[...], ((1,), (0,)), lax.Precision.HIGHEST).astype(bf16)
 
 
 def products(z, sc, tokens, grad, maps, fold, job_of):
     n = 2
+    shape = jax.ShapeDtypeStruct((z.rows, 2 * z.rank), bf16)
     return call(
-        functools.partial(products_kernel, z, n), "adapter_products", (z.blocks // n,), sc,
+        functools.partial(products_kernel, z, n), "adapter_products", (1,), sc,
         (tokens, grad, maps, fold, job_of),
-        [
-            pl.BlockSpec((n * z.halved, z.width), lambda i, _: (i, 0)),
-            pl.BlockSpec((n * z.halved, z.heads), lambda i, _: (i, 0)),
-            whole(maps), whole(fold), whole(job_of),
-        ],
-        jax.ShapeDtypeStruct((z.rows, 2 * z.rank), bf16),
-        pl.BlockSpec((n * z.halved, 2 * z.rank), lambda i, _: (i, 0)),
-        2 * z.rows * (z.width + z.heads) * z.wide, 2 * z.rows * (z.width + z.heads), TOKEN_LIMIT,
+        [ANY, whole(grad), whole(maps), whole(fold), whole(job_of)],
+        shape, whole(shape), 1000, 1000, TOKEN_LIMIT,
+        scratch=(
+            pltpu.VMEM((z.blocks // n, n * z.halved, z.width), bf16),
+            pltpu.SemaphoreType.DMA((z.blocks // n,)),
+        ),
     )
 
 
@@ -162,108 +175,98 @@
 
 
 def table_kernel(z, tiles, sc, tokens, grad, unfold, job_of, *refs):
-    got, (mine, theirs, back, down, back_t, down_t) = refs[: z.nd], refs[z.nd :]
+    got, (mine, theirs, back, down, back_t, down_t, held, sems) = refs[: z.nd], refs[z.nd :]
     half = mine.shape[0]
-    step = pl.program_id(0)
-
-    @pl.when(step == 0)
-    def _():
-        for d in range(z.nd):
-            for r in range(z.cap):
-                slot = d * z.cap + r
-                own = slice(r * z.halved, (r + 1) * z.halved)
-
-                @pl.when(z.get(sc, "out_fill", slot) > 0)
-                def _():
-                    at = z.get(sc, "out_pos", slot)
-                    values = got[(z.nd - d) % z.nd][own, z.rank :]
-                    back[rows_of(at, z), :] = widen(values, z.get(sc, "out_rel", at), unfold[...], job_of[...], z)
-
-                @pl.when(z.get(sc, "in_fill", slot) > 0)
-                def _():
-                    at = z.get(sc, "in_pos", slot)
-                    values = widen(got[d][own, : z.rank], z.get(sc, "in_rel", at), unfold[...], job_of[...], z)
-                    mask = row_mask(z.get(sc, "in_valid", at), z, z.wide)
-                    down[rows_of(at, z), :] = jnp.where(mask, values, 0).astype(bf16)
-
-        same = lax.broadcasted_iota(i32, (z.rows, z.rows), 0) == lax.broadcasted_iota(i32, (z.rows, z.rows), 1)
-        unit = jnp.where(same, 1.0, 0.0).astype(bf16)
-        back_t[...] = dot(back[...], unit, ((0,), (0,))).astype(bf16)
-        down_t[...] = dot(down[...], unit, ((0,), (0,))).astype(bf16)
-
-    def put(wide, values):
-        total = dot(wide[...], values[...], ((1,), (0,)))
-        mine[...] = total[:half]
-        theirs[...] = total[half:]
-
-    @pl.when(step < tiles)
-    def _():
-        put(back_t, tokens)
-
-    @pl.when(step == tiles)
-    def _():
-        put(down_t, grad)
+    part = z.width // tiles
+    copies = [
+        pltpu.make_async_copy(tokens.at[:, pl.ds(k * part, part)], held.at[k], sems.at[k]) for k in range(tiles)
+    ]
+    for copy in copies:
+        copy.start()
+    for d in range(z.nd):
+        for r in range(z.cap):
+            slot = d * z.cap + r
+            own = slice(r * z.halved, (r + 1) * z.halved)
+
+            @pl.when(z.get(sc, "out_fill", slot) > 0)
+            def _():
+                at = z.get(sc, "out_pos", slot)
+                values = got[(z.nd - d) % z.nd][own, z.rank :]
+                back[rows_of(at, z), :] = widen(values, z.get(sc, "out_rel", at), unfold[...], job_of[...], z)
+
+            @pl.when(z.get(sc, "in_fill", slot) > 0)
+            def _():
+                at = z.get(sc, "in_pos", slot)
+                values = widen(got[d][own, : z.rank], z.get(sc, "in_rel", at), unfold[...], job_of[...], z)
+                mask = row_mask(z.get(sc, "in_valid", at), z, z.wide)
+                down[rows_of(at, z), :] = jnp.where(mask, values, 0).astype(bf16)
+
+    same = lax.broadcasted_iota(i32, (z.rows, z.rows), 0) == lax.broadcasted_iota(i32, (z.rows, z.rows), 1)
+    unit = jnp.where(same, 1.0, 0.0).astype(bf16)
+    back_t[...] = dot(back[...], unit, ((0,), (0,))).astype(bf16)
+    down_t[...] = dot(down[...], unit, ((0,), (0,))).astype(bf16)
+    total = dot(down_t[...], grad[...], ((1,), (0,)))
+    mine[:, z.width :] = total[:half]
+    theirs[:, z.width :] = total[half:]
+    for k in range(tiles):
+        copies[k].wait()
+        total = dot(back_t[...], held[k], ((1,), (0,)))
+        mine[:, k * part : (k + 1) * part] = total[:half]
+        theirs[:, k * part : (k + 1) * part] = total[half:]
 
 
 def tables_of(z, sc, tokens, grad, unfold, job_of, got):
-    tiles = z.width // z.heads
-    half = z.wide // z.ns
-    shape = jax.ShapeDtypeStruct((half, z.width + z.heads), f32)
-    out = pl.BlockSpec((half, z.heads), lambda i, _: (0, i))
+    tiles = 4
+    shape = jax.ShapeDtypeStruct((z.wide // z.ns, z.width + z.heads), f32)
     return call(
-        functools.partial(table_kernel, z, tiles), "job_tables", (tiles + 1,), sc,
+        functools.partial(table_kernel, z, tiles), "job_tables", (1,), sc,
         (tokens, grad, unfold, job_of, *got),
-        [
-            pl.BlockSpec((z.rows, z.heads), lambda i, _: (0, jnp.minimum(i, tiles - 1))),
-            whole(grad), whole(unfold), whole(job_of),
-        ]
-        + [whole(x) for x in got],
-        (shape, shape), (out, out),
-        2 * z.wide * z.rows * (z.width + z.heads), 2 * z.rows * z.width + 4 * z.wide * z.width, TOKEN_LIMIT,
-        scratch=(pltpu.VMEM((z.rows, z.wide), bf16),) * 2 + (pltpu.VMEM((z.wide, z.rows), bf16),) * 2,
-    )
-
-
-def base_kernel(z, d, count, started, partial, slot, others, sc, tokens, *refs):
+        [ANY, whole(grad), whole(unfold), whole(job_of)] + [whole(x) for x in got],
+        (shape, shape), (whole(shape), whole(shape)), 1000, 1000, TOKEN_LIMIT,
+        scratch=(pltpu.VMEM((z.rows, z.wide), bf16),) * 2
+        + (pltpu.VMEM((z.wide, z.rows), bf16),) * 2
+        + (pltpu.VMEM((tiles, z.rows, z.width // tiles), bf16), pltpu.SemaphoreType.DMA((tiles,))),
+    )
+
+
+def base_kernel(z, d, count, started, partial, slot, others, at, features, sc, tokens, *refs):
     pieces, refs = refs[:count], refs[count:]
     if started:
         begun, refs = refs[0], refs[1:]
     earlier, refs = refs[: len(others)], refs[len(others) :]
-    outs, total = refs[:-1], refs[-1]
-    step = pl.program_id(0)
+    outs, (held, parts, sems) = refs[:-3], refs[-3:]
+    copies = []
     for k in range(count):
-
-        @pl.when(step == k)
-        def _():
-            part = dot(tokens[...], pieces[k][...], ((1,), (0,)))
-            if k > 0:
-                part = part + total[...]
-            elif started:
-                part = part + begun[...]
-            if k < count - 1:
-                total[...] = part
-            elif partial:
-                outs[0][...] = part
-            else:
-                done = part.astype(bf16)
-                outs[0][...] = done
-                for g in range(len(outs) - 1):
-                    outs[1 + g][...] = done
-                    for at, values in zip(others, earlier):
-
-                        @pl.when(z.get(sc, "pick", g * z.per_head + slot) == at)
-                        def _():
-                            outs[1 + g][...] = values[...]
+        start = pl.multiple_of(sc[at + k] * features, features)
+        copies.append(pltpu.make_async_copy(tokens.at[:, pl.ds(start, features)], held.at[k], sems.at[0, k]))
+        source = pieces[k].at[pl.ds(start, features), :] if d == 0 else pieces[k]
+        copies.append(pltpu.make_async_copy(source, parts.at[k], sems.at[1, k]))
+    for copy in copies:
+        copy.start()
+    total = begun[...] if started else None
+    for k in range(count):
+        copies[2 * k].wait()
+        copies[2 * k + 1].wait()
+        part = dot(held[k], parts[k], ((1,), (0,)))
+        total = part if total is None else total + part
+    if partial:
+        outs[0][...] = total
+        return
+    done = total.astype(bf16)
+    outs[0][...] = done
+    for g in range(len(outs) - 1):
+        outs[1 + g][...] = done
+        for where, values in zip(others, earlier):
+
+            @pl.when(z.get(sc, "pick", g * z.per_head + slot) == where)
+            def _():
+                outs[1 + g][...] = values[...]
 
 
 def base_product(z, sc, tokens, pieces, d, base, first=0, begun=None, partial=False):
     count, features = len(pieces), pieces[0].shape[0] if d else z.fq
-    at = z.at["quarter"] if features == z.fq else z.at["step"]
-    if d == 0:
-        specs = [pl.BlockSpec((z.fq, z.columns), lambda i, q, r=r: (q[at + r], 0)) for r in range(z.nq)]
-    else:
-        specs = [whole(x) for x in pieces]
-    inputs = [tokens, *pieces]
+    at = z.at["quarter"] if features == z.fq else z.at["step"] + first
+    inputs, specs = [tokens, *pieces], [ANY] * (1 + count)
     if begun is not None:
         inputs.append(begun)
         specs.append(whole(begun))
@@ -276,12 +279,15 @@
         specs += [whole(base[k]) for k in others]
         shapes += [jax.ShapeDtypeStruct((z.rows, z.columns), bf16)] * z.nt
     return call(
-        functools.partial(base_kernel, z, d, count, begun is not None, partial, slot, others),
-        "base_%d_%d" % (d, first), (count,), sc, inputs,
-        [pl.BlockSpec((z.rows, features), lambda i, q: (0, q[at + first + i]))] + specs,
+        functools.partial(base_kernel, z, d, count, begun is not None, partial, slot, others, at, features),
+        "base_%d_%d" % (d, first), (1,), sc, inputs, specs,
         tuple(shapes), tuple(whole(x) for x in shapes),
         1000, 1000, TOKEN_LIMIT,
-        scratch=(pltpu.VMEM((z.rows, z.columns), f32),),
+        scratch=(
+            pltpu.VMEM((count, z.rows, features), bf16),
+            pltpu.VMEM((count, features, z.columns), bf16),
+            pltpu.SemaphoreType.DMA((2, count)),
+        ),
     )
 
 
@@ -508,11 +514,11 @@
     base[0], parts = tie(base[0], parts)
     sums, *pays = sums_of(zz, sc, parts)
 
-    rounds[last - 1], over[1], pays, grads = tie(rounds[last - 1], over[1], pays, grads)
+    got = [shifted(pays[d], "dp", nd, d) for d in range(nd)]
+    rounds[last - 1], over[1], got, grads = tie(rounds[last - 1], over[1], got, grads)
     ends = [
         shifted(rounds[last - 1][c * zz.fe : (c + 1) * zz.fe], "dp", nd, 1) for c in range(zz.chunks)
     ]
-    got = [shifted(pays[d], "dp", nd, d) for d in range(nd)]
     mine, theirs = tables_of(zz, sc, own_tokens, own_grad, unfold, job_of, got)
     for d in range(2, last):
         over[d] = gather_shifts(rounds[d], "parts", np_)
@@ -544,31 +550,30 @@
     ahead, behind = [x for y in end_over[:-1] for x in spread_round(y)], end_over[-1]
     ahead += gather_shifts(behind[0], "sub", ns)
     begun = base_product(zz, sc, own_tokens, ahead, last, base, 0, None, True)[0]
-    begun, tables, behind, slots = tie(begun, tables, behind, slots)
+    begun, behind, slots = tie(begun, behind, slots)
     tail = spread_round(behind[1:])
     piece_list.append(ahead + tail)
+    finish(last, base_product(zz, sc, own_tokens, tail, last, base, len(ahead), begun))
+    base[-1], tables, grads = tie(base[-1], tables, grads)
     total = sum(x.astype(f32) for x in tables)
     counts = lax.dynamic_slice_in_dim(tokens_per_job, z * jobs_dev, jobs_dev).astype(f32)
     total = total.reshape(jobs_dev, r2, -1) * (adapter_scale / counts)[:, None, None]
     halves = gather_shifts(total, "sub", ns)
-    finish(last, base_product(zz, sc, own_tokens, tail, last, base, len(ahead), begun))
-    base[-1], halves, grads = tie(base[-1], halves, grads)
-    owned = jnp.concatenate(
-        [sum(jnp.where((s - h) % ns == k, x, 0.0) for k, x in enumerate(halves)) for h in range(ns)], axis=1
-    )
-    grad_down, grad_up = owned[:, :, :width], owned[:, :, width:]
-
     half = zz.nq // 2
     gradient = token_gradient_of(zz, sc, grads, maps, sums, unfold, job_of, piece_list, list(range(half)), None)
     given = [slots[j][d] for d in range(nt) for j in range(m)]
-    gradient, grad_down, grad_up, *given = tie(gradient, grad_down, grad_up, *given)
+    gradient, halves, *given = tie(gradient, halves, *given)
     layer = layer_of(zz, sc, sums, maps, unfold, job_of, given)
     *layer, gradient = tie(*layer, gradient)
+    owned = jnp.concatenate(
+        [sum(jnp.where((s - h) % ns == k, x, 0.0) for k, x in enumerate(halves)) for h in range(ns)], axis=1
+    )
+    grad_down, grad_up = owned[:, :, :width], owned[:, :, width:]
     landed = [shifted(layer[d], "dp", nd, d) for d in range(nd)]
     gradient = token_gradient_of(
         zz, sc, grads, maps, sums, unfold, job_of, piece_list, list(range(half, zz.nq)), gradient
     )
-    gradient, *landed = tie(gradient, *landed)
+    gradient, grad_down, grad_up, *landed = tie(gradient, grad_down, grad_up, *landed)
     layer_output = place(zz, sc, landed)
     return (
         layer_output.reshape(1, blocks, halved, heads),

time: 142 us -> 137 us (0.965)
  waiting for transfers between devices: 38.5 us -> 34.1 us
  Pallas kernels: 53.5 us -> 49.7 us
  local copies, waits for them, and re-layouts: 7.08 us -> 10.5 us
    ppermute x35, waiting for transfers between devices: 38.5 us -> 34.1 us  [shifted(): lax.ppermute(values, axis, [(i, (i + step) % count) for i in range(count)])]
    pallas_call x12, Pallas kernels: 53.5 us -> 49.7 us  [call(): pl.pallas_call(kernel, out_shape=out_shape, grid_spec=pltpu.PrefetchScala...]
    unnamed x78, local copies, waits for them, and re-layouts: 4.32 us -> 7.76 us
  transfers between devices with their start and end apart: 35 -> 35, of which waited for: 8 -> 9; matrix products, arithmetic and copies ran while one was open for 7% -> 7% of each run, Pallas kernels for 33% -> 31%
where the time goes in v6:
time: 137 us; the launch traced here: 136 us
  Pallas kernels  49.7 us (36%)
  waiting for transfers between devices  34.1 us (25%)
  starting transfers between devices  31.2 us (23%)
  local copies, waits for them, and re-layouts  10.5 us (8%)
  other arithmetic  8.27 us (6%)
  between operations  2.11 us (2%)
    pallas_call x12, Pallas kernels, call(): pl.pallas_call(kernel, out_shape=out_shape, grid_spec=pltpu.PrefetchScala...  49.7 us
    ppermute x35, waiting for transfers between devices, shifted(): lax.ppermute(values, axis, [(i, (i + step) % count) for i in range(count)])  34.1 us
    ppermute x35, starting transfers between devices, shifted(): lax.ppermute(values, axis, [(i, (i + step) % count) for i in range(count)])  31.2 us
    unnamed x78, local copies, waits for them, and re-layouts  7.76 us
  transfers between devices with their start and end apart: 35, of which 9 were waited for; matrix products, arithmetic and copies ran while one was open for 7% of the time, Pallas kernels for 31%

profile of v6, /device:TPU:0, one launch (start us, length us, event | category | flops | bytes accessed | tf_op | source)
XLA Modules:
  0.0 135.9 jit_solution(16425572423088113940)
XLA Ops:
  1.7 3.1 %collective-permute-start = (bf16[1,8,4608]{2,1,0:T(8,128)(2,1)S(1)}, bf16[1,8,4608]{2,1,0:T(8,128)(2,1)S(1)}, u32[]{:S(2)}, u32[]{:S(2)}) collective-permute-start(bf16[1,8,4608]{2,1,0:T(8,128)(2,1)S(1)} %dynamic-slice_bitcast_fusion), channel_id=1, source_target_pairs={{0,4},{4,8},{8,12},{12,0},{1,5},{5,9},{9,13},{13,1},{2,6},{6,10},{... | collective-permute-start | bytes 221192 | tf_op jit(solution)/shard_map/ppermute | solution.py:34
  4.7 2.6 %collective-permute-start.1 = (bf16[1,8,4608]{2,1,0:T(8,128)(2,1)S(1)}, bf16[1,8,4608]{2,1,0:T(8,128)(2,1)S(1)}, u32[]{:S(2)}, u32[]{:S(2)}) collective-permute-start(bf16[1,8,4608]{2,1,0:T(8,128)(2,1)S(1)} %dynamic-slice_bitcast_fusion), channel_id=1, source_target_pairs={{0,8},{4,12},{8,0},{12,4},{1,9},{5,13},{9,1},{13,5},{2,10},{6,14},... | collective-permute-start | bytes 221192 | tf_op jit(solution)/shard_map/ppermute | solution.py:34
  17.9 6.8 %collective-permute-done.3.refs_0_.refs_4_ = bf16[1024,256]{1,0:T(8,128)(2,1)} collective-permute-done((bf16[1024,256]{1,0:T(8,128)(2,1)S(1)}, bf16[1024,256]{1,0:T(8,128)(2,1)}, u32[]{:S(2)}, u32[]{:S(2)}) %collective-permute-start.3) | collective-permute-done | bytes 524320 | tf_op jit(solution)/shard_map/ppermute | solution.py:34
  25.8 1.5 %collective-permute-start.7 = (bf16[1024,256]{1,0:T(8,128)(2,1)}, bf16[1024,256]{1,0:T(8,128)(2,1)S(1)}, u32[]{:S(2)}, u32[]{:S(2)}) collective-permute-start(bf16[1024,256]{1,0:T(8,128)(2,1)} %collective-permute-done.3.refs_0_.refs_4_), channel_id=1, source_target_pairs={{0,16},{16,0},{1,17},{17,1},{2,18},{18,2},{3,19},{19,3},{4,20},{20... | collective-permute-start | bytes 1572872 | tf_op jit(solution)/shard_map/ppermute | solution.py:34
  27.4 5.5 %adapter_products.1.refs_0_ = bf16[512,32]{1,0:T(8,128)(2,1)S(1)} custom-call(s32[86]{0:T(128)S(1)} %concatenate.20.sc, bf16[512,4096]{1,0:T(8,128)(2,1)} %bitcast.28, bf16[512,512]{1,0:T(8,128)(2,1)S(1)} %bitcast.24, bf16[64,4608]{1,0:T(8,128)(2,1)S(1)} %pad_maximum_fusion.maps, f32[64,16]{1,0:T(8,128)S(1)} %fusion.2.fold, s32[1,64]{1,0:T(1,128)S(1)} %and_select_fusion.job_of), custom_call_target="tpu_custom_call" | custom-call | flops 1000 | bytes 1000 | tf_op jit(solution)/shard_map/adapter_products/pallas_call | solution.py:78
  32.9 1.6 %collective-permute-start.5 = (bf16[512,32]{1,0:T(8,128)(2,1)S(1)}, bf16[512,32]{1,0:T(8,128)(2,1)S(1)}, u32[]{:S(2)}, u32[]{:S(2)}) collective-permute-start(bf16[512,32]{1,0:T(8,128)(2,1)S(1)} %adapter_products.1.refs_0_), channel_id=1, source_target_pairs={{0,2},{2,0},{1,3},{3,1},{4,6},{6,4},{5,7},{7,5},{8,10},{10,8},{9,1... | collective-permute-start | bytes 98312 | tf_op jit(solution)/shard_map/ppermute | solution.py:34
  34.5 4.7 %base_0_0.1.refs_4_ = bf16[512,256]{1,0:T(8,128)(2,1)S(1)} custom-call(s32[86]{0:T(128)S(1)} %concatenate.20.sc, bf16[512,4096]{1,0:T(8,128)(2,1)} %bitcast.29, bf16[4096,256]{1,0:T(8,128)(2,1)S(1)} %copy-done, bf16[4096,256]{1,0:T(8,128)(2,1)S(1)} %copy-done, bf16[4096,256]{1,0:T(8,128)(2,1)S(1)} %copy-done, bf16[4096,256]{1,0:T(8,128)(2,1)S(1)} %copy-done), custom_call_target="tpu_custom_call" | custom-call | flops 1000 | bytes 1000 | tf_op jit(solution)/shard_map/base_0_0/pallas_call | solution.py:78
  39.8 2.9 %collective-permute-start.10 = (bf16[128,32]{1,0:T(8,128)(2,1)S(1)}, bf16[128,32]{1,0:T(8,128)(2,1)S(1)}, u32[]{:S(2)}, u32[]{:S(2)}) collective-permute-start(bf16[128,32]{1,0:T(8,128)(2,1)S(1)} %get-tuple-element.97), channel_id=1, source_target_pairs={{0,12},{4,0},{8,4},{12,8},{1,13},{5,1},{9,5},{13,9},{2,14},{6,2},{... | collective-permute-start | bytes 24584 | tf_op jit(solution)/shard_map/ppermute | solution.py:34
  44.4 4.1 %collective-permute-done.8.refs_1_ = bf16[128,32]{1,0:T(8,128)(2,1)S(1)} collective-permute-done((bf16[128,32]{1,0:T(8,128)(2,1)S(1)}, bf16[128,32]{1,0:T(8,128)(2,1)S(1)}, u32[]{:S(2)}, u32[]{:S(2)}) %collective-permute-start.8) | collective-permute-done | bytes 8224 | tf_op jit(solution)/shard_map/ppermute | solution.py:34
  50.7 4.7 %job_tables.1 = (f32[32,4608]{1,0:T(8,128)S(1)}, f32[32,4608]{1,0:T(8,128)S(1)}) custom-call(s32[86]{0:T(128)S(1)} %concatenate.20.sc, bf16[512,4096]{1,0:T(8,128)(2,1)} %bitcast.30, bf16[512,512]{1,0:T(8,128)(2,1)S(1)} %bitcast.25, bf16[16,64]{1,0:T(8,128)(2,1)S(1)} %fusion.3.unfold, s32[1,64]{1,0:T(1,128)S(1)} %and_select_fusion.job_of, ...), custom_call_target="tpu_custom_call" | custom-call | flops 1000 | bytes 1000 | tf_op jit(solution)/shard_map/job_tables/pallas_call | solution.py:78
  55.4 5.3 %collective-permute-done.12.refs_0_.refs_8_ = bf16[512,256]{1,0:T(8,128)(2,1)S(1)} collective-permute-done((bf16[512,256]{1,0:T(8,128)(2,1)S(1)}, bf16[512,256]{1,0:T(8,128)(2,1)S(1)}, u32[]{:S(2)}, u32[]{:S(2)}) %collective-permute-start.12) | collective-permute-done | bytes 262176 | tf_op jit(solution)/shard_map/ppermute | solution.py:34
  60.8 4.8 %base_1_0.1.refs_5_.refs_3_ = bf16[512,256]{1,0:T(8,128)(2,1)S(1)} custom-call(s32[86]{0:T(128)S(1)} %concatenate.20.sc, bf16[512,4096]{1,0:T(8,128)(2,1)} %bitcast.31, bf16[1024,256]{1,0:T(8,128)(2,1)} %collective-permute-done.3.refs_0_.refs_4_, bf16[1024,256]{1,0:T(8,128)(2,1)S(1)} %collective-permute-done.14.refs_1_.refs_5_, ...), custom_call_target="tpu_custom_call" | custom-call | flops 1000 | bytes 1000 | tf_op jit(solution)/shard_map/base_1_0/pallas_call | solution.py:78
  68.0 7.0 %collective-permute-done.13.refs_2_.refs_8_ = bf16[512,256]{1,0:T(8,128)(2,1)S(1)} collective-permute-done((bf16[512,256]{1,0:T(8,128)(2,1)S(1)}, bf16[512,256]{1,0:T(8,128)(2,1)S(1)}, u32[]{:S(2)}, u32[]{:S(2)}) %collective-permute-start.13) | collective-permute-done | bytes 262176 | tf_op jit(solution)/shard_map/ppermute | solution.py:34
  74.9 1.5 %collective-permute-start.27 = (bf16[512,256]{1,0:T(8,128)(2,1)S(1)}, bf16[512,256]{1,0:T(8,128)(2,1)S(1)}, u32[]{:S(2)}, u32[]{:S(2)}) collective-permute-start(bf16[512,256]{1,0:T(8,128)(2,1)S(1)} %collective-permute-done.16.refs_4_.refs_9_), channel_id=1, source_target_pairs={{0,16},{16,0},{1,17},{17,1},{2,18},{18,2},{3,19},{19,3},{4,20},{20... | collective-permute-start | bytes 786440 | tf_op jit(solution)/shard_map/ppermute | solution.py:34
  77.1 4.9 %base_2_0.1 = (bf16[512,256]{1,0:T(8,128)(2,1)S(1)}, bf16[512,256]{1,0:T(8,128)(2,1)S(1)}, bf16[512,256]{1,0:T(8,128)(2,1)S(1)}) custom-call(s32[86]{0:T(128)S(1)} %concatenate.20.sc, bf16[512,4096]{1,0:T(8,128)(2,1)} %bitcast.32, bf16[1024,256]{1,0:T(8,128)(2,1)S(1)} %collective-permute-done.6.refs_0_.refs_6_, ...), custom_call_target="tpu_custom_call" | custom-call | flops 1000 | bytes 1000 | tf_op jit(solution)/shard_map/base_2_0/pallas_call | solution.py:78
  82.9 3.9 %base_3_0.1.refs_2_ = f32[512,256]{1,0:T(8,128)S(1)} custom-call(s32[86]{0:T(128)S(1)} %concatenate.20.sc, bf16[512,4096]{1,0:T(8,128)(2,1)} %bitcast.33, bf16[512,256]{1,0:T(8,128)(2,1)S(1)} %collective-permute-done.12.refs_0_.refs_8_, bf16[512,256]{1,0:T(8,128)(2,1)S(1)} %collective-permute-done.24.refs_1_.refs_10_, ...), custom_call_target="tpu_custom_call" | custom-call | flops 1000 | bytes 1000 | tf_op jit(solution)/shard_map/base_3_0/pallas_call | solution.py:78
  86.9 3.5 %collective-permute-done.28.refs_2_ = bf16[512,256]{1,0:T(8,128)(2,1)S(1)} collective-permute-done((bf16[512,256]{1,0:T(8,128)(2,1)S(1)}, bf16[512,256]{1,0:T(8,128)(2,1)S(1)}, u32[]{:S(2)}, u32[]{:S(2)}) %collective-permute-start.28) | collective-permute-done | bytes 262176 | tf_op jit(solution)/shard_map/ppermute | solution.py:34
  95.1 4.9 %collective-permute-done.22 = bf16[8,4608]{1,0:T(8,128)(2,1)S(1)} collective-permute-done((bf16[8,4608]{1,0:T(8,128)(2,1)S(1)}, bf16[8,4608]{1,0:T(8,128)(2,1)S(1)}, u32[]{:S(2)}, u32[]{:S(2)}) %collective-permute-start.22) | collective-permute-done | bytes 73760 | tf_op jit(solution)/shard_map/ppermute | solution.py:34
  100.0 3.3 %base_3_6.1 = (bf16[512,256]{1,0:T(8,128)(2,1)}, bf16[512,256]{1,0:T(8,128)(2,1)S(1)}, bf16[512,256]{1,0:T(8,128)(2,1)}) custom-call(s32[86]{0:T(128)S(1)} %concatenate.20.sc, bf16[512,4096]{1,0:T(8,128)(2,1)} %bitcast.34, bf16[512,256]{1,0:T(8,128)(2,1)S(1)} %collective-permute-done.27.refs_0_.refs_9_, ...), custom_call_target="tpu_custom_call" | custom-call | flops 1000 | bytes 1000 | tf_op jit(solution)/shard_map/base_3_6/pallas_call | solution.py:78
  111.8 6.3 %token_gradient_0.1.refs_12_ = bf16[512,4096]{1,0:T(8,128)(2,1)} custom-call(s32[86]{0:T(128)S(1)} %concatenate.20.sc, bf16[64,4608]{1,0:T(8,128)(2,1)S(1)} %pad_maximum_fusion.maps, bf16[512,32]{1,0:T(8,128)(2,1)S(1)} %get-tuple-element.92.sums, bf16[16,64]{1,0:T(8,128)(2,1)S(1)} %fusion.3.unfold, s32[1,64]{1,0:T(1,128)S(1)} %and_select_fusion.job_of, ...), custom_call_target="tpu_custom_call" | custom-call | flops 1000 | bytes 1000 | tf_op jit(solution)/shard_map/token_gradient_0/pallas_call | solution.py:78
  118.2 3.2 %layer.1 = (bf16[128,512]{1,0:T(8,128)(2,1)S(1)}, bf16[128,512]{1,0:T(8,128)(2,1)S(1)}, bf16[128,512]{1,0:T(8,128)(2,1)S(1)}, bf16[128,512]{1,0:T(8,128)(2,1)S(1)}) custom-call(s32[86]{0:T(128)S(1)} %concatenate.20.sc, bf16[512,32]{1,0:T(8,128)(2,1)S(1)} %get-tuple-element.92.sums, bf16[64,4608]{1,0:T(8,128)(2,1)S(1)} %pad_maximum_fusion.maps, ...), custom_call_target="tpu_custom_call" | custom-call | flops 1000 | bytes 1000 | tf_op jit(solution)/shard_map/layer/pallas_call | solution.py:78
  121.5 1.6 %collective-permute-start.33 = (bf16[128,512]{1,0:T(8,128)(2,1)S(1)}, bf16[128,512]{1,0:T(8,128)(2,1)S(1)}, u32[]{:S(2)}, u32[]{:S(2)}) collective-permute-start(bf16[128,512]{1,0:T(8,128)(2,1)S(1)} %get-tuple-element.157), channel_id=1, source_target_pairs={{0,8},{4,12},{8,0},{12,4},{1,9},{5,13},{9,1},{13,5},{2,10},{6,14},... | collective-permute-start | bytes 393224 | tf_op jit(solution)/shard_map/ppermute | solution.py:34
  123.1 2.6 %collective-permute-start.34 = (bf16[128,512]{1,0:T(8,128)(2,1)S(1)}, bf16[128,512]{1,0:T(8,128)(2,1)S(1)}, u32[]{:S(2)}, u32[]{:S(2)}) collective-permute-start(bf16[128,512]{1,0:T(8,128)(2,1)S(1)} %get-tuple-element.158), channel_id=1, source_target_pairs={{0,12},{4,0},{8,4},{12,8},{1,13},{5,1},{9,5},{13,9},{2,14},{6,2},{... | collective-permute-start | bytes 393224 | tf_op jit(solution)/shard_map/ppermute | solution.py:34
  127.5 6.2 %token_gradient_2.1 = bf16[512,4096]{1,0:T(8,128)(2,1)} custom-call(s32[86]{0:T(128)S(1)} %concatenate.20.sc, bf16[64,4608]{1,0:T(8,128)(2,1)S(1)} %pad_maximum_fusion.maps, bf16[512,32]{1,0:T(8,128)(2,1)S(1)} %get-tuple-element.92.sums, bf16[16,64]{1,0:T(8,128)(2,1)S(1)} %fusion.3.unfold, ...), custom_call_target="tpu_custom_call", output_to_operand_aliasing={{}: (17, {})} | custom-call | flops 1000 | bytes 1000 | tf_op jit(solution)/shard_map/token_gradient_2/pallas_call | solution.py:78
  (186 shorter events, 37.2 us)
Async XLA Ops:
  1.7 16.2 %collective-permute-start = (bf16[1,8,4608]{2,1,0:T(8,128)(2,1)S(1)}, bf16[1,8,4608]{2,1,0:T(8,128)(2,1)S(1)}, u32[]{:S(2)}, u32[]{:S(2)}) collective-permute-start(bf16[1,8,4608]{2,1,0:T(8,128)(2,1)S(1)} %dynamic-slice_bitcast_fusion), channel_id=1, source_target_pairs={{0,4},{4,8},{8,12},{12,0},{1,5},{5,9},{9,13},{13,1},{2,6},{6,10},{... | collective-permute-start | bytes 221192 | tf_op jit(solution)/shard_map/ppermute | solution.py:34
  4.7 13.1 %collective-permute-start.1 = (bf16[1,8,4608]{2,1,0:T(8,128)(2,1)S(1)}, bf16[1,8,4608]{2,1,0:T(8,128)(2,1)S(1)}, u32[]{:S(2)}, u32[]{:S(2)}) collective-permute-start(bf16[1,8,4608]{2,1,0:T(8,128)(2,1)S(1)} %dynamic-slice_bitcast_fusion), channel_id=1, source_target_pairs={{0,8},{4,12},{8,0},{12,4},{1,9},{5,13},{9,1},{13,5},{2,10},{6,14},... | collective-permute-start | bytes 221192 | tf_op jit(solution)/shard_map/ppermute | solution.py:34
  7.3 10.5 %collective-permute-start.2 = (bf16[1,8,4608]{2,1,0:T(8,128)(2,1)S(1)}, bf16[1,8,4608]{2,1,0:T(8,128)(2,1)S(1)}, u32[]{:S(2)}, u32[]{:S(2)}) collective-permute-start(bf16[1,8,4608]{2,1,0:T(8,128)(2,1)S(1)} %dynamic-slice_bitcast_fusion), channel_id=1, source_target_pairs={{0,12},{4,0},{8,4},{12,8},{1,13},{5,1},{9,5},{13,9},{2,14},{6,2},{... | collective-permute-start | bytes 221192 | tf_op jit(solution)/shard_map/ppermute | solution.py:34
  9.8 14.9 %collective-permute-start.3 = (bf16[1024,256]{1,0:T(8,128)(2,1)S(1)}, bf16[1024,256]{1,0:T(8,128)(2,1)}, u32[]{:S(2)}, u32[]{:S(2)}) collective-permute-start(bf16[1024,256]{1,0:T(8,128)(2,1)S(1)} %constant_dynamic-slice_fusion), channel_id=1, source_target_pairs={{0,4},{4,8},{8,12},{12,0},{1,5},{5,9},{9,13},{13,1},{2,6},{6,10},{... | collective-permute-start | bytes 1572872 | tf_op jit(solution)/shard_map/ppermute | solution.py:34
  10.5 32.3 %collective-permute-start.11 = (bf16[512,512]{1,0:T(8,128)(2,1)}, bf16[512,512]{1,0:T(8,128)(2,1)}, u32[]{:S(2)}, u32[]{:S(2)}) collective-permute-start(bf16[512,512]{1,0:T(8,128)(2,1)} %bitcast.23), channel_id=1, source_target_pairs={{0,2},{2,0},{1,3},{3,1},{4,6},{6,4},{5,7},{7,5},{8,10},{10,8},{9,1... | collective-permute-start | bytes 1572872 | tf_op jit(solution)/shard_map/ppermute | solution.py:34
  24.8 23.7 %collective-permute-start.6 = (bf16[1024,256]{1,0:T(8,128)(2,1)}, bf16[1024,256]{1,0:T(8,128)(2,1)S(1)}, u32[]{:S(2)}, u32[]{:S(2)}) collective-permute-start(bf16[1024,256]{1,0:T(8,128)(2,1)} %collective-permute-done.3.refs_0_.refs_4_), channel_id=1, source_target_pairs={{0,4},{4,8},{8,12},{12,0},{1,5},{5,9},{9,13},{13,1},{2,6},{6,10},{... | collective-permute-start | bytes 1572872 | tf_op jit(solution)/shard_map/ppermute | solution.py:34
  25.8 22.7 %collective-permute-start.7 = (bf16[1024,256]{1,0:T(8,128)(2,1)}, bf16[1024,256]{1,0:T(8,128)(2,1)S(1)}, u32[]{:S(2)}, u32[]{:S(2)}) collective-permute-start(bf16[1024,256]{1,0:T(8,128)(2,1)} %collective-permute-done.3.refs_0_.refs_4_), channel_id=1, source_target_pairs={{0,16},{16,0},{1,17},{17,1},{2,18},{18,2},{3,19},{19,3},{4,20},{20... | collective-permute-start | bytes 1572872 | tf_op jit(solution)/shard_map/ppermute | solution.py:34
  48.5 12.2 %collective-permute-start.14 = (bf16[1024,256]{1,0:T(8,128)(2,1)}, bf16[1024,256]{1,0:T(8,128)(2,1)S(1)}, u32[]{:S(2)}, u32[]{:S(2)}) collective-permute-start(bf16[1024,256]{1,0:T(8,128)(2,1)} %collective-permute-done.3.refs_0_.refs_4_), channel_id=1, source_target_pairs={{0,1},{1,0},{2,3},{3,2},{4,5},{5,4},{6,7},{7,6},{8,9},{9,8},{10,11... | collective-permute-start | bytes 1572872 | tf_op jit(solution)/shard_map/ppermute | solution.py:34
  48.6 12.1 %collective-permute-start.15 = (bf16[1024,256]{1,0:T(8,128)(2,1)S(1)}, bf16[1024,256]{1,0:T(8,128)(2,1)S(1)}, u32[]{:S(2)}, u32[]{:S(2)}) collective-permute-start(bf16[1024,256]{1,0:T(8,128)(2,1)S(1)} %collective-permute-done.7.refs_2_.refs_4_), channel_id=1, source_target_pairs={{0,1},{1,0},{2,3},{3,2},{4,5},{5,4},{6,7},{7,6},{8,9},{9,8},{10,11... | collective-permute-start | bytes 1572872 | tf_op jit(solution)/shard_map/ppermute | solution.py:34
  49.1 16.5 %collective-permute-start.17 = (bf16[1024,256]{1,0:T(8,128)(2,1)S(1)}, bf16[1024,256]{1,0:T(8,128)(2,1)S(1)}, u32[]{:S(2)}, u32[]{:S(2)}) collective-permute-start(bf16[1024,256]{1,0:T(8,128)(2,1)S(1)} %collective-permute-done.6.refs_0_.refs_6_), channel_id=1, source_target_pairs={{0,16},{16,0},{1,17},{17,1},{2,18},{18,2},{3,19},{19,3},{4,20},{20... | collective-permute-start | bytes 1572872 | tf_op jit(solution)/shard_map/ppermute | solution.py:34
  49.7 11.1 %collective-permute-start.12 = (bf16[512,256]{1,0:T(8,128)(2,1)S(1)}, bf16[512,256]{1,0:T(8,128)(2,1)S(1)}, u32[]{:S(2)}, u32[]{:S(2)}) collective-permute-start(bf16[512,256]{1,0:T(8,128)(2,1)S(1)} %get-tuple-element.175), channel_id=1, source_target_pairs={{0,4},{4,8},{8,12},{12,0},{1,5},{5,9},{9,13},{13,1},{2,6},{6,10},{... | collective-permute-start | bytes 786440 | tf_op jit(solution)/shard_map/ppermute | solution.py:34
  50.6 15.0 %collective-permute-start.16 = (bf16[512,256]{1,0:T(8,128)(2,1)S(1)}, bf16[512,256]{1,0:T(8,128)(2,1)S(1)}, u32[]{:S(2)}, u32[]{:S(2)}) collective-permute-start(bf16[512,256]{1,0:T(8,128)(2,1)S(1)} %get-tuple-element.174), channel_id=1, source_target_pairs={{0,4},{4,8},{8,12},{12,0},{1,5},{5,9},{9,13},{13,1},{2,6},{6,10},{... | collective-permute-start | bytes 786440 | tf_op jit(solution)/shard_map/ppermute | solution.py:34
  60.7 21.3 %collective-permute-start.20 = (f32[32,4608]{1,0:T(8,128)S(1)}, f32[32,4608]{1,0:T(8,128)S(1)}, u32[]{:S(2)}, u32[]{:S(2)}) collective-permute-start(f32[32,4608]{1,0:T(8,128)S(1)} %get-tuple-element.120), channel_id=1, source_target_pairs={{0,1},{1,0},{2,3},{3,2},{4,5},{5,4},{6,7},{7,6},{8,9},{9,8},{10,11... | collective-permute-start | bytes 1769480 | tf_op jit(solution)/shard_map/ppermute | solution.py:34
  65.6 10.8 %collective-permute-start.18 = (bf16[1024,256]{1,0:T(8,128)(2,1)S(1)}, bf16[1024,256]{1,0:T(8,128)(2,1)S(1)}, u32[]{:S(2)}, u32[]{:S(2)}) collective-permute-start(bf16[1024,256]{1,0:T(8,128)(2,1)S(1)} %collective-permute-done.6.refs_0_.refs_6_), channel_id=1, source_target_pairs={{0,1},{1,0},{2,3},{3,2},{4,5},{5,4},{6,7},{7,6},{8,9},{9,8},{10,11... | collective-permute-start | bytes 1572872 | tf_op jit(solution)/shard_map/ppermute | solution.py:34
  66.2 10.3 %collective-permute-start.19 = (bf16[1024,256]{1,0:T(8,128)(2,1)S(1)}, bf16[1024,256]{1,0:T(8,128)(2,1)S(1)}, u32[]{:S(2)}, u32[]{:S(2)}) collective-permute-start(bf16[1024,256]{1,0:T(8,128)(2,1)S(1)} %collective-permute-done.17.refs_2_.refs_6_), channel_id=1, source_target_pairs={{0,1},{1,0},{2,3},{3,2},{4,5},{5,4},{6,7},{7,6},{8,9},{9,8},{10,11... | collective-permute-start | bytes 1572872 | tf_op jit(solution)/shard_map/ppermute | solution.py:34
  66.3 8.7 %collective-permute-start.13 = (bf16[512,256]{1,0:T(8,128)(2,1)S(1)}, bf16[512,256]{1,0:T(8,128)(2,1)S(1)}, u32[]{:S(2)}, u32[]{:S(2)}) collective-permute-start(bf16[512,256]{1,0:T(8,128)(2,1)S(1)} %collective-permute-done.12.refs_0_.refs_8_), channel_id=1, source_target_pairs={{0,16},{16,0},{1,17},{17,1},{2,18},{18,2},{3,19},{19,3},{4,20},{20... | collective-permute-start | bytes 786440 | tf_op jit(solution)/shard_map/ppermute | solution.py:34
  67.8 15.0 %collective-permute-start.26 = (bf16[512,256]{1,0:T(8,128)(2,1)S(1)}, bf16[512,256]{1,0:T(8,128)(2,1)S(1)}, u32[]{:S(2)}, u32[]{:S(2)}) collective-permute-start(bf16[512,256]{1,0:T(8,128)(2,1)S(1)} %collective-permute-done.16.refs_4_.refs_9_), channel_id=1, source_target_pairs={{0,1},{1,0},{2,3},{3,2},{4,5},{5,4},{6,7},{7,6},{8,9},{9,8},{10,11... | collective-permute-start | bytes 786440 | tf_op jit(solution)/shard_map/ppermute | solution.py:34
  74.9 11.9 %collective-permute-start.27 = (bf16[512,256]{1,0:T(8,128)(2,1)S(1)}, bf16[512,256]{1,0:T(8,128)(2,1)S(1)}, u32[]{:S(2)}, u32[]{:S(2)}) collective-permute-start(bf16[512,256]{1,0:T(8,128)(2,1)S(1)} %collective-permute-done.16.refs_4_.refs_9_), channel_id=1, source_target_pairs={{0,16},{16,0},{1,17},{17,1},{2,18},{18,2},{3,19},{19,3},{4,20},{20... | collective-permute-start | bytes 786440 | tf_op jit(solution)/shard_map/ppermute | solution.py:34
  90.4 9.7 %collective-permute-start.29 = (bf16[512,256]{1,0:T(8,128)(2,1)S(1)}, bf16[512,256]{1,0:T(8,128)(2,1)S(1)}, u32[]{:S(2)}, u32[]{:S(2)}) collective-permute-start(bf16[512,256]{1,0:T(8,128)(2,1)S(1)} %collective-permute-done.27.refs_0_.refs_9_), channel_id=1, source_target_pairs={{0,1},{1,0},{2,3},{3,2},{4,5},{5,4},{6,7},{7,6},{8,9},{9,8},{10,11... | collective-permute-start | bytes 786440 | tf_op jit(solution)/shard_map/ppermute | solution.py:34
  104.1 14.1 %collective-permute-start.31 = (bf16[512,256]{1,0:T(8,128)(2,1)}, bf16[512,256]{1,0:T(8,128)(2,1)}, u32[]{:S(2)}, u32[]{:S(2)}) collective-permute-start(bf16[512,256]{1,0:T(8,128)(2,1)} %get-tuple-element.142), channel_id=1, source_target_pairs={{0,2},{2,0},{1,3},{3,1},{4,6},{6,4},{5,7},{7,5},{8,10},{10,8},{9,1... | collective-permute-start | bytes 786440 | tf_op jit(solution)/shard_map/ppermute | solution.py:34
  104.8 13.4 %collective-permute-start.30 = (f32[1,8,4608]{2,1,0:T(8,128)S(1)}, f32[1,8,4608]{2,1,0:T(8,128)}, u32[]{:S(2)}, u32[]{:S(2)}) collective-permute-start(f32[1,8,4608]{2,1,0:T(8,128)S(1)} %multiply_bitcast_fusion), channel_id=1, source_target_pairs={{0,1},{1,0},{2,3},{3,2},{4,5},{5,4},{6,7},{7,6},{8,9},{9,8},{10,11... | collective-permute-start | bytes 442376 | tf_op jit(solution)/shard_map/ppermute | solution.py:34
  121.5 12.9 %collective-permute-start.32 = (bf16[128,512]{1,0:T(8,128)(2,1)S(1)}, bf16[128,512]{1,0:T(8,128)(2,1)S(1)}, u32[]{:S(2)}, u32[]{:S(2)}) collective-permute-start(bf16[128,512]{1,0:T(8,128)(2,1)S(1)} %get-tuple-element.156), channel_id=1, source_target_pairs={{0,4},{4,8},{8,12},{12,0},{1,5},{5,9},{9,13},{13,1},{2,6},{6,10},{... | collective-permute-start | bytes 393224 | tf_op jit(solution)/shard_map/ppermute | solution.py:34
  121.5 12.9 %collective-permute-start.33 = (bf16[128,512]{1,0:T(8,128)(2,1)S(1)}, bf16[128,512]{1,0:T(8,128)(2,1)S(1)}, u32[]{:S(2)}, u32[]{:S(2)}) collective-permute-start(bf16[128,512]{1,0:T(8,128)(2,1)S(1)} %get-tuple-element.157), channel_id=1, source_target_pairs={{0,8},{4,12},{8,0},{12,4},{1,9},{5,13},{9,1},{13,5},{2,10},{6,14},... | collective-permute-start | bytes 393224 | tf_op jit(solution)/shard_map/ppermute | solution.py:34
  123.1 11.3 %collective-permute-start.34 = (bf16[128,512]{1,0:T(8,128)(2,1)S(1)}, bf16[128,512]{1,0:T(8,128)(2,1)S(1)}, u32[]{:S(2)}, u32[]{:S(2)}) collective-permute-start(bf16[128,512]{1,0:T(8,128)(2,1)S(1)} %get-tuple-element.158), channel_id=1, source_target_pairs={{0,12},{4,0},{8,4},{12,8},{1,13},{5,1},{9,5},{13,9},{2,14},{6,2},{... | collective-permute-start | bytes 393224 | tf_op jit(solution)/shard_map/ppermute | solution.py:34
  (50 other events, 393.4 us)

commit v7 on v6

--- a/solution.py
+++ b/solution.py
@@ -10,7 +10,7 @@
 adapter_scale = 2.0
 f32, bf16, i32 = jnp.float32, jnp.bfloat16, jnp.int32
 MIB = 1 << 20
-TOKEN_LIMIT = 50 * MIB
+TOKEN_LIMIT = 16 * MIB
 
 
 def block_facts(tokens_per_job, block_ids, block_rows):
@@ -58,14 +58,12 @@
         self.nq = np_ * ns
         self.fq = width // self.nq
         self.per_head = nd // nt
-        self.chunks = 2
-        self.fe = self.fq // self.chunks
         at, self.at = 0, {}
         for name, count in (
             ("out_pos", self.slots), ("in_pos", self.slots), ("out_fill", self.slots), ("in_fill", self.slots),
             ("out_rel", blocks), ("in_rel", blocks), ("out_valid", blocks), ("in_valid", blocks),
             ("quarter", self.nq), ("shard", nd), ("head", self.per_head),
-            ("step", self.nq * self.chunks), ("pick", self.per_head * nt),
+            ("pick", self.per_head * nt),
         ):
             self.at[name] = at
             at += count
@@ -106,6 +104,27 @@
 def widen(values, rel, unfold, job_of, z):
     wide = dot(values, unfold, ((1,), (0,)))
     return jnp.where(job_of == rel, wide, 0.0).astype(bf16)
+
+
+def keep_kernel(parts, sc, tokens, out, sems):
+    size = tokens.shape[0] // parts
+    copies = [
+        pltpu.make_async_copy(tokens.at[pl.ds(k * size, size), :], out.at[pl.ds(k * size, size), :], sems.at[k])
+        for k in range(parts)
+    ]
+    for copy in copies:
+        copy.start()
+    for copy in copies:
+        copy.wait()
+
+
+def keep(z, sc, tokens):
+    parts = 4
+    return call(
+        functools.partial(keep_kernel, parts), "keep_tokens", (1,), sc, (tokens,), [ANY],
+        jax.ShapeDtypeStruct(tokens.shape, tokens.dtype), ANY, 1000, 1000, 8 * MIB,
+        scratch=(pltpu.SemaphoreType.DMA((parts,)),),
+    )
 
 
 def products_kernel(z, n, sc, tokens, grad, maps, fold, job_of, out, held, sems):
@@ -207,22 +226,23 @@
     down_t[...] = dot(down[...], unit, ((0,), (0,))).astype(bf16)
     total = dot(down_t[...], grad[...], ((1,), (0,)))
     mine[:, z.width :] = total[:half]
-    theirs[:, z.width :] = total[half:]
+    theirs[:, z.width :] = total[half:].astype(bf16)
     for k in range(tiles):
         copies[k].wait()
         total = dot(back_t[...], held[k], ((1,), (0,)))
         mine[:, k * part : (k + 1) * part] = total[:half]
-        theirs[:, k * part : (k + 1) * part] = total[half:]
+        theirs[:, k * part : (k + 1) * part] = total[half:].astype(bf16)
 
 
 def tables_of(z, sc, tokens, grad, unfold, job_of, got):
     tiles = 4
     shape = jax.ShapeDtypeStruct((z.wide // z.ns, z.width + z.heads), f32)
+    sent = jax.ShapeDtypeStruct(shape.shape, bf16)
     return call(
         functools.partial(table_kernel, z, tiles), "job_tables", (1,), sc,
         (tokens, grad, unfold, job_of, *got),
         [ANY, whole(grad), whole(unfold), whole(job_of)] + [whole(x) for x in got],
-        (shape, shape), (whole(shape), whole(shape)), 1000, 1000, TOKEN_LIMIT,
+        (shape, sent), (whole(shape), whole(sent)), 1000, 1000, TOKEN_LIMIT,
         scratch=(pltpu.VMEM((z.rows, z.wide), bf16),) * 2
         + (pltpu.VMEM((z.wide, z.rows), bf16),) * 2
         + (pltpu.VMEM((tiles, z.rows, z.width // tiles), bf16), pltpu.SemaphoreType.DMA((tiles,))),
@@ -264,8 +284,8 @@
 
 
 def base_product(z, sc, tokens, pieces, d, base, first=0, begun=None, partial=False):
-    count, features = len(pieces), pieces[0].shape[0] if d else z.fq
-    at = z.at["quarter"] if features == z.fq else z.at["step"] + first
+    count, features = len(pieces), z.fq
+    at = z.at["quarter"] + first
     inputs, specs = [tokens, *pieces], [ANY] * (1 + count)
     if begun is not None:
         inputs.append(begun)
@@ -350,8 +370,7 @@
 
 def gradient_kernel(z, count, per, aliased, sc, maps, sums, unfold, job_of, *refs):
     grads, refs = refs[: z.nt], refs[z.nt :]
-    whole_pieces, refs = refs[: (z.nd - 1) * count], refs[(z.nd - 1) * count :]
-    last_pieces, refs = refs[: count * per], refs[count * per :]
+    pieces, refs = refs[: z.nd * count], refs[z.nd * count :]
     out, grad, back = refs[1:] if aliased else refs
     step = pl.program_id(0)
     m = z.per_head
@@ -364,14 +383,13 @@
             own = slice(b * z.halved, (b + 1) * z.halved)
             back[own, :] = widen(sums[own, z.rank :], z.get(sc, "in_rel", b), unfold[...], job_of[...], z)
 
-    for i in range(count * per):
-
-        @pl.when(step == i)
+    for k in range(count):
+
+        @pl.when(step // per == k)
         def _():
             total = adapter_scale * dot(back[...], maps[...], ((1,), (0,)))
             for d in range(z.nd):
-                piece = last_pieces[i] if d == z.nd - 1 else whole_pieces[d * count + i // per]
-                total = total + dot(grad[z.get(sc, "shard", d)], piece[...], ((1,), (1,)))
+                total = total + dot(grad[z.get(sc, "shard", d)], pieces[d * count + k][...], ((1,), (1,)))
             for b in range(z.blocks):
                 own = slice(b * z.halved, (b + 1) * z.halved)
                 mask = row_mask(z.get(sc, "in_valid", b), z, total.shape[1])
@@ -379,12 +397,13 @@
 
 
 def token_gradient_of(z, sc, grads, maps, sums, unfold, job_of, piece_list, quarters, before):
-    tile, per = z.fe, z.chunks
+    tile = min(512, z.fq)
+    per = z.fq // tile
     at = z.at["quarter"]
     first, count = quarters[0], len(quarters)
     block = lambda i, q: (0, q[at + first + i // per] * per + i % per)
     specs, flat = [], []
-    for d in range(z.nd - 1):
+    for d in range(z.nd):
         for k, r in enumerate(quarters):
             inner = lambda i, k=k: jnp.clip(i - k * per, 0, per - 1)
             if d == 0:
@@ -393,10 +412,6 @@
                 index = lambda i, q, inner=inner: (inner(i), 0)
             specs.append(pl.BlockSpec((tile, z.columns), index))
             flat.append(piece_list[d][r])
-    for r in quarters:
-        for c in range(per):
-            flat.append(piece_list[z.nd - 1][c * z.nq + r])
-            specs.append(whole(flat[-1]))
     inputs = [maps, sums, unfold, job_of, *grads, *flat]
     in_specs = [pl.BlockSpec((z.wide, tile), block), whole(sums), whole(unfold), whole(job_of)]
     in_specs += [whole(x) for x in grads] + specs
@@ -435,12 +450,14 @@
     own_tokens = tokens.reshape(rows, width)
     own_grad = cotangent.reshape(rows, heads)
 
+    own_tokens = keep(zz, jnp.zeros((1,), i32), own_tokens)
     quarters = jnp.stack([(p - a) % np_ * ns + (s - b) % ns for a in range(np_) for b in range(ns)]).astype(i32)
     moving = lax.dynamic_slice_in_dim(frozen_value_weight, (p * ns + s) * zz.fq, zz.fq, axis=0)
-    rounds = [None, shifted(moving, "dp", nd, 1)]
 
     maps = jnp.concatenate([adapter_down, adapter_up], axis=2).reshape(jobs_dev, ns, r2, width + heads)
     maps = lax.dynamic_index_in_dim(maps, s, 1, keepdims=False)
+    maps, moving = tie(maps, moving)
+    rounds = [None, shifted(moving, "dp", nd, 1)]
     maps, rounds[1] = tie(gather_shifts(maps, "dp", nd), rounds[1])
     maps = jnp.concatenate(maps, axis=0).reshape(zz.jobs * r2, -1)
     maps = jnp.concatenate(gather_shifts(maps, "sub", ns), axis=0)
@@ -486,11 +503,10 @@
     shard_at = (t - shard_of // m) % nt * m + shard_of % m
     arrivals = [arrival((t + g) % nt) for g in range(nt)]
     head_at = (z - arrivals[0]) % nd - t * m
-    steps = (quarters[None, :] * zz.chunks + jnp.arange(zz.chunks, dtype=i32)[:, None]).reshape(-1)
     sc = jnp.concatenate(
         [
             x.astype(i32)
-            for x in (out_pos, in_pos, out_fill, in_fill, out_rel, in_rel, out_valid, in_valid, quarters, shard_at, head_at, steps, *arrivals)
+            for x in (out_pos, in_pos, out_fill, in_fill, out_rel, in_rel, out_valid, in_valid, quarters, shard_at, head_at, *arrivals)
         ]
     )
     column = jnp.arange(zz.wide, dtype=i32)
@@ -507,31 +523,28 @@
     over[1] = gather_shifts(rounds[1], "parts", np_)
     for d in range(2, last):
         rounds.append(shifted(rounds[-1], "dp", nd, 1))
+    swapped = gather_shifts(over[1][0], "sub", ns)
+    maps, swapped = tie(maps, swapped)
     part = products(zz, sc, own_tokens, own_grad, maps, fold, job_of)
     parts = gather_shifts(part, "tensor", nt)
     late_tokens, _ = tie(own_tokens, part)
     base = [base_product(zz, sc, late_tokens, [frozen_value_weight] * zz.nq, 0, None)[0]]
-    base[0], parts = tie(base[0], parts)
+    base[0], parts, grads = tie(base[0], parts, grads)
     sums, *pays = sums_of(zz, sc, parts)
-
-    got = [shifted(pays[d], "dp", nd, d) for d in range(nd)]
-    rounds[last - 1], over[1], got, grads = tie(rounds[last - 1], over[1], got, grads)
-    ends = [
-        shifted(rounds[last - 1][c * zz.fe : (c + 1) * zz.fe], "dp", nd, 1) for c in range(zz.chunks)
-    ]
-    mine, theirs = tables_of(zz, sc, own_tokens, own_grad, unfold, job_of, got)
+    rounds[last - 1], over[1], sums = tie(rounds[last - 1], over[1], sums)
+
+    end = shifted(rounds[last - 1], "dp", nd, 1)
     for d in range(2, last):
         over[d] = gather_shifts(rounds[d], "parts", np_)
-    mine, theirs, ends[0] = tie(mine, theirs, ends[0])
-    end_over = [gather_shifts(ends[0], "parts", np_)]
-    theirs = shifted(theirs, "sub", ns, 1)
-    piece_list = [[frozen_value_weight] * zz.nq, spread_round(over[1])]
-    late_tokens, mine = tie(own_tokens, mine)
-    base.append(base_product(zz, sc, late_tokens, piece_list[1], 1, base)[0])
-    base[1], ends[1:], over[2:last] = tie(base[1], ends[1:], over[2:last])
-    end_over += [gather_shifts(x, "parts", np_) for x in ends[1:]]
-    piece_list += [spread_round(over[d]) for d in range(2, last)]
-    end_over[0], *piece_list[2:] = tie(end_over[0], *piece_list[2:])
+    piece_list = [[frozen_value_weight] * zz.nq, swapped + spread_round(over[1][1:])]
+    crossed = [gather_shifts(over[d][0], "sub", ns) for d in range(2, last)]
+    piece_list[1], crossed = tie(piece_list[1], crossed)
+    base.append(base_product(zz, sc, own_tokens, piece_list[1], 1, base)[0])
+    base[1], end, over[2:last], pays = tie(base[1], end, over[2:last], pays)
+
+    behind = gather_shifts(end, "parts", np_)
+    got = [shifted(pays[d], "dp", nd, d) for d in range(nd)]
+    piece_list += [crossed[d - 2] + spread_round(over[d][1:]) for d in range(2, last)]
 
     slots = []
 
@@ -542,38 +555,42 @@
 
     for d in range(2, last):
         finish(d, base_product(zz, sc, own_tokens, piece_list[d], d, base))
-    base[-1], mine, theirs = tie(base[-1], mine, theirs)
-
-    summed = (mine + theirs).reshape(nd, jobs_dev * r2, -1)
-    sending = [summed[d].astype(bf16) for d in range(nd)]
-    tables = [sending[0]] + [shifted(sending[d], "dp", nd, -d) for d in range(1, nd)]
-    ahead, behind = [x for y in end_over[:-1] for x in spread_round(y)], end_over[-1]
-    ahead += gather_shifts(behind[0], "sub", ns)
+    base[-1], got = tie(base[-1], got)
+    mine, theirs = tables_of(zz, sc, own_tokens, own_grad, unfold, job_of, got)
+    theirs = shifted(theirs, "sub", ns, 1)
+    ahead = gather_shifts(end, "sub", ns)
+    ahead, mine = tie(ahead, mine)
     begun = base_product(zz, sc, own_tokens, ahead, last, base, 0, None, True)[0]
     begun, behind, slots = tie(begun, behind, slots)
     tail = spread_round(behind[1:])
     piece_list.append(ahead + tail)
     finish(last, base_product(zz, sc, own_tokens, tail, last, base, len(ahead), begun))
-    base[-1], tables, grads = tie(base[-1], tables, grads)
+    base[-1], mine, theirs, grads = tie(base[-1], mine, theirs, grads)
+
+    summed = (mine + theirs).reshape(nd, jobs_dev * r2, -1)
+    sending = [summed[d].astype(bf16) for d in range(nd)]
+    tables = [sending[0]] + [shifted(sending[d], "dp", nd, -d) for d in range(1, nd)]
+
+    half = zz.nq // 2
+    gradient = token_gradient_of(zz, sc, grads, maps, sums, unfold, job_of, piece_list, list(range(half)), None)
+    given = [slots[j][d] for d in range(nt) for j in range(m)]
+    gradient, given = tie(gradient, given)
+    layer = layer_of(zz, sc, sums, maps, unfold, job_of, given)
+    layer, gradient, tables = tie(layer, gradient, tables)
+    landed = [shifted(layer[d], "dp", nd, d) for d in range(nd)]
     total = sum(x.astype(f32) for x in tables)
     counts = lax.dynamic_slice_in_dim(tokens_per_job, z * jobs_dev, jobs_dev).astype(f32)
     total = total.reshape(jobs_dev, r2, -1) * (adapter_scale / counts)[:, None, None]
     halves = gather_shifts(total, "sub", ns)
-    half = zz.nq // 2
-    gradient = token_gradient_of(zz, sc, grads, maps, sums, unfold, job_of, piece_list, list(range(half)), None)
-    given = [slots[j][d] for d in range(nt) for j in range(m)]
-    gradient, halves, *given = tie(gradient, halves, *given)
-    layer = layer_of(zz, sc, sums, maps, unfold, job_of, given)
-    *layer, gradient = tie(*layer, gradient)
+    gradient, halves = tie(gradient, halves)
     owned = jnp.concatenate(
         [sum(jnp.where((s - h) % ns == k, x, 0.0) for k, x in enumerate(halves)) for h in range(ns)], axis=1
     )
     grad_down, grad_up = owned[:, :, :width], owned[:, :, width:]
-    landed = [shifted(layer[d], "dp", nd, d) for d in range(nd)]
     gradient = token_gradient_of(
         zz, sc, grads, maps, sums, unfold, job_of, piece_list, list(range(half, zz.nq)), gradient
     )
-    gradient, grad_down, grad_up, *landed = tie(gradient, grad_down, grad_up, *landed)
+    gradient, grad_down, grad_up, landed = tie(gradient, grad_down, grad_up, landed)
     layer_output = place(zz, sc, landed)
     return (
         layer_output.reshape(1, blocks, halved, heads),

time: 137 us -> 126 us (0.920)
  waiting for transfers between devices: 34.1 us -> 19.5 us
  local copies, waits for them, and re-layouts: 10.5 us -> 17.2 us
  Pallas kernels: 49.7 us -> 45.6 us
  starting transfers between devices: 31.2 us -> 32.8 us
    ppermute x35 -> x31, waiting for transfers between devices: 34.1 us -> 19.5 us  [shifted(): lax.ppermute(values, axis, [(i, (i + step) % count) for i in range(count)])]
    unnamed x78 -> x42, local copies, waits for them, and re-layouts: 7.76 us -> 14.6 us
    pallas_call x12 -> x13, Pallas kernels: 49.7 us -> 45.6 us  [call(): pl.pallas_call(kernel, out_shape=out_shape, grid_spec=pltpu.PrefetchScala...]
    ppermute x35 -> x31, starting transfers between devices: 31.2 us -> 32.8 us  [shifted(): lax.ppermute(values, axis, [(i, (i + step) % count) for i in range(count)])]
  transfers between devices with their start and end apart: 35 -> 31, of which waited for: 9 -> 5; matrix products, arithmetic and copies ran while one was open for 7% -> 7% of each run, Pallas kernels for 31% -> 33%
where the time goes in v7:
time: 126 us
  Pallas kernels  45.6 us (36%)
  starting transfers between devices  32.8 us (26%)
  waiting for transfers between devices  19.5 us (15%)
  local copies, waits for them, and re-layouts  17.2 us (14%)
  other arithmetic  8.77 us (7%)
  between operations  1.8 us (1%)
    pallas_call x13, Pallas kernels, call(): pl.pallas_call(kernel, out_shape=out_shape, grid_spec=pltpu.PrefetchScala...  45.6 us
    ppermute x31, starting transfers between devices, shifted(): lax.ppermute(values, axis, [(i, (i + step) % count) for i in range(count)])  32.8 us
    ppermute x31, waiting for transfers between devices, shifted(): lax.ppermute(values, axis, [(i, (i + step) % count) for i in range(count)])  19.5 us
    unnamed x42, local copies, waits for them, and re-layouts  14.6 us
  transfers between devices with their start and end apart: 31, of which 5 were waited for; matrix products, arithmetic and copies ran while one was open for 7% of the time, Pallas kernels for 33%

profile of v7, /device:TPU:0, one launch (start us, length us, event | category | flops | bytes accessed | tf_op | source)
XLA Modules:
  0.0 125.6 jit_solution(14768730808715551901)
XLA Ops:
  2.7 3.1 %collective-permute-start = (bf16[1,8,4608]{2,1,0:T(8,128)(2,1)S(1)}, bf16[1,8,4608]{2,1,0:T(8,128)(2,1)S(1)}, u32[]{:S(2)}, u32[]{:S(2)}) collective-permute-start(bf16[1,8,4608]{2,1,0:T(8,128)(2,1)S(1)} %dynamic-slice_bitcast_fusion), channel_id=1, source_target_pairs={{0,4},{4,8},{8,12},{12,0},{1,5},{5,9},{9,13},{13,1},{2,6},{6,10},{... | collective-permute-start | bytes 221192 | tf_op jit(solution)/shard_map/ppermute | solution.py:34
  5.8 2.6 %collective-permute-start.1 = (bf16[1,8,4608]{2,1,0:T(8,128)(2,1)S(1)}, bf16[1,8,4608]{2,1,0:T(8,128)(2,1)S(1)}, u32[]{:S(2)}, u32[]{:S(2)}) collective-permute-start(bf16[1,8,4608]{2,1,0:T(8,128)(2,1)S(1)} %dynamic-slice_bitcast_fusion), channel_id=1, source_target_pairs={{0,8},{4,12},{8,0},{12,4},{1,9},{5,13},{9,1},{13,5},{2,10},{6,14},... | collective-permute-start | bytes 221192 | tf_op jit(solution)/shard_map/ppermute | solution.py:34
  17.3 2.2 %copy-done.4 = bf16[1,8,64,4096]{3,2,1,0:T(8,128)(2,1)S(1)} copy-done((bf16[1,8,64,4096]{3,2,1,0:T(8,128)(2,1)S(1)}, bf16[1,8,64,4096]{3,2,1,0:T(8,128)(2,1)}, u32[]{:S(2)}) %copy-start.4) | copy-done | bytes 4194328
  19.8 2.0 %copy-done = bf16[512,4096]{1,0:T(8,128)(2,1)} copy-done((bf16[512,4096]{1,0:T(8,128)(2,1)}, bf16[512,4096]{1,0:T(8,128)(2,1)S(1)}, u32[]{:S(2)}) %copy-start) | copy-done | bytes 4194328
  22.0 2.8 %collective-permute-done.2 = bf16[1,8,4608]{2,1,0:T(8,128)(2,1)S(1)} collective-permute-done((bf16[1,8,4608]{2,1,0:T(8,128)(2,1)S(1)}, bf16[1,8,4608]{2,1,0:T(8,128)(2,1)S(1)}, u32[]{:S(2)}, u32[]{:S(2)}) %collective-permute-start.2) | collective-permute-done | bytes 73760 | tf_op jit(solution)/shard_map/ppermute | solution.py:34
  25.5 1.8 %collective-permute-start.6 = (bf16[1024,256]{1,0:T(8,128)(2,1)}, bf16[1024,256]{1,0:T(8,128)(2,1)S(1)}, u32[]{:S(2)}, u32[]{:S(2)}) collective-permute-start(bf16[1024,256]{1,0:T(8,128)(2,1)} %collective-permute-done.3.refs_0_.refs_4_), channel_id=1, source_target_pairs={{0,4},{4,8},{8,12},{12,0},{1,5},{5,9},{9,13},{13,1},{2,6},{6,10},{... | collective-permute-start | bytes 1572872 | tf_op jit(solution)/shard_map/ppermute | solution.py:34
  28.9 2.2 %copy-done.1 = bf16[512,4096]{1,0:T(8,128)(2,1)S(1)} copy-done((bf16[512,4096]{1,0:T(8,128)(2,1)S(1)}, bf16[512,4096]{1,0:T(8,128)(2,1)}, u32[]{:S(2)}) %copy-start.1) | copy-done | bytes 4194328
  31.1 5.1 %adapter_products.1.refs_0_ = bf16[512,32]{1,0:T(8,128)(2,1)S(1)} custom-call(s32[78]{0:T(128)S(1)} %concatenate.15.sc, bf16[512,4096]{1,0:T(8,128)(2,1)S(1)} %copy-done.1, bf16[512,512]{1,0:T(8,128)(2,1)S(1)} %bitcast.24, bf16[64,4608]{1,0:T(8,128)(2,1)S(1)} %pad_maximum_fusion.maps, f32[64,16]{1,0:T(8,128)S(1)} %fusion.2.fold, ...), custom_call_target="tpu_custom_call" | custom-call | flops 1000 | bytes 1000 | tf_op jit(solution)/shard_map/adapter_products/pallas_call | solution.py:76
  36.3 1.6 %collective-permute-start.8 = (bf16[512,32]{1,0:T(8,128)(2,1)S(1)}, bf16[512,32]{1,0:T(8,128)(2,1)S(1)}, u32[]{:S(2)}, u32[]{:S(2)}) collective-permute-start(bf16[512,32]{1,0:T(8,128)(2,1)S(1)} %adapter_products.1.refs_0_), channel_id=1, source_target_pairs={{0,2},{2,0},{1,3},{3,1},{4,6},{6,4},{5,7},{7,5},{8,10},{10,8},{9,1... | collective-permute-start | bytes 98312 | tf_op jit(solution)/shard_map/ppermute | solution.py:34
  37.8 4.1 %base_0_0.1.refs_4_ = bf16[512,256]{1,0:T(8,128)(2,1)S(1)} custom-call(s32[78]{0:T(128)S(1)} %concatenate.15.sc, bf16[512,4096]{1,0:T(8,128)(2,1)S(1)} %copy-done.1, bf16[4096,256]{1,0:T(8,128)(2,1)S(1)} %copy-done.2, bf16[4096,256]{1,0:T(8,128)(2,1)S(1)} %copy-done.2, bf16[4096,256]{1,0:T(8,128)(2,1)S(1)} %copy-done.2, bf16[4096,256]{1,0:T(8,128)(2,1)S(1)} %copy-done.2), custom_call_target="tpu_custom_call" | custom-call | flops 1000 | bytes 1000 | tf_op jit(solution)/shard_map/base_0_0/pallas_call | solution.py:76
  45.4 4.4 %base_1_0.1.refs_5_.refs_3_ = bf16[512,256]{1,0:T(8,128)(2,1)S(1)} custom-call(s32[78]{0:T(128)S(1)} %concatenate.15.sc, bf16[512,4096]{1,0:T(8,128)(2,1)S(1)} %copy-done.1, bf16[1024,256]{1,0:T(8,128)(2,1)} %collective-permute-done.3.refs_0_.refs_4_, bf16[1024,256]{1,0:T(8,128)(2,1)S(1)} %collective-permute-done.5.refs_1_.refs_5_, ...), custom_call_target="tpu_custom_call" | custom-call | flops 1000 | bytes 1000 | tf_op jit(solution)/shard_map/base_1_0/pallas_call | solution.py:76
  49.9 9.1 %collective-permute-done.12.refs_0_.refs_8_ = bf16[1024,256]{1,0:T(8,128)(2,1)S(1)} collective-permute-done((bf16[1024,256]{1,0:T(8,128)(2,1)S(1)}, bf16[1024,256]{1,0:T(8,128)(2,1)S(1)}, u32[]{:S(2)}, u32[]{:S(2)}) %collective-permute-start.12) | collective-permute-done | bytes 524320 | tf_op jit(solution)/shard_map/ppermute | solution.py:34
  60.4 1.9 %collective-permute-start.17 = (bf16[128,32]{1,0:T(8,128)(2,1)S(1)}, bf16[128,32]{1,0:T(8,128)(2,1)S(1)}, u32[]{:S(2)}, u32[]{:S(2)}) collective-permute-start(bf16[128,32]{1,0:T(8,128)(2,1)S(1)} %get-tuple-element.126), channel_id=1, source_target_pairs={{0,8},{4,12},{8,0},{12,4},{1,9},{5,13},{9,1},{13,5},{2,10},{6,14},... | collective-permute-start | bytes 24584 | tf_op jit(solution)/shard_map/ppermute | solution.py:34
  62.3 1.6 %collective-permute-start.18 = (bf16[128,32]{1,0:T(8,128)(2,1)S(1)}, bf16[128,32]{1,0:T(8,128)(2,1)S(1)}, u32[]{:S(2)}, u32[]{:S(2)}) collective-permute-start(bf16[128,32]{1,0:T(8,128)(2,1)S(1)} %get-tuple-element.127), channel_id=1, source_target_pairs={{0,12},{4,0},{8,4},{12,8},{1,13},{5,1},{9,5},{13,9},{2,14},{6,2},{... | collective-permute-start | bytes 24584 | tf_op jit(solution)/shard_map/ppermute | solution.py:34
  63.9 4.2 %base_2_0.1 = (bf16[512,256]{1,0:T(8,128)(2,1)S(1)}, bf16[512,256]{1,0:T(8,128)(2,1)S(1)}, bf16[512,256]{1,0:T(8,128)(2,1)S(1)}) custom-call(s32[78]{0:T(128)S(1)} %concatenate.15.sc, bf16[512,4096]{1,0:T(8,128)(2,1)S(1)} %copy-done.1, bf16[1024,256]{1,0:T(8,128)(2,1)S(1)} %collective-permute-done.6.refs_0_.refs_6_, ...), custom_call_target="tpu_custom_call" | custom-call | flops 1000 | bytes 1000 | tf_op jit(solution)/shard_map/base_2_0/pallas_call | solution.py:76
  68.1 5.6 %job_tables.1 = (f32[32,4608]{1,0:T(8,128)S(1)}, bf16[32,4608]{1,0:T(8,128)(2,1)S(1)}) custom-call(s32[78]{0:T(128)S(1)} %concatenate.15.sc, bf16[512,4096]{1,0:T(8,128)(2,1)S(1)} %copy-done.1, bf16[512,512]{1,0:T(8,128)(2,1)S(1)} %bitcast.25, bf16[16,64]{1,0:T(8,128)(2,1)S(1)} %fusion.3.unfold, s32[1,64]{1,0:T(1,128)S(1)} %and_select_fusion.job_of, ...), custom_call_target="tpu_custom_call" | custom-call | flops 1000 | bytes 1000 | tf_op jit(solution)/shard_map/job_tables/pallas_call | solution.py:76
  75.2 1.9 %base_3_0.1.refs_2_ = f32[512,256]{1,0:T(8,128)S(1)} custom-call(s32[78]{0:T(128)S(1)} %concatenate.15.sc, bf16[512,4096]{1,0:T(8,128)(2,1)S(1)} %copy-done.1, bf16[1024,256]{1,0:T(8,128)(2,1)S(1)} %collective-permute-done.12.refs_0_.refs_8_, bf16[1024,256]{1,0:T(8,128)(2,1)S(1)} %collective-permute-done.14.refs_1_.refs_9_), custom_call_target="tpu_custom_call" | custom-call | flops 1000 | bytes 1000 | tf_op jit(solution)/shard_map/base_3_0/pallas_call | solution.py:76
  77.1 5.4 %collective-permute-done.21.refs_2_ = bf16[512,256]{1,0:T(8,128)(2,1)S(1)} collective-permute-done((bf16[512,256]{1,0:T(8,128)(2,1)S(1)}, bf16[512,256]{1,0:T(8,128)(2,1)S(1)}, u32[]{:S(2)}, u32[]{:S(2)}) %collective-permute-start.21) | collective-permute-done | bytes 262176 | tf_op jit(solution)/shard_map/ppermute | solution.py:34
  82.6 1.8 %collective-permute-done.22.refs_1_.refs_9_ = bf16[1024,256]{1,0:T(8,128)(2,1)S(1)} collective-permute-done((bf16[1024,256]{1,0:T(8,128)(2,1)S(1)}, bf16[1024,256]{1,0:T(8,128)(2,1)S(1)}, u32[]{:S(2)}, u32[]{:S(2)}) %collective-permute-start.22) | collective-permute-done | bytes 524320 | tf_op jit(solution)/shard_map/ppermute | solution.py:34
  84.4 3.2 %base_3_2.1 = (bf16[512,256]{1,0:T(8,128)(2,1)}, bf16[512,256]{1,0:T(8,128)(2,1)S(1)}, bf16[512,256]{1,0:T(8,128)(2,1)S(1)}) custom-call(s32[78]{0:T(128)S(1)} %concatenate.15.sc, bf16[512,4096]{1,0:T(8,128)(2,1)S(1)} %copy-done.1, bf16[1024,256]{1,0:T(8,128)(2,1)S(1)} %collective-permute-done.20.refs_0_.refs_8_, ...), custom_call_target="tpu_custom_call" | custom-call | flops 1000 | bytes 1000 | tf_op jit(solution)/shard_map/base_3_2/pallas_call | solution.py:76
  91.2 1.9 %collective-permute-start.26 = (bf16[8,4608]{1,0:T(8,128)(2,1)S(1)}, bf16[8,4608]{1,0:T(8,128)(2,1)S(1)}, u32[]{:S(2)}, u32[]{:S(2)}) collective-permute-start(bf16[8,4608]{1,0:T(8,128)(2,1)S(1)} %get-tuple-element.190), channel_id=1, source_target_pairs={{0,4},{4,8},{8,12},{12,0},{1,5},{5,9},{9,13},{13,1},{2,6},{6,10},{... | collective-permute-start | bytes 221192 | tf_op jit(solution)/shard_map/ppermute | solution.py:34
  94.4 6.3 %token_gradient_0.1.refs_10_ = bf16[512,4096]{1,0:T(8,128)(2,1)} custom-call(s32[78]{0:T(128)S(1)} %concatenate.15.sc, bf16[64,4608]{1,0:T(8,128)(2,1)S(1)} %pad_maximum_fusion.maps, bf16[512,32]{1,0:T(8,128)(2,1)S(1)} %get-tuple-element.104.sums, bf16[16,64]{1,0:T(8,128)(2,1)S(1)} %fusion.3.unfold, s32[1,64]{1,0:T(1,128)S(1)} %and_select_fusion.job_of, ...), custom_call_target="tpu_custom_call" | custom-call | flops 1000 | bytes 1000 | tf_op jit(solution)/shard_map/token_gradient_0/pallas_call | solution.py:76
  100.7 2.1 %layer.1 = (bf16[128,512]{1,0:T(8,128)(2,1)S(1)}, bf16[128,512]{1,0:T(8,128)(2,1)S(1)}, bf16[128,512]{1,0:T(8,128)(2,1)S(1)}, bf16[128,512]{1,0:T(8,128)(2,1)S(1)}) custom-call(s32[78]{0:T(128)S(1)} %concatenate.15.sc, bf16[512,32]{1,0:T(8,128)(2,1)S(1)} %get-tuple-element.104.sums, bf16[64,4608]{1,0:T(8,128)(2,1)S(1)} %pad_maximum_fusion.maps, ...), custom_call_target="tpu_custom_call" | custom-call | flops 1000 | bytes 1000 | tf_op jit(solution)/shard_map/layer/pallas_call | solution.py:76
  117.3 6.2 %token_gradient_2.1 = bf16[512,4096]{1,0:T(8,128)(2,1)} custom-call(s32[78]{0:T(128)S(1)} %concatenate.15.sc, bf16[64,4608]{1,0:T(8,128)(2,1)S(1)} %pad_maximum_fusion.maps, bf16[512,32]{1,0:T(8,128)(2,1)S(1)} %get-tuple-element.104.sums, bf16[16,64]{1,0:T(8,128)(2,1)S(1)} %fusion.3.unfold, ...), custom_call_target="tpu_custom_call", output_to_operand_aliasing={{}: (15, {})} | custom-call | flops 1000 | bytes 1000 | tf_op jit(solution)/shard_map/token_gradient_2/pallas_call | solution.py:76
  (138 shorter events, 40.8 us)
Async XLA Ops:
  2.7 19.3 %collective-permute-start = (bf16[1,8,4608]{2,1,0:T(8,128)(2,1)S(1)}, bf16[1,8,4608]{2,1,0:T(8,128)(2,1)S(1)}, u32[]{:S(2)}, u32[]{:S(2)}) collective-permute-start(bf16[1,8,4608]{2,1,0:T(8,128)(2,1)S(1)} %dynamic-slice_bitcast_fusion), channel_id=1, source_target_pairs={{0,4},{4,8},{8,12},{12,0},{1,5},{5,9},{9,13},{13,1},{2,6},{6,10},{... | collective-permute-start | bytes 221192 | tf_op jit(solution)/shard_map/ppermute | solution.py:34
  5.8 16.2 %collective-permute-start.1 = (bf16[1,8,4608]{2,1,0:T(8,128)(2,1)S(1)}, bf16[1,8,4608]{2,1,0:T(8,128)(2,1)S(1)}, u32[]{:S(2)}, u32[]{:S(2)}) collective-permute-start(bf16[1,8,4608]{2,1,0:T(8,128)(2,1)S(1)} %dynamic-slice_bitcast_fusion), channel_id=1, source_target_pairs={{0,8},{4,12},{8,0},{12,4},{1,9},{5,13},{9,1},{13,5},{2,10},{6,14},... | collective-permute-start | bytes 221192 | tf_op jit(solution)/shard_map/ppermute | solution.py:34
  8.3 16.4 %collective-permute-start.2 = (bf16[1,8,4608]{2,1,0:T(8,128)(2,1)S(1)}, bf16[1,8,4608]{2,1,0:T(8,128)(2,1)S(1)}, u32[]{:S(2)}, u32[]{:S(2)}) collective-permute-start(bf16[1,8,4608]{2,1,0:T(8,128)(2,1)S(1)} %dynamic-slice_bitcast_fusion), channel_id=1, source_target_pairs={{0,12},{4,0},{8,4},{12,8},{1,13},{5,1},{9,5},{13,9},{2,14},{6,2},{... | collective-permute-start | bytes 221192 | tf_op jit(solution)/shard_map/ppermute | solution.py:34
  9.7 15.1 %collective-permute-start.3 = (bf16[1024,256]{1,0:T(8,128)(2,1)S(1)}, bf16[1024,256]{1,0:T(8,128)(2,1)}, u32[]{:S(2)}, u32[]{:S(2)}) collective-permute-start(bf16[1024,256]{1,0:T(8,128)(2,1)S(1)} %constant_dynamic-slice_fusion), channel_id=1, source_target_pairs={{0,4},{4,8},{8,12},{12,0},{1,5},{5,9},{9,13},{13,1},{2,6},{6,10},{... | collective-permute-start | bytes 1572872 | tf_op jit(solution)/shard_map/ppermute | solution.py:34
  10.4 31.6 %collective-permute-start.9 = (bf16[512,512]{1,0:T(8,128)(2,1)}, bf16[512,512]{1,0:T(8,128)(2,1)}, u32[]{:S(2)}, u32[]{:S(2)}) collective-permute-start(bf16[512,512]{1,0:T(8,128)(2,1)} %bitcast.23), channel_id=1, source_target_pairs={{0,2},{2,0},{1,3},{3,1},{4,6},{6,4},{5,7},{7,5},{8,10},{10,8},{9,1... | collective-permute-start | bytes 1572872 | tf_op jit(solution)/shard_map/ppermute | solution.py:34
  25.5 17.1 %collective-permute-start.6 = (bf16[1024,256]{1,0:T(8,128)(2,1)}, bf16[1024,256]{1,0:T(8,128)(2,1)S(1)}, u32[]{:S(2)}, u32[]{:S(2)}) collective-permute-start(bf16[1024,256]{1,0:T(8,128)(2,1)} %collective-permute-done.3.refs_0_.refs_4_), channel_id=1, source_target_pairs={{0,4},{4,8},{8,12},{12,0},{1,5},{5,9},{9,13},{13,1},{2,6},{6,10},{... | collective-permute-start | bytes 1572872 | tf_op jit(solution)/shard_map/ppermute | solution.py:34
  27.3 15.3 %collective-permute-start.7 = (bf16[1024,256]{1,0:T(8,128)(2,1)}, bf16[1024,256]{1,0:T(8,128)(2,1)S(1)}, u32[]{:S(2)}, u32[]{:S(2)}) collective-permute-start(bf16[1024,256]{1,0:T(8,128)(2,1)} %collective-permute-done.3.refs_0_.refs_4_), channel_id=1, source_target_pairs={{0,16},{16,0},{1,17},{17,1},{2,18},{18,2},{3,19},{19,3},{4,20},{20... | collective-permute-start | bytes 1572872 | tf_op jit(solution)/shard_map/ppermute | solution.py:34
  36.3 5.7 %collective-permute-start.8 = (bf16[512,32]{1,0:T(8,128)(2,1)S(1)}, bf16[512,32]{1,0:T(8,128)(2,1)S(1)}, u32[]{:S(2)}, u32[]{:S(2)}) collective-permute-start(bf16[512,32]{1,0:T(8,128)(2,1)S(1)} %adapter_products.1.refs_0_), channel_id=1, source_target_pairs={{0,2},{2,0},{1,3},{3,1},{4,6},{6,4},{5,7},{7,5},{8,10},{10,8},{9,1... | collective-permute-start | bytes 98312 | tf_op jit(solution)/shard_map/ppermute | solution.py:34
  43.2 15.7 %collective-permute-start.12 = (bf16[1024,256]{1,0:T(8,128)(2,1)S(1)}, bf16[1024,256]{1,0:T(8,128)(2,1)S(1)}, u32[]{:S(2)}, u32[]{:S(2)}) collective-permute-start(bf16[1024,256]{1,0:T(8,128)(2,1)S(1)} %collective-permute-done.6.refs_0_.refs_6_), channel_id=1, source_target_pairs={{0,4},{4,8},{8,12},{12,0},{1,5},{5,9},{9,13},{13,1},{2,6},{6,10},{... | collective-permute-start | bytes 1572872 | tf_op jit(solution)/shard_map/ppermute | solution.py:34
  44.4 14.6 %collective-permute-start.13 = (bf16[1024,256]{1,0:T(8,128)(2,1)S(1)}, bf16[1024,256]{1,0:T(8,128)(2,1)S(1)}, u32[]{:S(2)}, u32[]{:S(2)}) collective-permute-start(bf16[1024,256]{1,0:T(8,128)(2,1)S(1)} %collective-permute-done.6.refs_0_.refs_6_), channel_id=1, source_target_pairs={{0,16},{16,0},{1,17},{17,1},{2,18},{18,2},{3,19},{19,3},{4,20},{20... | collective-permute-start | bytes 1572872 | tf_op jit(solution)/shard_map/ppermute | solution.py:34
  59.0 16.2 %collective-permute-start.14 = (bf16[1024,256]{1,0:T(8,128)(2,1)S(1)}, bf16[1024,256]{1,0:T(8,128)(2,1)S(1)}, u32[]{:S(2)}, u32[]{:S(2)}) collective-permute-start(bf16[1024,256]{1,0:T(8,128)(2,1)S(1)} %collective-permute-done.12.refs_0_.refs_8_), channel_id=1, source_target_pairs={{0,1},{1,0},{2,3},{3,2},{4,5},{5,4},{6,7},{7,6},{8,9},{9,8},{10,11... | collective-permute-start | bytes 1572872 | tf_op jit(solution)/shard_map/ppermute | solution.py:34
  59.5 17.6 %collective-permute-start.20 = (bf16[1024,256]{1,0:T(8,128)(2,1)S(1)}, bf16[1024,256]{1,0:T(8,128)(2,1)S(1)}, u32[]{:S(2)}, u32[]{:S(2)}) collective-permute-start(bf16[1024,256]{1,0:T(8,128)(2,1)S(1)} %collective-permute-done.12.refs_0_.refs_8_), channel_id=1, source_target_pairs={{0,16},{16,0},{1,17},{17,1},{2,18},{18,2},{3,19},{19,3},{4,20},{20... | collective-permute-start | bytes 1572872 | tf_op jit(solution)/shard_map/ppermute | solution.py:34
  60.0 8.1 %collective-permute-start.16 = (bf16[128,32]{1,0:T(8,128)(2,1)S(1)}, bf16[128,32]{1,0:T(8,128)(2,1)S(1)}, u32[]{:S(2)}, u32[]{:S(2)}) collective-permute-start(bf16[128,32]{1,0:T(8,128)(2,1)S(1)} %get-tuple-element.125), channel_id=1, source_target_pairs={{0,4},{4,8},{8,12},{12,0},{1,5},{5,9},{9,13},{13,1},{2,6},{6,10},{... | collective-permute-start | bytes 24584 | tf_op jit(solution)/shard_map/ppermute | solution.py:34
  60.4 7.7 %collective-permute-start.17 = (bf16[128,32]{1,0:T(8,128)(2,1)S(1)}, bf16[128,32]{1,0:T(8,128)(2,1)S(1)}, u32[]{:S(2)}, u32[]{:S(2)}) collective-permute-start(bf16[128,32]{1,0:T(8,128)(2,1)S(1)} %get-tuple-element.126), channel_id=1, source_target_pairs={{0,8},{4,12},{8,0},{12,4},{1,9},{5,13},{9,1},{13,5},{2,10},{6,14},... | collective-permute-start | bytes 24584 | tf_op jit(solution)/shard_map/ppermute | solution.py:34
  62.3 5.8 %collective-permute-start.18 = (bf16[128,32]{1,0:T(8,128)(2,1)S(1)}, bf16[128,32]{1,0:T(8,128)(2,1)S(1)}, u32[]{:S(2)}, u32[]{:S(2)}) collective-permute-start(bf16[128,32]{1,0:T(8,128)(2,1)S(1)} %get-tuple-element.127), channel_id=1, source_target_pairs={{0,12},{4,0},{8,4},{12,8},{1,13},{5,1},{9,5},{13,9},{2,14},{6,2},{... | collective-permute-start | bytes 24584 | tf_op jit(solution)/shard_map/ppermute | solution.py:34
  73.7 8.8 %collective-permute-start.19 = (bf16[32,4608]{1,0:T(8,128)(2,1)S(1)}, bf16[32,4608]{1,0:T(8,128)(2,1)S(1)}, u32[]{:S(2)}, u32[]{:S(2)}) collective-permute-start(bf16[32,4608]{1,0:T(8,128)(2,1)S(1)} %get-tuple-element.134), channel_id=1, source_target_pairs={{0,1},{1,0},{2,3},{3,2},{4,5},{5,4},{6,7},{7,6},{8,9},{9,8},{10,11... | collective-permute-start | bytes 884744 | tf_op jit(solution)/shard_map/ppermute | solution.py:34
  73.8 8.7 %collective-permute-start.21 = (bf16[512,256]{1,0:T(8,128)(2,1)S(1)}, bf16[512,256]{1,0:T(8,128)(2,1)S(1)}, u32[]{:S(2)}, u32[]{:S(2)}) collective-permute-start(bf16[512,256]{1,0:T(8,128)(2,1)S(1)} %get-tuple-element.142), channel_id=1, source_target_pairs={{0,2},{2,0},{1,3},{3,1},{4,6},{6,4},{5,7},{7,5},{8,10},{10,8},{9,1... | collective-permute-start | bytes 786440 | tf_op jit(solution)/shard_map/ppermute | solution.py:34
  87.7 13.1 %collective-permute-start.23 = (bf16[512,256]{1,0:T(8,128)(2,1)S(1)}, bf16[512,256]{1,0:T(8,128)(2,1)S(1)}, u32[]{:S(2)}, u32[]{:S(2)}) collective-permute-start(bf16[512,256]{1,0:T(8,128)(2,1)S(1)} %get-tuple-element.149), channel_id=1, source_target_pairs={{0,2},{2,0},{1,3},{3,1},{4,6},{6,4},{5,7},{7,5},{8,10},{10,8},{9,1... | collective-permute-start | bytes 786440 | tf_op jit(solution)/shard_map/ppermute | solution.py:34
  89.1 15.6 %collective-permute-start.24 = (bf16[8,4608]{1,0:T(8,128)(2,1)S(1)}, bf16[8,4608]{1,0:T(8,128)(2,1)S(1)}, u32[]{:S(2)}, u32[]{:S(2)}) collective-permute-start(bf16[8,4608]{1,0:T(8,128)(2,1)S(1)} %get-tuple-element.192), channel_id=1, source_target_pairs={{0,12},{4,0},{8,4},{12,8},{1,13},{5,1},{9,5},{13,9},{2,14},{6,2},{... | collective-permute-start | bytes 221192 | tf_op jit(solution)/shard_map/ppermute | solution.py:34
  90.6 14.1 %collective-permute-start.25 = (bf16[8,4608]{1,0:T(8,128)(2,1)S(1)}, bf16[8,4608]{1,0:T(8,128)(2,1)S(1)}, u32[]{:S(2)}, u32[]{:S(2)}) collective-permute-start(bf16[8,4608]{1,0:T(8,128)(2,1)S(1)} %get-tuple-element.191), channel_id=1, source_target_pairs={{0,8},{4,12},{8,0},{12,4},{1,9},{5,13},{9,1},{13,5},{2,10},{6,14},... | collective-permute-start | bytes 221192 | tf_op jit(solution)/shard_map/ppermute | solution.py:34
  91.2 13.6 %collective-permute-start.26 = (bf16[8,4608]{1,0:T(8,128)(2,1)S(1)}, bf16[8,4608]{1,0:T(8,128)(2,1)S(1)}, u32[]{:S(2)}, u32[]{:S(2)}) collective-permute-start(bf16[8,4608]{1,0:T(8,128)(2,1)S(1)} %get-tuple-element.190), channel_id=1, source_target_pairs={{0,4},{4,8},{8,12},{12,0},{1,5},{5,9},{9,13},{13,1},{2,6},{6,10},{... | collective-permute-start | bytes 221192 | tf_op jit(solution)/shard_map/ppermute | solution.py:34
  105.5 18.7 %collective-permute-start.28 = (bf16[128,512]{1,0:T(8,128)(2,1)}, bf16[128,512]{1,0:T(8,128)(2,1)S(1)}, u32[]{:S(2)}, u32[]{:S(2)}) collective-permute-start(bf16[128,512]{1,0:T(8,128)(2,1)} %copy-done.19), channel_id=1, source_target_pairs={{0,4},{4,8},{8,12},{12,0},{1,5},{5,9},{9,13},{13,1},{2,6},{6,10},{... | collective-permute-start | bytes 393224 | tf_op jit(solution)/shard_map/ppermute | solution.py:34
  106.4 17.8 %collective-permute-start.29 = (bf16[128,512]{1,0:T(8,128)(2,1)}, bf16[128,512]{1,0:T(8,128)(2,1)S(1)}, u32[]{:S(2)}, u32[]{:S(2)}) collective-permute-start(bf16[128,512]{1,0:T(8,128)(2,1)} %copy-done.18), channel_id=1, source_target_pairs={{0,8},{4,12},{8,0},{12,4},{1,9},{5,13},{9,1},{13,5},{2,10},{6,14},... | collective-permute-start | bytes 393224 | tf_op jit(solution)/shard_map/ppermute | solution.py:34
  107.9 16.3 %collective-permute-start.30 = (bf16[128,512]{1,0:T(8,128)(2,1)}, bf16[128,512]{1,0:T(8,128)(2,1)S(1)}, u32[]{:S(2)}, u32[]{:S(2)}) collective-permute-start(bf16[128,512]{1,0:T(8,128)(2,1)} %copy-done.17), channel_id=1, source_target_pairs={{0,12},{4,0},{8,4},{12,8},{1,13},{5,1},{9,5},{13,9},{2,14},{6,2},{... | collective-permute-start | bytes 393224 | tf_op jit(solution)/shard_map/ppermute | solution.py:34
  (28 other events, 101.7 us)

commit v8 on v7

--- a/solution.py
+++ b/solution.py
@@ -104,27 +104,6 @@
 def widen(values, rel, unfold, job_of, z):
     wide = dot(values, unfold, ((1,), (0,)))
     return jnp.where(job_of == rel, wide, 0.0).astype(bf16)
-
-
-def keep_kernel(parts, sc, tokens, out, sems):
-    size = tokens.shape[0] // parts
-    copies = [
-        pltpu.make_async_copy(tokens.at[pl.ds(k * size, size), :], out.at[pl.ds(k * size, size), :], sems.at[k])
-        for k in range(parts)
-    ]
-    for copy in copies:
-        copy.start()
-    for copy in copies:
-        copy.wait()
-
-
-def keep(z, sc, tokens):
-    parts = 4
-    return call(
-        functools.partial(keep_kernel, parts), "keep_tokens", (1,), sc, (tokens,), [ANY],
-        jax.ShapeDtypeStruct(tokens.shape, tokens.dtype), ANY, 1000, 1000, 8 * MIB,
-        scratch=(pltpu.SemaphoreType.DMA((parts,)),),
-    )
 
 
 def products_kernel(z, n, sc, tokens, grad, maps, fold, job_of, out, held, sems):
@@ -246,68 +225,6 @@
         scratch=(pltpu.VMEM((z.rows, z.wide), bf16),) * 2
         + (pltpu.VMEM((z.wide, z.rows), bf16),) * 2
         + (pltpu.VMEM((tiles, z.rows, z.width // tiles), bf16), pltpu.SemaphoreType.DMA((tiles,))),
-    )
-
-
-def base_kernel(z, d, count, started, partial, slot, others, at, features, sc, tokens, *refs):
-    pieces, refs = refs[:count], refs[count:]
-    if started:
-        begun, refs = refs[0], refs[1:]
-    earlier, refs = refs[: len(others)], refs[len(others) :]
-    outs, (held, parts, sems) = refs[:-3], refs[-3:]
-    copies = []
-    for k in range(count):
-        start = pl.multiple_of(sc[at + k] * features, features)
-        copies.append(pltpu.make_async_copy(tokens.at[:, pl.ds(start, features)], held.at[k], sems.at[0, k]))
-        source = pieces[k].at[pl.ds(start, features), :] if d == 0 else pieces[k]
-        copies.append(pltpu.make_async_copy(source, parts.at[k], sems.at[1, k]))
-    for copy in copies:
-        copy.start()
-    total = begun[...] if started else None
-    for k in range(count):
-        copies[2 * k].wait()
-        copies[2 * k + 1].wait()
-        part = dot(held[k], parts[k], ((1,), (0,)))
-        total = part if total is None else total + part
-    if partial:
-        outs[0][...] = total
-        return
-    done = total.astype(bf16)
-    outs[0][...] = done
-    for g in range(len(outs) - 1):
-        outs[1 + g][...] = done
-        for where, values in zip(others, earlier):
-
-            @pl.when(z.get(sc, "pick", g * z.per_head + slot) == where)
-            def _():
-                outs[1 + g][...] = values[...]
-
-
-def base_product(z, sc, tokens, pieces, d, base, first=0, begun=None, partial=False):
-    count, features = len(pieces), z.fq
-    at = z.at["quarter"] + first
-    inputs, specs = [tokens, *pieces], [ANY] * (1 + count)
-    if begun is not None:
-        inputs.append(begun)
-        specs.append(whole(begun))
-    slot = d - (z.nd - z.per_head)
-    others = []
-    shapes = [jax.ShapeDtypeStruct((z.rows, z.columns), f32 if partial else bf16)]
-    if slot >= 0 and not partial:
-        others = list(range(slot, d))
-        inputs += [base[k] for k in others]
-        specs += [whole(base[k]) for k in others]
-        shapes += [jax.ShapeDtypeStruct((z.rows, z.columns), bf16)] * z.nt
-    return call(
-        functools.partial(base_kernel, z, d, count, begun is not None, partial, slot, others, at, features),
-        "base_%d_%d" % (d, first), (1,), sc, inputs, specs,
-        tuple(shapes), tuple(whole(x) for x in shapes),
-        1000, 1000, TOKEN_LIMIT,
-        scratch=(
-            pltpu.VMEM((count, z.rows, features), bf16),
-            pltpu.VMEM((count, features, z.columns), bf16),
-            pltpu.SemaphoreType.DMA((2, count)),
-        ),
     )
 
 
@@ -424,7 +341,7 @@
         functools.partial(gradient_kernel, z, count, per, before is not None),
         "token_gradient_%d" % first, (count * per,), sc, inputs, in_specs,
         jax.ShapeDtypeStruct((z.rows, z.width), bf16), pl.BlockSpec((z.rows, tile), block),
-        1000, 1000, 32 * MIB,
+        1000, 1000, 14 * MIB,
         scratch=(pltpu.VMEM((z.nd, z.rows, z.columns), bf16), pltpu.VMEM((z.rows, z.wide), bf16)),
         alias=alias,
     )
@@ -450,7 +367,6 @@
     own_tokens = tokens.reshape(rows, width)
     own_grad = cotangent.reshape(rows, heads)
 
-    own_tokens = keep(zz, jnp.zeros((1,), i32), own_tokens)
     quarters = jnp.stack([(p - a) % np_ * ns + (s - b) % ns for a in range(np_) for b in range(ns)]).astype(i32)
     moving = lax.dynamic_slice_in_dim(frozen_value_weight, (p * ns + s) * zz.fq, zz.fq, axis=0)
 
@@ -458,7 +374,8 @@
     maps = lax.dynamic_index_in_dim(maps, s, 1, keepdims=False)
     maps, moving = tie(maps, moving)
     rounds = [None, shifted(moving, "dp", nd, 1)]
-    maps, rounds[1] = tie(gather_shifts(maps, "dp", nd), rounds[1])
+    token_quarters = [lax.dynamic_slice_in_dim(own_tokens, quarters[r] * zz.fq, zz.fq, 1) for r in range(zz.nq)]
+    maps, rounds[1], token_quarters = tie(gather_shifts(maps, "dp", nd), rounds[1], token_quarters)
     maps = jnp.concatenate(maps, axis=0).reshape(zz.jobs * r2, -1)
     maps = jnp.concatenate(gather_shifts(maps, "sub", ns), axis=0)
     grads = gather_shifts(own_grad, "tensor", nt)
@@ -515,6 +432,9 @@
     unfold = (jnp.arange(rank, dtype=i32)[:, None] == rank_of[None, :]).astype(bf16)
     fold = unfold.astype(f32).T
 
+    def product(pieces, first=0):
+        return sum(dot(token_quarters[first + r], x, ((1,), (0,))) for r, x in enumerate(pieces))
+
     def spread_round(over_parts):
         return [x for y in over_parts for x in gather_shifts(y, "sub", ns)]
 
@@ -527,8 +447,8 @@
     maps, swapped = tie(maps, swapped)
     part = products(zz, sc, own_tokens, own_grad, maps, fold, job_of)
     parts = gather_shifts(part, "tensor", nt)
-    late_tokens, _ = tie(own_tokens, part)
-    base = [base_product(zz, sc, late_tokens, [frozen_value_weight] * zz.nq, 0, None)[0]]
+    late_weight, _ = tie(frozen_value_weight, part)
+    base = [dot(own_tokens, late_weight, ((1,), (0,))).astype(bf16)]
     base[0], parts, grads = tie(base[0], parts, grads)
     sums, *pays = sums_of(zz, sc, parts)
     rounds[last - 1], over[1], sums = tie(rounds[last - 1], over[1], sums)
@@ -539,7 +459,7 @@
     piece_list = [[frozen_value_weight] * zz.nq, swapped + spread_round(over[1][1:])]
     crossed = [gather_shifts(over[d][0], "sub", ns) for d in range(2, last)]
     piece_list[1], crossed = tie(piece_list[1], crossed)
-    base.append(base_product(zz, sc, own_tokens, piece_list[1], 1, base)[0])
+    base.append(product(piece_list[1]).astype(bf16))
     base[1], end, over[2:last], pays = tie(base[1], end, over[2:last], pays)
 
     behind = gather_shifts(end, "parts", np_)
@@ -548,23 +468,30 @@
 
     slots = []
 
-    def finish(d, made):
-        base.append(made[0])
-        if len(made) > 1:
-            slots.append([made[1]] + [shifted(made[1 + g], "tensor", nt, g) for g in range(1, nt)])
+    def finish(values):
+        base.append(values.astype(bf16))
+        due = len(base) - 1 - (nd - m)
+        if due >= 0:
+            made = []
+            for g in range(nt):
+                picked = base[-1]
+                for k in range(due, len(base) - 1):
+                    picked = jnp.where(arrivals[g][due] == k, base[k], picked)
+                made.append(shifted(picked, "tensor", nt, g))
+            slots.append(made)
 
     for d in range(2, last):
-        finish(d, base_product(zz, sc, own_tokens, piece_list[d], d, base))
+        finish(product(piece_list[d]))
     base[-1], got = tie(base[-1], got)
     mine, theirs = tables_of(zz, sc, own_tokens, own_grad, unfold, job_of, got)
     theirs = shifted(theirs, "sub", ns, 1)
     ahead = gather_shifts(end, "sub", ns)
     ahead, mine = tie(ahead, mine)
-    begun = base_product(zz, sc, own_tokens, ahead, last, base, 0, None, True)[0]
+    begun = product(ahead)
     begun, behind, slots = tie(begun, behind, slots)
     tail = spread_round(behind[1:])
     piece_list.append(ahead + tail)
-    finish(last, base_product(zz, sc, own_tokens, tail, last, base, len(ahead), begun))
+    finish(begun + product(tail, len(ahead)))
     base[-1], mine, theirs, grads = tie(base[-1], mine, theirs, grads)
 
     summed = (mine + theirs).reshape(nd, jobs_dev * r2, -1)

time: 126 us -> 122 us (0.968)
  Pallas kernels: 45.6 us -> 27.4 us
  matrix products: 0 us -> 7.65 us
  between operations: 1.8 us -> 6.97 us
  starting transfers between devices: 32.8 us -> 36.1 us
  local copies, waits for them, and re-layouts: 17.2 us -> 14.9 us
    pallas_call x13 -> x7, Pallas kernels: 45.6 us -> 27.4 us  [call(): pl.pallas_call(kernel, out_shape=out_shape, grid_spec=pltpu.PrefetchScala...]
    dot_general x0 -> x13, matrix products: none -> 7.65 us  [dot(): lax.dot_general(a, b, (dims, ((), ())), precision=precision, preferred_el...]
    unnamed x42 -> x38, local copies, waits for them, and re-layouts: 14.6 us -> 8.23 us
    ppermute x31, starting transfers between devices: 32.8 us -> 36.1 us  [shifted(): lax.ppermute(values, axis, [(i, (i + step) % count) for i in range(count)])]
    dynamic_slice x0 -> x1, local copies, waits for them, and re-layouts: none -> 2.81 us  [body(): lax.dynamic_slice_in_dim(own_tokens, quarters[r] * zz.fq, zz.fq, 1)]
  transfers between devices with their start and end apart: 31 -> 31, of which waited for: 5 -> 6; matrix products, arithmetic and copies ran while one was open for 7% -> 17% of each run, Pallas kernels for 33% -> 21%
where the time goes in v8:
time: 122 us; the launch traced here: 121 us
  starting transfers between devices  36.1 us (30%)
  Pallas kernels  27.4 us (22%)
  waiting for transfers between devices  19 us (16%)
  local copies, waits for them, and re-layouts  14.9 us (12%)
  other arithmetic  9.02 us (7%)
  matrix products  7.65 us (6%)
  between operations  6.97 us (6%)
    ppermute x31, starting transfers between devices, shifted(): lax.ppermute(values, axis, [(i, (i + step) % count) for i in range(count)])  36.1 us
    pallas_call x7, Pallas kernels, call(): pl.pallas_call(kernel, out_shape=out_shape, grid_spec=pltpu.PrefetchScala...  27.4 us
    ppermute x31, waiting for transfers between devices, shifted(): lax.ppermute(values, axis, [(i, (i + step) % count) for i in range(count)])  19 us
    unnamed x38, local copies, waits for them, and re-layouts  8.23 us
    dot_general x13, matrix products, dot(): lax.dot_general(a, b, (dims, ((), ())), precision=precision, preferred_el...  7.65 us
    dynamic_slice x1, local copies, waits for them, and re-layouts, body(): lax.dynamic_slice_in_dim(own_tokens, quarters[r] * zz.fq, zz.fq, 1)  2.81 us
  transfers between devices with their start and end apart: 31, of which 6 were waited for; matrix products, arithmetic and copies ran while one was open for 17% of the time, Pallas kernels for 21%

profile of v8, /device:TPU:0, one launch (start us, length us, event | category | flops | bytes accessed | tf_op | source)
XLA Modules:
  0.0 121.0 jit_solution(4075194491102085170)
XLA Ops:
  2.7 3.1 %collective-permute-start = (bf16[1,8,4608]{2,1,0:T(8,128)(2,1)S(1)}, bf16[1,8,4608]{2,1,0:T(8,128)(2,1)S(1)}, u32[]{:S(2)}, u32[]{:S(2)}) collective-permute-start(bf16[1,8,4608]{2,1,0:T(8,128)(2,1)S(1)} %dynamic-slice_bitcast_fusion), channel_id=1, source_target_pairs={{0,4},{4,8},{8,12},{12,0},{1,5},{5,9},{9,13},{13,1},{2,6},{6,10},{... | collective-permute-start | bytes 221192 | tf_op jit(solution)/shard_map/ppermute | solution.py:34
  5.8 2.6 %collective-permute-start.1 = (bf16[1,8,4608]{2,1,0:T(8,128)(2,1)S(1)}, bf16[1,8,4608]{2,1,0:T(8,128)(2,1)S(1)}, u32[]{:S(2)}, u32[]{:S(2)}) collective-permute-start(bf16[1,8,4608]{2,1,0:T(8,128)(2,1)S(1)} %dynamic-slice_bitcast_fusion), channel_id=1, source_target_pairs={{0,8},{4,12},{8,0},{12,4},{1,9},{5,13},{9,1},{13,5},{2,10},{6,14},... | collective-permute-start | bytes 221192 | tf_op jit(solution)/shard_map/ppermute | solution.py:34
  10.4 1.5 %collective-permute-start.9 = (bf16[512,512]{1,0:T(8,128)(2,1)}, bf16[512,512]{1,0:T(8,128)(2,1)}, u32[]{:S(2)}, u32[]{:S(2)}) collective-permute-start(bf16[512,512]{1,0:T(8,128)(2,1)} %bitcast.63), channel_id=1, source_target_pairs={{0,2},{2,0},{1,3},{3,1},{4,6},{6,4},{5,7},{7,5},{8,10},{10,8},{9,1... | collective-permute-start | bytes 1572872 | tf_op jit(solution)/shard_map/ppermute | solution.py:34
  17.5 2.8 %constant_dynamic-slice_fusion = (bf16[512,1024]{1,0:T(8,128)(2,1)S(1)}, bf16[512,1024]{1,0:T(8,128)(2,1)S(1)}, bf16[512,1024]{1,0:T(8,128)(2,1)S(1)}, bf16[512,1024]{1,0:T(8,128)(2,1)S(1)}) fusion(bf16[512,4096]{1,0:T(8,128)(2,1)} %bitcast.59, s32[]{:T(128)S(6)} %select_n.388, s32[]{:T(128)S(6)} %select_n.387, s32[]{:T(128)S(6)} %select_n.386, s32[]{:T(128)S(6)} %select_n.385), kind=kLoop, calls=%fused_computation.79 | loop fusion | bytes 8388624 | tf_op jit(solution)/shard_map/dynamic_slice | solution.py:377
  20.3 4.4 %collective-permute-done.2 = bf16[1,8,4608]{2,1,0:T(8,128)(2,1)S(1)} collective-permute-done((bf16[1,8,4608]{2,1,0:T(8,128)(2,1)S(1)}, bf16[1,8,4608]{2,1,0:T(8,128)(2,1)S(1)}, u32[]{:S(2)}, u32[]{:S(2)}) %collective-permute-start.2) | collective-permute-done | bytes 73760 | tf_op jit(solution)/shard_map/ppermute | solution.py:34
  25.5 1.8 %collective-permute-start.6 = (bf16[1024,256]{1,0:T(8,128)(2,1)}, bf16[1024,256]{1,0:T(8,128)(2,1)S(1)}, u32[]{:S(2)}, u32[]{:S(2)}) collective-permute-start(bf16[1024,256]{1,0:T(8,128)(2,1)} %collective-permute-done.3.refs_4_), channel_id=1, source_target_pairs={{0,4},{4,8},{8,12},{12,0},{1,5},{5,9},{9,13},{13,1},{2,6},{6,10},{... | collective-permute-start | bytes 1572872 | tf_op jit(solution)/shard_map/ppermute | solution.py:34
  27.3 1.5 %collective-permute-start.7 = (bf16[1024,256]{1,0:T(8,128)(2,1)}, bf16[1024,256]{1,0:T(8,128)(2,1)S(1)}, u32[]{:S(2)}, u32[]{:S(2)}) collective-permute-start(bf16[1024,256]{1,0:T(8,128)(2,1)} %collective-permute-done.3.refs_4_), channel_id=1, source_target_pairs={{0,16},{16,0},{1,17},{17,1},{2,18},{18,2},{3,19},{19,3},{4,20},{20... | collective-permute-start | bytes 1572872 | tf_op jit(solution)/shard_map/ppermute | solution.py:34
  28.9 5.1 %adapter_products.1.refs_0_ = bf16[512,32]{1,0:T(8,128)(2,1)S(1)} custom-call(s32[78]{0:T(128)S(1)} %concatenate.15.sc, bf16[512,4096]{1,0:T(8,128)(2,1)S(1)} %bitcast.60, bf16[512,512]{1,0:T(8,128)(2,1)S(1)} %bitcast.64, bf16[64,4608]{1,0:T(8,128)(2,1)S(1)} %pad_maximum_fusion.maps, f32[64,16]{1,0:T(8,128)S(1)} %fusion.9.fold, ...), custom_call_target="tpu_custom_call" | custom-call | flops 1000 | bytes 1000 | tf_op jit(solution)/shard_map/adapter_products/pallas_call | solution.py:76
  34.1 1.6 %collective-permute-start.8 = (bf16[512,32]{1,0:T(8,128)(2,1)S(1)}, bf16[512,32]{1,0:T(8,128)(2,1)S(1)}, u32[]{:S(2)}, u32[]{:S(2)}) collective-permute-start(bf16[512,32]{1,0:T(8,128)(2,1)S(1)} %adapter_products.1.refs_0_), channel_id=1, source_target_pairs={{0,2},{2,0},{1,3},{3,1},{4,6},{6,4},{5,7},{7,5},{8,10},{10,8},{9,1... | collective-permute-start | bytes 98312 | tf_op jit(solution)/shard_map/ppermute | solution.py:34
  36.9 2.2 %collective-permute-done.8.refs_1_ = bf16[512,32]{1,0:T(8,128)(2,1)S(1)} collective-permute-done((bf16[512,32]{1,0:T(8,128)(2,1)S(1)}, bf16[512,32]{1,0:T(8,128)(2,1)S(1)}, u32[]{:S(2)}, u32[]{:S(2)}) %collective-permute-start.8) | collective-permute-done | bytes 32800 | tf_op jit(solution)/shard_map/ppermute | solution.py:34
  39.8 1.6 %collective-permute-done.6.refs_6_ = bf16[1024,256]{1,0:T(8,128)(2,1)S(1)} collective-permute-done((bf16[1024,256]{1,0:T(8,128)(2,1)}, bf16[1024,256]{1,0:T(8,128)(2,1)S(1)}, u32[]{:S(2)}, u32[]{:S(2)}) %collective-permute-start.6) | collective-permute-done | bytes 524320 | tf_op jit(solution)/shard_map/ppermute | solution.py:34
  46.5 1.5 %collective-permute-start.13 = (bf16[1024,256]{1,0:T(8,128)(2,1)S(1)}, bf16[1024,256]{1,0:T(8,128)(2,1)S(1)}, u32[]{:S(2)}, u32[]{:S(2)}) collective-permute-start(bf16[1024,256]{1,0:T(8,128)(2,1)S(1)} %collective-permute-done.6.refs_6_), channel_id=1, source_target_pairs={{0,16},{16,0},{1,17},{17,1},{2,18},{18,2},{3,19},{19,3},{4,20},{20... | collective-permute-start | bytes 1572872 | tf_op jit(solution)/shard_map/ppermute | solution.py:34
  49.4 1.5 %fusion.4 = bf16[512,256]{1,0:T(8,128)(2,1)S(1)} fusion(f32[512,256]{1,0:T(8,128)S(1)} %fusion.47, f32[512,256]{1,0:T(8,128)S(1)} %fusion.46, f32[512,256]{1,0:T(8,128)S(1)} %fusion.45, bf16[512,1024]{1,0:T(8,128)(2,1)S(1)} %get-tuple-element.104, bf16[1024,256]{1,0:T(8,128)(2,1)} %collective-permute-done.3.refs_4_), kind=kOutput, calls=%fused_computation.8 | convolution fusion | flops 268959744 | bytes 3407872 | tf_op jit(solution)/shard_map/dot_general | solution.py:42
  50.9 10.4 %collective-permute-done.12.refs_8_ = bf16[1024,256]{1,0:T(8,128)(2,1)S(1)} collective-permute-done((bf16[1024,256]{1,0:T(8,128)(2,1)S(1)}, bf16[1024,256]{1,0:T(8,128)(2,1)S(1)}, u32[]{:S(2)}, u32[]{:S(2)}) %collective-permute-start.12) | collective-permute-done | bytes 524320 | tf_op jit(solution)/shard_map/ppermute | solution.py:34
  61.3 1.7 %collective-permute-start.19 = (bf16[1024,256]{1,0:T(8,128)(2,1)S(1)}, bf16[1024,256]{1,0:T(8,128)(2,1)S(1)}, u32[]{:S(2)}, u32[]{:S(2)}) collective-permute-start(bf16[1024,256]{1,0:T(8,128)(2,1)S(1)} %collective-permute-done.12.refs_8_), channel_id=1, source_target_pairs={{0,16},{16,0},{1,17},{17,1},{2,18},{18,2},{3,19},{19,3},{4,20},{20... | collective-permute-start | bytes 1572872 | tf_op jit(solution)/shard_map/ppermute | solution.py:34
  63.2 2.3 %collective-permute-start.17 = (bf16[128,32]{1,0:T(8,128)(2,1)S(1)}, bf16[128,32]{1,0:T(8,128)(2,1)S(1)}, u32[]{:S(2)}, u32[]{:S(2)}) collective-permute-start(bf16[128,32]{1,0:T(8,128)(2,1)S(1)} %get-tuple-element.126), channel_id=1, source_target_pairs={{0,8},{4,12},{8,0},{12,4},{1,9},{5,13},{9,1},{13,5},{2,10},{6,14},... | collective-permute-start | bytes 24584 | tf_op jit(solution)/shard_map/ppermute | solution.py:34
  66.5 1.6 %collective-permute-start.18 = (bf16[128,32]{1,0:T(8,128)(2,1)S(1)}, bf16[128,32]{1,0:T(8,128)(2,1)S(1)}, u32[]{:S(2)}, u32[]{:S(2)}) collective-permute-start(bf16[128,32]{1,0:T(8,128)(2,1)S(1)} %get-tuple-element.127), channel_id=1, source_target_pairs={{0,12},{4,0},{8,4},{12,8},{1,13},{5,1},{9,5},{13,9},{2,14},{6,2},{... | collective-permute-start | bytes 24584 | tf_op jit(solution)/shard_map/ppermute | solution.py:34
  69.1 1.5 %collective-permute-start.20 = (bf16[512,256]{1,0:T(8,128)(2,1)S(1)}, bf16[512,256]{1,0:T(8,128)(2,1)S(1)}, u32[]{:S(2)}, u32[]{:S(2)}) collective-permute-start(bf16[512,256]{1,0:T(8,128)(2,1)S(1)} %get-tuple-element.192), channel_id=1, source_target_pairs={{0,2},{2,0},{1,3},{3,1},{4,6},{6,4},{5,7},{7,5},{8,10},{10,8},{9,1... | collective-permute-start | bytes 786440 | tf_op jit(solution)/shard_map/ppermute | solution.py:34
  70.6 5.6 %job_tables.1 = (f32[32,4608]{1,0:T(8,128)S(1)}, bf16[32,4608]{1,0:T(8,128)(2,1)S(1)}) custom-call(s32[78]{0:T(128)S(1)} %concatenate.15.sc, bf16[512,4096]{1,0:T(8,128)(2,1)S(1)} %bitcast.62, bf16[512,512]{1,0:T(8,128)(2,1)S(1)} %bitcast.65, bf16[16,64]{1,0:T(8,128)(2,1)S(1)} %fusion.10.unfold, s32[1,64]{1,0:T(1,128)S(1)} %and_select_fusion.job_of, ...), custom_call_target="tpu_custom_call" | custom-call | flops 1000 | bytes 1000 | tf_op jit(solution)/shard_map/job_tables/pallas_call | solution.py:76
  84.4 3.3 %collective-permute-start.24 = (bf16[8,4608]{1,0:T(8,128)(2,1)S(1)}, bf16[8,4608]{1,0:T(8,128)(2,1)S(1)}, u32[]{:S(2)}, u32[]{:S(2)}) collective-permute-start(bf16[8,4608]{1,0:T(8,128)(2,1)S(1)} %get-tuple-element.198), channel_id=1, source_target_pairs={{0,12},{4,0},{8,4},{12,8},{1,13},{5,1},{9,5},{13,9},{2,14},{6,2},{... | collective-permute-start | bytes 221192 | tf_op jit(solution)/shard_map/ppermute | solution.py:34
  88.4 6.3 %token_gradient_0.1.refs_10_ = bf16[512,4096]{1,0:T(8,128)(2,1)} custom-call(s32[78]{0:T(128)S(1)} %concatenate.15.sc, bf16[64,4608]{1,0:T(8,128)(2,1)S(1)} %pad_maximum_fusion.maps, bf16[512,32]{1,0:T(8,128)(2,1)S(1)} %get-tuple-element.103.sums, bf16[16,64]{1,0:T(8,128)(2,1)S(1)} %fusion.10.unfold, s32[1,64]{1,0:T(1,128)S(1)} %and_select_fusion.job_of, ...), custom_call_target="tpu_custom_call" | custom-call | flops 1000 | bytes 1000 | tf_op jit(solution)/shard_map/token_gradient_0/pallas_call | solution.py:76
  94.7 2.1 %layer.1 = (bf16[128,512]{1,0:T(8,128)(2,1)S(1)}, bf16[128,512]{1,0:T(8,128)(2,1)S(1)}, bf16[128,512]{1,0:T(8,128)(2,1)S(1)}, bf16[128,512]{1,0:T(8,128)(2,1)S(1)}) custom-call(s32[78]{0:T(128)S(1)} %concatenate.15.sc, bf16[512,32]{1,0:T(8,128)(2,1)S(1)} %get-tuple-element.103.sums, bf16[64,4608]{1,0:T(8,128)(2,1)S(1)} %pad_maximum_fusion.maps, ...), custom_call_target="tpu_custom_call" | custom-call | flops 1000 | bytes 1000 | tf_op jit(solution)/shard_map/layer/pallas_call | solution.py:76
  99.5 2.9 %collective-permute-start.28 = (bf16[128,512]{1,0:T(8,128)(2,1)}, bf16[128,512]{1,0:T(8,128)(2,1)S(1)}, u32[]{:S(2)}, u32[]{:S(2)}) collective-permute-start(bf16[128,512]{1,0:T(8,128)(2,1)} %copy-done.17), channel_id=1, source_target_pairs={{0,4},{4,8},{8,12},{12,0},{1,5},{5,9},{9,13},{13,1},{2,6},{6,10},{... | collective-permute-start | bytes 393224 | tf_op jit(solution)/shard_map/ppermute | solution.py:34
  112.7 6.2 %token_gradient_2.1 = bf16[512,4096]{1,0:T(8,128)(2,1)} custom-call(s32[78]{0:T(128)S(1)} %concatenate.15.sc, bf16[64,4608]{1,0:T(8,128)(2,1)S(1)} %pad_maximum_fusion.maps, bf16[512,32]{1,0:T(8,128)(2,1)S(1)} %get-tuple-element.103.sums, bf16[16,64]{1,0:T(8,128)(2,1)S(1)} %fusion.10.unfold, ...), custom_call_target="tpu_custom_call", output_to_operand_aliasing={{}: (15, {})} | custom-call | flops 1000 | bytes 1000 | tf_op jit(solution)/shard_map/token_gradient_2/pallas_call | solution.py:76
  (147 shorter events, 38.9 us)
Async XLA Ops:
  2.7 17.6 %collective-permute-start = (bf16[1,8,4608]{2,1,0:T(8,128)(2,1)S(1)}, bf16[1,8,4608]{2,1,0:T(8,128)(2,1)S(1)}, u32[]{:S(2)}, u32[]{:S(2)}) collective-permute-start(bf16[1,8,4608]{2,1,0:T(8,128)(2,1)S(1)} %dynamic-slice_bitcast_fusion), channel_id=1, source_target_pairs={{0,4},{4,8},{8,12},{12,0},{1,5},{5,9},{9,13},{13,1},{2,6},{6,10},{... | collective-permute-start | bytes 221192 | tf_op jit(solution)/shard_map/ppermute | solution.py:34
  5.8 14.6 %collective-permute-start.1 = (bf16[1,8,4608]{2,1,0:T(8,128)(2,1)S(1)}, bf16[1,8,4608]{2,1,0:T(8,128)(2,1)S(1)}, u32[]{:S(2)}, u32[]{:S(2)}) collective-permute-start(bf16[1,8,4608]{2,1,0:T(8,128)(2,1)S(1)} %dynamic-slice_bitcast_fusion), channel_id=1, source_target_pairs={{0,8},{4,12},{8,0},{12,4},{1,9},{5,13},{9,1},{13,5},{2,10},{6,14},... | collective-permute-start | bytes 221192 | tf_op jit(solution)/shard_map/ppermute | solution.py:34
  8.3 16.4 %collective-permute-start.2 = (bf16[1,8,4608]{2,1,0:T(8,128)(2,1)S(1)}, bf16[1,8,4608]{2,1,0:T(8,128)(2,1)S(1)}, u32[]{:S(2)}, u32[]{:S(2)}) collective-permute-start(bf16[1,8,4608]{2,1,0:T(8,128)(2,1)S(1)} %dynamic-slice_bitcast_fusion), channel_id=1, source_target_pairs={{0,12},{4,0},{8,4},{12,8},{1,13},{5,1},{9,5},{13,9},{2,14},{6,2},{... | collective-permute-start | bytes 221192 | tf_op jit(solution)/shard_map/ppermute | solution.py:34
  9.7 15.1 %collective-permute-start.3 = (bf16[1024,256]{1,0:T(8,128)(2,1)S(1)}, bf16[1024,256]{1,0:T(8,128)(2,1)}, u32[]{:S(2)}, u32[]{:S(2)}) collective-permute-start(bf16[1024,256]{1,0:T(8,128)(2,1)S(1)} %constant_dynamic-slice_fusion.4), channel_id=1, source_target_pairs={{0,4},{4,8},{8,12},{12,0},{1,5},{5,9},{9,13},{13,1},{2,6},{6,10},{... | collective-permute-start | bytes 1572872 | tf_op jit(solution)/shard_map/ppermute | solution.py:34
  10.4 26.6 %collective-permute-start.9 = (bf16[512,512]{1,0:T(8,128)(2,1)}, bf16[512,512]{1,0:T(8,128)(2,1)}, u32[]{:S(2)}, u32[]{:S(2)}) collective-permute-start(bf16[512,512]{1,0:T(8,128)(2,1)} %bitcast.63), channel_id=1, source_target_pairs={{0,2},{2,0},{1,3},{3,1},{4,6},{6,4},{5,7},{7,5},{8,10},{10,8},{9,1... | collective-permute-start | bytes 1572872 | tf_op jit(solution)/shard_map/ppermute | solution.py:34
  25.5 15.9 %collective-permute-start.6 = (bf16[1024,256]{1,0:T(8,128)(2,1)}, bf16[1024,256]{1,0:T(8,128)(2,1)S(1)}, u32[]{:S(2)}, u32[]{:S(2)}) collective-permute-start(bf16[1024,256]{1,0:T(8,128)(2,1)} %collective-permute-done.3.refs_4_), channel_id=1, source_target_pairs={{0,4},{4,8},{8,12},{12,0},{1,5},{5,9},{9,13},{13,1},{2,6},{6,10},{... | collective-permute-start | bytes 1572872 | tf_op jit(solution)/shard_map/ppermute | solution.py:34
  27.3 14.1 %collective-permute-start.7 = (bf16[1024,256]{1,0:T(8,128)(2,1)}, bf16[1024,256]{1,0:T(8,128)(2,1)S(1)}, u32[]{:S(2)}, u32[]{:S(2)}) collective-permute-start(bf16[1024,256]{1,0:T(8,128)(2,1)} %collective-permute-done.3.refs_4_), channel_id=1, source_target_pairs={{0,16},{16,0},{1,17},{17,1},{2,18},{18,2},{3,19},{19,3},{4,20},{20... | collective-permute-start | bytes 1572872 | tf_op jit(solution)/shard_map/ppermute | solution.py:34
  41.4 6.6 %collective-permute-start.10 = (bf16[1024,256]{1,0:T(8,128)(2,1)S(1)}, bf16[1024,256]{1,0:T(8,128)(2,1)S(1)}, u32[]{:S(2)}, u32[]{:S(2)}) collective-permute-start(bf16[1024,256]{1,0:T(8,128)(2,1)S(1)} %collective-permute-done.7.refs_4_), channel_id=1, source_target_pairs={{0,1},{1,0},{2,3},{3,2},{4,5},{5,4},{6,7},{7,6},{8,9},{9,8},{10,11... | collective-permute-start | bytes 1572872 | tf_op jit(solution)/shard_map/ppermute | solution.py:34
  41.4 6.6 %collective-permute-start.11 = (bf16[1024,256]{1,0:T(8,128)(2,1)S(1)}, bf16[1024,256]{1,0:T(8,128)(2,1)S(1)}, u32[]{:S(2)}, u32[]{:S(2)}) collective-permute-start(bf16[1024,256]{1,0:T(8,128)(2,1)S(1)} %collective-permute-done.6.refs_6_), channel_id=1, source_target_pairs={{0,1},{1,0},{2,3},{3,2},{4,5},{5,4},{6,7},{7,6},{8,9},{9,8},{10,11... | collective-permute-start | bytes 1572872 | tf_op jit(solution)/shard_map/ppermute | solution.py:34
  45.6 15.7 %collective-permute-start.12 = (bf16[1024,256]{1,0:T(8,128)(2,1)S(1)}, bf16[1024,256]{1,0:T(8,128)(2,1)S(1)}, u32[]{:S(2)}, u32[]{:S(2)}) collective-permute-start(bf16[1024,256]{1,0:T(8,128)(2,1)S(1)} %collective-permute-done.6.refs_6_), channel_id=1, source_target_pairs={{0,4},{4,8},{8,12},{12,0},{1,5},{5,9},{9,13},{13,1},{2,6},{6,10},{... | collective-permute-start | bytes 1572872 | tf_op jit(solution)/shard_map/ppermute | solution.py:34
  46.5 14.8 %collective-permute-start.13 = (bf16[1024,256]{1,0:T(8,128)(2,1)S(1)}, bf16[1024,256]{1,0:T(8,128)(2,1)S(1)}, u32[]{:S(2)}, u32[]{:S(2)}) collective-permute-start(bf16[1024,256]{1,0:T(8,128)(2,1)S(1)} %collective-permute-done.6.refs_6_), channel_id=1, source_target_pairs={{0,16},{16,0},{1,17},{17,1},{2,18},{18,2},{3,19},{19,3},{4,20},{20... | collective-permute-start | bytes 1572872 | tf_op jit(solution)/shard_map/ppermute | solution.py:34
  61.3 14.9 %collective-permute-start.14 = (bf16[1024,256]{1,0:T(8,128)(2,1)S(1)}, bf16[1024,256]{1,0:T(8,128)(2,1)S(1)}, u32[]{:S(2)}, u32[]{:S(2)}) collective-permute-start(bf16[1024,256]{1,0:T(8,128)(2,1)S(1)} %collective-permute-done.12.refs_8_), channel_id=1, source_target_pairs={{0,1},{1,0},{2,3},{3,2},{4,5},{5,4},{6,7},{7,6},{8,9},{9,8},{10,11... | collective-permute-start | bytes 1572872 | tf_op jit(solution)/shard_map/ppermute | solution.py:34
  61.3 15.8 %collective-permute-start.19 = (bf16[1024,256]{1,0:T(8,128)(2,1)S(1)}, bf16[1024,256]{1,0:T(8,128)(2,1)S(1)}, u32[]{:S(2)}, u32[]{:S(2)}) collective-permute-start(bf16[1024,256]{1,0:T(8,128)(2,1)S(1)} %collective-permute-done.12.refs_8_), channel_id=1, source_target_pairs={{0,16},{16,0},{1,17},{17,1},{2,18},{18,2},{3,19},{19,3},{4,20},{20... | collective-permute-start | bytes 1572872 | tf_op jit(solution)/shard_map/ppermute | solution.py:34
  63.2 5.9 %collective-permute-start.16 = (bf16[128,32]{1,0:T(8,128)(2,1)S(1)}, bf16[128,32]{1,0:T(8,128)(2,1)S(1)}, u32[]{:S(2)}, u32[]{:S(2)}) collective-permute-start(bf16[128,32]{1,0:T(8,128)(2,1)S(1)} %get-tuple-element.125), channel_id=1, source_target_pairs={{0,4},{4,8},{8,12},{12,0},{1,5},{5,9},{9,13},{13,1},{2,6},{6,10},{... | collective-permute-start | bytes 24584 | tf_op jit(solution)/shard_map/ppermute | solution.py:34
  63.2 7.4 %collective-permute-start.17 = (bf16[128,32]{1,0:T(8,128)(2,1)S(1)}, bf16[128,32]{1,0:T(8,128)(2,1)S(1)}, u32[]{:S(2)}, u32[]{:S(2)}) collective-permute-start(bf16[128,32]{1,0:T(8,128)(2,1)S(1)} %get-tuple-element.126), channel_id=1, source_target_pairs={{0,8},{4,12},{8,0},{12,4},{1,9},{5,13},{9,1},{13,5},{2,10},{6,14},... | collective-permute-start | bytes 24584 | tf_op jit(solution)/shard_map/ppermute | solution.py:34
  69.1 8.0 %collective-permute-start.20 = (bf16[512,256]{1,0:T(8,128)(2,1)S(1)}, bf16[512,256]{1,0:T(8,128)(2,1)S(1)}, u32[]{:S(2)}, u32[]{:S(2)}) collective-permute-start(bf16[512,256]{1,0:T(8,128)(2,1)S(1)} %get-tuple-element.192), channel_id=1, source_target_pairs={{0,2},{2,0},{1,3},{3,1},{4,6},{6,4},{5,7},{7,5},{8,10},{10,8},{9,1... | collective-permute-start | bytes 786440 | tf_op jit(solution)/shard_map/ppermute | solution.py:34
  82.9 11.8 %collective-permute-start.23 = (bf16[512,256]{1,0:T(8,128)(2,1)S(1)}, bf16[512,256]{1,0:T(8,128)(2,1)S(1)}, u32[]{:S(2)}, u32[]{:S(2)}) collective-permute-start(bf16[512,256]{1,0:T(8,128)(2,1)S(1)} %get-tuple-element.186), channel_id=1, source_target_pairs={{0,2},{2,0},{1,3},{3,1},{4,6},{6,4},{5,7},{7,5},{8,10},{10,8},{9,1... | collective-permute-start | bytes 786440 | tf_op jit(solution)/shard_map/ppermute | solution.py:34
  84.4 14.4 %collective-permute-start.24 = (bf16[8,4608]{1,0:T(8,128)(2,1)S(1)}, bf16[8,4608]{1,0:T(8,128)(2,1)S(1)}, u32[]{:S(2)}, u32[]{:S(2)}) collective-permute-start(bf16[8,4608]{1,0:T(8,128)(2,1)S(1)} %get-tuple-element.198), channel_id=1, source_target_pairs={{0,12},{4,0},{8,4},{12,8},{1,13},{5,1},{9,5},{13,9},{2,14},{6,2},{... | collective-permute-start | bytes 221192 | tf_op jit(solution)/shard_map/ppermute | solution.py:34
  87.7 11.0 %collective-permute-start.25 = (bf16[8,4608]{1,0:T(8,128)(2,1)S(1)}, bf16[8,4608]{1,0:T(8,128)(2,1)S(1)}, u32[]{:S(2)}, u32[]{:S(2)}) collective-permute-start(bf16[8,4608]{1,0:T(8,128)(2,1)S(1)} %get-tuple-element.197), channel_id=1, source_target_pairs={{0,8},{4,12},{8,0},{12,4},{1,9},{5,13},{9,1},{13,5},{2,10},{6,14},... | collective-permute-start | bytes 221192 | tf_op jit(solution)/shard_map/ppermute | solution.py:34
  87.9 10.8 %collective-permute-start.26 = (bf16[8,4608]{1,0:T(8,128)(2,1)S(1)}, bf16[8,4608]{1,0:T(8,128)(2,1)S(1)}, u32[]{:S(2)}, u32[]{:S(2)}) collective-permute-start(bf16[8,4608]{1,0:T(8,128)(2,1)S(1)} %get-tuple-element.196), channel_id=1, source_target_pairs={{0,4},{4,8},{8,12},{12,0},{1,5},{5,9},{9,13},{13,1},{2,6},{6,10},{... | collective-permute-start | bytes 221192 | tf_op jit(solution)/shard_map/ppermute | solution.py:34
  99.4 5.2 %collective-permute-start.27 = (f32[1,8,4608]{2,1,0:T(8,128)}, f32[1,8,4608]{2,1,0:T(8,128)}, u32[]{:S(2)}, u32[]{:S(2)}) collective-permute-start(f32[1,8,4608]{2,1,0:T(8,128)} %multiply_bitcast_fusion), channel_id=1, source_target_pairs={{0,1},{1,0},{2,3},{3,2},{4,5},{5,4},{6,7},{7,6},{8,9},{9,8},{10,11... | collective-permute-start | bytes 442376 | tf_op jit(solution)/shard_map/ppermute | solution.py:34
  99.5 20.1 %collective-permute-start.28 = (bf16[128,512]{1,0:T(8,128)(2,1)}, bf16[128,512]{1,0:T(8,128)(2,1)S(1)}, u32[]{:S(2)}, u32[]{:S(2)}) collective-permute-start(bf16[128,512]{1,0:T(8,128)(2,1)} %copy-done.17), channel_id=1, source_target_pairs={{0,4},{4,8},{8,12},{12,0},{1,5},{5,9},{9,13},{13,1},{2,6},{6,10},{... | collective-permute-start | bytes 393224 | tf_op jit(solution)/shard_map/ppermute | solution.py:34
  102.3 17.2 %collective-permute-start.29 = (bf16[128,512]{1,0:T(8,128)(2,1)}, bf16[128,512]{1,0:T(8,128)(2,1)S(1)}, u32[]{:S(2)}, u32[]{:S(2)}) collective-permute-start(bf16[128,512]{1,0:T(8,128)(2,1)} %copy-done.16), channel_id=1, source_target_pairs={{0,8},{4,12},{8,0},{12,4},{1,9},{5,13},{9,1},{13,5},{2,10},{6,14},... | collective-permute-start | bytes 393224 | tf_op jit(solution)/shard_map/ppermute | solution.py:34
  103.4 16.1 %collective-permute-start.30 = (bf16[128,512]{1,0:T(8,128)(2,1)}, bf16[128,512]{1,0:T(8,128)(2,1)S(1)}, u32[]{:S(2)}, u32[]{:S(2)}) collective-permute-start(bf16[128,512]{1,0:T(8,128)(2,1)} %copy-done.15), channel_id=1, source_target_pairs={{0,12},{4,0},{8,4},{12,8},{1,13},{5,1},{9,5},{13,9},{2,14},{6,2},{... | collective-permute-start | bytes 393224 | tf_op jit(solution)/shard_map/ppermute | solution.py:34
  (26 other events, 87.9 us)

commit v9 on v8

--- a/solution.py
+++ b/solution.py
@@ -81,7 +81,7 @@
         ),
         input_output_aliases=alias or {},
         compiler_params=pltpu.CompilerParams(vmem_limit_bytes=limit),
-        cost_estimate=pl.CostEstimate(flops=1000, bytes_accessed=1000, transcendentals=0),
+        cost_estimate=pl.CostEstimate(flops=flops, bytes_accessed=moved, transcendentals=0),
         name=name,
     )(scalars, *inputs)
 
@@ -168,7 +168,7 @@
     shapes += [jax.ShapeDtypeStruct((z.cap * z.halved, 2 * z.rank), bf16)] * z.nd
     return call(
         functools.partial(sums_kernel, z), "adapter_sums", (1,), sc, parts, [whole(x) for x in parts],
-        tuple(shapes), tuple(whole(x) for x in shapes), 1000, 8 * z.rows * z.rank, 8 * MIB,
+        tuple(shapes), tuple(whole(x) for x in shapes), 1000, 1000, 8 * MIB,
     )
 
 
@@ -261,7 +261,7 @@
         [whole(sums), pl.BlockSpec((z.wide, z.heads), lambda i, _: (0, at)), whole(unfold), whole(job_of)]
         + [whole(x) for x in given],
         tuple(shapes), tuple(whole(x) for x in shapes),
-        2 * z.rows * z.wide * z.heads, 6 * z.rows * z.heads, 16 * MIB,
+        2 * z.rows * z.wide * z.heads, 6 * z.rows * z.heads, 12 * MIB,
         scratch=(pltpu.VMEM((z.rows, z.heads), f32),),
     )
 
@@ -341,7 +341,8 @@
         functools.partial(gradient_kernel, z, count, per, before is not None),
         "token_gradient_%d" % first, (count * per,), sc, inputs, in_specs,
         jax.ShapeDtypeStruct((z.rows, z.width), bf16), pl.BlockSpec((z.rows, tile), block),
-        1000, 1000, 14 * MIB,
+        1000 if alias is None else 2 * z.rows * count * z.fq * (z.nd * z.columns + z.wide),
+        1000 if alias is None else 2 * count * z.fq * (z.rows + z.nd * z.columns), 14 * MIB,
         scratch=(pltpu.VMEM((z.nd, z.rows, z.columns), bf16), pltpu.VMEM((z.rows, z.wide), bf16)),
         alias=alias,
     )
@@ -375,7 +376,18 @@
     maps, moving = tie(maps, moving)
     rounds = [None, shifted(moving, "dp", nd, 1)]
     token_quarters = [lax.dynamic_slice_in_dim(own_tokens, quarters[r] * zz.fq, zz.fq, 1) for r in range(zz.nq)]
-    maps, rounds[1], token_quarters = tie(gather_shifts(maps, "dp", nd), rounds[1], token_quarters)
+    def arrival(index):
+        found = (z - index * m - jnp.arange(m, dtype=i32)) % nd
+        place_of = jnp.sum((found[None, :] < found[:, None]).astype(i32), axis=1)
+        match = place_of[None, :] == jnp.arange(m, dtype=i32)[:, None]
+        return jnp.sum(jnp.where(match, found[None, :], 0), axis=1, dtype=i32)
+
+    arrivals = [arrival((t + g) % nt) for g in range(nt)]
+    chosen = [[[x[j] == k for k in range(nd)] for j in range(m)] for x in arrivals]
+    scale = adapter_scale / lax.dynamic_slice_in_dim(tokens_per_job, z * jobs_dev, jobs_dev).astype(f32)
+    maps, rounds[1], token_quarters, chosen, scale = tie(
+        gather_shifts(maps, "dp", nd), rounds[1], token_quarters, chosen, scale
+    )
     maps = jnp.concatenate(maps, axis=0).reshape(zz.jobs * r2, -1)
     maps = jnp.concatenate(gather_shifts(maps, "sub", ns), axis=0)
     grads = gather_shifts(own_grad, "tensor", nt)
@@ -410,15 +422,8 @@
     out_rel, out_valid = facts(z * blocks + positions)
     in_rel, in_valid = facts(block_ids)
 
-    def arrival(index):
-        found = (z - index * m - jnp.arange(m, dtype=i32)) % nd
-        place_of = jnp.sum((found[None, :] < found[:, None]).astype(i32), axis=1)
-        match = place_of[None, :] == jnp.arange(m, dtype=i32)[:, None]
-        return jnp.sum(jnp.where(match, found[None, :], 0), axis=1, dtype=i32)
-
     shard_of = (z - jnp.arange(nd, dtype=i32)) % nd
     shard_at = (t - shard_of // m) % nt * m + shard_of % m
-    arrivals = [arrival((t + g) % nt) for g in range(nt)]
     head_at = (z - arrivals[0]) % nd - t * m
     sc = jnp.concatenate(
         [
@@ -476,7 +481,7 @@
             for g in range(nt):
                 picked = base[-1]
                 for k in range(due, len(base) - 1):
-                    picked = jnp.where(arrivals[g][due] == k, base[k], picked)
+                    picked = jnp.where(chosen[g][due][k], base[k], picked)
                 made.append(shifted(picked, "tensor", nt, g))
             slots.append(made)
 
@@ -506,8 +511,7 @@
     layer, gradient, tables = tie(layer, gradient, tables)
     landed = [shifted(layer[d], "dp", nd, d) for d in range(nd)]
     total = sum(x.astype(f32) for x in tables)
-    counts = lax.dynamic_slice_in_dim(tokens_per_job, z * jobs_dev, jobs_dev).astype(f32)
-    total = total.reshape(jobs_dev, r2, -1) * (adapter_scale / counts)[:, None, None]
+    total = total.reshape(jobs_dev, r2, -1) * scale[:, None, None]
     halves = gather_shifts(total, "sub", ns)
     gradient, halves = tie(gradient, halves)
     owned = jnp.concatenate(

time: 122 us -> 118 us (0.967)
  starting transfers between devices: 36.1 us -> 30.6 us
    ppermute x31, starting transfers between devices: 36.1 us -> 30.6 us  [shifted(): lax.ppermute(values, axis, [(i, (i + step) % count) for i in range(count)])]
    unnamed x38 -> x36, local copies, waits for them, and re-layouts: 8.23 us -> 8.24 us
  transfers between devices with their start and end apart: 31 -> 31, of which waited for: 6 -> 9; matrix products, arithmetic and copies ran while one was open for 17% -> 18% of each run, Pallas kernels for 21% -> 22%
where the time goes in v9:
time: 118 us; the launch traced here: 117 us
  starting transfers between devices  30.6 us (26%)
  Pallas kernels  27.4 us (23%)
  waiting for transfers between devices  20.1 us (17%)
  local copies, waits for them, and re-layouts  15.6 us (13%)
  other arithmetic  9.01 us (8%)
  matrix products  7.64 us (6%)
  between operations  6.91 us (6%)
    ppermute x31, starting transfers between devices, shifted(): lax.ppermute(values, axis, [(i, (i + step) % count) for i in range(count)])  30.6 us
    pallas_call x7, Pallas kernels, call(): pl.pallas_call(kernel, out_shape=out_shape, grid_spec=pltpu.PrefetchScala...  27.4 us
    ppermute x31, waiting for transfers between devices, shifted(): lax.ppermute(values, axis, [(i, (i + step) % count) for i in range(count)])  20.1 us
    unnamed x36, local copies, waits for them, and re-layouts  8.24 us
    dot_general x13, matrix products, dot(): lax.dot_general(a, b, (dims, ((), ())), precision=precision, preferred_el...  7.64 us
    dynamic_slice x1, local copies, waits for them, and re-layouts, body(): lax.dynamic_slice_in_dim(own_tokens, quarters[r] * zz.fq, zz.fq, 1)  2.81 us
  transfers between devices with their start and end apart: 31, of which 9 were waited for; matrix products, arithmetic and copies ran while one was open for 18% of the time, Pallas kernels for 22%

profile of v9, /device:TPU:0, one launch (start us, length us, event | category | flops | bytes accessed | tf_op | source)
XLA Modules:
  0.0 117.3 jit_solution(8272004000129065265)
XLA Ops:
  2.7 3.1 %collective-permute-start = (bf16[1,8,4608]{2,1,0:T(8,128)(2,1)S(1)}, bf16[1,8,4608]{2,1,0:T(8,128)(2,1)S(1)}, u32[]{:S(2)}, u32[]{:S(2)}) collective-permute-start(bf16[1,8,4608]{2,1,0:T(8,128)(2,1)S(1)} %dynamic-slice_bitcast_fusion), channel_id=1, source_target_pairs={{0,4},{4,8},{8,12},{12,0},{1,5},{5,9},{9,13},{13,1},{2,6},{6,10},{... | collective-permute-start | bytes 221192 | tf_op jit(solution)/shard_map/ppermute | solution.py:34
  5.8 2.6 %collective-permute-start.1 = (bf16[1,8,4608]{2,1,0:T(8,128)(2,1)S(1)}, bf16[1,8,4608]{2,1,0:T(8,128)(2,1)S(1)}, u32[]{:S(2)}, u32[]{:S(2)}) collective-permute-start(bf16[1,8,4608]{2,1,0:T(8,128)(2,1)S(1)} %dynamic-slice_bitcast_fusion), channel_id=1, source_target_pairs={{0,8},{4,12},{8,0},{12,4},{1,9},{5,13},{9,1},{13,5},{2,10},{6,14},... | collective-permute-start | bytes 221192 | tf_op jit(solution)/shard_map/ppermute | solution.py:34
  8.3 1.3 %collective-permute-start.2 = (bf16[1,8,4608]{2,1,0:T(8,128)(2,1)S(1)}, bf16[1,8,4608]{2,1,0:T(8,128)(2,1)S(1)}, u32[]{:S(2)}, u32[]{:S(2)}) collective-permute-start(bf16[1,8,4608]{2,1,0:T(8,128)(2,1)S(1)} %dynamic-slice_bitcast_fusion), channel_id=1, source_target_pairs={{0,12},{4,0},{8,4},{12,8},{1,13},{5,1},{9,5},{13,9},{2,14},{6,2},{... | collective-permute-start | bytes 221192 | tf_op jit(solution)/shard_map/ppermute | solution.py:34
  10.4 1.5 %collective-permute-start.9 = (bf16[512,512]{1,0:T(8,128)(2,1)}, bf16[512,512]{1,0:T(8,128)(2,1)}, u32[]{:S(2)}, u32[]{:S(2)}) collective-permute-start(bf16[512,512]{1,0:T(8,128)(2,1)} %bitcast.63), channel_id=1, source_target_pairs={{0,2},{2,0},{1,3},{3,1},{4,6},{6,4},{5,7},{7,5},{8,10},{10,8},{9,1... | collective-permute-start | bytes 1572872 | tf_op jit(solution)/shard_map/ppermute | solution.py:34
  25.7 2.8 %constant_dynamic-slice_fusion = (bf16[512,1024]{1,0:T(8,128)(2,1)S(1)}, bf16[512,1024]{1,0:T(8,128)(2,1)S(1)}, bf16[512,1024]{1,0:T(8,128)(2,1)S(1)}, bf16[512,1024]{1,0:T(8,128)(2,1)S(1)}) fusion(bf16[512,4096]{1,0:T(8,128)(2,1)} %bitcast.59, s32[]{:T(128)S(6)} %select_n.388, s32[]{:T(128)S(6)} %select_n.387, s32[]{:T(128)S(6)} %select_n.386, s32[]{:T(128)S(6)} %select_n.385), kind=kLoop, calls=%fused_computation.79 | loop fusion | bytes 8388624 | tf_op jit(solution)/shard_map/dynamic_slice | solution.py:378
  29.6 1.5 %collective-permute-start.7 = (bf16[1024,256]{1,0:T(8,128)(2,1)}, bf16[1024,256]{1,0:T(8,128)(2,1)S(1)}, u32[]{:S(2)}, u32[]{:S(2)}) collective-permute-start(bf16[1024,256]{1,0:T(8,128)(2,1)} %collective-permute-done.3.refs_4_), channel_id=1, source_target_pairs={{0,16},{16,0},{1,17},{17,1},{2,18},{18,2},{3,19},{19,3},{4,20},{20... | collective-permute-start | bytes 1572872 | tf_op jit(solution)/shard_map/ppermute | solution.py:34
  31.3 5.1 %adapter_products.1.refs_0_ = bf16[512,32]{1,0:T(8,128)(2,1)S(1)} custom-call(s32[78]{0:T(128)S(1)} %concatenate.15.sc, bf16[512,4096]{1,0:T(8,128)(2,1)S(1)} %bitcast.60, bf16[512,512]{1,0:T(8,128)(2,1)S(1)} %bitcast.64, bf16[64,4608]{1,0:T(8,128)(2,1)S(1)} %pad_maximum_fusion.maps, f32[64,16]{1,0:T(8,128)S(1)} %fusion.9.fold, ...), custom_call_target="tpu_custom_call" | custom-call | flops 1000 | bytes 1000 | tf_op jit(solution)/shard_map/adapter_products/pallas_call | solution.py:76
  37.0 1.3 %fusion.6 = bf16[512,256]{1,0:T(8,128)(2,1)S(1)} fusion(bf16[512,4096]{1,0:T(8,128)(2,1)S(1)} %bitcast.61, bf16[4096,256]{1,0:T(8,128)(2,1)S(1)} %copy-done), kind=kOutput, calls=%fused_computation.11 | convolution fusion | flops 1073872896 | bytes 6553600 | tf_op jit(solution)/shard_map/dot_general | solution.py:42
  38.3 3.8 %collective-permute-done.8.refs_1_ = bf16[512,32]{1,0:T(8,128)(2,1)S(1)} collective-permute-done((bf16[512,32]{1,0:T(8,128)(2,1)S(1)}, bf16[512,32]{1,0:T(8,128)(2,1)S(1)}, u32[]{:S(2)}, u32[]{:S(2)}) %collective-permute-start.8) | collective-permute-done | bytes 32800 | tf_op jit(solution)/shard_map/ppermute | solution.py:34
  42.7 2.5 %collective-permute-done.6.refs_6_ = bf16[1024,256]{1,0:T(8,128)(2,1)S(1)} collective-permute-done((bf16[1024,256]{1,0:T(8,128)(2,1)}, bf16[1024,256]{1,0:T(8,128)(2,1)S(1)}, u32[]{:S(2)}, u32[]{:S(2)}) %collective-permute-start.6) | collective-permute-done | bytes 524320 | tf_op jit(solution)/shard_map/ppermute | solution.py:34
  45.8 1.6 %collective-permute-start.13 = (bf16[1024,256]{1,0:T(8,128)(2,1)S(1)}, bf16[1024,256]{1,0:T(8,128)(2,1)S(1)}, u32[]{:S(2)}, u32[]{:S(2)}) collective-permute-start(bf16[1024,256]{1,0:T(8,128)(2,1)S(1)} %collective-permute-done.6.refs_6_), channel_id=1, source_target_pairs={{0,16},{16,0},{1,17},{17,1},{2,18},{18,2},{3,19},{19,3},{4,20},{20... | collective-permute-start | bytes 1572872 | tf_op jit(solution)/shard_map/ppermute | solution.py:34
  49.3 1.5 %fusion.4 = bf16[512,256]{1,0:T(8,128)(2,1)S(1)} fusion(f32[512,256]{1,0:T(8,128)S(1)} %fusion.47, f32[512,256]{1,0:T(8,128)S(1)} %fusion.46, f32[512,256]{1,0:T(8,128)S(1)} %fusion.45, bf16[512,1024]{1,0:T(8,128)(2,1)S(1)} %get-tuple-element.113, bf16[1024,256]{1,0:T(8,128)(2,1)} %collective-permute-done.3.refs_4_), kind=kOutput, calls=%fused_computation.8 | convolution fusion | flops 268959744 | bytes 3407872 | tf_op jit(solution)/shard_map/dot_general | solution.py:42
  50.8 10.7 %collective-permute-done.12.refs_8_ = bf16[1024,256]{1,0:T(8,128)(2,1)S(1)} collective-permute-done((bf16[1024,256]{1,0:T(8,128)(2,1)S(1)}, bf16[1024,256]{1,0:T(8,128)(2,1)S(1)}, u32[]{:S(2)}, u32[]{:S(2)}) %collective-permute-start.12) | collective-permute-done | bytes 524320 | tf_op jit(solution)/shard_map/ppermute | solution.py:34
  61.5 1.6 %collective-permute-start.19 = (bf16[1024,256]{1,0:T(8,128)(2,1)S(1)}, bf16[1024,256]{1,0:T(8,128)(2,1)S(1)}, u32[]{:S(2)}, u32[]{:S(2)}) collective-permute-start(bf16[1024,256]{1,0:T(8,128)(2,1)S(1)} %collective-permute-done.12.refs_8_), channel_id=1, source_target_pairs={{0,16},{16,0},{1,17},{17,1},{2,18},{18,2},{3,19},{19,3},{4,20},{20... | collective-permute-start | bytes 1572872 | tf_op jit(solution)/shard_map/ppermute | solution.py:34
  63.3 2.2 %collective-permute-start.17 = (bf16[128,32]{1,0:T(8,128)(2,1)S(1)}, bf16[128,32]{1,0:T(8,128)(2,1)S(1)}, u32[]{:S(2)}, u32[]{:S(2)}) collective-permute-start(bf16[128,32]{1,0:T(8,128)(2,1)S(1)} %get-tuple-element.135), channel_id=1, source_target_pairs={{0,8},{4,12},{8,0},{12,4},{1,9},{5,13},{9,1},{13,5},{2,10},{6,14},... | collective-permute-start | bytes 24584 | tf_op jit(solution)/shard_map/ppermute | solution.py:34
  66.5 1.6 %collective-permute-start.18 = (bf16[128,32]{1,0:T(8,128)(2,1)S(1)}, bf16[128,32]{1,0:T(8,128)(2,1)S(1)}, u32[]{:S(2)}, u32[]{:S(2)}) collective-permute-start(bf16[128,32]{1,0:T(8,128)(2,1)S(1)} %get-tuple-element.136), channel_id=1, source_target_pairs={{0,12},{4,0},{8,4},{12,8},{1,13},{5,1},{9,5},{13,9},{2,14},{6,2},{... | collective-permute-start | bytes 24584 | tf_op jit(solution)/shard_map/ppermute | solution.py:34
  70.5 5.6 %job_tables.1 = (f32[32,4608]{1,0:T(8,128)S(1)}, bf16[32,4608]{1,0:T(8,128)(2,1)S(1)}) custom-call(s32[78]{0:T(128)S(1)} %concatenate.15.sc, bf16[512,4096]{1,0:T(8,128)(2,1)S(1)} %bitcast.62, bf16[512,512]{1,0:T(8,128)(2,1)S(1)} %bitcast.65, bf16[16,64]{1,0:T(8,128)(2,1)S(1)} %fusion.10.unfold, s32[1,64]{1,0:T(1,128)S(1)} %and_select_fusion.job_of, ...), custom_call_target="tpu_custom_call" | custom-call | flops 1000 | bytes 1000 | tf_op jit(solution)/shard_map/job_tables/pallas_call | solution.py:76
  77.6 1.4 %collective-permute-done.21.refs_9_ = bf16[1024,256]{1,0:T(8,128)(2,1)S(1)} collective-permute-done((bf16[1024,256]{1,0:T(8,128)(2,1)S(1)}, bf16[1024,256]{1,0:T(8,128)(2,1)S(1)}, u32[]{:S(2)}, u32[]{:S(2)}) %collective-permute-start.21) | collective-permute-done | bytes 524320 | tf_op jit(solution)/shard_map/ppermute | solution.py:34
  80.9 3.2 %collective-permute-start.24 = (bf16[8,4608]{1,0:T(8,128)(2,1)S(1)}, bf16[8,4608]{1,0:T(8,128)(2,1)S(1)}, u32[]{:S(2)}, u32[]{:S(2)}) collective-permute-start(bf16[8,4608]{1,0:T(8,128)(2,1)S(1)} %get-tuple-element.216), channel_id=1, source_target_pairs={{0,12},{4,0},{8,4},{12,8},{1,13},{5,1},{9,5},{13,9},{2,14},{6,2},{... | collective-permute-start | bytes 221192 | tf_op jit(solution)/shard_map/ppermute | solution.py:34
  85.0 6.3 %token_gradient_0.1.refs_10_ = bf16[512,4096]{1,0:T(8,128)(2,1)} custom-call(s32[78]{0:T(128)S(1)} %concatenate.15.sc, bf16[64,4608]{1,0:T(8,128)(2,1)S(1)} %pad_maximum_fusion.maps, bf16[512,32]{1,0:T(8,128)(2,1)S(1)} %get-tuple-element.112.sums, bf16[16,64]{1,0:T(8,128)(2,1)S(1)} %fusion.10.unfold, s32[1,64]{1,0:T(1,128)S(1)} %and_select_fusion.job_of, ...), custom_call_target="tpu_custom_call" | custom-call | flops 1000 | bytes 1000 | tf_op jit(solution)/shard_map/token_gradient_0/pallas_call | solution.py:76
  91.3 2.0 %layer.1 = (bf16[128,512]{1,0:T(8,128)(2,1)S(1)}, bf16[128,512]{1,0:T(8,128)(2,1)S(1)}, bf16[128,512]{1,0:T(8,128)(2,1)S(1)}, bf16[128,512]{1,0:T(8,128)(2,1)S(1)}) custom-call(s32[78]{0:T(128)S(1)} %concatenate.15.sc, bf16[512,32]{1,0:T(8,128)(2,1)S(1)} %get-tuple-element.112.sums, bf16[64,4608]{1,0:T(8,128)(2,1)S(1)} %pad_maximum_fusion.maps, ...), custom_call_target="tpu_custom_call" | custom-call | flops 33554432 | bytes 1572864 | tf_op jit(solution)/shard_map/layer/pallas_call | solution.py:76
  96.1 2.6 %collective-permute-start.28 = (bf16[128,512]{1,0:T(8,128)(2,1)}, bf16[128,512]{1,0:T(8,128)(2,1)S(1)}, u32[]{:S(2)}, u32[]{:S(2)}) collective-permute-start(bf16[128,512]{1,0:T(8,128)(2,1)} %copy-done.17), channel_id=1, source_target_pairs={{0,4},{4,8},{8,12},{12,0},{1,5},{5,9},{9,13},{13,1},{2,6},{6,10},{... | collective-permute-start | bytes 393224 | tf_op jit(solution)/shard_map/ppermute | solution.py:34
  109.0 6.2 %token_gradient_2.1 = bf16[512,4096]{1,0:T(8,128)(2,1)} custom-call(s32[78]{0:T(128)S(1)} %concatenate.15.sc, bf16[64,4608]{1,0:T(8,128)(2,1)S(1)} %pad_maximum_fusion.maps, bf16[512,32]{1,0:T(8,128)(2,1)S(1)} %get-tuple-element.112.sums, bf16[16,64]{1,0:T(8,128)(2,1)S(1)} %fusion.10.unfold, ...), custom_call_target="tpu_custom_call", output_to_operand_aliasing={{}: (15, {})} | custom-call | flops 2281701376 | bytes 6291456 | tf_op jit(solution)/shard_map/token_gradient_2/pallas_call | solution.py:76
  115.9 1.4 %place.1 = bf16[512,512]{1,0:T(8,128)(2,1)} custom-call(s32[78]{0:T(128)S(1)} %concatenate.15.sc, bf16[128,512]{1,0:T(8,128)(2,1)S(1)} %get-tuple-element.189.refs_0_, bf16[128,512]{1,0:T(8,128)(2,1)S(1)} %collective-permute-done.28.refs_1_, bf16[128,512]{1,0:T(8,128)(2,1)S(1)} %collective-permute-done.29.refs_2_, ...), custom_call_target="tpu_custom_call" | custom-call | flops 1000 | bytes 1048576 | tf_op jit(solution)/shard_map/place/pallas_call | solution.py:76
  (145 shorter events, 37.0 us)
Async XLA Ops:
  2.7 25.9 %collective-permute-start = (bf16[1,8,4608]{2,1,0:T(8,128)(2,1)S(1)}, bf16[1,8,4608]{2,1,0:T(8,128)(2,1)S(1)}, u32[]{:S(2)}, u32[]{:S(2)}) collective-permute-start(bf16[1,8,4608]{2,1,0:T(8,128)(2,1)S(1)} %dynamic-slice_bitcast_fusion), channel_id=1, source_target_pairs={{0,4},{4,8},{8,12},{12,0},{1,5},{5,9},{9,13},{13,1},{2,6},{6,10},{... | collective-permute-start | bytes 221192 | tf_op jit(solution)/shard_map/ppermute | solution.py:34
  5.8 22.8 %collective-permute-start.1 = (bf16[1,8,4608]{2,1,0:T(8,128)(2,1)S(1)}, bf16[1,8,4608]{2,1,0:T(8,128)(2,1)S(1)}, u32[]{:S(2)}, u32[]{:S(2)}) collective-permute-start(bf16[1,8,4608]{2,1,0:T(8,128)(2,1)S(1)} %dynamic-slice_bitcast_fusion), channel_id=1, source_target_pairs={{0,8},{4,12},{8,0},{12,4},{1,9},{5,13},{9,1},{13,5},{2,10},{6,14},... | collective-permute-start | bytes 221192 | tf_op jit(solution)/shard_map/ppermute | solution.py:34
  8.3 20.2 %collective-permute-start.2 = (bf16[1,8,4608]{2,1,0:T(8,128)(2,1)S(1)}, bf16[1,8,4608]{2,1,0:T(8,128)(2,1)S(1)}, u32[]{:S(2)}, u32[]{:S(2)}) collective-permute-start(bf16[1,8,4608]{2,1,0:T(8,128)(2,1)S(1)} %dynamic-slice_bitcast_fusion), channel_id=1, source_target_pairs={{0,12},{4,0},{8,4},{12,8},{1,13},{5,1},{9,5},{13,9},{2,14},{6,2},{... | collective-permute-start | bytes 221192 | tf_op jit(solution)/shard_map/ppermute | solution.py:34
  9.7 18.9 %collective-permute-start.3 = (bf16[1024,256]{1,0:T(8,128)(2,1)S(1)}, bf16[1024,256]{1,0:T(8,128)(2,1)}, u32[]{:S(2)}, u32[]{:S(2)}) collective-permute-start(bf16[1024,256]{1,0:T(8,128)(2,1)S(1)} %constant_dynamic-slice_fusion.4), channel_id=1, source_target_pairs={{0,4},{4,8},{8,12},{12,0},{1,5},{5,9},{9,13},{13,1},{2,6},{6,10},{... | collective-permute-start | bytes 1572872 | tf_op jit(solution)/shard_map/ppermute | solution.py:34
  10.4 27.9 %collective-permute-start.9 = (bf16[512,512]{1,0:T(8,128)(2,1)}, bf16[512,512]{1,0:T(8,128)(2,1)}, u32[]{:S(2)}, u32[]{:S(2)}) collective-permute-start(bf16[512,512]{1,0:T(8,128)(2,1)} %bitcast.63), channel_id=1, source_target_pairs={{0,2},{2,0},{1,3},{3,1},{4,6},{6,4},{5,7},{7,5},{8,10},{10,8},{9,1... | collective-permute-start | bytes 1572872 | tf_op jit(solution)/shard_map/ppermute | solution.py:34
  29.3 15.9 %collective-permute-start.6 = (bf16[1024,256]{1,0:T(8,128)(2,1)}, bf16[1024,256]{1,0:T(8,128)(2,1)S(1)}, u32[]{:S(2)}, u32[]{:S(2)}) collective-permute-start(bf16[1024,256]{1,0:T(8,128)(2,1)} %collective-permute-done.3.refs_4_), channel_id=1, source_target_pairs={{0,4},{4,8},{8,12},{12,0},{1,5},{5,9},{9,13},{13,1},{2,6},{6,10},{... | collective-permute-start | bytes 1572872 | tf_op jit(solution)/shard_map/ppermute | solution.py:34
  29.6 15.7 %collective-permute-start.7 = (bf16[1024,256]{1,0:T(8,128)(2,1)}, bf16[1024,256]{1,0:T(8,128)(2,1)S(1)}, u32[]{:S(2)}, u32[]{:S(2)}) collective-permute-start(bf16[1024,256]{1,0:T(8,128)(2,1)} %collective-permute-done.3.refs_4_), channel_id=1, source_target_pairs={{0,16},{16,0},{1,17},{17,1},{2,18},{18,2},{3,19},{19,3},{4,20},{20... | collective-permute-start | bytes 1572872 | tf_op jit(solution)/shard_map/ppermute | solution.py:34
  36.4 5.7 %collective-permute-start.8 = (bf16[512,32]{1,0:T(8,128)(2,1)S(1)}, bf16[512,32]{1,0:T(8,128)(2,1)S(1)}, u32[]{:S(2)}, u32[]{:S(2)}) collective-permute-start(bf16[512,32]{1,0:T(8,128)(2,1)S(1)} %adapter_products.1.refs_0_), channel_id=1, source_target_pairs={{0,2},{2,0},{1,3},{3,1},{4,6},{6,4},{5,7},{7,5},{8,10},{10,8},{9,1... | collective-permute-start | bytes 98312 | tf_op jit(solution)/shard_map/ppermute | solution.py:34
  45.8 15.7 %collective-permute-start.12 = (bf16[1024,256]{1,0:T(8,128)(2,1)S(1)}, bf16[1024,256]{1,0:T(8,128)(2,1)S(1)}, u32[]{:S(2)}, u32[]{:S(2)}) collective-permute-start(bf16[1024,256]{1,0:T(8,128)(2,1)S(1)} %collective-permute-done.6.refs_6_), channel_id=1, source_target_pairs={{0,4},{4,8},{8,12},{12,0},{1,5},{5,9},{9,13},{13,1},{2,6},{6,10},{... | collective-permute-start | bytes 1572872 | tf_op jit(solution)/shard_map/ppermute | solution.py:34
  45.8 15.7 %collective-permute-start.13 = (bf16[1024,256]{1,0:T(8,128)(2,1)S(1)}, bf16[1024,256]{1,0:T(8,128)(2,1)S(1)}, u32[]{:S(2)}, u32[]{:S(2)}) collective-permute-start(bf16[1024,256]{1,0:T(8,128)(2,1)S(1)} %collective-permute-done.6.refs_6_), channel_id=1, source_target_pairs={{0,16},{16,0},{1,17},{17,1},{2,18},{18,2},{3,19},{19,3},{4,20},{20... | collective-permute-start | bytes 1572872 | tf_op jit(solution)/shard_map/ppermute | solution.py:34
  61.5 14.6 %collective-permute-start.14 = (bf16[1024,256]{1,0:T(8,128)(2,1)S(1)}, bf16[1024,256]{1,0:T(8,128)(2,1)S(1)}, u32[]{:S(2)}, u32[]{:S(2)}) collective-permute-start(bf16[1024,256]{1,0:T(8,128)(2,1)S(1)} %collective-permute-done.12.refs_8_), channel_id=1, source_target_pairs={{0,1},{1,0},{2,3},{3,2},{4,5},{5,4},{6,7},{7,6},{8,9},{9,8},{10,11... | collective-permute-start | bytes 1572872 | tf_op jit(solution)/shard_map/ppermute | solution.py:34
  61.5 15.5 %collective-permute-start.19 = (bf16[1024,256]{1,0:T(8,128)(2,1)S(1)}, bf16[1024,256]{1,0:T(8,128)(2,1)S(1)}, u32[]{:S(2)}, u32[]{:S(2)}) collective-permute-start(bf16[1024,256]{1,0:T(8,128)(2,1)S(1)} %collective-permute-done.12.refs_8_), channel_id=1, source_target_pairs={{0,16},{16,0},{1,17},{17,1},{2,18},{18,2},{3,19},{19,3},{4,20},{20... | collective-permute-start | bytes 1572872 | tf_op jit(solution)/shard_map/ppermute | solution.py:34
  63.2 5.9 %collective-permute-start.16 = (bf16[128,32]{1,0:T(8,128)(2,1)S(1)}, bf16[128,32]{1,0:T(8,128)(2,1)S(1)}, u32[]{:S(2)}, u32[]{:S(2)}) collective-permute-start(bf16[128,32]{1,0:T(8,128)(2,1)S(1)} %get-tuple-element.134), channel_id=1, source_target_pairs={{0,4},{4,8},{8,12},{12,0},{1,5},{5,9},{9,13},{13,1},{2,6},{6,10},{... | collective-permute-start | bytes 24584 | tf_op jit(solution)/shard_map/ppermute | solution.py:34
  63.3 6.3 %collective-permute-start.17 = (bf16[128,32]{1,0:T(8,128)(2,1)S(1)}, bf16[128,32]{1,0:T(8,128)(2,1)S(1)}, u32[]{:S(2)}, u32[]{:S(2)}) collective-permute-start(bf16[128,32]{1,0:T(8,128)(2,1)S(1)} %get-tuple-element.135), channel_id=1, source_target_pairs={{0,8},{4,12},{8,0},{12,4},{1,9},{5,13},{9,1},{13,5},{2,10},{6,14},... | collective-permute-start | bytes 24584 | tf_op jit(solution)/shard_map/ppermute | solution.py:34
  66.5 4.0 %collective-permute-start.18 = (bf16[128,32]{1,0:T(8,128)(2,1)S(1)}, bf16[128,32]{1,0:T(8,128)(2,1)S(1)}, u32[]{:S(2)}, u32[]{:S(2)}) collective-permute-start(bf16[128,32]{1,0:T(8,128)(2,1)S(1)} %get-tuple-element.136), channel_id=1, source_target_pairs={{0,12},{4,0},{8,4},{12,8},{1,13},{5,1},{9,5},{13,9},{2,14},{6,2},{... | collective-permute-start | bytes 24584 | tf_op jit(solution)/shard_map/ppermute | solution.py:34
  69.1 8.0 %collective-permute-start.20 = (bf16[512,256]{1,0:T(8,128)(2,1)S(1)}, bf16[512,256]{1,0:T(8,128)(2,1)S(1)}, u32[]{:S(2)}, u32[]{:S(2)}) collective-permute-start(bf16[512,256]{1,0:T(8,128)(2,1)S(1)} %get-tuple-element.210), channel_id=1, source_target_pairs={{0,2},{2,0},{1,3},{3,1},{4,6},{6,4},{5,7},{7,5},{8,10},{10,8},{9,1... | collective-permute-start | bytes 786440 | tf_op jit(solution)/shard_map/ppermute | solution.py:34
  80.0 11.3 %collective-permute-start.23 = (bf16[512,256]{1,0:T(8,128)(2,1)S(1)}, bf16[512,256]{1,0:T(8,128)(2,1)S(1)}, u32[]{:S(2)}, u32[]{:S(2)}) collective-permute-start(bf16[512,256]{1,0:T(8,128)(2,1)S(1)} %get-tuple-element.204), channel_id=1, source_target_pairs={{0,2},{2,0},{1,3},{3,1},{4,6},{6,4},{5,7},{7,5},{8,10},{10,8},{9,1... | collective-permute-start | bytes 786440 | tf_op jit(solution)/shard_map/ppermute | solution.py:34
  80.9 14.5 %collective-permute-start.24 = (bf16[8,4608]{1,0:T(8,128)(2,1)S(1)}, bf16[8,4608]{1,0:T(8,128)(2,1)S(1)}, u32[]{:S(2)}, u32[]{:S(2)}) collective-permute-start(bf16[8,4608]{1,0:T(8,128)(2,1)S(1)} %get-tuple-element.216), channel_id=1, source_target_pairs={{0,12},{4,0},{8,4},{12,8},{1,13},{5,1},{9,5},{13,9},{2,14},{6,2},{... | collective-permute-start | bytes 221192 | tf_op jit(solution)/shard_map/ppermute | solution.py:34
  84.0 11.3 %collective-permute-start.25 = (bf16[8,4608]{1,0:T(8,128)(2,1)S(1)}, bf16[8,4608]{1,0:T(8,128)(2,1)S(1)}, u32[]{:S(2)}, u32[]{:S(2)}) collective-permute-start(bf16[8,4608]{1,0:T(8,128)(2,1)S(1)} %get-tuple-element.215), channel_id=1, source_target_pairs={{0,8},{4,12},{8,0},{12,4},{1,9},{5,13},{9,1},{13,5},{2,10},{6,14},... | collective-permute-start | bytes 221192 | tf_op jit(solution)/shard_map/ppermute | solution.py:34
  84.3 11.1 %collective-permute-start.26 = (bf16[8,4608]{1,0:T(8,128)(2,1)S(1)}, bf16[8,4608]{1,0:T(8,128)(2,1)S(1)}, u32[]{:S(2)}, u32[]{:S(2)}) collective-permute-start(bf16[8,4608]{1,0:T(8,128)(2,1)S(1)} %get-tuple-element.214), channel_id=1, source_target_pairs={{0,4},{4,8},{8,12},{12,0},{1,5},{5,9},{9,13},{13,1},{2,6},{6,10},{... | collective-permute-start | bytes 221192 | tf_op jit(solution)/shard_map/ppermute | solution.py:34
  96.1 5.0 %collective-permute-start.27 = (f32[1,8,4608]{2,1,0:T(8,128)}, f32[1,8,4608]{2,1,0:T(8,128)}, u32[]{:S(2)}, u32[]{:S(2)}) collective-permute-start(f32[1,8,4608]{2,1,0:T(8,128)} %multiply_bitcast_fusion), channel_id=1, source_target_pairs={{0,1},{1,0},{2,3},{3,2},{4,5},{5,4},{6,7},{7,6},{8,9},{9,8},{10,11... | collective-permute-start | bytes 442376 | tf_op jit(solution)/shard_map/ppermute | solution.py:34
  96.1 19.8 %collective-permute-start.28 = (bf16[128,512]{1,0:T(8,128)(2,1)}, bf16[128,512]{1,0:T(8,128)(2,1)S(1)}, u32[]{:S(2)}, u32[]{:S(2)}) collective-permute-start(bf16[128,512]{1,0:T(8,128)(2,1)} %copy-done.17), channel_id=1, source_target_pairs={{0,4},{4,8},{8,12},{12,0},{1,5},{5,9},{9,13},{13,1},{2,6},{6,10},{... | collective-permute-start | bytes 393224 | tf_op jit(solution)/shard_map/ppermute | solution.py:34
  98.7 17.2 %collective-permute-start.29 = (bf16[128,512]{1,0:T(8,128)(2,1)}, bf16[128,512]{1,0:T(8,128)(2,1)S(1)}, u32[]{:S(2)}, u32[]{:S(2)}) collective-permute-start(bf16[128,512]{1,0:T(8,128)(2,1)} %copy-done.16), channel_id=1, source_target_pairs={{0,8},{4,12},{8,0},{12,4},{1,9},{5,13},{9,1},{13,5},{2,10},{6,14},... | collective-permute-start | bytes 393224 | tf_op jit(solution)/shard_map/ppermute | solution.py:34
  99.8 16.1 %collective-permute-start.30 = (bf16[128,512]{1,0:T(8,128)(2,1)}, bf16[128,512]{1,0:T(8,128)(2,1)S(1)}, u32[]{:S(2)}, u32[]{:S(2)}) collective-permute-start(bf16[128,512]{1,0:T(8,128)(2,1)} %copy-done.15), channel_id=1, source_target_pairs={{0,12},{4,0},{8,4},{12,8},{1,13},{5,1},{9,5},{13,9},{2,14},{6,2},{... | collective-permute-start | bytes 393224 | tf_op jit(solution)/shard_map/ppermute | solution.py:34
  (25 other events, 57.0 us)

commit v10 on v9

--- a/solution.py
+++ b/solution.py
@@ -342,7 +342,8 @@
         "token_gradient_%d" % first, (count * per,), sc, inputs, in_specs,
         jax.ShapeDtypeStruct((z.rows, z.width), bf16), pl.BlockSpec((z.rows, tile), block),
         1000 if alias is None else 2 * z.rows * count * z.fq * (z.nd * z.columns + z.wide),
-        1000 if alias is None else 2 * count * z.fq * (z.rows + z.nd * z.columns), 14 * MIB,
+        1000 if alias is None else 2 * count * z.fq * (z.rows + z.nd * z.columns),
+        (14 if alias is None else 61) * MIB,
         scratch=(pltpu.VMEM((z.nd, z.rows, z.columns), bf16), pltpu.VMEM((z.rows, z.wide), bf16)),
         alias=alias,
     )
@@ -518,6 +519,7 @@
         [sum(jnp.where((s - h) % ns == k, x, 0.0) for k, x in enumerate(halves)) for h in range(ns)], axis=1
     )
     grad_down, grad_up = owned[:, :, :width], owned[:, :, width:]
+    gradient, grad_down, grad_up = tie(gradient, grad_down, grad_up)
     gradient = token_gradient_of(
         zz, sc, grads, maps, sums, unfold, job_of, piece_list, list(range(half, zz.nq)), gradient
     )

time: 118 us -> 111 us (0.941)
  local copies, waits for them, and re-layouts: 15.6 us -> 7.8 us
  Pallas kernels: 27.4 us -> 29.3 us
  other arithmetic: 9.01 us -> 7.35 us
    unnamed x36 -> x30, local copies, waits for them, and re-layouts: 8.24 us -> 0.39 us
    pallas_call x7, Pallas kernels: 27.4 us -> 29.3 us  [call(): pl.pallas_call(kernel, out_shape=out_shape, grid_spec=pltpu.PrefetchScala...]
  transfers between devices with their start and end apart: 31 -> 31, of which waited for: 9 -> 9; matrix products, arithmetic and copies ran while one was open for 18% -> 18% of each run, Pallas kernels for 22% -> 25%
where the time goes in v10:
time: 111 us; the launch traced here: 110 us
  starting transfers between devices  30.9 us (28%)
  Pallas kernels  29.3 us (26%)
  waiting for transfers between devices  20.1 us (18%)
  local copies, waits for them, and re-layouts  7.8 us (7%)
  matrix products  7.64 us (7%)
  other arithmetic  7.35 us (7%)
  between operations  6.99 us (6%)
    ppermute x31, starting transfers between devices, shifted(): lax.ppermute(values, axis, [(i, (i + step) % count) for i in range(count)])  30.9 us
    pallas_call x7, Pallas kernels, call(): pl.pallas_call(kernel, out_shape=out_shape, grid_spec=pltpu.PrefetchScala...  29.3 us
    ppermute x31, waiting for transfers between devices, shifted(): lax.ppermute(values, axis, [(i, (i + step) % count) for i in range(count)])  20.1 us
    dot_general x13, matrix products, dot(): lax.dot_general(a, b, (dims, ((), ())), precision=precision, preferred_el...  7.64 us
    dynamic_slice x1, local copies, waits for them, and re-layouts, body(): lax.dynamic_slice_in_dim(own_tokens, quarters[r] * zz.fq, zz.fq, 1)  2.81 us
  transfers between devices with their start and end apart: 31, of which 9 were waited for; matrix products, arithmetic and copies ran while one was open for 18% of the time, Pallas kernels for 25%

profile of v10, /device:TPU:0, one launch (start us, length us, event | category | flops | bytes accessed | tf_op | source)
XLA Modules:
  0.0 110.1 jit_solution(4786143775574625056)
XLA Ops:
  2.7 3.1 %collective-permute-start = (bf16[1,8,4608]{2,1,0:T(8,128)(2,1)S(1)}, bf16[1,8,4608]{2,1,0:T(8,128)(2,1)S(1)}, u32[]{:S(2)}, u32[]{:S(2)}) collective-permute-start(bf16[1,8,4608]{2,1,0:T(8,128)(2,1)S(1)} %dynamic-slice_bitcast_fusion), channel_id=1, source_target_pairs={{0,4},{4,8},{8,12},{12,0},{1,5},{5,9},{9,13},{13,1},{2,6},{6,10},{... | collective-permute-start | bytes 221192 | tf_op jit(solution)/shard_map/ppermute | solution.py:34
  5.8 2.6 %collective-permute-start.1 = (bf16[1,8,4608]{2,1,0:T(8,128)(2,1)S(1)}, bf16[1,8,4608]{2,1,0:T(8,128)(2,1)S(1)}, u32[]{:S(2)}, u32[]{:S(2)}) collective-permute-start(bf16[1,8,4608]{2,1,0:T(8,128)(2,1)S(1)} %dynamic-slice_bitcast_fusion), channel_id=1, source_target_pairs={{0,8},{4,12},{8,0},{12,4},{1,9},{5,13},{9,1},{13,5},{2,10},{6,14},... | collective-permute-start | bytes 221192 | tf_op jit(solution)/shard_map/ppermute | solution.py:34
  8.3 1.3 %collective-permute-start.2 = (bf16[1,8,4608]{2,1,0:T(8,128)(2,1)S(1)}, bf16[1,8,4608]{2,1,0:T(8,128)(2,1)S(1)}, u32[]{:S(2)}, u32[]{:S(2)}) collective-permute-start(bf16[1,8,4608]{2,1,0:T(8,128)(2,1)S(1)} %dynamic-slice_bitcast_fusion), channel_id=1, source_target_pairs={{0,12},{4,0},{8,4},{12,8},{1,13},{5,1},{9,5},{13,9},{2,14},{6,2},{... | collective-permute-start | bytes 221192 | tf_op jit(solution)/shard_map/ppermute | solution.py:34
  10.4 1.5 %collective-permute-start.9 = (bf16[512,512]{1,0:T(8,128)(2,1)}, bf16[512,512]{1,0:T(8,128)(2,1)}, u32[]{:S(2)}, u32[]{:S(2)}) collective-permute-start(bf16[512,512]{1,0:T(8,128)(2,1)} %bitcast.63), channel_id=1, source_target_pairs={{0,2},{2,0},{1,3},{3,1},{4,6},{6,4},{5,7},{7,5},{8,10},{10,8},{9,1... | collective-permute-start | bytes 1572872 | tf_op jit(solution)/shard_map/ppermute | solution.py:34
  25.7 2.8 %constant_dynamic-slice_fusion = (bf16[512,1024]{1,0:T(8,128)(2,1)S(1)}, bf16[512,1024]{1,0:T(8,128)(2,1)S(1)}, bf16[512,1024]{1,0:T(8,128)(2,1)S(1)}, bf16[512,1024]{1,0:T(8,128)(2,1)S(1)}) fusion(bf16[512,4096]{1,0:T(8,128)(2,1)} %bitcast.59, s32[]{:T(128)S(6)} %select_n.388, s32[]{:T(128)S(6)} %select_n.387, s32[]{:T(128)S(6)} %select_n.386, s32[]{:T(128)S(6)} %select_n.385), kind=kLoop, calls=%fused_computation.79 | loop fusion | bytes 8388624 | tf_op jit(solution)/shard_map/dynamic_slice | solution.py:379
  29.6 1.5 %collective-permute-start.7 = (bf16[1024,256]{1,0:T(8,128)(2,1)}, bf16[1024,256]{1,0:T(8,128)(2,1)S(1)}, u32[]{:S(2)}, u32[]{:S(2)}) collective-permute-start(bf16[1024,256]{1,0:T(8,128)(2,1)} %collective-permute-done.3.refs_4_), channel_id=1, source_target_pairs={{0,16},{16,0},{1,17},{17,1},{2,18},{18,2},{3,19},{19,3},{4,20},{20... | collective-permute-start | bytes 1572872 | tf_op jit(solution)/shard_map/ppermute | solution.py:34
  31.3 5.1 %adapter_products.1.refs_0_ = bf16[512,32]{1,0:T(8,128)(2,1)S(1)} custom-call(s32[78]{0:T(128)S(1)} %concatenate.15.sc, bf16[512,4096]{1,0:T(8,128)(2,1)S(1)} %bitcast.60, bf16[512,512]{1,0:T(8,128)(2,1)S(1)} %bitcast.65, bf16[64,4608]{1,0:T(8,128)(2,1)S(1)} %pad_maximum_fusion.maps, f32[64,16]{1,0:T(8,128)S(1)} %fusion.9.fold, ...), custom_call_target="tpu_custom_call" | custom-call | flops 1000 | bytes 1000 | tf_op jit(solution)/shard_map/adapter_products/pallas_call | solution.py:76
  38.3 3.8 %collective-permute-done.8.refs_1_ = bf16[512,32]{1,0:T(8,128)(2,1)S(1)} collective-permute-done((bf16[512,32]{1,0:T(8,128)(2,1)S(1)}, bf16[512,32]{1,0:T(8,128)(2,1)S(1)}, u32[]{:S(2)}, u32[]{:S(2)}) %collective-permute-start.8) | collective-permute-done | bytes 32800 | tf_op jit(solution)/shard_map/ppermute | solution.py:34
  42.8 2.5 %collective-permute-done.6.refs_6_ = bf16[1024,256]{1,0:T(8,128)(2,1)S(1)} collective-permute-done((bf16[1024,256]{1,0:T(8,128)(2,1)}, bf16[1024,256]{1,0:T(8,128)(2,1)S(1)}, u32[]{:S(2)}, u32[]{:S(2)}) %collective-permute-start.6) | collective-permute-done | bytes 524320 | tf_op jit(solution)/shard_map/ppermute | solution.py:34
  45.9 1.6 %collective-permute-start.13 = (bf16[1024,256]{1,0:T(8,128)(2,1)S(1)}, bf16[1024,256]{1,0:T(8,128)(2,1)S(1)}, u32[]{:S(2)}, u32[]{:S(2)}) collective-permute-start(bf16[1024,256]{1,0:T(8,128)(2,1)S(1)} %collective-permute-done.6.refs_6_), channel_id=1, source_target_pairs={{0,16},{16,0},{1,17},{17,1},{2,18},{18,2},{3,19},{19,3},{4,20},{20... | collective-permute-start | bytes 1572872 | tf_op jit(solution)/shard_map/ppermute | solution.py:34
  49.3 1.5 %fusion.4 = bf16[512,256]{1,0:T(8,128)(2,1)S(1)} fusion(f32[512,256]{1,0:T(8,128)S(1)} %fusion.47, f32[512,256]{1,0:T(8,128)S(1)} %fusion.46, f32[512,256]{1,0:T(8,128)S(1)} %fusion.45, bf16[512,1024]{1,0:T(8,128)(2,1)S(1)} %get-tuple-element.116, bf16[1024,256]{1,0:T(8,128)(2,1)} %collective-permute-done.3.refs_4_), kind=kOutput, calls=%fused_computation.8 | convolution fusion | flops 268959744 | bytes 3407872 | tf_op jit(solution)/shard_map/dot_general | solution.py:42
  50.8 10.7 %collective-permute-done.12.refs_8_ = bf16[1024,256]{1,0:T(8,128)(2,1)S(1)} collective-permute-done((bf16[1024,256]{1,0:T(8,128)(2,1)S(1)}, bf16[1024,256]{1,0:T(8,128)(2,1)S(1)}, u32[]{:S(2)}, u32[]{:S(2)}) %collective-permute-start.12) | collective-permute-done | bytes 524320 | tf_op jit(solution)/shard_map/ppermute | solution.py:34
  61.6 1.6 %collective-permute-start.19 = (bf16[1024,256]{1,0:T(8,128)(2,1)S(1)}, bf16[1024,256]{1,0:T(8,128)(2,1)S(1)}, u32[]{:S(2)}, u32[]{:S(2)}) collective-permute-start(bf16[1024,256]{1,0:T(8,128)(2,1)S(1)} %collective-permute-done.12.refs_8_), channel_id=1, source_target_pairs={{0,16},{16,0},{1,17},{17,1},{2,18},{18,2},{3,19},{19,3},{4,20},{20... | collective-permute-start | bytes 1572872 | tf_op jit(solution)/shard_map/ppermute | solution.py:34
  63.4 2.2 %collective-permute-start.17 = (bf16[128,32]{1,0:T(8,128)(2,1)S(1)}, bf16[128,32]{1,0:T(8,128)(2,1)S(1)}, u32[]{:S(2)}, u32[]{:S(2)}) collective-permute-start(bf16[128,32]{1,0:T(8,128)(2,1)S(1)} %get-tuple-element.138), channel_id=1, source_target_pairs={{0,8},{4,12},{8,0},{12,4},{1,9},{5,13},{9,1},{13,5},{2,10},{6,14},... | collective-permute-start | bytes 24584 | tf_op jit(solution)/shard_map/ppermute | solution.py:34
  66.5 1.6 %collective-permute-start.18 = (bf16[128,32]{1,0:T(8,128)(2,1)S(1)}, bf16[128,32]{1,0:T(8,128)(2,1)S(1)}, u32[]{:S(2)}, u32[]{:S(2)}) collective-permute-start(bf16[128,32]{1,0:T(8,128)(2,1)S(1)} %get-tuple-element.139), channel_id=1, source_target_pairs={{0,12},{4,0},{8,4},{12,8},{1,13},{5,1},{9,5},{13,9},{2,14},{6,2},{... | collective-permute-start | bytes 24584 | tf_op jit(solution)/shard_map/ppermute | solution.py:34
  70.6 5.6 %job_tables.1 = (f32[32,4608]{1,0:T(8,128)S(1)}, bf16[32,4608]{1,0:T(8,128)(2,1)S(1)}) custom-call(s32[78]{0:T(128)S(1)} %concatenate.15.sc, bf16[512,4096]{1,0:T(8,128)(2,1)S(1)} %bitcast.62, bf16[512,512]{1,0:T(8,128)(2,1)S(1)} %bitcast.66, bf16[16,64]{1,0:T(8,128)(2,1)S(1)} %fusion.10.unfold, s32[1,64]{1,0:T(1,128)S(1)} %and_select_fusion.job_of, ...), custom_call_target="tpu_custom_call" | custom-call | flops 1000 | bytes 1000 | tf_op jit(solution)/shard_map/job_tables/pallas_call | solution.py:76
  77.7 1.4 %collective-permute-done.21.refs_9_ = bf16[1024,256]{1,0:T(8,128)(2,1)S(1)} collective-permute-done((bf16[1024,256]{1,0:T(8,128)(2,1)S(1)}, bf16[1024,256]{1,0:T(8,128)(2,1)S(1)}, u32[]{:S(2)}, u32[]{:S(2)}) %collective-permute-start.21) | collective-permute-done | bytes 524320 | tf_op jit(solution)/shard_map/ppermute | solution.py:34
  81.3 3.2 %collective-permute-start.24 = (bf16[8,4608]{1,0:T(8,128)(2,1)S(1)}, bf16[8,4608]{1,0:T(8,128)(2,1)S(1)}, u32[]{:S(2)}, u32[]{:S(2)}) collective-permute-start(bf16[8,4608]{1,0:T(8,128)(2,1)S(1)} %get-tuple-element.222), channel_id=1, source_target_pairs={{0,12},{4,0},{8,4},{12,8},{1,13},{5,1},{9,5},{13,9},{2,14},{6,2},{... | collective-permute-start | bytes 221192 | tf_op jit(solution)/shard_map/ppermute | solution.py:34
  85.4 6.3 %token_gradient_0.1.refs_10_ = bf16[512,4096]{1,0:T(8,128)(2,1)} custom-call(s32[78]{0:T(128)S(1)} %concatenate.15.sc, bf16[64,4608]{1,0:T(8,128)(2,1)S(1)} %pad_maximum_fusion.maps, bf16[512,32]{1,0:T(8,128)(2,1)S(1)} %get-tuple-element.115.sums, bf16[16,64]{1,0:T(8,128)(2,1)S(1)} %fusion.10.unfold, s32[1,64]{1,0:T(1,128)S(1)} %and_select_fusion.job_of, ...), custom_call_target="tpu_custom_call" | custom-call | flops 1000 | bytes 1000 | tf_op jit(solution)/shard_map/token_gradient_0/pallas_call | solution.py:76
  91.8 2.1 %layer.1 = (bf16[128,512]{1,0:T(8,128)(2,1)S(1)}, bf16[128,512]{1,0:T(8,128)(2,1)S(1)}, bf16[128,512]{1,0:T(8,128)(2,1)S(1)}, bf16[128,512]{1,0:T(8,128)(2,1)S(1)}) custom-call(s32[78]{0:T(128)S(1)} %concatenate.15.sc, bf16[512,32]{1,0:T(8,128)(2,1)S(1)} %get-tuple-element.115.sums, bf16[64,4608]{1,0:T(8,128)(2,1)S(1)} %pad_maximum_fusion.maps, ...), custom_call_target="tpu_custom_call" | custom-call | flops 33554432 | bytes 1572864 | tf_op jit(solution)/shard_map/layer/pallas_call | solution.py:76
  94.0 2.7 %collective-permute-start.28 = (bf16[128,512]{1,0:T(8,128)(2,1)S(1)}, bf16[128,512]{1,0:T(8,128)(2,1)S(1)}, u32[]{:S(2)}, u32[]{:S(2)}) collective-permute-start(bf16[128,512]{1,0:T(8,128)(2,1)S(1)} %get-tuple-element.192), channel_id=1, source_target_pairs={{0,4},{4,8},{8,12},{12,0},{1,5},{5,9},{9,13},{13,1},{2,6},{6,10},{... | collective-permute-start | bytes 393224 | tf_op jit(solution)/shard_map/ppermute | solution.py:34
  97.8 1.3 %collective-permute-start.30 = (bf16[128,512]{1,0:T(8,128)(2,1)S(1)}, bf16[128,512]{1,0:T(8,128)(2,1)S(1)}, u32[]{:S(2)}, u32[]{:S(2)}) collective-permute-start(bf16[128,512]{1,0:T(8,128)(2,1)S(1)} %get-tuple-element.194), channel_id=1, source_target_pairs={{0,12},{4,0},{8,4},{12,8},{1,13},{5,1},{9,5},{13,9},{2,14},{6,2},{... | collective-permute-start | bytes 393224 | tf_op jit(solution)/shard_map/ppermute | solution.py:34
  100.5 8.2 %token_gradient_2.1 = bf16[512,4096]{1,0:T(8,128)(2,1)} custom-call(s32[78]{0:T(128)} %copy-done.6, bf16[64,4608]{1,0:T(8,128)(2,1)} %copy-done.2, bf16[512,32]{1,0:T(8,128)(2,1)} %copy-done.4, bf16[16,64]{1,0:T(8,128)(2,1)} %copy-done.5, s32[1,64]{1,0:T(1,128)} %copy-done.8, bf16[512,512]{1,0:T(8,128)(2,1)} %bitcast.64, ...), custom_call_target="tpu_custom_call", output_to_operand_aliasing={{}: (15, {})} | custom-call | flops 2281701376 | bytes 6291456 | tf_op jit(solution)/shard_map/token_gradient_2/pallas_call | solution.py:76
  108.7 1.4 %place.1 = bf16[512,512]{1,0:T(8,128)(2,1)} custom-call(s32[78]{0:T(128)S(1)} %copy-done.7, bf16[128,512]{1,0:T(8,128)(2,1)S(1)} %get-tuple-element.195.refs_0_, bf16[128,512]{1,0:T(8,128)(2,1)S(1)} %collective-permute-done.28.refs_1_, bf16[128,512]{1,0:T(8,128)(2,1)S(1)} %collective-permute-done.29.refs_2_, bf16[128,512]{1,0:T(8,128)(2,1)S(1)} %collective-permute-done.30.refs_3_), custom_call_target="tpu_custom_call" | custom-call | flops 1000 | bytes 1048576 | tf_op jit(solution)/shard_map/place/pallas_call | solution.py:76
  (139 shorter events, 27.5 us)
Async XLA Ops:
  2.7 25.9 %collective-permute-start = (bf16[1,8,4608]{2,1,0:T(8,128)(2,1)S(1)}, bf16[1,8,4608]{2,1,0:T(8,128)(2,1)S(1)}, u32[]{:S(2)}, u32[]{:S(2)}) collective-permute-start(bf16[1,8,4608]{2,1,0:T(8,128)(2,1)S(1)} %dynamic-slice_bitcast_fusion), channel_id=1, source_target_pairs={{0,4},{4,8},{8,12},{12,0},{1,5},{5,9},{9,13},{13,1},{2,6},{6,10},{... | collective-permute-start | bytes 221192 | tf_op jit(solution)/shard_map/ppermute | solution.py:34
  5.8 22.8 %collective-permute-start.1 = (bf16[1,8,4608]{2,1,0:T(8,128)(2,1)S(1)}, bf16[1,8,4608]{2,1,0:T(8,128)(2,1)S(1)}, u32[]{:S(2)}, u32[]{:S(2)}) collective-permute-start(bf16[1,8,4608]{2,1,0:T(8,128)(2,1)S(1)} %dynamic-slice_bitcast_fusion), channel_id=1, source_target_pairs={{0,8},{4,12},{8,0},{12,4},{1,9},{5,13},{9,1},{13,5},{2,10},{6,14},... | collective-permute-start | bytes 221192 | tf_op jit(solution)/shard_map/ppermute | solution.py:34
  8.3 20.3 %collective-permute-start.2 = (bf16[1,8,4608]{2,1,0:T(8,128)(2,1)S(1)}, bf16[1,8,4608]{2,1,0:T(8,128)(2,1)S(1)}, u32[]{:S(2)}, u32[]{:S(2)}) collective-permute-start(bf16[1,8,4608]{2,1,0:T(8,128)(2,1)S(1)} %dynamic-slice_bitcast_fusion), channel_id=1, source_target_pairs={{0,12},{4,0},{8,4},{12,8},{1,13},{5,1},{9,5},{13,9},{2,14},{6,2},{... | collective-permute-start | bytes 221192 | tf_op jit(solution)/shard_map/ppermute | solution.py:34
  9.7 18.9 %collective-permute-start.3 = (bf16[1024,256]{1,0:T(8,128)(2,1)S(1)}, bf16[1024,256]{1,0:T(8,128)(2,1)}, u32[]{:S(2)}, u32[]{:S(2)}) collective-permute-start(bf16[1024,256]{1,0:T(8,128)(2,1)S(1)} %constant_dynamic-slice_fusion.4), channel_id=1, source_target_pairs={{0,4},{4,8},{8,12},{12,0},{1,5},{5,9},{9,13},{13,1},{2,6},{6,10},{... | collective-permute-start | bytes 1572872 | tf_op jit(solution)/shard_map/ppermute | solution.py:34
  10.4 27.9 %collective-permute-start.9 = (bf16[512,512]{1,0:T(8,128)(2,1)}, bf16[512,512]{1,0:T(8,128)(2,1)}, u32[]{:S(2)}, u32[]{:S(2)}) collective-permute-start(bf16[512,512]{1,0:T(8,128)(2,1)} %bitcast.63), channel_id=1, source_target_pairs={{0,2},{2,0},{1,3},{3,1},{4,6},{6,4},{5,7},{7,5},{8,10},{10,8},{9,1... | collective-permute-start | bytes 1572872 | tf_op jit(solution)/shard_map/ppermute | solution.py:34
  29.4 15.9 %collective-permute-start.6 = (bf16[1024,256]{1,0:T(8,128)(2,1)}, bf16[1024,256]{1,0:T(8,128)(2,1)S(1)}, u32[]{:S(2)}, u32[]{:S(2)}) collective-permute-start(bf16[1024,256]{1,0:T(8,128)(2,1)} %collective-permute-done.3.refs_4_), channel_id=1, source_target_pairs={{0,4},{4,8},{8,12},{12,0},{1,5},{5,9},{9,13},{13,1},{2,6},{6,10},{... | collective-permute-start | bytes 1572872 | tf_op jit(solution)/shard_map/ppermute | solution.py:34
  29.6 15.7 %collective-permute-start.7 = (bf16[1024,256]{1,0:T(8,128)(2,1)}, bf16[1024,256]{1,0:T(8,128)(2,1)S(1)}, u32[]{:S(2)}, u32[]{:S(2)}) collective-permute-start(bf16[1024,256]{1,0:T(8,128)(2,1)} %collective-permute-done.3.refs_4_), channel_id=1, source_target_pairs={{0,16},{16,0},{1,17},{17,1},{2,18},{18,2},{3,19},{19,3},{4,20},{20... | collective-permute-start | bytes 1572872 | tf_op jit(solution)/shard_map/ppermute | solution.py:34
  36.4 5.7 %collective-permute-start.8 = (bf16[512,32]{1,0:T(8,128)(2,1)S(1)}, bf16[512,32]{1,0:T(8,128)(2,1)S(1)}, u32[]{:S(2)}, u32[]{:S(2)}) collective-permute-start(bf16[512,32]{1,0:T(8,128)(2,1)S(1)} %adapter_products.1.refs_0_), channel_id=1, source_target_pairs={{0,2},{2,0},{1,3},{3,1},{4,6},{6,4},{5,7},{7,5},{8,10},{10,8},{9,1... | collective-permute-start | bytes 98312 | tf_op jit(solution)/shard_map/ppermute | solution.py:34
  45.8 15.7 %collective-permute-start.12 = (bf16[1024,256]{1,0:T(8,128)(2,1)S(1)}, bf16[1024,256]{1,0:T(8,128)(2,1)S(1)}, u32[]{:S(2)}, u32[]{:S(2)}) collective-permute-start(bf16[1024,256]{1,0:T(8,128)(2,1)S(1)} %collective-permute-done.6.refs_6_), channel_id=1, source_target_pairs={{0,4},{4,8},{8,12},{12,0},{1,5},{5,9},{9,13},{13,1},{2,6},{6,10},{... | collective-permute-start | bytes 1572872 | tf_op jit(solution)/shard_map/ppermute | solution.py:34
  45.9 15.7 %collective-permute-start.13 = (bf16[1024,256]{1,0:T(8,128)(2,1)S(1)}, bf16[1024,256]{1,0:T(8,128)(2,1)S(1)}, u32[]{:S(2)}, u32[]{:S(2)}) collective-permute-start(bf16[1024,256]{1,0:T(8,128)(2,1)S(1)} %collective-permute-done.6.refs_6_), channel_id=1, source_target_pairs={{0,16},{16,0},{1,17},{17,1},{2,18},{18,2},{3,19},{19,3},{4,20},{20... | collective-permute-start | bytes 1572872 | tf_op jit(solution)/shard_map/ppermute | solution.py:34
  61.6 14.6 %collective-permute-start.14 = (bf16[1024,256]{1,0:T(8,128)(2,1)S(1)}, bf16[1024,256]{1,0:T(8,128)(2,1)S(1)}, u32[]{:S(2)}, u32[]{:S(2)}) collective-permute-start(bf16[1024,256]{1,0:T(8,128)(2,1)S(1)} %collective-permute-done.12.refs_8_), channel_id=1, source_target_pairs={{0,1},{1,0},{2,3},{3,2},{4,5},{5,4},{6,7},{7,6},{8,9},{9,8},{10,11... | collective-permute-start | bytes 1572872 | tf_op jit(solution)/shard_map/ppermute | solution.py:34
  61.6 15.5 %collective-permute-start.19 = (bf16[1024,256]{1,0:T(8,128)(2,1)S(1)}, bf16[1024,256]{1,0:T(8,128)(2,1)S(1)}, u32[]{:S(2)}, u32[]{:S(2)}) collective-permute-start(bf16[1024,256]{1,0:T(8,128)(2,1)S(1)} %collective-permute-done.12.refs_8_), channel_id=1, source_target_pairs={{0,16},{16,0},{1,17},{17,1},{2,18},{18,2},{3,19},{19,3},{4,20},{20... | collective-permute-start | bytes 1572872 | tf_op jit(solution)/shard_map/ppermute | solution.py:34
  63.3 5.9 %collective-permute-start.16 = (bf16[128,32]{1,0:T(8,128)(2,1)S(1)}, bf16[128,32]{1,0:T(8,128)(2,1)S(1)}, u32[]{:S(2)}, u32[]{:S(2)}) collective-permute-start(bf16[128,32]{1,0:T(8,128)(2,1)S(1)} %get-tuple-element.137), channel_id=1, source_target_pairs={{0,4},{4,8},{8,12},{12,0},{1,5},{5,9},{9,13},{13,1},{2,6},{6,10},{... | collective-permute-start | bytes 24584 | tf_op jit(solution)/shard_map/ppermute | solution.py:34
  63.4 6.4 %collective-permute-start.17 = (bf16[128,32]{1,0:T(8,128)(2,1)S(1)}, bf16[128,32]{1,0:T(8,128)(2,1)S(1)}, u32[]{:S(2)}, u32[]{:S(2)}) collective-permute-start(bf16[128,32]{1,0:T(8,128)(2,1)S(1)} %get-tuple-element.138), channel_id=1, source_target_pairs={{0,8},{4,12},{8,0},{12,4},{1,9},{5,13},{9,1},{13,5},{2,10},{6,14},... | collective-permute-start | bytes 24584 | tf_op jit(solution)/shard_map/ppermute | solution.py:34
  66.5 4.0 %collective-permute-start.18 = (bf16[128,32]{1,0:T(8,128)(2,1)S(1)}, bf16[128,32]{1,0:T(8,128)(2,1)S(1)}, u32[]{:S(2)}, u32[]{:S(2)}) collective-permute-start(bf16[128,32]{1,0:T(8,128)(2,1)S(1)} %get-tuple-element.139), channel_id=1, source_target_pairs={{0,12},{4,0},{8,4},{12,8},{1,13},{5,1},{9,5},{13,9},{2,14},{6,2},{... | collective-permute-start | bytes 24584 | tf_op jit(solution)/shard_map/ppermute | solution.py:34
  69.2 8.0 %collective-permute-start.20 = (bf16[512,256]{1,0:T(8,128)(2,1)S(1)}, bf16[512,256]{1,0:T(8,128)(2,1)S(1)}, u32[]{:S(2)}, u32[]{:S(2)}) collective-permute-start(bf16[512,256]{1,0:T(8,128)(2,1)S(1)} %get-tuple-element.216), channel_id=1, source_target_pairs={{0,2},{2,0},{1,3},{3,1},{4,6},{6,4},{5,7},{7,5},{8,10},{10,8},{9,1... | collective-permute-start | bytes 786440 | tf_op jit(solution)/shard_map/ppermute | solution.py:34
  80.5 11.3 %collective-permute-start.23 = (bf16[512,256]{1,0:T(8,128)(2,1)S(1)}, bf16[512,256]{1,0:T(8,128)(2,1)S(1)}, u32[]{:S(2)}, u32[]{:S(2)}) collective-permute-start(bf16[512,256]{1,0:T(8,128)(2,1)S(1)} %get-tuple-element.210), channel_id=1, source_target_pairs={{0,2},{2,0},{1,3},{3,1},{4,6},{6,4},{5,7},{7,5},{8,10},{10,8},{9,1... | collective-permute-start | bytes 786440 | tf_op jit(solution)/shard_map/ppermute | solution.py:34
  81.3 12.5 %collective-permute-start.24 = (bf16[8,4608]{1,0:T(8,128)(2,1)S(1)}, bf16[8,4608]{1,0:T(8,128)(2,1)S(1)}, u32[]{:S(2)}, u32[]{:S(2)}) collective-permute-start(bf16[8,4608]{1,0:T(8,128)(2,1)S(1)} %get-tuple-element.222), channel_id=1, source_target_pairs={{0,12},{4,0},{8,4},{12,8},{1,13},{5,1},{9,5},{13,9},{2,14},{6,2},{... | collective-permute-start | bytes 221192 | tf_op jit(solution)/shard_map/ppermute | solution.py:34
  84.5 9.4 %collective-permute-start.25 = (bf16[8,4608]{1,0:T(8,128)(2,1)S(1)}, bf16[8,4608]{1,0:T(8,128)(2,1)S(1)}, u32[]{:S(2)}, u32[]{:S(2)}) collective-permute-start(bf16[8,4608]{1,0:T(8,128)(2,1)S(1)} %get-tuple-element.221), channel_id=1, source_target_pairs={{0,8},{4,12},{8,0},{12,4},{1,9},{5,13},{9,1},{13,5},{2,10},{6,14},... | collective-permute-start | bytes 221192 | tf_op jit(solution)/shard_map/ppermute | solution.py:34
  84.7 9.2 %collective-permute-start.26 = (bf16[8,4608]{1,0:T(8,128)(2,1)S(1)}, bf16[8,4608]{1,0:T(8,128)(2,1)S(1)}, u32[]{:S(2)}, u32[]{:S(2)}) collective-permute-start(bf16[8,4608]{1,0:T(8,128)(2,1)S(1)} %get-tuple-element.220), channel_id=1, source_target_pairs={{0,4},{4,8},{8,12},{12,0},{1,5},{5,9},{9,13},{13,1},{2,6},{6,10},{... | collective-permute-start | bytes 221192 | tf_op jit(solution)/shard_map/ppermute | solution.py:34
  93.9 5.2 %collective-permute-start.27 = (f32[1,8,4608]{2,1,0:T(8,128)S(1)}, f32[1,8,4608]{2,1,0:T(8,128)S(1)}, u32[]{:S(2)}, u32[]{:S(2)}) collective-permute-start(f32[1,8,4608]{2,1,0:T(8,128)S(1)} %multiply_bitcast_fusion), channel_id=1, source_target_pairs={{0,1},{1,0},{2,3},{3,2},{4,5},{5,4},{6,7},{7,6},{8,9},{9,8},{10,11... | collective-permute-start | bytes 442376 | tf_op jit(solution)/shard_map/ppermute | solution.py:34
  94.0 14.6 %collective-permute-start.28 = (bf16[128,512]{1,0:T(8,128)(2,1)S(1)}, bf16[128,512]{1,0:T(8,128)(2,1)S(1)}, u32[]{:S(2)}, u32[]{:S(2)}) collective-permute-start(bf16[128,512]{1,0:T(8,128)(2,1)S(1)} %get-tuple-element.192), channel_id=1, source_target_pairs={{0,4},{4,8},{8,12},{12,0},{1,5},{5,9},{9,13},{13,1},{2,6},{6,10},{... | collective-permute-start | bytes 393224 | tf_op jit(solution)/shard_map/ppermute | solution.py:34
  96.7 12.0 %collective-permute-start.29 = (bf16[128,512]{1,0:T(8,128)(2,1)S(1)}, bf16[128,512]{1,0:T(8,128)(2,1)S(1)}, u32[]{:S(2)}, u32[]{:S(2)}) collective-permute-start(bf16[128,512]{1,0:T(8,128)(2,1)S(1)} %get-tuple-element.193), channel_id=1, source_target_pairs={{0,8},{4,12},{8,0},{12,4},{1,9},{5,13},{9,1},{13,5},{2,10},{6,14},... | collective-permute-start | bytes 393224 | tf_op jit(solution)/shard_map/ppermute | solution.py:34
  97.8 10.9 %collective-permute-start.30 = (bf16[128,512]{1,0:T(8,128)(2,1)S(1)}, bf16[128,512]{1,0:T(8,128)(2,1)S(1)}, u32[]{:S(2)}, u32[]{:S(2)}) collective-permute-start(bf16[128,512]{1,0:T(8,128)(2,1)S(1)} %get-tuple-element.194), channel_id=1, source_target_pairs={{0,12},{4,0},{8,4},{12,8},{1,13},{5,1},{9,5},{13,9},{2,14},{6,2},{... | collective-permute-start | bytes 393224 | tf_op jit(solution)/shard_map/ppermute | solution.py:34
  (22 other events, 342.2 us)

commit v11 on v10

--- a/solution.py
+++ b/solution.py
@@ -314,7 +314,7 @@
 
 
 def token_gradient_of(z, sc, grads, maps, sums, unfold, job_of, piece_list, quarters, before):
-    tile = min(512, z.fq)
+    tile = min(256, z.fq)
     per = z.fq // tile
     at = z.at["quarter"]
     first, count = quarters[0], len(quarters)

time: 111 us -> 114 us (1.027)
  Pallas kernels: 29.3 us -> 32.5 us
    pallas_call x7, Pallas kernels: 29.3 us -> 32.5 us  [call(): pl.pallas_call(kernel, out_shape=out_shape, grid_spec=pltpu.PrefetchScala...]
  transfers between devices with their start and end apart: 31 -> 31, of which waited for: 9 -> 9; matrix products, arithmetic and copies ran while one was open for 18% -> 18% of each run, Pallas kernels for 25% -> 27%
where the time goes in v11:
time: 114 us; the launch traced here: 113 us
  Pallas kernels  32.5 us (29%)
  starting transfers between devices  30.9 us (27%)
  waiting for transfers between devices  20.1 us (18%)
  local copies, waits for them, and re-layouts  7.8 us (7%)
  matrix products  7.64 us (7%)
  other arithmetic  7.35 us (6%)
  between operations  6.98 us (6%)
    pallas_call x7, Pallas kernels, call(): pl.pallas_call(kernel, out_shape=out_shape, grid_spec=pltpu.PrefetchScala...  32.5 us
    ppermute x31, starting transfers between devices, shifted(): lax.ppermute(values, axis, [(i, (i + step) % count) for i in range(count)])  30.9 us
    ppermute x31, waiting for transfers between devices, shifted(): lax.ppermute(values, axis, [(i, (i + step) % count) for i in range(count)])  20.1 us
    dot_general x13, matrix products, dot(): lax.dot_general(a, b, (dims, ((), ())), precision=precision, preferred_el...  7.64 us
    dynamic_slice x1, local copies, waits for them, and re-layouts, body(): lax.dynamic_slice_in_dim(own_tokens, quarters[r] * zz.fq, zz.fq, 1)  2.81 us
  transfers between devices with their start and end apart: 31, of which 9 were waited for; matrix products, arithmetic and copies ran while one was open for 18% of the time, Pallas kernels for 27%

profile of v11, /device:TPU:0, one launch (start us, length us, event | category | flops | bytes accessed | tf_op | source)
XLA Modules:
  0.0 113.3 jit_solution(322481287557678818)
XLA Ops:
  2.7 3.1 %collective-permute-start = (bf16[1,8,4608]{2,1,0:T(8,128)(2,1)S(1)}, bf16[1,8,4608]{2,1,0:T(8,128)(2,1)S(1)}, u32[]{:S(2)}, u32[]{:S(2)}) collective-permute-start(bf16[1,8,4608]{2,1,0:T(8,128)(2,1)S(1)} %dynamic-slice_bitcast_fusion), channel_id=1, source_target_pairs={{0,4},{4,8},{8,12},{12,0},{1,5},{5,9},{9,13},{13,1},{2,6},{6,10},{... | collective-permute-start | bytes 221192 | tf_op jit(solution)/shard_map/ppermute | solution.py:34
  5.8 2.6 %collective-permute-start.1 = (bf16[1,8,4608]{2,1,0:T(8,128)(2,1)S(1)}, bf16[1,8,4608]{2,1,0:T(8,128)(2,1)S(1)}, u32[]{:S(2)}, u32[]{:S(2)}) collective-permute-start(bf16[1,8,4608]{2,1,0:T(8,128)(2,1)S(1)} %dynamic-slice_bitcast_fusion), channel_id=1, source_target_pairs={{0,8},{4,12},{8,0},{12,4},{1,9},{5,13},{9,1},{13,5},{2,10},{6,14},... | collective-permute-start | bytes 221192 | tf_op jit(solution)/shard_map/ppermute | solution.py:34
  8.3 1.3 %collective-permute-start.2 = (bf16[1,8,4608]{2,1,0:T(8,128)(2,1)S(1)}, bf16[1,8,4608]{2,1,0:T(8,128)(2,1)S(1)}, u32[]{:S(2)}, u32[]{:S(2)}) collective-permute-start(bf16[1,8,4608]{2,1,0:T(8,128)(2,1)S(1)} %dynamic-slice_bitcast_fusion), channel_id=1, source_target_pairs={{0,12},{4,0},{8,4},{12,8},{1,13},{5,1},{9,5},{13,9},{2,14},{6,2},{... | collective-permute-start | bytes 221192 | tf_op jit(solution)/shard_map/ppermute | solution.py:34
  10.4 1.5 %collective-permute-start.9 = (bf16[512,512]{1,0:T(8,128)(2,1)}, bf16[512,512]{1,0:T(8,128)(2,1)}, u32[]{:S(2)}, u32[]{:S(2)}) collective-permute-start(bf16[512,512]{1,0:T(8,128)(2,1)} %bitcast.63), channel_id=1, source_target_pairs={{0,2},{2,0},{1,3},{3,1},{4,6},{6,4},{5,7},{7,5},{8,10},{10,8},{9,1... | collective-permute-start | bytes 1572872 | tf_op jit(solution)/shard_map/ppermute | solution.py:34
  25.7 2.8 %constant_dynamic-slice_fusion = (bf16[512,1024]{1,0:T(8,128)(2,1)S(1)}, bf16[512,1024]{1,0:T(8,128)(2,1)S(1)}, bf16[512,1024]{1,0:T(8,128)(2,1)S(1)}, bf16[512,1024]{1,0:T(8,128)(2,1)S(1)}) fusion(bf16[512,4096]{1,0:T(8,128)(2,1)} %bitcast.59, s32[]{:T(128)S(6)} %select_n.388, s32[]{:T(128)S(6)} %select_n.387, s32[]{:T(128)S(6)} %select_n.386, s32[]{:T(128)S(6)} %select_n.385), kind=kLoop, calls=%fused_computation.79 | loop fusion | bytes 8388624 | tf_op jit(solution)/shard_map/dynamic_slice | solution.py:379
  29.6 1.5 %collective-permute-start.7 = (bf16[1024,256]{1,0:T(8,128)(2,1)}, bf16[1024,256]{1,0:T(8,128)(2,1)S(1)}, u32[]{:S(2)}, u32[]{:S(2)}) collective-permute-start(bf16[1024,256]{1,0:T(8,128)(2,1)} %collective-permute-done.3.refs_4_), channel_id=1, source_target_pairs={{0,16},{16,0},{1,17},{17,1},{2,18},{18,2},{3,19},{19,3},{4,20},{20... | collective-permute-start | bytes 1572872 | tf_op jit(solution)/shard_map/ppermute | solution.py:34
  31.3 5.1 %adapter_products.1.refs_0_ = bf16[512,32]{1,0:T(8,128)(2,1)S(1)} custom-call(s32[78]{0:T(128)S(1)} %concatenate.15.sc, bf16[512,4096]{1,0:T(8,128)(2,1)S(1)} %bitcast.60, bf16[512,512]{1,0:T(8,128)(2,1)S(1)} %bitcast.65, bf16[64,4608]{1,0:T(8,128)(2,1)S(1)} %pad_maximum_fusion.maps, f32[64,16]{1,0:T(8,128)S(1)} %fusion.9.fold, ...), custom_call_target="tpu_custom_call" | custom-call | flops 1000 | bytes 1000 | tf_op jit(solution)/shard_map/adapter_products/pallas_call | solution.py:76
  38.3 3.8 %collective-permute-done.8.refs_1_ = bf16[512,32]{1,0:T(8,128)(2,1)S(1)} collective-permute-done((bf16[512,32]{1,0:T(8,128)(2,1)S(1)}, bf16[512,32]{1,0:T(8,128)(2,1)S(1)}, u32[]{:S(2)}, u32[]{:S(2)}) %collective-permute-start.8) | collective-permute-done | bytes 32800 | tf_op jit(solution)/shard_map/ppermute | solution.py:34
  42.8 2.5 %collective-permute-done.6.refs_6_ = bf16[1024,256]{1,0:T(8,128)(2,1)S(1)} collective-permute-done((bf16[1024,256]{1,0:T(8,128)(2,1)}, bf16[1024,256]{1,0:T(8,128)(2,1)S(1)}, u32[]{:S(2)}, u32[]{:S(2)}) %collective-permute-start.6) | collective-permute-done | bytes 524320 | tf_op jit(solution)/shard_map/ppermute | solution.py:34
  45.9 1.6 %collective-permute-start.13 = (bf16[1024,256]{1,0:T(8,128)(2,1)S(1)}, bf16[1024,256]{1,0:T(8,128)(2,1)S(1)}, u32[]{:S(2)}, u32[]{:S(2)}) collective-permute-start(bf16[1024,256]{1,0:T(8,128)(2,1)S(1)} %collective-permute-done.6.refs_6_), channel_id=1, source_target_pairs={{0,16},{16,0},{1,17},{17,1},{2,18},{18,2},{3,19},{19,3},{4,20},{20... | collective-permute-start | bytes 1572872 | tf_op jit(solution)/shard_map/ppermute | solution.py:34
  49.3 1.5 %fusion.4 = bf16[512,256]{1,0:T(8,128)(2,1)S(1)} fusion(f32[512,256]{1,0:T(8,128)S(1)} %fusion.47, f32[512,256]{1,0:T(8,128)S(1)} %fusion.46, f32[512,256]{1,0:T(8,128)S(1)} %fusion.45, bf16[512,1024]{1,0:T(8,128)(2,1)S(1)} %get-tuple-element.116, bf16[1024,256]{1,0:T(8,128)(2,1)} %collective-permute-done.3.refs_4_), kind=kOutput, calls=%fused_computation.8 | convolution fusion | flops 268959744 | bytes 3407872 | tf_op jit(solution)/shard_map/dot_general | solution.py:42
  50.8 10.7 %collective-permute-done.12.refs_8_ = bf16[1024,256]{1,0:T(8,128)(2,1)S(1)} collective-permute-done((bf16[1024,256]{1,0:T(8,128)(2,1)S(1)}, bf16[1024,256]{1,0:T(8,128)(2,1)S(1)}, u32[]{:S(2)}, u32[]{:S(2)}) %collective-permute-start.12) | collective-permute-done | bytes 524320 | tf_op jit(solution)/shard_map/ppermute | solution.py:34
  61.6 1.6 %collective-permute-start.19 = (bf16[1024,256]{1,0:T(8,128)(2,1)S(1)}, bf16[1024,256]{1,0:T(8,128)(2,1)S(1)}, u32[]{:S(2)}, u32[]{:S(2)}) collective-permute-start(bf16[1024,256]{1,0:T(8,128)(2,1)S(1)} %collective-permute-done.12.refs_8_), channel_id=1, source_target_pairs={{0,16},{16,0},{1,17},{17,1},{2,18},{18,2},{3,19},{19,3},{4,20},{20... | collective-permute-start | bytes 1572872 | tf_op jit(solution)/shard_map/ppermute | solution.py:34
  63.4 2.2 %collective-permute-start.17 = (bf16[128,32]{1,0:T(8,128)(2,1)S(1)}, bf16[128,32]{1,0:T(8,128)(2,1)S(1)}, u32[]{:S(2)}, u32[]{:S(2)}) collective-permute-start(bf16[128,32]{1,0:T(8,128)(2,1)S(1)} %get-tuple-element.138), channel_id=1, source_target_pairs={{0,8},{4,12},{8,0},{12,4},{1,9},{5,13},{9,1},{13,5},{2,10},{6,14},... | collective-permute-start | bytes 24584 | tf_op jit(solution)/shard_map/ppermute | solution.py:34
  66.5 1.6 %collective-permute-start.18 = (bf16[128,32]{1,0:T(8,128)(2,1)S(1)}, bf16[128,32]{1,0:T(8,128)(2,1)S(1)}, u32[]{:S(2)}, u32[]{:S(2)}) collective-permute-start(bf16[128,32]{1,0:T(8,128)(2,1)S(1)} %get-tuple-element.139), channel_id=1, source_target_pairs={{0,12},{4,0},{8,4},{12,8},{1,13},{5,1},{9,5},{13,9},{2,14},{6,2},{... | collective-permute-start | bytes 24584 | tf_op jit(solution)/shard_map/ppermute | solution.py:34
  70.6 5.6 %job_tables.1 = (f32[32,4608]{1,0:T(8,128)S(1)}, bf16[32,4608]{1,0:T(8,128)(2,1)S(1)}) custom-call(s32[78]{0:T(128)S(1)} %concatenate.15.sc, bf16[512,4096]{1,0:T(8,128)(2,1)S(1)} %bitcast.62, bf16[512,512]{1,0:T(8,128)(2,1)S(1)} %bitcast.66, bf16[16,64]{1,0:T(8,128)(2,1)S(1)} %fusion.10.unfold, s32[1,64]{1,0:T(1,128)S(1)} %and_select_fusion.job_of, ...), custom_call_target="tpu_custom_call" | custom-call | flops 1000 | bytes 1000 | tf_op jit(solution)/shard_map/job_tables/pallas_call | solution.py:76
  77.7 1.4 %collective-permute-done.21.refs_9_ = bf16[1024,256]{1,0:T(8,128)(2,1)S(1)} collective-permute-done((bf16[1024,256]{1,0:T(8,128)(2,1)S(1)}, bf16[1024,256]{1,0:T(8,128)(2,1)S(1)}, u32[]{:S(2)}, u32[]{:S(2)}) %collective-permute-start.21) | collective-permute-done | bytes 524320 | tf_op jit(solution)/shard_map/ppermute | solution.py:34
  81.3 3.2 %collective-permute-start.24 = (bf16[8,4608]{1,0:T(8,128)(2,1)S(1)}, bf16[8,4608]{1,0:T(8,128)(2,1)S(1)}, u32[]{:S(2)}, u32[]{:S(2)}) collective-permute-start(bf16[8,4608]{1,0:T(8,128)(2,1)S(1)} %get-tuple-element.222), channel_id=1, source_target_pairs={{0,12},{4,0},{8,4},{12,8},{1,13},{5,1},{9,5},{13,9},{2,14},{6,2},{... | collective-permute-start | bytes 221192 | tf_op jit(solution)/shard_map/ppermute | solution.py:34
  85.4 7.7 %token_gradient_0.1.refs_10_ = bf16[512,4096]{1,0:T(8,128)(2,1)} custom-call(s32[78]{0:T(128)S(1)} %concatenate.15.sc, bf16[64,4608]{1,0:T(8,128)(2,1)S(1)} %pad_maximum_fusion.maps, bf16[512,32]{1,0:T(8,128)(2,1)S(1)} %get-tuple-element.115.sums, bf16[16,64]{1,0:T(8,128)(2,1)S(1)} %fusion.10.unfold, s32[1,64]{1,0:T(1,128)S(1)} %and_select_fusion.job_of, ...), custom_call_target="tpu_custom_call" | custom-call | flops 1000 | bytes 1000 | tf_op jit(solution)/shard_map/token_gradient_0/pallas_call | solution.py:76
  93.2 2.1 %layer.1 = (bf16[128,512]{1,0:T(8,128)(2,1)S(1)}, bf16[128,512]{1,0:T(8,128)(2,1)S(1)}, bf16[128,512]{1,0:T(8,128)(2,1)S(1)}, bf16[128,512]{1,0:T(8,128)(2,1)S(1)}) custom-call(s32[78]{0:T(128)S(1)} %concatenate.15.sc, bf16[512,32]{1,0:T(8,128)(2,1)S(1)} %get-tuple-element.115.sums, bf16[64,4608]{1,0:T(8,128)(2,1)S(1)} %pad_maximum_fusion.maps, ...), custom_call_target="tpu_custom_call" | custom-call | flops 33554432 | bytes 1572864 | tf_op jit(solution)/shard_map/layer/pallas_call | solution.py:76
  95.4 2.7 %collective-permute-start.28 = (bf16[128,512]{1,0:T(8,128)(2,1)S(1)}, bf16[128,512]{1,0:T(8,128)(2,1)S(1)}, u32[]{:S(2)}, u32[]{:S(2)}) collective-permute-start(bf16[128,512]{1,0:T(8,128)(2,1)S(1)} %get-tuple-element.192), channel_id=1, source_target_pairs={{0,4},{4,8},{8,12},{12,0},{1,5},{5,9},{9,13},{13,1},{2,6},{6,10},{... | collective-permute-start | bytes 393224 | tf_op jit(solution)/shard_map/ppermute | solution.py:34
  99.2 1.3 %collective-permute-start.30 = (bf16[128,512]{1,0:T(8,128)(2,1)S(1)}, bf16[128,512]{1,0:T(8,128)(2,1)S(1)}, u32[]{:S(2)}, u32[]{:S(2)}) collective-permute-start(bf16[128,512]{1,0:T(8,128)(2,1)S(1)} %get-tuple-element.194), channel_id=1, source_target_pairs={{0,12},{4,0},{8,4},{12,8},{1,13},{5,1},{9,5},{13,9},{2,14},{6,2},{... | collective-permute-start | bytes 393224 | tf_op jit(solution)/shard_map/ppermute | solution.py:34
  101.9 9.9 %token_gradient_2.1 = bf16[512,4096]{1,0:T(8,128)(2,1)} custom-call(s32[78]{0:T(128)} %copy-done.6, bf16[64,4608]{1,0:T(8,128)(2,1)} %copy-done.2, bf16[512,32]{1,0:T(8,128)(2,1)} %copy-done.4, bf16[16,64]{1,0:T(8,128)(2,1)} %copy-done.5, s32[1,64]{1,0:T(1,128)} %copy-done.8, bf16[512,512]{1,0:T(8,128)(2,1)} %bitcast.64, ...), custom_call_target="tpu_custom_call", output_to_operand_aliasing={{}: (15, {})} | custom-call | flops 2281701376 | bytes 6291456 | tf_op jit(solution)/shard_map/token_gradient_2/pallas_call | solution.py:76
  111.8 1.4 %place.1 = bf16[512,512]{1,0:T(8,128)(2,1)} custom-call(s32[78]{0:T(128)S(1)} %copy-done.7, bf16[128,512]{1,0:T(8,128)(2,1)S(1)} %get-tuple-element.195.refs_0_, bf16[128,512]{1,0:T(8,128)(2,1)S(1)} %collective-permute-done.28.refs_1_, bf16[128,512]{1,0:T(8,128)(2,1)S(1)} %collective-permute-done.29.refs_2_, bf16[128,512]{1,0:T(8,128)(2,1)S(1)} %collective-permute-done.30.refs_3_), custom_call_target="tpu_custom_call" | custom-call | flops 1000 | bytes 1048576 | tf_op jit(solution)/shard_map/place/pallas_call | solution.py:76
  (139 shorter events, 27.5 us)
Async XLA Ops:
  2.7 25.9 %collective-permute-start = (bf16[1,8,4608]{2,1,0:T(8,128)(2,1)S(1)}, bf16[1,8,4608]{2,1,0:T(8,128)(2,1)S(1)}, u32[]{:S(2)}, u32[]{:S(2)}) collective-permute-start(bf16[1,8,4608]{2,1,0:T(8,128)(2,1)S(1)} %dynamic-slice_bitcast_fusion), channel_id=1, source_target_pairs={{0,4},{4,8},{8,12},{12,0},{1,5},{5,9},{9,13},{13,1},{2,6},{6,10},{... | collective-permute-start | bytes 221192 | tf_op jit(solution)/shard_map/ppermute | solution.py:34
  5.8 22.8 %collective-permute-start.1 = (bf16[1,8,4608]{2,1,0:T(8,128)(2,1)S(1)}, bf16[1,8,4608]{2,1,0:T(8,128)(2,1)S(1)}, u32[]{:S(2)}, u32[]{:S(2)}) collective-permute-start(bf16[1,8,4608]{2,1,0:T(8,128)(2,1)S(1)} %dynamic-slice_bitcast_fusion), channel_id=1, source_target_pairs={{0,8},{4,12},{8,0},{12,4},{1,9},{5,13},{9,1},{13,5},{2,10},{6,14},... | collective-permute-start | bytes 221192 | tf_op jit(solution)/shard_map/ppermute | solution.py:34
  8.3 20.3 %collective-permute-start.2 = (bf16[1,8,4608]{2,1,0:T(8,128)(2,1)S(1)}, bf16[1,8,4608]{2,1,0:T(8,128)(2,1)S(1)}, u32[]{:S(2)}, u32[]{:S(2)}) collective-permute-start(bf16[1,8,4608]{2,1,0:T(8,128)(2,1)S(1)} %dynamic-slice_bitcast_fusion), channel_id=1, source_target_pairs={{0,12},{4,0},{8,4},{12,8},{1,13},{5,1},{9,5},{13,9},{2,14},{6,2},{... | collective-permute-start | bytes 221192 | tf_op jit(solution)/shard_map/ppermute | solution.py:34
  9.7 18.9 %collective-permute-start.3 = (bf16[1024,256]{1,0:T(8,128)(2,1)S(1)}, bf16[1024,256]{1,0:T(8,128)(2,1)}, u32[]{:S(2)}, u32[]{:S(2)}) collective-permute-start(bf16[1024,256]{1,0:T(8,128)(2,1)S(1)} %constant_dynamic-slice_fusion.4), channel_id=1, source_target_pairs={{0,4},{4,8},{8,12},{12,0},{1,5},{5,9},{9,13},{13,1},{2,6},{6,10},{... | collective-permute-start | bytes 1572872 | tf_op jit(solution)/shard_map/ppermute | solution.py:34
  10.4 27.9 %collective-permute-start.9 = (bf16[512,512]{1,0:T(8,128)(2,1)}, bf16[512,512]{1,0:T(8,128)(2,1)}, u32[]{:S(2)}, u32[]{:S(2)}) collective-permute-start(bf16[512,512]{1,0:T(8,128)(2,1)} %bitcast.63), channel_id=1, source_target_pairs={{0,2},{2,0},{1,3},{3,1},{4,6},{6,4},{5,7},{7,5},{8,10},{10,8},{9,1... | collective-permute-start | bytes 1572872 | tf_op jit(solution)/shard_map/ppermute | solution.py:34
  29.4 15.9 %collective-permute-start.6 = (bf16[1024,256]{1,0:T(8,128)(2,1)}, bf16[1024,256]{1,0:T(8,128)(2,1)S(1)}, u32[]{:S(2)}, u32[]{:S(2)}) collective-permute-start(bf16[1024,256]{1,0:T(8,128)(2,1)} %collective-permute-done.3.refs_4_), channel_id=1, source_target_pairs={{0,4},{4,8},{8,12},{12,0},{1,5},{5,9},{9,13},{13,1},{2,6},{6,10},{... | collective-permute-start | bytes 1572872 | tf_op jit(solution)/shard_map/ppermute | solution.py:34
  29.6 15.7 %collective-permute-start.7 = (bf16[1024,256]{1,0:T(8,128)(2,1)}, bf16[1024,256]{1,0:T(8,128)(2,1)S(1)}, u32[]{:S(2)}, u32[]{:S(2)}) collective-permute-start(bf16[1024,256]{1,0:T(8,128)(2,1)} %collective-permute-done.3.refs_4_), channel_id=1, source_target_pairs={{0,16},{16,0},{1,17},{17,1},{2,18},{18,2},{3,19},{19,3},{4,20},{20... | collective-permute-start | bytes 1572872 | tf_op jit(solution)/shard_map/ppermute | solution.py:34
  36.4 5.7 %collective-permute-start.8 = (bf16[512,32]{1,0:T(8,128)(2,1)S(1)}, bf16[512,32]{1,0:T(8,128)(2,1)S(1)}, u32[]{:S(2)}, u32[]{:S(2)}) collective-permute-start(bf16[512,32]{1,0:T(8,128)(2,1)S(1)} %adapter_products.1.refs_0_), channel_id=1, source_target_pairs={{0,2},{2,0},{1,3},{3,1},{4,6},{6,4},{5,7},{7,5},{8,10},{10,8},{9,1... | collective-permute-start | bytes 98312 | tf_op jit(solution)/shard_map/ppermute | solution.py:34
  45.8 15.7 %collective-permute-start.12 = (bf16[1024,256]{1,0:T(8,128)(2,1)S(1)}, bf16[1024,256]{1,0:T(8,128)(2,1)S(1)}, u32[]{:S(2)}, u32[]{:S(2)}) collective-permute-start(bf16[1024,256]{1,0:T(8,128)(2,1)S(1)} %collective-permute-done.6.refs_6_), channel_id=1, source_target_pairs={{0,4},{4,8},{8,12},{12,0},{1,5},{5,9},{9,13},{13,1},{2,6},{6,10},{... | collective-permute-start | bytes 1572872 | tf_op jit(solution)/shard_map/ppermute | solution.py:34
  45.9 15.7 %collective-permute-start.13 = (bf16[1024,256]{1,0:T(8,128)(2,1)S(1)}, bf16[1024,256]{1,0:T(8,128)(2,1)S(1)}, u32[]{:S(2)}, u32[]{:S(2)}) collective-permute-start(bf16[1024,256]{1,0:T(8,128)(2,1)S(1)} %collective-permute-done.6.refs_6_), channel_id=1, source_target_pairs={{0,16},{16,0},{1,17},{17,1},{2,18},{18,2},{3,19},{19,3},{4,20},{20... | collective-permute-start | bytes 1572872 | tf_op jit(solution)/shard_map/ppermute | solution.py:34
  61.6 14.6 %collective-permute-start.14 = (bf16[1024,256]{1,0:T(8,128)(2,1)S(1)}, bf16[1024,256]{1,0:T(8,128)(2,1)S(1)}, u32[]{:S(2)}, u32[]{:S(2)}) collective-permute-start(bf16[1024,256]{1,0:T(8,128)(2,1)S(1)} %collective-permute-done.12.refs_8_), channel_id=1, source_target_pairs={{0,1},{1,0},{2,3},{3,2},{4,5},{5,4},{6,7},{7,6},{8,9},{9,8},{10,11... | collective-permute-start | bytes 1572872 | tf_op jit(solution)/shard_map/ppermute | solution.py:34
  61.6 15.5 %collective-permute-start.19 = (bf16[1024,256]{1,0:T(8,128)(2,1)S(1)}, bf16[1024,256]{1,0:T(8,128)(2,1)S(1)}, u32[]{:S(2)}, u32[]{:S(2)}) collective-permute-start(bf16[1024,256]{1,0:T(8,128)(2,1)S(1)} %collective-permute-done.12.refs_8_), channel_id=1, source_target_pairs={{0,16},{16,0},{1,17},{17,1},{2,18},{18,2},{3,19},{19,3},{4,20},{20... | collective-permute-start | bytes 1572872 | tf_op jit(solution)/shard_map/ppermute | solution.py:34
  63.3 5.9 %collective-permute-start.16 = (bf16[128,32]{1,0:T(8,128)(2,1)S(1)}, bf16[128,32]{1,0:T(8,128)(2,1)S(1)}, u32[]{:S(2)}, u32[]{:S(2)}) collective-permute-start(bf16[128,32]{1,0:T(8,128)(2,1)S(1)} %get-tuple-element.137), channel_id=1, source_target_pairs={{0,4},{4,8},{8,12},{12,0},{1,5},{5,9},{9,13},{13,1},{2,6},{6,10},{... | collective-permute-start | bytes 24584 | tf_op jit(solution)/shard_map/ppermute | solution.py:34
  63.4 6.4 %collective-permute-start.17 = (bf16[128,32]{1,0:T(8,128)(2,1)S(1)}, bf16[128,32]{1,0:T(8,128)(2,1)S(1)}, u32[]{:S(2)}, u32[]{:S(2)}) collective-permute-start(bf16[128,32]{1,0:T(8,128)(2,1)S(1)} %get-tuple-element.138), channel_id=1, source_target_pairs={{0,8},{4,12},{8,0},{12,4},{1,9},{5,13},{9,1},{13,5},{2,10},{6,14},... | collective-permute-start | bytes 24584 | tf_op jit(solution)/shard_map/ppermute | solution.py:34
  66.5 4.0 %collective-permute-start.18 = (bf16[128,32]{1,0:T(8,128)(2,1)S(1)}, bf16[128,32]{1,0:T(8,128)(2,1)S(1)}, u32[]{:S(2)}, u32[]{:S(2)}) collective-permute-start(bf16[128,32]{1,0:T(8,128)(2,1)S(1)} %get-tuple-element.139), channel_id=1, source_target_pairs={{0,12},{4,0},{8,4},{12,8},{1,13},{5,1},{9,5},{13,9},{2,14},{6,2},{... | collective-permute-start | bytes 24584 | tf_op jit(solution)/shard_map/ppermute | solution.py:34
  69.2 8.0 %collective-permute-start.20 = (bf16[512,256]{1,0:T(8,128)(2,1)S(1)}, bf16[512,256]{1,0:T(8,128)(2,1)S(1)}, u32[]{:S(2)}, u32[]{:S(2)}) collective-permute-start(bf16[512,256]{1,0:T(8,128)(2,1)S(1)} %get-tuple-element.216), channel_id=1, source_target_pairs={{0,2},{2,0},{1,3},{3,1},{4,6},{6,4},{5,7},{7,5},{8,10},{10,8},{9,1... | collective-permute-start | bytes 786440 | tf_op jit(solution)/shard_map/ppermute | solution.py:34
  80.5 12.7 %collective-permute-start.23 = (bf16[512,256]{1,0:T(8,128)(2,1)S(1)}, bf16[512,256]{1,0:T(8,128)(2,1)S(1)}, u32[]{:S(2)}, u32[]{:S(2)}) collective-permute-start(bf16[512,256]{1,0:T(8,128)(2,1)S(1)} %get-tuple-element.210), channel_id=1, source_target_pairs={{0,2},{2,0},{1,3},{3,1},{4,6},{6,4},{5,7},{7,5},{8,10},{10,8},{9,1... | collective-permute-start | bytes 786440 | tf_op jit(solution)/shard_map/ppermute | solution.py:34
  81.3 13.9 %collective-permute-start.24 = (bf16[8,4608]{1,0:T(8,128)(2,1)S(1)}, bf16[8,4608]{1,0:T(8,128)(2,1)S(1)}, u32[]{:S(2)}, u32[]{:S(2)}) collective-permute-start(bf16[8,4608]{1,0:T(8,128)(2,1)S(1)} %get-tuple-element.222), channel_id=1, source_target_pairs={{0,12},{4,0},{8,4},{12,8},{1,13},{5,1},{9,5},{13,9},{2,14},{6,2},{... | collective-permute-start | bytes 221192 | tf_op jit(solution)/shard_map/ppermute | solution.py:34
  84.5 10.8 %collective-permute-start.25 = (bf16[8,4608]{1,0:T(8,128)(2,1)S(1)}, bf16[8,4608]{1,0:T(8,128)(2,1)S(1)}, u32[]{:S(2)}, u32[]{:S(2)}) collective-permute-start(bf16[8,4608]{1,0:T(8,128)(2,1)S(1)} %get-tuple-element.221), channel_id=1, source_target_pairs={{0,8},{4,12},{8,0},{12,4},{1,9},{5,13},{9,1},{13,5},{2,10},{6,14},... | collective-permute-start | bytes 221192 | tf_op jit(solution)/shard_map/ppermute | solution.py:34
  84.7 10.5 %collective-permute-start.26 = (bf16[8,4608]{1,0:T(8,128)(2,1)S(1)}, bf16[8,4608]{1,0:T(8,128)(2,1)S(1)}, u32[]{:S(2)}, u32[]{:S(2)}) collective-permute-start(bf16[8,4608]{1,0:T(8,128)(2,1)S(1)} %get-tuple-element.220), channel_id=1, source_target_pairs={{0,4},{4,8},{8,12},{12,0},{1,5},{5,9},{9,13},{13,1},{2,6},{6,10},{... | collective-permute-start | bytes 221192 | tf_op jit(solution)/shard_map/ppermute | solution.py:34
  95.3 5.2 %collective-permute-start.27 = (f32[1,8,4608]{2,1,0:T(8,128)S(1)}, f32[1,8,4608]{2,1,0:T(8,128)S(1)}, u32[]{:S(2)}, u32[]{:S(2)}) collective-permute-start(f32[1,8,4608]{2,1,0:T(8,128)S(1)} %multiply_bitcast_fusion), channel_id=1, source_target_pairs={{0,1},{1,0},{2,3},{3,2},{4,5},{5,4},{6,7},{7,6},{8,9},{9,8},{10,11... | collective-permute-start | bytes 442376 | tf_op jit(solution)/shard_map/ppermute | solution.py:34
  95.4 16.4 %collective-permute-start.28 = (bf16[128,512]{1,0:T(8,128)(2,1)S(1)}, bf16[128,512]{1,0:T(8,128)(2,1)S(1)}, u32[]{:S(2)}, u32[]{:S(2)}) collective-permute-start(bf16[128,512]{1,0:T(8,128)(2,1)S(1)} %get-tuple-element.192), channel_id=1, source_target_pairs={{0,4},{4,8},{8,12},{12,0},{1,5},{5,9},{9,13},{13,1},{2,6},{6,10},{... | collective-permute-start | bytes 393224 | tf_op jit(solution)/shard_map/ppermute | solution.py:34
  98.1 13.8 %collective-permute-start.29 = (bf16[128,512]{1,0:T(8,128)(2,1)S(1)}, bf16[128,512]{1,0:T(8,128)(2,1)S(1)}, u32[]{:S(2)}, u32[]{:S(2)}) collective-permute-start(bf16[128,512]{1,0:T(8,128)(2,1)S(1)} %get-tuple-element.193), channel_id=1, source_target_pairs={{0,8},{4,12},{8,0},{12,4},{1,9},{5,13},{9,1},{13,5},{2,10},{6,14},... | collective-permute-start | bytes 393224 | tf_op jit(solution)/shard_map/ppermute | solution.py:34
  99.2 12.6 %collective-permute-start.30 = (bf16[128,512]{1,0:T(8,128)(2,1)S(1)}, bf16[128,512]{1,0:T(8,128)(2,1)S(1)}, u32[]{:S(2)}, u32[]{:S(2)}) collective-permute-start(bf16[128,512]{1,0:T(8,128)(2,1)S(1)} %get-tuple-element.194), channel_id=1, source_target_pairs={{0,12},{4,0},{8,4},{12,8},{1,13},{5,1},{9,5},{13,9},{2,14},{6,2},{... | collective-permute-start | bytes 393224 | tf_op jit(solution)/shard_map/ppermute | solution.py:34
  (22 other events, 350.9 us)

commit v12 on v11

--- a/solution.py
+++ b/solution.py
@@ -314,7 +314,7 @@
 
 
 def token_gradient_of(z, sc, grads, maps, sums, unfold, job_of, piece_list, quarters, before):
-    tile = min(256, z.fq)
+    tile = min(1024, z.fq)
     per = z.fq // tile
     at = z.at["quarter"]
     first, count = quarters[0], len(quarters)
@@ -343,7 +343,7 @@
         jax.ShapeDtypeStruct((z.rows, z.width), bf16), pl.BlockSpec((z.rows, tile), block),
         1000 if alias is None else 2 * z.rows * count * z.fq * (z.nd * z.columns + z.wide),
         1000 if alias is None else 2 * count * z.fq * (z.rows + z.nd * z.columns),
-        (14 if alias is None else 61) * MIB,
+        (20 if alias is None else 61) * MIB,
         scratch=(pltpu.VMEM((z.nd, z.rows, z.columns), bf16), pltpu.VMEM((z.rows, z.wide), bf16)),
         alias=alias,
     )

time: 114 us -> 110 us (0.965)
  Pallas kernels: 32.5 us -> 28.7 us
    pallas_call x7, Pallas kernels: 32.5 us -> 28.7 us  [call(): pl.pallas_call(kernel, out_shape=out_shape, grid_spec=pltpu.PrefetchScala...]
  transfers between devices with their start and end apart: 31 -> 31, of which waited for: 9 -> 9; matrix products, arithmetic and copies ran while one was open for 18% -> 19% of each run, Pallas kernels for 27% -> 25%
where the time goes in v12:
time: 110 us; the launch traced here: 109 us
  starting transfers between devices  30.9 us (28%)
  Pallas kernels  28.7 us (26%)
  waiting for transfers between devices  20.1 us (18%)
  matrix products  7.63 us (7%)
  local copies, waits for them, and re-layouts  7.48 us (7%)
  other arithmetic  7.34 us (7%)
  between operations  7 us (6%)
    ppermute x31, starting transfers between devices, shifted(): lax.ppermute(values, axis, [(i, (i + step) % count) for i in range(count)])  30.9 us
    pallas_call x7, Pallas kernels, call(): pl.pallas_call(kernel, out_shape=out_shape, grid_spec=pltpu.PrefetchScala...  28.7 us
    ppermute x31, waiting for transfers between devices, shifted(): lax.ppermute(values, axis, [(i, (i + step) % count) for i in range(count)])  20.1 us
    dot_general x13, matrix products, dot(): lax.dot_general(a, b, (dims, ((), ())), precision=precision, preferred_el...  7.63 us
    dynamic_slice x1, local copies, waits for them, and re-layouts, body(): lax.dynamic_slice_in_dim(own_tokens, quarters[r] * zz.fq, zz.fq, 1)  2.81 us
  transfers between devices with their start and end apart: 31, of which 9 were waited for; matrix products, arithmetic and copies ran while one was open for 19% of the time, Pallas kernels for 25%

profile of v12, /device:TPU:0, one launch (start us, length us, event | category | flops | bytes accessed | tf_op | source)
XLA Modules:
  0.0 109.1 jit_solution(2978588180056338442)
XLA Ops:
  2.7 3.1 %collective-permute-start = (bf16[1,8,4608]{2,1,0:T(8,128)(2,1)S(1)}, bf16[1,8,4608]{2,1,0:T(8,128)(2,1)S(1)}, u32[]{:S(2)}, u32[]{:S(2)}) collective-permute-start(bf16[1,8,4608]{2,1,0:T(8,128)(2,1)S(1)} %dynamic-slice_bitcast_fusion), channel_id=1, source_target_pairs={{0,4},{4,8},{8,12},{12,0},{1,5},{5,9},{9,13},{13,1},{2,6},{6,10},{... | collective-permute-start | bytes 221192 | tf_op jit(solution)/shard_map/ppermute | solution.py:34
  5.8 2.6 %collective-permute-start.1 = (bf16[1,8,4608]{2,1,0:T(8,128)(2,1)S(1)}, bf16[1,8,4608]{2,1,0:T(8,128)(2,1)S(1)}, u32[]{:S(2)}, u32[]{:S(2)}) collective-permute-start(bf16[1,8,4608]{2,1,0:T(8,128)(2,1)S(1)} %dynamic-slice_bitcast_fusion), channel_id=1, source_target_pairs={{0,8},{4,12},{8,0},{12,4},{1,9},{5,13},{9,1},{13,5},{2,10},{6,14},... | collective-permute-start | bytes 221192 | tf_op jit(solution)/shard_map/ppermute | solution.py:34
  8.3 1.3 %collective-permute-start.2 = (bf16[1,8,4608]{2,1,0:T(8,128)(2,1)S(1)}, bf16[1,8,4608]{2,1,0:T(8,128)(2,1)S(1)}, u32[]{:S(2)}, u32[]{:S(2)}) collective-permute-start(bf16[1,8,4608]{2,1,0:T(8,128)(2,1)S(1)} %dynamic-slice_bitcast_fusion), channel_id=1, source_target_pairs={{0,12},{4,0},{8,4},{12,8},{1,13},{5,1},{9,5},{13,9},{2,14},{6,2},{... | collective-permute-start | bytes 221192 | tf_op jit(solution)/shard_map/ppermute | solution.py:34
  10.4 1.5 %collective-permute-start.9 = (bf16[512,512]{1,0:T(8,128)(2,1)}, bf16[512,512]{1,0:T(8,128)(2,1)}, u32[]{:S(2)}, u32[]{:S(2)}) collective-permute-start(bf16[512,512]{1,0:T(8,128)(2,1)} %bitcast.63), channel_id=1, source_target_pairs={{0,2},{2,0},{1,3},{3,1},{4,6},{6,4},{5,7},{7,5},{8,10},{10,8},{9,1... | collective-permute-start | bytes 1572872 | tf_op jit(solution)/shard_map/ppermute | solution.py:34
  25.7 2.8 %constant_dynamic-slice_fusion = (bf16[512,1024]{1,0:T(8,128)(2,1)S(1)}, bf16[512,1024]{1,0:T(8,128)(2,1)S(1)}, bf16[512,1024]{1,0:T(8,128)(2,1)S(1)}, bf16[512,1024]{1,0:T(8,128)(2,1)S(1)}) fusion(bf16[512,4096]{1,0:T(8,128)(2,1)} %bitcast.59, s32[]{:T(128)S(6)} %select_n.388, s32[]{:T(128)S(6)} %select_n.387, s32[]{:T(128)S(6)} %select_n.386, s32[]{:T(128)S(6)} %select_n.385), kind=kLoop, calls=%fused_computation.79 | loop fusion | bytes 8388624 | tf_op jit(solution)/shard_map/dynamic_slice | solution.py:379
  29.6 1.5 %collective-permute-start.7 = (bf16[1024,256]{1,0:T(8,128)(2,1)}, bf16[1024,256]{1,0:T(8,128)(2,1)S(1)}, u32[]{:S(2)}, u32[]{:S(2)}) collective-permute-start(bf16[1024,256]{1,0:T(8,128)(2,1)} %collective-permute-done.3.refs_4_), channel_id=1, source_target_pairs={{0,16},{16,0},{1,17},{17,1},{2,18},{18,2},{3,19},{19,3},{4,20},{20... | collective-permute-start | bytes 1572872 | tf_op jit(solution)/shard_map/ppermute | solution.py:34
  31.3 5.1 %adapter_products.1.refs_0_ = bf16[512,32]{1,0:T(8,128)(2,1)S(1)} custom-call(s32[78]{0:T(128)S(1)} %concatenate.15.sc, bf16[512,4096]{1,0:T(8,128)(2,1)S(1)} %bitcast.60, bf16[512,512]{1,0:T(8,128)(2,1)S(1)} %bitcast.65, bf16[64,4608]{1,0:T(8,128)(2,1)S(1)} %pad_maximum_fusion.maps, f32[64,16]{1,0:T(8,128)S(1)} %fusion.9.fold, ...), custom_call_target="tpu_custom_call" | custom-call | flops 1000 | bytes 1000 | tf_op jit(solution)/shard_map/adapter_products/pallas_call | solution.py:76
  38.3 3.8 %collective-permute-done.8.refs_1_ = bf16[512,32]{1,0:T(8,128)(2,1)S(1)} collective-permute-done((bf16[512,32]{1,0:T(8,128)(2,1)S(1)}, bf16[512,32]{1,0:T(8,128)(2,1)S(1)}, u32[]{:S(2)}, u32[]{:S(2)}) %collective-permute-start.8) | collective-permute-done | bytes 32800 | tf_op jit(solution)/shard_map/ppermute | solution.py:34
  42.8 2.5 %collective-permute-done.6.refs_6_ = bf16[1024,256]{1,0:T(8,128)(2,1)S(1)} collective-permute-done((bf16[1024,256]{1,0:T(8,128)(2,1)}, bf16[1024,256]{1,0:T(8,128)(2,1)S(1)}, u32[]{:S(2)}, u32[]{:S(2)}) %collective-permute-start.6) | collective-permute-done | bytes 524320 | tf_op jit(solution)/shard_map/ppermute | solution.py:34
  45.9 1.6 %collective-permute-start.13 = (bf16[1024,256]{1,0:T(8,128)(2,1)S(1)}, bf16[1024,256]{1,0:T(8,128)(2,1)S(1)}, u32[]{:S(2)}, u32[]{:S(2)}) collective-permute-start(bf16[1024,256]{1,0:T(8,128)(2,1)S(1)} %collective-permute-done.6.refs_6_), channel_id=1, source_target_pairs={{0,16},{16,0},{1,17},{17,1},{2,18},{18,2},{3,19},{19,3},{4,20},{20... | collective-permute-start | bytes 1572872 | tf_op jit(solution)/shard_map/ppermute | solution.py:34
  49.3 1.5 %fusion.4 = bf16[512,256]{1,0:T(8,128)(2,1)S(1)} fusion(f32[512,256]{1,0:T(8,128)S(1)} %fusion.47, f32[512,256]{1,0:T(8,128)S(1)} %fusion.46, f32[512,256]{1,0:T(8,128)S(1)} %fusion.45, bf16[512,1024]{1,0:T(8,128)(2,1)S(1)} %get-tuple-element.116, bf16[1024,256]{1,0:T(8,128)(2,1)} %collective-permute-done.3.refs_4_), kind=kOutput, calls=%fused_computation.8 | convolution fusion | flops 268959744 | bytes 3407872 | tf_op jit(solution)/shard_map/dot_general | solution.py:42
  50.8 10.7 %collective-permute-done.12.refs_8_ = bf16[1024,256]{1,0:T(8,128)(2,1)S(1)} collective-permute-done((bf16[1024,256]{1,0:T(8,128)(2,1)S(1)}, bf16[1024,256]{1,0:T(8,128)(2,1)S(1)}, u32[]{:S(2)}, u32[]{:S(2)}) %collective-permute-start.12) | collective-permute-done | bytes 524320 | tf_op jit(solution)/shard_map/ppermute | solution.py:34
  61.6 1.6 %collective-permute-start.19 = (bf16[1024,256]{1,0:T(8,128)(2,1)S(1)}, bf16[1024,256]{1,0:T(8,128)(2,1)S(1)}, u32[]{:S(2)}, u32[]{:S(2)}) collective-permute-start(bf16[1024,256]{1,0:T(8,128)(2,1)S(1)} %collective-permute-done.12.refs_8_), channel_id=1, source_target_pairs={{0,16},{16,0},{1,17},{17,1},{2,18},{18,2},{3,19},{19,3},{4,20},{20... | collective-permute-start | bytes 1572872 | tf_op jit(solution)/shard_map/ppermute | solution.py:34
  63.4 2.2 %collective-permute-start.17 = (bf16[128,32]{1,0:T(8,128)(2,1)S(1)}, bf16[128,32]{1,0:T(8,128)(2,1)S(1)}, u32[]{:S(2)}, u32[]{:S(2)}) collective-permute-start(bf16[128,32]{1,0:T(8,128)(2,1)S(1)} %get-tuple-element.138), channel_id=1, source_target_pairs={{0,8},{4,12},{8,0},{12,4},{1,9},{5,13},{9,1},{13,5},{2,10},{6,14},... | collective-permute-start | bytes 24584 | tf_op jit(solution)/shard_map/ppermute | solution.py:34
  66.5 1.6 %collective-permute-start.18 = (bf16[128,32]{1,0:T(8,128)(2,1)S(1)}, bf16[128,32]{1,0:T(8,128)(2,1)S(1)}, u32[]{:S(2)}, u32[]{:S(2)}) collective-permute-start(bf16[128,32]{1,0:T(8,128)(2,1)S(1)} %get-tuple-element.139), channel_id=1, source_target_pairs={{0,12},{4,0},{8,4},{12,8},{1,13},{5,1},{9,5},{13,9},{2,14},{6,2},{... | collective-permute-start | bytes 24584 | tf_op jit(solution)/shard_map/ppermute | solution.py:34
  70.6 5.6 %job_tables.1 = (f32[32,4608]{1,0:T(8,128)S(1)}, bf16[32,4608]{1,0:T(8,128)(2,1)S(1)}) custom-call(s32[78]{0:T(128)S(1)} %concatenate.15.sc, bf16[512,4096]{1,0:T(8,128)(2,1)S(1)} %bitcast.62, bf16[512,512]{1,0:T(8,128)(2,1)S(1)} %bitcast.66, bf16[16,64]{1,0:T(8,128)(2,1)S(1)} %fusion.10.unfold, s32[1,64]{1,0:T(1,128)S(1)} %and_select_fusion.job_of, ...), custom_call_target="tpu_custom_call" | custom-call | flops 1000 | bytes 1000 | tf_op jit(solution)/shard_map/job_tables/pallas_call | solution.py:76
  77.7 1.4 %collective-permute-done.21.refs_9_ = bf16[1024,256]{1,0:T(8,128)(2,1)S(1)} collective-permute-done((bf16[1024,256]{1,0:T(8,128)(2,1)S(1)}, bf16[1024,256]{1,0:T(8,128)(2,1)S(1)}, u32[]{:S(2)}, u32[]{:S(2)}) %collective-permute-start.21) | collective-permute-done | bytes 524320 | tf_op jit(solution)/shard_map/ppermute | solution.py:34
  80.9 3.2 %collective-permute-start.24 = (bf16[8,4608]{1,0:T(8,128)(2,1)S(1)}, bf16[8,4608]{1,0:T(8,128)(2,1)S(1)}, u32[]{:S(2)}, u32[]{:S(2)}) collective-permute-start(bf16[8,4608]{1,0:T(8,128)(2,1)S(1)} %get-tuple-element.222), channel_id=1, source_target_pairs={{0,12},{4,0},{8,4},{12,8},{1,13},{5,1},{9,5},{13,9},{2,14},{6,2},{... | collective-permute-start | bytes 221192 | tf_op jit(solution)/shard_map/ppermute | solution.py:34
  85.1 6.1 %token_gradient_0.1.refs_10_ = bf16[512,4096]{1,0:T(8,128)(2,1)} custom-call(s32[78]{0:T(128)S(1)} %concatenate.15.sc, bf16[64,4608]{1,0:T(8,128)(2,1)S(1)} %pad_maximum_fusion.maps, bf16[512,32]{1,0:T(8,128)(2,1)S(1)} %get-tuple-element.115.sums, bf16[16,64]{1,0:T(8,128)(2,1)S(1)} %fusion.10.unfold, s32[1,64]{1,0:T(1,128)S(1)} %and_select_fusion.job_of, ...), custom_call_target="tpu_custom_call" | custom-call | flops 1000 | bytes 1000 | tf_op jit(solution)/shard_map/token_gradient_0/pallas_call | solution.py:76
  91.2 2.1 %layer.1 = (bf16[128,512]{1,0:T(8,128)(2,1)S(1)}, bf16[128,512]{1,0:T(8,128)(2,1)S(1)}, bf16[128,512]{1,0:T(8,128)(2,1)S(1)}, bf16[128,512]{1,0:T(8,128)(2,1)S(1)}) custom-call(s32[78]{0:T(128)S(1)} %concatenate.15.sc, bf16[512,32]{1,0:T(8,128)(2,1)S(1)} %get-tuple-element.115.sums, bf16[64,4608]{1,0:T(8,128)(2,1)S(1)} %pad_maximum_fusion.maps, ...), custom_call_target="tpu_custom_call" | custom-call | flops 33554432 | bytes 1572864 | tf_op jit(solution)/shard_map/layer/pallas_call | solution.py:76
  93.4 2.6 %collective-permute-start.28 = (bf16[128,512]{1,0:T(8,128)(2,1)S(1)}, bf16[128,512]{1,0:T(8,128)(2,1)S(1)}, u32[]{:S(2)}, u32[]{:S(2)}) collective-permute-start(bf16[128,512]{1,0:T(8,128)(2,1)S(1)} %get-tuple-element.192), channel_id=1, source_target_pairs={{0,4},{4,8},{8,12},{12,0},{1,5},{5,9},{9,13},{13,1},{2,6},{6,10},{... | collective-permute-start | bytes 393224 | tf_op jit(solution)/shard_map/ppermute | solution.py:34
  97.2 1.3 %collective-permute-start.30 = (bf16[128,512]{1,0:T(8,128)(2,1)S(1)}, bf16[128,512]{1,0:T(8,128)(2,1)S(1)}, u32[]{:S(2)}, u32[]{:S(2)}) collective-permute-start(bf16[128,512]{1,0:T(8,128)(2,1)S(1)} %get-tuple-element.194), channel_id=1, source_target_pairs={{0,12},{4,0},{8,4},{12,8},{1,13},{5,1},{9,5},{13,9},{2,14},{6,2},{... | collective-permute-start | bytes 393224 | tf_op jit(solution)/shard_map/ppermute | solution.py:34
  99.9 7.7 %token_gradient_2.1 = bf16[512,4096]{1,0:T(8,128)(2,1)} custom-call(s32[78]{0:T(128)} %copy-done.6, bf16[64,4608]{1,0:T(8,128)(2,1)} %copy-done.2, bf16[512,32]{1,0:T(8,128)(2,1)} %copy-done.4, bf16[16,64]{1,0:T(8,128)(2,1)} %copy-done.5, s32[1,64]{1,0:T(1,128)} %copy-done.8, bf16[512,512]{1,0:T(8,128)(2,1)} %bitcast.64, ...), custom_call_target="tpu_custom_call", output_to_operand_aliasing={{}: (15, {})} | custom-call | flops 2281701376 | bytes 6291456 | tf_op jit(solution)/shard_map/token_gradient_2/pallas_call | solution.py:76
  107.7 1.4 %place.1 = bf16[512,512]{1,0:T(8,128)(2,1)} custom-call(s32[78]{0:T(128)S(1)} %copy-done.7, bf16[128,512]{1,0:T(8,128)(2,1)S(1)} %get-tuple-element.195.refs_0_, bf16[128,512]{1,0:T(8,128)(2,1)S(1)} %collective-permute-done.28.refs_1_, bf16[128,512]{1,0:T(8,128)(2,1)S(1)} %collective-permute-done.29.refs_2_, bf16[128,512]{1,0:T(8,128)(2,1)S(1)} %collective-permute-done.30.refs_3_), custom_call_target="tpu_custom_call" | custom-call | flops 1000 | bytes 1048576 | tf_op jit(solution)/shard_map/place/pallas_call | solution.py:76
  (139 shorter events, 27.2 us)
Async XLA Ops:
  2.7 25.9 %collective-permute-start = (bf16[1,8,4608]{2,1,0:T(8,128)(2,1)S(1)}, bf16[1,8,4608]{2,1,0:T(8,128)(2,1)S(1)}, u32[]{:S(2)}, u32[]{:S(2)}) collective-permute-start(bf16[1,8,4608]{2,1,0:T(8,128)(2,1)S(1)} %dynamic-slice_bitcast_fusion), channel_id=1, source_target_pairs={{0,4},{4,8},{8,12},{12,0},{1,5},{5,9},{9,13},{13,1},{2,6},{6,10},{... | collective-permute-start | bytes 221192 | tf_op jit(solution)/shard_map/ppermute | solution.py:34
  5.8 22.8 %collective-permute-start.1 = (bf16[1,8,4608]{2,1,0:T(8,128)(2,1)S(1)}, bf16[1,8,4608]{2,1,0:T(8,128)(2,1)S(1)}, u32[]{:S(2)}, u32[]{:S(2)}) collective-permute-start(bf16[1,8,4608]{2,1,0:T(8,128)(2,1)S(1)} %dynamic-slice_bitcast_fusion), channel_id=1, source_target_pairs={{0,8},{4,12},{8,0},{12,4},{1,9},{5,13},{9,1},{13,5},{2,10},{6,14},... | collective-permute-start | bytes 221192 | tf_op jit(solution)/shard_map/ppermute | solution.py:34
  8.3 20.3 %collective-permute-start.2 = (bf16[1,8,4608]{2,1,0:T(8,128)(2,1)S(1)}, bf16[1,8,4608]{2,1,0:T(8,128)(2,1)S(1)}, u32[]{:S(2)}, u32[]{:S(2)}) collective-permute-start(bf16[1,8,4608]{2,1,0:T(8,128)(2,1)S(1)} %dynamic-slice_bitcast_fusion), channel_id=1, source_target_pairs={{0,12},{4,0},{8,4},{12,8},{1,13},{5,1},{9,5},{13,9},{2,14},{6,2},{... | collective-permute-start | bytes 221192 | tf_op jit(solution)/shard_map/ppermute | solution.py:34
  9.7 18.9 %collective-permute-start.3 = (bf16[1024,256]{1,0:T(8,128)(2,1)S(1)}, bf16[1024,256]{1,0:T(8,128)(2,1)}, u32[]{:S(2)}, u32[]{:S(2)}) collective-permute-start(bf16[1024,256]{1,0:T(8,128)(2,1)S(1)} %constant_dynamic-slice_fusion.4), channel_id=1, source_target_pairs={{0,4},{4,8},{8,12},{12,0},{1,5},{5,9},{9,13},{13,1},{2,6},{6,10},{... | collective-permute-start | bytes 1572872 | tf_op jit(solution)/shard_map/ppermute | solution.py:34
  10.4 27.9 %collective-permute-start.9 = (bf16[512,512]{1,0:T(8,128)(2,1)}, bf16[512,512]{1,0:T(8,128)(2,1)}, u32[]{:S(2)}, u32[]{:S(2)}) collective-permute-start(bf16[512,512]{1,0:T(8,128)(2,1)} %bitcast.63), channel_id=1, source_target_pairs={{0,2},{2,0},{1,3},{3,1},{4,6},{6,4},{5,7},{7,5},{8,10},{10,8},{9,1... | collective-permute-start | bytes 1572872 | tf_op jit(solution)/shard_map/ppermute | solution.py:34
  29.4 15.9 %collective-permute-start.6 = (bf16[1024,256]{1,0:T(8,128)(2,1)}, bf16[1024,256]{1,0:T(8,128)(2,1)S(1)}, u32[]{:S(2)}, u32[]{:S(2)}) collective-permute-start(bf16[1024,256]{1,0:T(8,128)(2,1)} %collective-permute-done.3.refs_4_), channel_id=1, source_target_pairs={{0,4},{4,8},{8,12},{12,0},{1,5},{5,9},{9,13},{13,1},{2,6},{6,10},{... | collective-permute-start | bytes 1572872 | tf_op jit(solution)/shard_map/ppermute | solution.py:34
  29.6 15.7 %collective-permute-start.7 = (bf16[1024,256]{1,0:T(8,128)(2,1)}, bf16[1024,256]{1,0:T(8,128)(2,1)S(1)}, u32[]{:S(2)}, u32[]{:S(2)}) collective-permute-start(bf16[1024,256]{1,0:T(8,128)(2,1)} %collective-permute-done.3.refs_4_), channel_id=1, source_target_pairs={{0,16},{16,0},{1,17},{17,1},{2,18},{18,2},{3,19},{19,3},{4,20},{20... | collective-permute-start | bytes 1572872 | tf_op jit(solution)/shard_map/ppermute | solution.py:34
  36.4 5.7 %collective-permute-start.8 = (bf16[512,32]{1,0:T(8,128)(2,1)S(1)}, bf16[512,32]{1,0:T(8,128)(2,1)S(1)}, u32[]{:S(2)}, u32[]{:S(2)}) collective-permute-start(bf16[512,32]{1,0:T(8,128)(2,1)S(1)} %adapter_products.1.refs_0_), channel_id=1, source_target_pairs={{0,2},{2,0},{1,3},{3,1},{4,6},{6,4},{5,7},{7,5},{8,10},{10,8},{9,1... | collective-permute-start | bytes 98312 | tf_op jit(solution)/shard_map/ppermute | solution.py:34
  45.8 15.7 %collective-permute-start.12 = (bf16[1024,256]{1,0:T(8,128)(2,1)S(1)}, bf16[1024,256]{1,0:T(8,128)(2,1)S(1)}, u32[]{:S(2)}, u32[]{:S(2)}) collective-permute-start(bf16[1024,256]{1,0:T(8,128)(2,1)S(1)} %collective-permute-done.6.refs_6_), channel_id=1, source_target_pairs={{0,4},{4,8},{8,12},{12,0},{1,5},{5,9},{9,13},{13,1},{2,6},{6,10},{... | collective-permute-start | bytes 1572872 | tf_op jit(solution)/shard_map/ppermute | solution.py:34
  45.9 15.7 %collective-permute-start.13 = (bf16[1024,256]{1,0:T(8,128)(2,1)S(1)}, bf16[1024,256]{1,0:T(8,128)(2,1)S(1)}, u32[]{:S(2)}, u32[]{:S(2)}) collective-permute-start(bf16[1024,256]{1,0:T(8,128)(2,1)S(1)} %collective-permute-done.6.refs_6_), channel_id=1, source_target_pairs={{0,16},{16,0},{1,17},{17,1},{2,18},{18,2},{3,19},{19,3},{4,20},{20... | collective-permute-start | bytes 1572872 | tf_op jit(solution)/shard_map/ppermute | solution.py:34
  61.6 14.6 %collective-permute-start.14 = (bf16[1024,256]{1,0:T(8,128)(2,1)S(1)}, bf16[1024,256]{1,0:T(8,128)(2,1)S(1)}, u32[]{:S(2)}, u32[]{:S(2)}) collective-permute-start(bf16[1024,256]{1,0:T(8,128)(2,1)S(1)} %collective-permute-done.12.refs_8_), channel_id=1, source_target_pairs={{0,1},{1,0},{2,3},{3,2},{4,5},{5,4},{6,7},{7,6},{8,9},{9,8},{10,11... | collective-permute-start | bytes 1572872 | tf_op jit(solution)/shard_map/ppermute | solution.py:34
  61.6 15.5 %collective-permute-start.19 = (bf16[1024,256]{1,0:T(8,128)(2,1)S(1)}, bf16[1024,256]{1,0:T(8,128)(2,1)S(1)}, u32[]{:S(2)}, u32[]{:S(2)}) collective-permute-start(bf16[1024,256]{1,0:T(8,128)(2,1)S(1)} %collective-permute-done.12.refs_8_), channel_id=1, source_target_pairs={{0,16},{16,0},{1,17},{17,1},{2,18},{18,2},{3,19},{19,3},{4,20},{20... | collective-permute-start | bytes 1572872 | tf_op jit(solution)/shard_map/ppermute | solution.py:34
  63.3 5.9 %collective-permute-start.16 = (bf16[128,32]{1,0:T(8,128)(2,1)S(1)}, bf16[128,32]{1,0:T(8,128)(2,1)S(1)}, u32[]{:S(2)}, u32[]{:S(2)}) collective-permute-start(bf16[128,32]{1,0:T(8,128)(2,1)S(1)} %get-tuple-element.137), channel_id=1, source_target_pairs={{0,4},{4,8},{8,12},{12,0},{1,5},{5,9},{9,13},{13,1},{2,6},{6,10},{... | collective-permute-start | bytes 24584 | tf_op jit(solution)/shard_map/ppermute | solution.py:34
  63.4 6.4 %collective-permute-start.17 = (bf16[128,32]{1,0:T(8,128)(2,1)S(1)}, bf16[128,32]{1,0:T(8,128)(2,1)S(1)}, u32[]{:S(2)}, u32[]{:S(2)}) collective-permute-start(bf16[128,32]{1,0:T(8,128)(2,1)S(1)} %get-tuple-element.138), channel_id=1, source_target_pairs={{0,8},{4,12},{8,0},{12,4},{1,9},{5,13},{9,1},{13,5},{2,10},{6,14},... | collective-permute-start | bytes 24584 | tf_op jit(solution)/shard_map/ppermute | solution.py:34
  66.5 4.0 %collective-permute-start.18 = (bf16[128,32]{1,0:T(8,128)(2,1)S(1)}, bf16[128,32]{1,0:T(8,128)(2,1)S(1)}, u32[]{:S(2)}, u32[]{:S(2)}) collective-permute-start(bf16[128,32]{1,0:T(8,128)(2,1)S(1)} %get-tuple-element.139), channel_id=1, source_target_pairs={{0,12},{4,0},{8,4},{12,8},{1,13},{5,1},{9,5},{13,9},{2,14},{6,2},{... | collective-permute-start | bytes 24584 | tf_op jit(solution)/shard_map/ppermute | solution.py:34
  69.2 8.0 %collective-permute-start.20 = (bf16[512,256]{1,0:T(8,128)(2,1)S(1)}, bf16[512,256]{1,0:T(8,128)(2,1)S(1)}, u32[]{:S(2)}, u32[]{:S(2)}) collective-permute-start(bf16[512,256]{1,0:T(8,128)(2,1)S(1)} %get-tuple-element.216), channel_id=1, source_target_pairs={{0,2},{2,0},{1,3},{3,1},{4,6},{6,4},{5,7},{7,5},{8,10},{10,8},{9,1... | collective-permute-start | bytes 786440 | tf_op jit(solution)/shard_map/ppermute | solution.py:34
  80.1 11.0 %collective-permute-start.23 = (bf16[512,256]{1,0:T(8,128)(2,1)S(1)}, bf16[512,256]{1,0:T(8,128)(2,1)S(1)}, u32[]{:S(2)}, u32[]{:S(2)}) collective-permute-start(bf16[512,256]{1,0:T(8,128)(2,1)S(1)} %get-tuple-element.210), channel_id=1, source_target_pairs={{0,2},{2,0},{1,3},{3,1},{4,6},{6,4},{5,7},{7,5},{8,10},{10,8},{9,1... | collective-permute-start | bytes 786440 | tf_op jit(solution)/shard_map/ppermute | solution.py:34
  80.9 12.3 %collective-permute-start.24 = (bf16[8,4608]{1,0:T(8,128)(2,1)S(1)}, bf16[8,4608]{1,0:T(8,128)(2,1)S(1)}, u32[]{:S(2)}, u32[]{:S(2)}) collective-permute-start(bf16[8,4608]{1,0:T(8,128)(2,1)S(1)} %get-tuple-element.222), channel_id=1, source_target_pairs={{0,12},{4,0},{8,4},{12,8},{1,13},{5,1},{9,5},{13,9},{2,14},{6,2},{... | collective-permute-start | bytes 221192 | tf_op jit(solution)/shard_map/ppermute | solution.py:34
  84.1 9.2 %collective-permute-start.25 = (bf16[8,4608]{1,0:T(8,128)(2,1)S(1)}, bf16[8,4608]{1,0:T(8,128)(2,1)S(1)}, u32[]{:S(2)}, u32[]{:S(2)}) collective-permute-start(bf16[8,4608]{1,0:T(8,128)(2,1)S(1)} %get-tuple-element.221), channel_id=1, source_target_pairs={{0,8},{4,12},{8,0},{12,4},{1,9},{5,13},{9,1},{13,5},{2,10},{6,14},... | collective-permute-start | bytes 221192 | tf_op jit(solution)/shard_map/ppermute | solution.py:34
  84.3 9.0 %collective-permute-start.26 = (bf16[8,4608]{1,0:T(8,128)(2,1)S(1)}, bf16[8,4608]{1,0:T(8,128)(2,1)S(1)}, u32[]{:S(2)}, u32[]{:S(2)}) collective-permute-start(bf16[8,4608]{1,0:T(8,128)(2,1)S(1)} %get-tuple-element.220), channel_id=1, source_target_pairs={{0,4},{4,8},{8,12},{12,0},{1,5},{5,9},{9,13},{13,1},{2,6},{6,10},{... | collective-permute-start | bytes 221192 | tf_op jit(solution)/shard_map/ppermute | solution.py:34
  93.3 5.2 %collective-permute-start.27 = (f32[1,8,4608]{2,1,0:T(8,128)S(1)}, f32[1,8,4608]{2,1,0:T(8,128)S(1)}, u32[]{:S(2)}, u32[]{:S(2)}) collective-permute-start(f32[1,8,4608]{2,1,0:T(8,128)S(1)} %multiply_bitcast_fusion), channel_id=1, source_target_pairs={{0,1},{1,0},{2,3},{3,2},{4,5},{5,4},{6,7},{7,6},{8,9},{9,8},{10,11... | collective-permute-start | bytes 442376 | tf_op jit(solution)/shard_map/ppermute | solution.py:34
  93.4 14.2 %collective-permute-start.28 = (bf16[128,512]{1,0:T(8,128)(2,1)S(1)}, bf16[128,512]{1,0:T(8,128)(2,1)S(1)}, u32[]{:S(2)}, u32[]{:S(2)}) collective-permute-start(bf16[128,512]{1,0:T(8,128)(2,1)S(1)} %get-tuple-element.192), channel_id=1, source_target_pairs={{0,4},{4,8},{8,12},{12,0},{1,5},{5,9},{9,13},{13,1},{2,6},{6,10},{... | collective-permute-start | bytes 393224 | tf_op jit(solution)/shard_map/ppermute | solution.py:34
  96.1 11.6 %collective-permute-start.29 = (bf16[128,512]{1,0:T(8,128)(2,1)S(1)}, bf16[128,512]{1,0:T(8,128)(2,1)S(1)}, u32[]{:S(2)}, u32[]{:S(2)}) collective-permute-start(bf16[128,512]{1,0:T(8,128)(2,1)S(1)} %get-tuple-element.193), channel_id=1, source_target_pairs={{0,8},{4,12},{8,0},{12,4},{1,9},{5,13},{9,1},{13,5},{2,10},{6,14},... | collective-permute-start | bytes 393224 | tf_op jit(solution)/shard_map/ppermute | solution.py:34
  97.2 10.5 %collective-permute-start.30 = (bf16[128,512]{1,0:T(8,128)(2,1)S(1)}, bf16[128,512]{1,0:T(8,128)(2,1)S(1)}, u32[]{:S(2)}, u32[]{:S(2)}) collective-permute-start(bf16[128,512]{1,0:T(8,128)(2,1)S(1)} %get-tuple-element.194), channel_id=1, source_target_pairs={{0,12},{4,0},{8,4},{12,8},{1,13},{5,1},{9,5},{13,9},{2,14},{6,2},{... | collective-permute-start | bytes 393224 | tf_op jit(solution)/shard_map/ppermute | solution.py:34
  (22 other events, 338.3 us)
